TPU v7x, 32 devices: a whole 2x2x4 slice. The times are simulated.
32 devices in a mesh: lat: 4 (over x, core), lon: 8 (over z, y).
Axes of the slice: x: 2, y: 2, z: 4, core: 2. Of those that a mesh axis runs over, the one named last changes fastest.
Arguments:
- student: bfloat16 [2, 16, 256, 256], P(None, 'lat', 'lon'), may hold values from -6 to 6
- teacher: bfloat16 [2, 16, 256, 256], P(None, None, ('lon', 'lat')), may hold values from -6 to 6
- dw_weight: float32 [7, 7, 256], replicated, may hold values from -0.875 to 0.875
- norm_gain: float32 [256], replicated, may hold values from 0.1 to 1.9
- w_in: bfloat16 [256, 1024], replicated, may hold values from -0.375 to 0.375
- w_out: bfloat16 [1024, 256], replicated, may hold values from -0.1875 to 0.1875
- layer_scale: float32 [256], replicated, may hold values from 0.3 to 1.5
Outputs:
- grad_student: bfloat16 [2, 16, 256, 256], P(None, 'lat', 'lon')
- grad_w_in: float32 [256, 1024], replicated
- grad_w_out: float32 [1024, 256], replicated
- grad_dw: float32 [7, 7, 256], replicated
All inputs are finite; a program needn't handle non-finite values.
Results may differ from a plain program's by a relative error of at most 0.0034.
The roundings to bfloat16 on the way count: a program that leaves them out, or rounds other values in their place, can miss the bound.
Values may be sent and summed in bfloat16 or wider, within the bound.
No kernel may reach another device: no remote copies, remote signals or barrier semaphores. Data moves between devices by JAX's collectives and lax.ppermute only.
A program may use at most 64 MiB of HBM per device.

v0:
```python
import jax
import jax.numpy as jnp
from jax import lax
from jax.sharding import PartitionSpec as P

slope_coef = 0.7978845608028654
cubic_coef = 0.044715
norm_eps = 1e-06


def with_halo(block, sides, width, periodic):
    for axis, dim in sides:
        count = lax.axis_size(axis)
        forward = [(i, i + 1) for i in range(count - 1)]
        if periodic:
            forward.append((count - 1, 0))
        backward = [(target, source) for source, target in forward]
        low = lax.ppermute(
            lax.slice_in_dim(block, block.shape[dim] - width, None, axis=dim), axis, forward
        )
        high = lax.ppermute(lax.slice_in_dim(block, 0, width, axis=dim), axis, backward)
        block = jnp.concatenate([low, block, high], axis=dim)
    return block


def gelu_tanh(values):
    tanh_arg = slope_coef * (values + cubic_coef * values * values * values)
    return 0.5 * values * (1.0 + jnp.tanh(tanh_arg))


def gelu_slope(values):
    tangent = jnp.tanh(slope_coef * (values + cubic_coef * values * values * values))
    return 0.5 * (1.0 + tangent) + 0.5 * values * (1.0 - tangent * tangent) * slope_coef * (
        1.0 + 3.0 * cubic_coef * values * values
    )


def apply_stencil(padded, dw_weight, tile_rows, tile_cols, flipped):
    kernel_size = dw_weight.shape[0]
    result = jnp.zeros((padded.shape[0], tile_rows, tile_cols, padded.shape[3]), jnp.float32)
    for row_off in range(kernel_size):
        for col_off in range(kernel_size):
            row_start = kernel_size - 1 - row_off if flipped else row_off
            col_start = kernel_size - 1 - col_off if flipped else col_off
            result = (
                result
                + dw_weight[row_off, col_off]
                * padded[:, row_start : row_start + tile_rows, col_start : col_start + tile_cols]
            )
    return result


def local(student, teacher, dw_weight, norm_gain, w_in, w_out, layer_scale):
    batch_size, tile_rows, tile_cols, channel_count = student.shape
    kernel_size = dw_weight.shape[0]
    half_kernel = kernel_size // 2
    cell_total = batch_size * tile_rows * lax.axis_size("lat") * tile_cols * lax.axis_size("lon")
    lon_padded = with_halo(student, (("lon", 2),), half_kernel, True)
    padded_bf = with_halo(lon_padded, (("lat", 1),), half_kernel, False)
    padded = padded_bf.astype(jnp.float32)
    smoothed = apply_stencil(padded, dw_weight, tile_rows, tile_cols, False).reshape(
        -1, channel_count
    )
    average = jnp.mean(smoothed, axis=-1, keepdims=True)
    centred = smoothed - average
    variance = jnp.mean(centred * centred, axis=-1, keepdims=True)
    inv_std = lax.rsqrt(variance + norm_eps)
    unit_norm = centred * inv_std
    normed = (unit_norm * norm_gain).astype(jnp.bfloat16)
    preact = jnp.dot(normed, w_in, preferred_element_type=jnp.float32)
    hidden = gelu_tanh(preact).astype(jnp.bfloat16)
    mlp_out = jnp.dot(hidden, w_out, preferred_element_type=jnp.float32)
    output = student.reshape(-1, channel_count).astype(jnp.float32) + layer_scale * mlp_out
    target = lax.all_to_all(teacher, "lat", split_axis=1, concat_axis=2, tiled=True)
    misfit = output - target.reshape(-1, channel_count).astype(jnp.float32)
    out_grad = (layer_scale * misfit).astype(jnp.bfloat16)
    part_out = lax.dot_general(
        hidden, out_grad, (((0,), (0,)), ((), ())), preferred_element_type=jnp.float32
    )
    hidden_grad = lax.dot_general(
        out_grad, w_out, (((1,), (1,)), ((), ())), preferred_element_type=jnp.float32
    )
    preact_grad = (hidden_grad * gelu_slope(preact)).astype(jnp.bfloat16)
    part_in = lax.dot_general(
        normed, preact_grad, (((0,), (0,)), ((), ())), preferred_element_type=jnp.float32
    )
    normed_grad = lax.dot_general(
        preact_grad, w_in, (((1,), (1,)), ((), ())), preferred_element_type=jnp.float32
    )
    unit_grad = normed_grad * norm_gain
    first_mean = jnp.mean(unit_grad, axis=-1, keepdims=True)
    second_mean = jnp.mean(unit_grad * unit_norm, axis=-1, keepdims=True)
    conv_grad = (inv_std * (unit_grad - first_mean - unit_norm * second_mean)).astype(jnp.bfloat16)
    conv_grid = conv_grad.reshape(student.shape)
    grad_lon = with_halo(conv_grid, (("lon", 2),), half_kernel, True)
    padded_grad = with_halo(grad_lon, (("lat", 1),), half_kernel, False).astype(jnp.float32)
    back_conv = apply_stencil(padded_grad, dw_weight, tile_rows, tile_cols, True)
    grad_student = (misfit.reshape(student.shape) + back_conv).astype(jnp.bfloat16)
    conv_grad_f = conv_grid.astype(jnp.float32)
    kernel_terms = []
    for row_off in range(kernel_size):
        for col_off in range(kernel_size):
            kernel_terms.append(
                jnp.sum(
                    padded[:, row_off : row_off + tile_rows, col_off : col_off + tile_cols]
                    * conv_grad_f,
                    axis=(0, 1, 2),
                )
            )
    part_dw = jnp.stack(kernel_terms).reshape(kernel_size, kernel_size, channel_count)
    sum_in, sum_out, sum_dw = lax.psum((part_in, part_out, part_dw), ("lat", "lon"))
    return (grad_student, sum_in / cell_total, sum_out / cell_total, sum_dw / cell_total)


def solution(mesh):
    placed = (
        P(None, "lat", "lon", None),
        P(None, None, ("lon", "lat"), None),
        P(),
        P(),
        P(),
        P(),
        P(),
    )
    return jax.shard_map(
        local,
        mesh=mesh,
        in_specs=placed,
        out_specs=(P(None, "lat", "lon", None), P(), P(), P()),
        check_vma=False,
    )
```

profile of v0, /device:TPU:0, one launch (start us, length us, event | category | flops | bytes accessed | tf_op | source)
XLA Modules:
  0.0 185.1 jit_solution(9501663832777897091)
XLA Ops:
  7.2 0.9 fusion.114
  8.0 3.0 %collective-permute-start = (bf16[2,4,3,256]{3,2,1,0:T(4,128)(2,1)S(1)}, bf16[2,4,3,256]{3,2,1,0:T(4,128)(2,1)S(1)}, u32[]{:S(2)}, u32[]{:S(2)}) collective-permute-start(bf16[2,4,3,256]{3,2,1,0:T(4,128)(2,1)S(1)} %get-tuple-element.66), channel_id=1, source_target_pairs={{0,1},{1,2},{2,3},{3,4},{4,5},{5,6},{6,7},{7,0},{8,9},{9,10},{10,1... | collective-permute-start | bytes 36872 | tf_op jit(solution)/shard_map/ppermute | solution.py:18
  11.1 3.1 %collective-permute-start.1 = (bf16[2,4,3,256]{3,2,1,0:T(4,128)(2,1)S(1)}, bf16[2,4,3,256]{3,2,1,0:T(4,128)(2,1)S(1)}, u32[]{:S(2)}, u32[]{:S(2)}) collective-permute-start(bf16[2,4,3,256]{3,2,1,0:T(4,128)(2,1)S(1)} %get-tuple-element.67), channel_id=1, source_target_pairs={{1,0},{2,1},{3,2},{4,3},{5,4},{6,5},{7,6},{0,7},{9,8},{10,9},{11,1... | collective-permute-start | bytes 36872 | tf_op jit(solution)/shard_map/ppermute | solution.py:21
  14.2 1.6 copy.12
  15.7 3.5 %all-to-all-start = ((bf16[2,16,8,256]{3,2,0,1:T(8,128)(2,1)}), bf16[2,16,8,256]{3,2,0,1:T(8,128)(2,1)S(1)}, u32[]{:S(2)}, u32[]{:S(2)}) async-start(bf16[2,16,8,256]{3,2,0,1:T(8,128)(2,1)} %copy.12), calls=%async_computation | async-start | bytes 262144 | tf_op jit(solution)/shard_map/all_to_all | solution.py:74
  19.4 2.3 %collective-permute-start.2 = (bf16[2,3,38,256]{3,2,1,0:T(8,128)(2,1)S(1)}, bf16[2,3,38,256]{3,2,1,0:T(8,128)(2,1)S(1)}, u32[]{:S(2)}, u32[]{:S(2)}) collective-permute-start(bf16[2,3,38,256]{3,2,1,0:T(8,128)(2,1)S(1)} %get-tuple-element.62), channel_id=1, source_target_pairs={{0,8},{8,16},{16,24},{1,9},{9,17},{17,25},{2,10},{10,18},{18,26},{... | collective-permute-start | bytes 350216 | tf_op jit(solution)/shard_map/ppermute | solution.py:18
  21.8 1.3 collective-permute-start.3
  23.1 0.7 all-to-all-done
  23.8 2.3 %collective-permute-done.3 = bf16[2,3,38,256]{3,2,1,0:T(8,128)(2,1)S(1)} collective-permute-done((bf16[2,3,38,256]{3,2,1,0:T(8,128)(2,1)S(1)}, bf16[2,3,38,256]{3,2,1,0:T(8,128)(2,1)S(1)}, u32[]{:S(2)}, u32[]{:S(2)}) %collective-permute-start.3) | collective-permute-done | bytes 116768 | tf_op jit(solution)/shard_map/ppermute | solution.py:21
  26.2 1.9 %fusion.110 = (f32[2,4,32]{2,1,0:T(4,128)S(1)}, f32[2,4,32,256]{3,2,1,0:T(8,128)S(1)}) fusion(f32[2,10,38,256]{3,2,1,0:T(8,128)S(1)} %maximum_convert_fusion, f32[256]{0:T(256)S(1)} %bitcast.276, f32[256]{0:T(256)S(1)} %bitcast.278, f32[256]{0:T(256)S(1)} %bitcast.184, f32[256]{0:T(256)S(1)} %bitcast.186, f32[256]{0:T(256)S(1)} %bitcast.188, ...), kind=kLoop, calls=%fused_computation.232 | loop fusion | flops 6422272 | bytes 13158400 | tf_op jit(solution)/shard_map/reduce_sum | solution.py:64
  28.1 0.2 multiply_reduce_fusion.1
  28.4 0.6 copy-done.4
  29.2 0.3 fusion.118
  29.5 0.7 copy-done.5
  30.2 0.5 fusion.2
  30.7 0.8 fusion
  31.5 0.5 fusion.109
  32.0 0.6 fusion.56
  32.6 0.5 fusion.38
  33.2 0.4 fusion.20
  33.6 1.6 fusion.108
  35.1 1.3 fusion.119
  36.7 4.7 %collective-permute-start.5 = (bf16[2,4,3,256]{3,2,1,0:T(4,128)(2,1)S(1)}, bf16[2,4,3,256]{3,2,1,0:T(4,128)(2,1)S(1)}, u32[]{:S(2)}, u32[]{:S(2)}) collective-permute-start(bf16[2,4,3,256]{3,2,1,0:T(4,128)(2,1)S(1)} %get-tuple-element.65), channel_id=1, source_target_pairs={{1,0},{2,1},{3,2},{4,3},{5,4},{6,5},{7,6},{0,7},{9,8},{10,9},{11,1... | collective-permute-start | bytes 36872 | tf_op jit(solution)/shard_map/ppermute | solution.py:21
  41.4 39.1 %psum.23 = f32[7,7,256]{2,1,0:T(8,128)S(1)} all-reduce(f32[7,7,256]{2,1,0:T(8,128)S(1)} %reshape.123), channel_id=1, replica_groups=mesh['lat'=4,'lon'=8] {'lat','lon'}, use_global_device_ids=true, to_apply=%region_55.0 | all-reduce | flops 12544 | bytes 100352 | tf_op jit(solution)/shard_map/psum | solution.py:111
  80.6 1.4 collective-permute-start.6
  82.0 1.3 collective-permute-start.7
  83.3 0.6 broadcast_multiply_fusion.2
  83.9 3.7 %collective-permute-done.7 = bf16[2,3,38,256]{3,2,1,0:T(8,128)(2,1)S(1)} collective-permute-done((bf16[2,3,38,256]{3,2,1,0:T(8,128)(2,1)S(1)}, bf16[2,3,38,256]{3,2,1,0:T(8,128)(2,1)S(1)}, u32[]{:S(2)}, u32[]{:S(2)}) %collective-permute-start.7) | collective-permute-done | bytes 116768 | tf_op jit(solution)/shard_map/ppermute | solution.py:21
  87.7 2.5 %fusion.59 = bf16[2,4,32,256]{3,2,1,0:T(8,128)(2,1)} fusion(f32[2,4,32,256]{3,2,1,0:T(8,128)S(1)} %bitcast.181, f32[2,10,38,256]{3,2,1,0:T(8,128)S(1)} %maximum_convert_fusion.1, f32[256]{0:T(256)S(1)} %bitcast.277, f32[256]{0:T(256)S(1)} %bitcast.279, f32[256]{0:T(256)S(1)} %bitcast.185, f32[256]{0:T(256)S(1)} %bitcast.187, f32[256]{0:T(256)S(1)} %bitcast.189, ...), kind=kLoop, calls=%fused_computation.119 | loop fusion | flops 6488064 | bytes 13288448 | tf_op jit(solution)/shard_map/convert_element_type | solution.py:98
  90.2 84.5 %all-reduce.3.cloned.1.call-done = (f32[256,1024]{1,0:T(8,128)}, f32[1024,256]{1,0:T(8,128)}) async-done(((f32[256,1024]{1,0:T(8,128)}, f32[1024,256]{1,0:T(8,128)}), (f32[256,1024]{1,0:T(8,128)}, f32[1024,256]{1,0:T(8,128)})) %all-reduce.3.cloned.1.call-update) | async-done | bytes 2097168 | tf_op jit(solution)/shard_map/psum | solution.py:111
  174.8 2.4 %broadcast_multiply_fusion = f32[1024,256]{1,0:T(8,128)} fusion(f32[1024,256]{1,0:T(8,128)} %get-tuple-element.56), kind=kLoop, calls=%fused_computation.63 | loop fusion | flops 262144 | bytes 2097152 | tf_op jit(solution)/shard_map/div | solution.py:112
  177.1 1.1 broadcast_multiply_fusion.1
  (40 shorter events, 1.0 us)
Async XLA Ops:
  7.2 22.0 %copy-start = (bf16[256,1024]{1,0:T(8,128)(2,1)S(1)}, bf16[256,1024]{1,0:T(8,128)(2,1)}, u32[]{:S(2)}) copy-start(bf16[256,1024]{1,0:T(8,128)(2,1)} %param.11) | copy-start | bytes 1572868
  8.0 11.3 %collective-permute-start = (bf16[2,4,3,256]{3,2,1,0:T(4,128)(2,1)S(1)}, bf16[2,4,3,256]{3,2,1,0:T(4,128)(2,1)S(1)}, u32[]{:S(2)}, u32[]{:S(2)}) collective-permute-start(bf16[2,4,3,256]{3,2,1,0:T(4,128)(2,1)S(1)} %get-tuple-element.66), channel_id=1, source_target_pairs={{0,1},{1,2},{2,3},{3,4},{4,5},{5,6},{6,7},{7,0},{8,9},{9,10},{10,1... | collective-permute-start | bytes 36872 | tf_op jit(solution)/shard_map/ppermute | solution.py:18
  11.1 8.3 %collective-permute-start.1 = (bf16[2,4,3,256]{3,2,1,0:T(4,128)(2,1)S(1)}, bf16[2,4,3,256]{3,2,1,0:T(4,128)(2,1)S(1)}, u32[]{:S(2)}, u32[]{:S(2)}) collective-permute-start(bf16[2,4,3,256]{3,2,1,0:T(4,128)(2,1)S(1)} %get-tuple-element.67), channel_id=1, source_target_pairs={{1,0},{2,1},{3,2},{4,3},{5,4},{6,5},{7,6},{0,7},{9,8},{10,9},{11,1... | collective-permute-start | bytes 36872 | tf_op jit(solution)/shard_map/ppermute | solution.py:21
  15.7 3.5 %copy-start.3 = (f32[7,7,256]{2,1,0:T(8,128)S(1)}, f32[7,7,256]{2,1,0:T(8,128)}, u32[]{:S(2)}) copy-start(f32[7,7,256]{2,1,0:T(8,128)} %param.9) | copy-start | bytes 150532
  15.7 3.6 %copy-start.2 = (bf16[2,4,32,256]{3,2,1,0:T(8,128)(2,1)S(1)}, bf16[2,4,32,256]{3,2,1,0:T(8,128)(2,1)}, u32[]{:S(2)}) copy-start(bf16[2,4,32,256]{3,2,1,0:T(8,128)(2,1)} %param.7) | copy-start | bytes 393220
  15.7 8.1 %all-to-all-start = ((bf16[2,16,8,256]{3,2,0,1:T(8,128)(2,1)}), bf16[2,16,8,256]{3,2,0,1:T(8,128)(2,1)S(1)}, u32[]{:S(2)}, u32[]{:S(2)}) async-start(bf16[2,16,8,256]{3,2,0,1:T(8,128)(2,1)} %copy.12), calls=%async_computation | async-start | bytes 262144 | tf_op jit(solution)/shard_map/all_to_all | solution.py:74
  19.2 155.6 %all-reduce.3.cloned.1.call-start = ((), (), s32[]{:S(2)}) async-start(), calls=%async_computation.1 | async-start | bytes 4194304 | tf_op jit(solution)/shard_map/psum | solution.py:111
  19.4 4.4 %collective-permute-start.2 = (bf16[2,3,38,256]{3,2,1,0:T(8,128)(2,1)S(1)}, bf16[2,3,38,256]{3,2,1,0:T(8,128)(2,1)S(1)}, u32[]{:S(2)}, u32[]{:S(2)}) collective-permute-start(bf16[2,3,38,256]{3,2,1,0:T(8,128)(2,1)S(1)} %get-tuple-element.62), channel_id=1, source_target_pairs={{0,8},{8,16},{16,24},{1,9},{9,17},{17,25},{2,10},{10,18},{18,26},{... | collective-permute-start | bytes 350216 | tf_op jit(solution)/shard_map/ppermute | solution.py:18
  21.8 4.4 %collective-permute-start.3 = (bf16[2,3,38,256]{3,2,1,0:T(8,128)(2,1)S(1)}, bf16[2,3,38,256]{3,2,1,0:T(8,128)(2,1)S(1)}, u32[]{:S(2)}, u32[]{:S(2)}) collective-permute-start(bf16[2,3,38,256]{3,2,1,0:T(8,128)(2,1)S(1)} %get-tuple-element.63), channel_id=1, source_target_pairs={{8,0},{16,8},{24,16},{9,1},{17,9},{25,17},{10,2},{18,10},{26,18},{... | collective-permute-start | bytes 350216 | tf_op jit(solution)/shard_map/ppermute | solution.py:21
  28.4 0.7 copy-start.4
  29.2 1.0 copy-start.5
  29.5 0.7 copy-start.6
  36.6 43.9 %collective-permute-start.4 = (bf16[2,4,3,256]{3,2,1,0:T(4,128)(2,1)S(1)}, bf16[2,4,3,256]{3,2,1,0:T(4,128)(2,1)S(1)}, u32[]{:S(2)}, u32[]{:S(2)}) collective-permute-start(bf16[2,4,3,256]{3,2,1,0:T(4,128)(2,1)S(1)} %get-tuple-element.64), channel_id=1, source_target_pairs={{0,1},{1,2},{2,3},{3,4},{4,5},{5,6},{6,7},{7,0},{8,9},{9,10},{10,1... | collective-permute-start | bytes 36872 | tf_op jit(solution)/shard_map/ppermute | solution.py:18
  36.7 43.8 %collective-permute-start.5 = (bf16[2,4,3,256]{3,2,1,0:T(4,128)(2,1)S(1)}, bf16[2,4,3,256]{3,2,1,0:T(4,128)(2,1)S(1)}, u32[]{:S(2)}, u32[]{:S(2)}) collective-permute-start(bf16[2,4,3,256]{3,2,1,0:T(4,128)(2,1)S(1)} %get-tuple-element.65), channel_id=1, source_target_pairs={{1,0},{2,1},{3,2},{4,3},{5,4},{6,5},{7,6},{0,7},{9,8},{10,9},{11,1... | collective-permute-start | bytes 36872 | tf_op jit(solution)/shard_map/ppermute | solution.py:21
  80.6 3.3 %collective-permute-start.6 = (bf16[2,3,38,256]{3,2,1,0:T(8,128)(2,1)S(1)}, bf16[2,3,38,256]{3,2,1,0:T(8,128)(2,1)S(1)}, u32[]{:S(2)}, u32[]{:S(2)}) collective-permute-start(bf16[2,3,38,256]{3,2,1,0:T(8,128)(2,1)S(1)} %get-tuple-element.60), channel_id=1, source_target_pairs={{0,8},{8,16},{16,24},{1,9},{9,17},{17,25},{2,10},{10,18},{18,26},{... | collective-permute-start | bytes 350216 | tf_op jit(solution)/shard_map/ppermute | solution.py:18
  82.0 5.6 %collective-permute-start.7 = (bf16[2,3,38,256]{3,2,1,0:T(8,128)(2,1)S(1)}, bf16[2,3,38,256]{3,2,1,0:T(8,128)(2,1)S(1)}, u32[]{:S(2)}, u32[]{:S(2)}) collective-permute-start(bf16[2,3,38,256]{3,2,1,0:T(8,128)(2,1)S(1)} %get-tuple-element.61), channel_id=1, source_target_pairs={{8,0},{16,8},{24,16},{9,1},{17,9},{25,17},{10,2},{18,10},{26,18},{... | collective-permute-start | bytes 350216 | tf_op jit(solution)/shard_map/ppermute | solution.py:21
  174.8 2.4 %copy-start.1 = (f32[256,1024]{1,0:T(8,128)S(1)}, f32[256,1024]{1,0:T(8,128)}, u32[]{:S(2)}) copy-start(f32[256,1024]{1,0:T(8,128)} %get-tuple-element.55) | copy-start | bytes 3145732
Sparse Core Ops, SparseCore 0:
  41.6 133.1 all-reduce.2
where the time goes:
time: 186 us; the launch traced here: 185 us
  waiting for transfers between devices  91.3 us (49%)
  blocking collectives  39.1 us (21%)
  starting transfers between devices  20.6 us (11%)
  between operations  14.3 us (8%)
  other arithmetic  10.6 us (6%)
  matrix products  4.88 us (3%)
  local copies, waits for them, and re-layouts  4.22 us (2%)
    psum x1, waiting for transfers between devices, local(): lax.psum((part_in, part_out, part_dw), ('lat', 'lon'))  84.5 us
    psum x1, blocking collectives, local(): lax.psum((part_in, part_out, part_dw), ('lat', 'lon'))  39.1 us
    ppermute x4, starting transfers between devices, with_halo(): lax.ppermute(lax.slice_in_dim(block, 0, width, axis=dim), axis, backward)  10.4 us
    ppermute x4, starting transfers between devices, with_halo(): lax.ppermute(lax.slice_in_dim(block, block.shape[dim] - width, None, axis...  6.75 us
    ppermute x4, waiting for transfers between devices, with_halo(): lax.ppermute(lax.slice_in_dim(block, 0, width, axis=dim), axis, backward)  6.01 us
  transfers between devices with their start and end apart: 10, of which 4 were waited for; matrix products, arithmetic and copies ran while one was open for 3% of the time, Pallas kernels for 0%

commit v1 on v0

--- a/solution.py
+++ b/solution.py
@@ -48,6 +48,56 @@
                 * padded[:, row_start : row_start + tile_rows, col_start : col_start + tile_cols]
             )
     return result
+
+
+def bits_of(axis):
+    return [(axis, 1 << k) for k in range((lax.axis_size(axis) - 1).bit_length())]
+
+
+def swap(value, axis, bit):
+    return lax.ppermute(value, axis, [(i, i ^ bit) for i in range(lax.axis_size(axis))])
+
+
+def rows_at(value, half, upper):
+    return lax.dynamic_slice_in_dim(value, upper * half, half, axis=0)
+
+
+def split_rows(value, counts):
+    pieces, start = [], 0
+    for count in counts:
+        pieces.append(lax.slice_in_dim(value, start, start + count, axis=0))
+        start += count
+    return pieces
+
+
+def sum_over_mesh(parts, divisor):
+    lat_bits, lon_bits = bits_of("lat"), bits_of("lon")
+    halving = lat_bits[:2] + lon_bits[:1]
+    whole = lon_bits[1:] + lat_bits[2:]
+    parts = list(parts)
+    for axis, bit in halving:
+        upper = (lax.axis_index(axis) & bit) // bit
+        halves = [part.shape[0] // 2 for part in parts]
+        sent = [rows_at(p, h, 1 - upper).astype(jnp.bfloat16) for p, h in zip(parts, halves)]
+        got = swap(jnp.concatenate(sent, axis=0), axis, bit)
+        parts = [
+            rows_at(p, h, upper) + g.astype(jnp.float32)
+            for p, h, g in zip(parts, halves, split_rows(got, halves))
+        ]
+    counts = [part.shape[0] for part in parts]
+    total = jnp.concatenate(parts, axis=0)
+    for axis, bit in whole:
+        total = total + swap(total, axis, bit)
+    parts = split_rows((total / divisor).astype(jnp.bfloat16), counts)
+    for axis, bit in reversed(halving):
+        upper = (lax.axis_index(axis) & bit) // bit
+        counts = [part.shape[0] for part in parts]
+        got = split_rows(swap(jnp.concatenate(parts, axis=0), axis, bit), counts)
+        parts = [
+            jnp.where(upper == 1, jnp.concatenate([g, p]), jnp.concatenate([p, g]))
+            for p, g in zip(parts, got)
+        ]
+    return [part.astype(jnp.float32) for part in parts]
 
 
 def local(student, teacher, dw_weight, norm_gain, w_in, w_out, layer_scale):
@@ -108,8 +158,15 @@
                 )
             )
     part_dw = jnp.stack(kernel_terms).reshape(kernel_size, kernel_size, channel_count)
-    sum_in, sum_out, sum_dw = lax.psum((part_in, part_out, part_dw), ("lat", "lon"))
-    return (grad_student, sum_in / cell_total, sum_out / cell_total, sum_dw / cell_total)
+    dw_rows = part_dw.reshape(-1, channel_count)
+    hidden_size = part_in.shape[1]
+    per_row = hidden_size // channel_count
+    pad_rows = -dw_rows.shape[0] % (8 * per_row)
+    dw_wide = jnp.pad(dw_rows, ((0, pad_rows), (0, 0))).reshape(-1, hidden_size)
+    (sum_out,) = sum_over_mesh((part_out,), cell_total)
+    sum_in, sum_dw = sum_over_mesh((part_in, dw_wide), cell_total)
+    sum_dw = sum_dw.reshape(-1, channel_count)[: kernel_size * kernel_size]
+    return (grad_student, sum_in, sum_out, sum_dw.reshape(dw_weight.shape))
 
 
 def solution(mesh):

time: 186 us -> 91.3 us (0.49)
  waiting for transfers between devices: 91.3 us -> 39.3 us
  blocking collectives: 39.1 us -> 0 us
  starting transfers between devices: 20.6 us -> 33.7 us
  between operations: 14.3 us -> 1.27 us
  matrix products: 4.88 us -> 2.94 us
    psum x1 -> x0, waiting for transfers between devices: 84.5 us -> none  [local(): lax.psum((part_in, part_out, part_dw), ('lat', 'lon'))]
    psum x1 -> x0, blocking collectives: 39.1 us -> none  [local(): lax.psum((part_in, part_out, part_dw), ('lat', 'lon'))]
    ppermute x0 -> x16, waiting for transfers between devices: none -> 29.9 us  [swap(): lax.ppermute(value, axis, [(i, i ^ bit) for i in range(lax.axis_size(axis...]
    ppermute x0 -> x16, starting transfers between devices: none -> 13.3 us  [swap(): lax.ppermute(value, axis, [(i, i ^ bit) for i in range(lax.axis_size(axis...]
    ppermute x4, waiting for transfers between devices: 0.01 us -> 7.91 us  [with_halo(): lax.ppermute(lax.slice_in_dim(block, block.shape[dim] - width, None, axis...]
    ppermute x4, waiting for transfers between devices: 6.01 us -> 1.4 us  [with_halo(): lax.ppermute(lax.slice_in_dim(block, 0, width, axis=dim), axis, backward)]
    div x3 -> x0, other arithmetic: 4.07 us -> none  [the longest x1 2.35 us: local(): sum_out / cell_total]
    ppermute x4, starting transfers between devices: 10.4 us -> 7.85 us  [with_halo(): lax.ppermute(lax.slice_in_dim(block, 0, width, axis=dim), axis, backward)]
  transfers between devices with their start and end apart: 10 -> 25, of which waited for: 4 -> 14; matrix products, arithmetic and copies ran while one was open for 3% -> 6% of each run, Pallas kernels for 0% -> 0%
where the time goes in v1:
time: 91.3 us; the launch traced here: 91 us
  waiting for transfers between devices  39.3 us (43%)
  starting transfers between devices  33.7 us (37%)
  other arithmetic  9.42 us (10%)
  local copies, waits for them, and re-layouts  4.38 us (5%)
  matrix products  2.94 us (3%)
  between operations  1.27 us (1%)
    ppermute x16, waiting for transfers between devices, swap(): lax.ppermute(value, axis, [(i, i ^ bit) for i in range(lax.axis_size(axis...  29.9 us
    ppermute x16, starting transfers between devices, swap(): lax.ppermute(value, axis, [(i, i ^ bit) for i in range(lax.axis_size(axis...  13.3 us
    ppermute x4, starting transfers between devices, with_halo(): lax.ppermute(lax.slice_in_dim(block, block.shape[dim] - width, None, axis...  8.27 us
    ppermute x4, waiting for transfers between devices, with_halo(): lax.ppermute(lax.slice_in_dim(block, block.shape[dim] - width, None, axis...  7.91 us
    ppermute x4, starting transfers between devices, with_halo(): lax.ppermute(lax.slice_in_dim(block, 0, width, axis=dim), axis, backward)  7.85 us
    all_to_all x1, starting transfers between devices, local(): lax.all_to_all(teacher, 'lat', split_axis=1, concat_axis=2, tiled=True)  4.34 us
    unnamed x13, local copies, waits for them, and re-layouts  2.96 us
    convert_element_type x1, other arithmetic, local(): (misfit.reshape(student.shape) + back_conv).astype(jnp.bfloat16)  2.49 us
  transfers between devices with their start and end apart: 25, of which 14 were waited for; matrix products, arithmetic and copies ran while one was open for 6% of the time, Pallas kernels for 0%

profile of v1, /device:TPU:0, one launch (start us, length us, event | category | flops | bytes accessed | tf_op | source)
XLA Modules:
  0.0 91.0 jit_solution(10305909215688406992)
XLA Ops:
  0.6 1.6 %copy.12 = bf16[2,16,8,256]{3,2,0,1:T(8,128)(2,1)} copy(bf16[2,16,8,256]{3,2,1,0:T(8,128)(2,1)} %param.8) | data formatting | bytes 262144 | tf_op args[1]
  2.3 4.3 %all-to-all-start = ((bf16[2,16,8,256]{3,2,0,1:T(8,128)(2,1)}), bf16[2,16,8,256]{3,2,0,1:T(8,128)(2,1)S(1)}, u32[]{:S(2)}, u32[]{:S(2)}) async-start(bf16[2,16,8,256]{3,2,0,1:T(8,128)(2,1)} %copy.12), calls=%async_computation | async-start | bytes 262144 | tf_op jit(solution)/shard_map/all_to_all | solution.py:124
  6.6 5.2 %collective-permute-start.1 = (bf16[2,4,3,256]{3,2,1,0:T(4,128)(2,1)S(1)}, bf16[2,4,3,256]{3,2,1,0:T(4,128)(2,1)S(1)}, u32[]{:S(2)}, u32[]{:S(2)}) collective-permute-start(bf16[2,4,3,256]{3,2,1,0:T(4,128)(2,1)S(1)} %get-tuple-element.65), channel_id=1, source_target_pairs={{1,0},{2,1},{3,2},{4,3},{5,4},{6,5},{7,6},{0,7},{9,8},{10,9},{11,1... | collective-permute-start | bytes 36872 | tf_op jit(solution)/shard_map/ppermute | solution.py:21
  11.9 1.4 %collective-permute-done.1 = bf16[2,4,3,256]{3,2,1,0:T(4,128)(2,1)S(1)} collective-permute-done((bf16[2,4,3,256]{3,2,1,0:T(4,128)(2,1)S(1)}, bf16[2,4,3,256]{3,2,1,0:T(4,128)(2,1)S(1)}, u32[]{:S(2)}, u32[]{:S(2)}) %collective-permute-start.1) | collective-permute-done | bytes 12320 | tf_op jit(solution)/shard_map/ppermute | solution.py:21
  13.3 5.0 %collective-permute-done = bf16[2,4,3,256]{3,2,1,0:T(4,128)(2,1)S(1)} collective-permute-done((bf16[2,4,3,256]{3,2,1,0:T(4,128)(2,1)S(1)}, bf16[2,4,3,256]{3,2,1,0:T(4,128)(2,1)S(1)}, u32[]{:S(2)}, u32[]{:S(2)}) %collective-permute-start) | collective-permute-done | bytes 12320 | tf_op jit(solution)/shard_map/ppermute | solution.py:18
  18.4 1.3 %collective-permute-start.3 = (bf16[2,3,38,256]{3,2,1,0:T(8,128)(2,1)S(1)}, bf16[2,3,38,256]{3,2,1,0:T(8,128)(2,1)S(1)}, u32[]{:S(2)}, u32[]{:S(2)}) collective-permute-start(bf16[2,3,38,256]{3,2,1,0:T(8,128)(2,1)S(1)} %get-tuple-element.61), channel_id=1, source_target_pairs={{8,0},{16,8},{24,16},{9,1},{17,9},{25,17},{10,2},{18,10},{26,18},{... | collective-permute-start | bytes 350216 | tf_op jit(solution)/shard_map/ppermute | solution.py:21
  19.7 3.0 %collective-permute-start.2 = (bf16[2,3,38,256]{3,2,1,0:T(8,128)(2,1)S(1)}, bf16[2,3,38,256]{3,2,1,0:T(8,128)(2,1)S(1)}, u32[]{:S(2)}, u32[]{:S(2)}) collective-permute-start(bf16[2,3,38,256]{3,2,1,0:T(8,128)(2,1)S(1)} %get-tuple-element.60), channel_id=1, source_target_pairs={{0,8},{8,16},{16,24},{1,9},{9,17},{17,25},{2,10},{10,18},{18,26},{... | collective-permute-start | bytes 350216 | tf_op jit(solution)/shard_map/ppermute | solution.py:18
  22.8 0.8 collective-permute-done.2
  23.7 1.8 %fusion.113 = (f32[2,4,32]{2,1,0:T(4,128)S(1)}, f32[2,4,32,256]{3,2,1,0:T(8,128)S(1)}) fusion(f32[2,10,38,256]{3,2,1,0:T(8,128)S(1)} %maximum_convert_fusion, f32[256]{0:T(256)S(1)} %bitcast.276, f32[256]{0:T(256)S(1)} %bitcast.278, f32[256]{0:T(256)S(1)} %bitcast.184, f32[256]{0:T(256)S(1)} %bitcast.186, f32[256]{0:T(256)S(1)} %bitcast.188, ...), kind=kLoop, calls=%fused_computation.268 | loop fusion | flops 6422272 | bytes 13158400 | tf_op jit(solution)/shard_map/reduce_sum | solution.py:114
  27.1 0.7 copy-done.4
  28.3 0.8 fusion
  32.1 2.0 %collective-permute-start.4 = (bf16[2,4,3,256]{3,2,1,0:T(4,128)(2,1)S(1)}, bf16[2,4,3,256]{3,2,1,0:T(4,128)(2,1)S(1)}, u32[]{:S(2)}, u32[]{:S(2)}) collective-permute-start(bf16[2,4,3,256]{3,2,1,0:T(4,128)(2,1)S(1)} %get-tuple-element.62), channel_id=1, source_target_pairs={{0,1},{1,2},{2,3},{3,4},{4,5},{5,6},{6,7},{7,0},{8,9},{9,10},{10,1... | collective-permute-start | bytes 36872 | tf_op jit(solution)/shard_map/ppermute | solution.py:18
  34.4 2.0 %collective-permute-start.16 = (bf16[512,256]{1,0:T(8,128)(2,1)S(1)}, bf16[512,256]{1,0:T(8,128)(2,1)S(1)}, u32[]{:S(2)}, u32[]{:S(2)}) collective-permute-start(bf16[512,256]{1,0:T(8,128)(2,1)S(1)} %dynamic-slice_convert_fusion), channel_id=1, source_target_pairs={{0,8},{8,0},{16,24},{24,16},{1,9},{9,1},{17,25},{25,17},{2,10},{10... | collective-permute-start | bytes 786440 | tf_op jit(solution)/shard_map/ppermute | solution.py:58
  36.5 2.1 %collective-permute-done.4 = bf16[2,4,3,256]{3,2,1,0:T(4,128)(2,1)S(1)} collective-permute-done((bf16[2,4,3,256]{3,2,1,0:T(4,128)(2,1)S(1)}, bf16[2,4,3,256]{3,2,1,0:T(4,128)(2,1)S(1)}, u32[]{:S(2)}, u32[]{:S(2)}) %collective-permute-start.4) | collective-permute-done | bytes 12320 | tf_op jit(solution)/shard_map/ppermute | solution.py:18
  38.8 4.9 %collective-permute-start.17 = (bf16[256,256]{1,0:T(8,128)(2,1)S(1)}, bf16[256,256]{1,0:T(8,128)(2,1)S(1)}, u32[]{:S(2)}, u32[]{:S(2)}) collective-permute-start(bf16[256,256]{1,0:T(8,128)(2,1)S(1)} %dynamic-slice_convert_fusion.2), channel_id=1, source_target_pairs={{0,16},{8,24},{16,0},{24,8},{1,17},{9,25},{17,1},{25,9},{2,18},{10... | collective-permute-start | bytes 393224 | tf_op jit(solution)/shard_map/ppermute | solution.py:58
  43.9 3.2 %collective-permute-done.17 = bf16[256,256]{1,0:T(8,128)(2,1)S(1)} collective-permute-done((bf16[256,256]{1,0:T(8,128)(2,1)S(1)}, bf16[256,256]{1,0:T(8,128)(2,1)S(1)}, u32[]{:S(2)}, u32[]{:S(2)}) %collective-permute-start.17) | collective-permute-done | bytes 131104 | tf_op jit(solution)/shard_map/ppermute | solution.py:58
  47.3 1.7 %collective-permute-done.9 = bf16[68,1024]{1,0:T(8,128)(2,1)S(1)} collective-permute-done((bf16[68,1024]{1,0:T(8,128)(2,1)S(1)}, bf16[68,1024]{1,0:T(8,128)(2,1)S(1)}, u32[]{:S(2)}, u32[]{:S(2)}) %collective-permute-start.9) | collective-permute-done | bytes 139296 | tf_op jit(solution)/shard_map/ppermute | solution.py:58
  49.5 2.1 %collective-permute-done.18 = bf16[128,256]{1,0:T(8,128)(2,1)S(1)} collective-permute-done((bf16[128,256]{1,0:T(8,128)(2,1)S(1)}, bf16[128,256]{1,0:T(8,128)(2,1)S(1)}, u32[]{:S(2)}, u32[]{:S(2)}) %collective-permute-start.18) | collective-permute-done | bytes 65568 | tf_op jit(solution)/shard_map/ppermute | solution.py:58
  51.6 2.0 %collective-permute-done.10 = bf16[34,1024]{1,0:T(8,128)(2,1)S(1)} collective-permute-done((bf16[34,1024]{1,0:T(8,128)(2,1)S(1)}, bf16[34,1024]{1,0:T(8,128)(2,1)S(1)}, u32[]{:S(2)}, u32[]{:S(2)}) %collective-permute-start.10) | collective-permute-done | bytes 69664 | tf_op jit(solution)/shard_map/ppermute | solution.py:58
  53.8 1.3 %collective-permute-start.7 = (bf16[2,3,38,256]{3,2,1,0:T(8,128)(2,1)S(1)}, bf16[2,3,38,256]{3,2,1,0:T(8,128)(2,1)S(1)}, u32[]{:S(2)}, u32[]{:S(2)}) collective-permute-start(bf16[2,3,38,256]{3,2,1,0:T(8,128)(2,1)S(1)} %get-tuple-element.59), channel_id=1, source_target_pairs={{8,0},{16,8},{24,16},{9,1},{17,9},{25,17},{10,2},{18,10},{26,18},{... | collective-permute-start | bytes 350216 | tf_op jit(solution)/shard_map/ppermute | solution.py:21
  55.1 3.2 %collective-permute-start.6 = (bf16[2,3,38,256]{3,2,1,0:T(8,128)(2,1)S(1)}, bf16[2,3,38,256]{3,2,1,0:T(8,128)(2,1)S(1)}, u32[]{:S(2)}, u32[]{:S(2)}) collective-permute-start(bf16[2,3,38,256]{3,2,1,0:T(8,128)(2,1)S(1)} %get-tuple-element.58), channel_id=1, source_target_pairs={{0,8},{8,16},{16,24},{1,9},{9,17},{17,25},{2,10},{10,18},{18,26},{... | collective-permute-start | bytes 350216 | tf_op jit(solution)/shard_map/ppermute | solution.py:18
  58.4 0.8 collective-permute-start.20
  59.2 2.3 %collective-permute-start.12 = (f32[34,1024]{1,0:T(8,128)S(1)}, f32[34,1024]{1,0:T(8,128)S(1)}, u32[]{:S(2)}, u32[]{:S(2)}) collective-permute-start(f32[34,1024]{1,0:T(8,128)S(1)} %fusion.111), channel_id=1, source_target_pairs={{0,4},{1,5},{2,6},{3,7},{4,0},{5,1},{6,2},{7,3},{8,12},{9,13},{10,... | collective-permute-start | bytes 417800 | tf_op jit(solution)/shard_map/ppermute | solution.py:58
  61.5 10.5 %collective-permute-done.20 = f32[128,256]{1,0:T(8,128)S(1)} collective-permute-done((f32[128,256]{1,0:T(8,128)S(1)}, f32[128,256]{1,0:T(8,128)S(1)}, u32[]{:S(2)}, u32[]{:S(2)}) %collective-permute-start.20) | collective-permute-done | bytes 131104 | tf_op jit(solution)/shard_map/ppermute | solution.py:58
  72.2 3.3 %collective-permute-done.12 = f32[34,1024]{1,0:T(8,128)S(1)} collective-permute-done((f32[34,1024]{1,0:T(8,128)S(1)}, f32[34,1024]{1,0:T(8,128)S(1)}, u32[]{:S(2)}, u32[]{:S(2)}) %collective-permute-start.12) | collective-permute-done | bytes 139296 | tf_op jit(solution)/shard_map/ppermute | solution.py:58
  76.4 2.0 %collective-permute-start.22 = (bf16[256,256]{1,0:T(8,128)(2,1)S(1)}, bf16[256,256]{1,0:T(8,128)(2,1)S(1)}, u32[]{:S(2)}, u32[]{:S(2)}) collective-permute-start(bf16[256,256]{1,0:T(8,128)(2,1)S(1)} %maximum_select_fusion.5), channel_id=1, source_target_pairs={{0,16},{8,24},{16,0},{24,8},{1,17},{9,25},{17,1},{25,9},{2,18},{10... | collective-permute-start | bytes 393224 | tf_op jit(solution)/shard_map/ppermute | solution.py:58
  78.4 1.7 %collective-permute-done.13 = bf16[34,1024]{1,0:T(8,128)(2,1)S(1)} collective-permute-done((bf16[34,1024]{1,0:T(8,128)(2,1)S(1)}, bf16[34,1024]{1,0:T(8,128)(2,1)S(1)}, u32[]{:S(2)}, u32[]{:S(2)}) %collective-permute-start.13) | collective-permute-done | bytes 69664 | tf_op jit(solution)/shard_map/ppermute | solution.py:58
  80.3 1.6 %collective-permute-done.22 = bf16[256,256]{1,0:T(8,128)(2,1)S(1)} collective-permute-done((bf16[256,256]{1,0:T(8,128)(2,1)S(1)}, bf16[256,256]{1,0:T(8,128)(2,1)S(1)}, u32[]{:S(2)}, u32[]{:S(2)}) %collective-permute-start.22) | collective-permute-done | bytes 131104 | tf_op jit(solution)/shard_map/ppermute | solution.py:58
  82.1 3.3 %collective-permute-done.14 = bf16[68,1024]{1,0:T(8,128)(2,1)S(1)} collective-permute-done((bf16[68,1024]{1,0:T(8,128)(2,1)S(1)}, bf16[68,1024]{1,0:T(8,128)(2,1)S(1)}, u32[]{:S(2)}, u32[]{:S(2)}) %collective-permute-start.14) | collective-permute-done | bytes 139296 | tf_op jit(solution)/shard_map/ppermute | solution.py:58
  85.6 2.5 %fusion.61 = bf16[2,4,32,256]{3,2,1,0:T(8,128)(2,1)} fusion(f32[2,4,32,256]{3,2,1,0:T(8,128)S(1)} %bitcast.181, f32[2,10,38,256]{3,2,1,0:T(8,128)S(1)} %maximum_convert_fusion.1, f32[256]{0:T(256)S(1)} %bitcast.277, f32[256]{0:T(256)S(1)} %bitcast.279, f32[256]{0:T(256)S(1)} %bitcast.185, f32[256]{0:T(256)S(1)} %bitcast.187, f32[256]{0:T(256)S(1)} %bitcast.189, ...), kind=kLoop, calls=%fused_computation.127 | loop fusion | flops 6488064 | bytes 13288448 | tf_op jit(solution)/shard_map/convert_element_type | solution.py:148
  88.1 1.1 %fusion.9 = f32[1024,256]{1,0:T(8,128)} fusion(bf16[512,256]{1,0:T(8,128)(2,1)S(1)} %maximum_select_fusion.3, bf16[512,256]{1,0:T(8,128)(2,1)S(1)} %collective-permute-done.23, pred[]{:T(512)S(6)} %eq.6), kind=kLoop, calls=%fused_computation.66 | loop fusion | flops 2621440 | bytes 1572865 | tf_op jit(solution)/shard_map/convert_element_type | solution.py:100
  89.2 1.1 %fusion.8 = f32[256,1024]{1,0:T(8,128)} fusion(bf16[128,1024]{1,0:T(8,128)(2,1)S(1)} %maximum_select_fusion.2, bf16[128,1024]{1,0:T(8,128)(2,1)S(1)} %slice.896, pred[]{:T(512)S(6)} %eq.6), kind=kLoop, calls=%fused_computation.64 | loop fusion | flops 2621440 | bytes 1572865 | tf_op jit(solution)/shard_map/convert_element_type | solution.py:100
  (112 shorter events, 9.1 us)
Async XLA Ops:
  0.6 26.1 %copy-start = (bf16[256,1024]{1,0:T(8,128)(2,1)S(1)}, bf16[256,1024]{1,0:T(8,128)(2,1)}, u32[]{:S(2)}) copy-start(bf16[256,1024]{1,0:T(8,128)(2,1)} %param.11) | copy-start | bytes 1572868
  2.3 4.3 %copy-start.1 = (bf16[2,4,32,256]{3,2,1,0:T(8,128)(2,1)S(1)}, bf16[2,4,32,256]{3,2,1,0:T(8,128)(2,1)}, u32[]{:S(2)}) copy-start(bf16[2,4,32,256]{3,2,1,0:T(8,128)(2,1)} %param.7) | copy-start | bytes 393220
  2.3 20.5 %all-to-all-start = ((bf16[2,16,8,256]{3,2,0,1:T(8,128)(2,1)}), bf16[2,16,8,256]{3,2,0,1:T(8,128)(2,1)S(1)}, u32[]{:S(2)}, u32[]{:S(2)}) async-start(bf16[2,16,8,256]{3,2,0,1:T(8,128)(2,1)} %copy.12), calls=%async_computation | async-start | bytes 262144 | tf_op jit(solution)/shard_map/all_to_all | solution.py:124
  6.6 5.2 %copy-start.2 = (f32[7,7,256]{2,1,0:T(8,128)S(1)}, f32[7,7,256]{2,1,0:T(8,128)}, u32[]{:S(2)}) copy-start(f32[7,7,256]{2,1,0:T(8,128)} %param.9) | copy-start | bytes 150532
  6.6 6.6 %collective-permute-start.1 = (bf16[2,4,3,256]{3,2,1,0:T(4,128)(2,1)S(1)}, bf16[2,4,3,256]{3,2,1,0:T(4,128)(2,1)S(1)}, u32[]{:S(2)}, u32[]{:S(2)}) collective-permute-start(bf16[2,4,3,256]{3,2,1,0:T(4,128)(2,1)S(1)} %get-tuple-element.65), channel_id=1, source_target_pairs={{1,0},{2,1},{3,2},{4,3},{5,4},{6,5},{7,6},{0,7},{9,8},{10,9},{11,1... | collective-permute-start | bytes 36872 | tf_op jit(solution)/shard_map/ppermute | solution.py:21
  11.8 6.4 %collective-permute-start = (bf16[2,4,3,256]{3,2,1,0:T(4,128)(2,1)S(1)}, bf16[2,4,3,256]{3,2,1,0:T(4,128)(2,1)S(1)}, u32[]{:S(2)}, u32[]{:S(2)}) collective-permute-start(bf16[2,4,3,256]{3,2,1,0:T(4,128)(2,1)S(1)} %get-tuple-element.64), channel_id=1, source_target_pairs={{0,1},{1,2},{2,3},{3,4},{4,5},{5,6},{6,7},{7,0},{8,9},{9,10},{10,1... | collective-permute-start | bytes 36872 | tf_op jit(solution)/shard_map/ppermute | solution.py:18
  18.4 4.4 %collective-permute-start.3 = (bf16[2,3,38,256]{3,2,1,0:T(8,128)(2,1)S(1)}, bf16[2,3,38,256]{3,2,1,0:T(8,128)(2,1)S(1)}, u32[]{:S(2)}, u32[]{:S(2)}) collective-permute-start(bf16[2,3,38,256]{3,2,1,0:T(8,128)(2,1)S(1)} %get-tuple-element.61), channel_id=1, source_target_pairs={{8,0},{16,8},{24,16},{9,1},{17,9},{25,17},{10,2},{18,10},{26,18},{... | collective-permute-start | bytes 350216 | tf_op jit(solution)/shard_map/ppermute | solution.py:21
  19.7 4.0 %collective-permute-start.2 = (bf16[2,3,38,256]{3,2,1,0:T(8,128)(2,1)S(1)}, bf16[2,3,38,256]{3,2,1,0:T(8,128)(2,1)S(1)}, u32[]{:S(2)}, u32[]{:S(2)}) collective-permute-start(bf16[2,3,38,256]{3,2,1,0:T(8,128)(2,1)S(1)} %get-tuple-element.60), channel_id=1, source_target_pairs={{0,8},{8,16},{16,24},{1,9},{9,17},{17,25},{2,10},{10,18},{18,26},{... | collective-permute-start | bytes 350216 | tf_op jit(solution)/shard_map/ppermute | solution.py:18
  25.9 0.7 copy-start.3
  26.7 1.0 %copy-start.4 = (bf16[1024,256]{1,0:T(8,128)(2,1)S(1)}, bf16[1024,256]{1,0:T(8,128)(2,1)}, u32[]{:S(2)}) copy-start(bf16[1024,256]{1,0:T(8,128)(2,1)} %param.12) | copy-start | bytes 1572868
  27.0 0.7 copy-start.5
  32.1 4.5 %collective-permute-start.5 = (bf16[2,4,3,256]{3,2,1,0:T(4,128)(2,1)S(1)}, bf16[2,4,3,256]{3,2,1,0:T(4,128)(2,1)S(1)}, u32[]{:S(2)}, u32[]{:S(2)}) collective-permute-start(bf16[2,4,3,256]{3,2,1,0:T(4,128)(2,1)S(1)} %get-tuple-element.63), channel_id=1, source_target_pairs={{1,0},{2,1},{3,2},{4,3},{5,4},{6,5},{7,6},{0,7},{9,8},{10,9},{11,1... | collective-permute-start | bytes 36872 | tf_op jit(solution)/shard_map/ppermute | solution.py:21
  32.1 6.5 %collective-permute-start.4 = (bf16[2,4,3,256]{3,2,1,0:T(4,128)(2,1)S(1)}, bf16[2,4,3,256]{3,2,1,0:T(4,128)(2,1)S(1)}, u32[]{:S(2)}, u32[]{:S(2)}) collective-permute-start(bf16[2,4,3,256]{3,2,1,0:T(4,128)(2,1)S(1)} %get-tuple-element.62), channel_id=1, source_target_pairs={{0,1},{1,2},{2,3},{3,4},{4,5},{5,6},{6,7},{7,0},{8,9},{9,10},{10,1... | collective-permute-start | bytes 36872 | tf_op jit(solution)/shard_map/ppermute | solution.py:18
  34.4 4.3 %collective-permute-start.16 = (bf16[512,256]{1,0:T(8,128)(2,1)S(1)}, bf16[512,256]{1,0:T(8,128)(2,1)S(1)}, u32[]{:S(2)}, u32[]{:S(2)}) collective-permute-start(bf16[512,256]{1,0:T(8,128)(2,1)S(1)} %dynamic-slice_convert_fusion), channel_id=1, source_target_pairs={{0,8},{8,0},{16,24},{24,16},{1,9},{9,1},{17,25},{25,17},{2,10},{10... | collective-permute-start | bytes 786440 | tf_op jit(solution)/shard_map/ppermute | solution.py:58
  36.4 7.2 %collective-permute-start.8 = (bf16[136,1024]{1,0:T(8,128)(2,1)S(1)}, bf16[136,1024]{1,0:T(8,128)(2,1)S(1)}, u32[]{:S(2)}, u32[]{:S(2)}) collective-permute-start(bf16[136,1024]{1,0:T(8,128)(2,1)S(1)} %pad_maximum_fusion), channel_id=1, source_target_pairs={{0,8},{8,0},{16,24},{24,16},{1,9},{9,1},{17,25},{25,17},{2,10},{10... | collective-permute-start | bytes 835592 | tf_op jit(solution)/shard_map/ppermute | solution.py:58
  38.8 8.4 %collective-permute-start.17 = (bf16[256,256]{1,0:T(8,128)(2,1)S(1)}, bf16[256,256]{1,0:T(8,128)(2,1)S(1)}, u32[]{:S(2)}, u32[]{:S(2)}) collective-permute-start(bf16[256,256]{1,0:T(8,128)(2,1)S(1)} %dynamic-slice_convert_fusion.2), channel_id=1, source_target_pairs={{0,16},{8,24},{16,0},{24,8},{1,17},{9,25},{17,1},{25,9},{2,18},{10... | collective-permute-start | bytes 393224 | tf_op jit(solution)/shard_map/ppermute | solution.py:58
  43.8 5.2 %collective-permute-start.9 = (bf16[68,1024]{1,0:T(8,128)(2,1)S(1)}, bf16[68,1024]{1,0:T(8,128)(2,1)S(1)}, u32[]{:S(2)}, u32[]{:S(2)}) collective-permute-start(bf16[68,1024]{1,0:T(8,128)(2,1)S(1)} %pad_maximum_fusion.5), channel_id=1, source_target_pairs={{0,16},{8,24},{16,0},{24,8},{1,17},{9,25},{17,1},{25,9},{2,18},{10... | collective-permute-start | bytes 417800 | tf_op jit(solution)/shard_map/ppermute | solution.py:58
  47.2 4.3 %collective-permute-start.18 = (bf16[128,256]{1,0:T(8,128)(2,1)S(1)}, bf16[128,256]{1,0:T(8,128)(2,1)S(1)}, u32[]{:S(2)}, u32[]{:S(2)}) collective-permute-start(bf16[128,256]{1,0:T(8,128)(2,1)S(1)} %dynamic-slice_convert_fusion.4), channel_id=1, source_target_pairs={{0,1},{1,0},{2,3},{3,2},{4,5},{5,4},{6,7},{7,6},{8,9},{9,8},{10,11... | collective-permute-start | bytes 196616 | tf_op jit(solution)/shard_map/ppermute | solution.py:58
  49.1 4.5 %collective-permute-start.10 = (bf16[34,1024]{1,0:T(8,128)(2,1)S(1)}, bf16[34,1024]{1,0:T(8,128)(2,1)S(1)}, u32[]{:S(2)}, u32[]{:S(2)}) collective-permute-start(bf16[34,1024]{1,0:T(8,128)(2,1)S(1)} %pad_maximum_fusion.7), channel_id=1, source_target_pairs={{0,1},{1,0},{2,3},{3,2},{4,5},{5,4},{6,7},{7,6},{8,9},{9,8},{10,11... | collective-permute-start | bytes 208904 | tf_op jit(solution)/shard_map/ppermute | solution.py:58
  51.6 6.8 %collective-permute-start.19 = (f32[128,256]{1,0:T(8,128)S(1)}, f32[128,256]{1,0:T(8,128)S(1)}, u32[]{:S(2)}, u32[]{:S(2)}) collective-permute-start(f32[128,256]{1,0:T(8,128)S(1)} %convert_add_fusion.4), channel_id=1, source_target_pairs={{0,2},{1,3},{2,0},{3,1},{4,6},{5,7},{6,4},{7,5},{8,10},{9,11},{10,... | collective-permute-start | bytes 393224 | tf_op jit(solution)/shard_map/ppermute | solution.py:58
  53.7 5.5 %collective-permute-start.11 = (f32[34,1024]{1,0:T(8,128)S(1)}, f32[34,1024]{1,0:T(8,128)S(1)}, u32[]{:S(2)}, u32[]{:S(2)}) collective-permute-start(f32[34,1024]{1,0:T(8,128)S(1)} %pad_maximum_fusion.4), channel_id=1, source_target_pairs={{0,2},{1,3},{2,0},{3,1},{4,6},{5,7},{6,4},{7,5},{8,10},{9,11},{10,... | collective-permute-start | bytes 417800 | tf_op jit(solution)/shard_map/ppermute | solution.py:58
  53.8 26.4 %collective-permute-start.7 = (bf16[2,3,38,256]{3,2,1,0:T(8,128)(2,1)S(1)}, bf16[2,3,38,256]{3,2,1,0:T(8,128)(2,1)S(1)}, u32[]{:S(2)}, u32[]{:S(2)}) collective-permute-start(bf16[2,3,38,256]{3,2,1,0:T(8,128)(2,1)S(1)} %get-tuple-element.59), channel_id=1, source_target_pairs={{8,0},{16,8},{24,16},{9,1},{17,9},{25,17},{10,2},{18,10},{26,18},{... | collective-permute-start | bytes 350216 | tf_op jit(solution)/shard_map/ppermute | solution.py:21
  55.1 25.1 %collective-permute-start.6 = (bf16[2,3,38,256]{3,2,1,0:T(8,128)(2,1)S(1)}, bf16[2,3,38,256]{3,2,1,0:T(8,128)(2,1)S(1)}, u32[]{:S(2)}, u32[]{:S(2)}) collective-permute-start(bf16[2,3,38,256]{3,2,1,0:T(8,128)(2,1)S(1)} %get-tuple-element.58), channel_id=1, source_target_pairs={{0,8},{8,16},{16,24},{1,9},{9,17},{17,25},{2,10},{10,18},{18,26},{... | collective-permute-start | bytes 350216 | tf_op jit(solution)/shard_map/ppermute | solution.py:18
  58.4 13.6 %collective-permute-start.20 = (f32[128,256]{1,0:T(8,128)S(1)}, f32[128,256]{1,0:T(8,128)S(1)}, u32[]{:S(2)}, u32[]{:S(2)}) collective-permute-start(f32[128,256]{1,0:T(8,128)S(1)} %add.551), channel_id=1, source_target_pairs={{0,4},{1,5},{2,6},{3,7},{4,0},{5,1},{6,2},{7,3},{8,12},{9,13},{10,... | collective-permute-start | bytes 393224 | tf_op jit(solution)/shard_map/ppermute | solution.py:58
  59.2 16.3 %collective-permute-start.12 = (f32[34,1024]{1,0:T(8,128)S(1)}, f32[34,1024]{1,0:T(8,128)S(1)}, u32[]{:S(2)}, u32[]{:S(2)}) collective-permute-start(f32[34,1024]{1,0:T(8,128)S(1)} %fusion.111), channel_id=1, source_target_pairs={{0,4},{1,5},{2,6},{3,7},{4,0},{5,1},{6,2},{7,3},{8,12},{9,13},{10,... | collective-permute-start | bytes 417800 | tf_op jit(solution)/shard_map/ppermute | solution.py:58
  72.0 4.3 %collective-permute-start.21 = (bf16[128,256]{1,0:T(8,128)(2,1)S(1)}, bf16[128,256]{1,0:T(8,128)(2,1)S(1)}, u32[]{:S(2)}, u32[]{:S(2)}) collective-permute-start(bf16[128,256]{1,0:T(8,128)(2,1)S(1)} %multiply_convert_fusion.5), channel_id=1, source_target_pairs={{0,1},{1,0},{2,3},{3,2},{4,5},{5,4},{6,7},{7,6},{8,9},{9,8},{10,11... | collective-permute-start | bytes 196616 | tf_op jit(solution)/shard_map/ppermute | solution.py:58
  75.5 4.5 %collective-permute-start.13 = (bf16[34,1024]{1,0:T(8,128)(2,1)S(1)}, bf16[34,1024]{1,0:T(8,128)(2,1)S(1)}, u32[]{:S(2)}, u32[]{:S(2)}) collective-permute-start(bf16[34,1024]{1,0:T(8,128)(2,1)S(1)} %multiply_convert_fusion.4), channel_id=1, source_target_pairs={{0,1},{1,0},{2,3},{3,2},{4,5},{5,4},{6,7},{7,6},{8,9},{9,8},{10,11... | collective-permute-start | bytes 208904 | tf_op jit(solution)/shard_map/ppermute | solution.py:58
  76.4 5.5 %collective-permute-start.22 = (bf16[256,256]{1,0:T(8,128)(2,1)S(1)}, bf16[256,256]{1,0:T(8,128)(2,1)S(1)}, u32[]{:S(2)}, u32[]{:S(2)}) collective-permute-start(bf16[256,256]{1,0:T(8,128)(2,1)S(1)} %maximum_select_fusion.5), channel_id=1, source_target_pairs={{0,16},{8,24},{16,0},{24,8},{1,17},{9,25},{17,1},{25,9},{2,18},{10... | collective-permute-start | bytes 393224 | tf_op jit(solution)/shard_map/ppermute | solution.py:58
  80.1 5.2 %collective-permute-start.14 = (bf16[68,1024]{1,0:T(8,128)(2,1)S(1)}, bf16[68,1024]{1,0:T(8,128)(2,1)S(1)}, u32[]{:S(2)}, u32[]{:S(2)}) collective-permute-start(bf16[68,1024]{1,0:T(8,128)(2,1)S(1)} %pad_maximum_fusion.6), channel_id=1, source_target_pairs={{0,16},{8,24},{16,0},{24,8},{1,17},{9,25},{17,1},{25,9},{2,18},{10... | collective-permute-start | bytes 417800 | tf_op jit(solution)/shard_map/ppermute | solution.py:58
  82.0 6.0 %collective-permute-start.23 = (bf16[512,256]{1,0:T(8,128)(2,1)S(1)}, bf16[512,256]{1,0:T(8,128)(2,1)S(1)}, u32[]{:S(2)}, u32[]{:S(2)}) collective-permute-start(bf16[512,256]{1,0:T(8,128)(2,1)S(1)} %maximum_select_fusion.3), channel_id=1, source_target_pairs={{0,8},{8,0},{16,24},{24,16},{1,9},{9,1},{17,25},{25,17},{2,10},{10... | collective-permute-start | bytes 786440 | tf_op jit(solution)/shard_map/ppermute | solution.py:58
  85.5 3.7 %collective-permute-start.15 = (bf16[136,1024]{1,0:T(8,128)(2,1)S(1)}, bf16[136,1024]{1,0:T(8,128)(2,1)S(1)}, u32[]{:S(2)}, u32[]{:S(2)}) collective-permute-start(bf16[136,1024]{1,0:T(8,128)(2,1)S(1)} %pad_maximum_fusion.1), channel_id=1, source_target_pairs={{0,8},{8,0},{16,24},{24,16},{1,9},{9,1},{17,25},{25,17},{2,10},{10... | collective-permute-start | bytes 835592 | tf_op jit(solution)/shard_map/ppermute | solution.py:58

commit v2 on v1

--- a/solution.py
+++ b/solution.py
@@ -8,19 +8,49 @@
 norm_eps = 1e-06
 
 
+def bits_of(axis):
+    return [1 << k for k in range((lax.axis_size(axis) - 1).bit_length())]
+
+
+def swap(value, axis, bit):
+    return lax.ppermute(value, axis, [(i, i ^ bit) for i in range(lax.axis_size(axis))])
+
+
 def with_halo(block, sides, width, periodic):
     for axis, dim in sides:
         count = lax.axis_size(axis)
-        forward = [(i, i + 1) for i in range(count - 1)]
-        if periodic:
-            forward.append((count - 1, 0))
-        backward = [(target, source) for source, target in forward]
-        low = lax.ppermute(
-            lax.slice_in_dim(block, block.shape[dim] - width, None, axis=dim), axis, forward
+        odd = lax.axis_index(axis) % 2
+        inner = [(i, i ^ 1) for i in range(count)]
+        outer = [(i, (i + 1) % count) for i in range(1, count, 2)]
+        if not periodic:
+            outer = [(i, j) for i, j in outer if j]
+        outer = outer + [(j, i) for i, j in outer]
+        low = lax.slice_in_dim(block, 0, width, axis=dim)
+        high = lax.slice_in_dim(block, block.shape[dim] - width, None, axis=dim)
+        from_outer = lax.ppermute(jnp.where(odd == 1, high, low), axis, outer)
+        from_inner = lax.ppermute(jnp.where(odd == 1, low, high), axis, inner)
+        before = jnp.where(odd == 1, from_inner, from_outer)
+        after = jnp.where(odd == 1, from_outer, from_inner)
+        block = jnp.concatenate([before, block, after], axis=dim)
+    return block
+
+
+def to_bands(teacher, axis):
+    batch_size, rows, cols, channel_count = teacher.shape
+    count = lax.axis_size(axis)
+    band = rows // count
+    state = teacher.reshape(batch_size, count, band, cols, channel_count)
+    for bit in bits_of(axis):
+        upper = (lax.axis_index(axis) // bit) % 2
+        state = state.reshape(batch_size, -1, 2, band, state.shape[3], channel_count)
+        mine = lax.dynamic_index_in_dim(state, upper, axis=2, keepdims=False)
+        got = swap(lax.dynamic_index_in_dim(state, 1 - upper, axis=2, keepdims=False), axis, bit)
+        state = jnp.where(
+            upper == 1,
+            jnp.concatenate([got, mine], axis=3),
+            jnp.concatenate([mine, got], axis=3),
         )
-        high = lax.ppermute(lax.slice_in_dim(block, 0, width, axis=dim), axis, backward)
-        block = jnp.concatenate([low, block, high], axis=dim)
-    return block
+    return state.reshape(batch_size, band, -1, channel_count)
 
 
 def gelu_tanh(values):
@@ -50,14 +80,6 @@
     return result
 
 
-def bits_of(axis):
-    return [(axis, 1 << k) for k in range((lax.axis_size(axis) - 1).bit_length())]
-
-
-def swap(value, axis, bit):
-    return lax.ppermute(value, axis, [(i, i ^ bit) for i in range(lax.axis_size(axis))])
-
-
 def rows_at(value, half, upper):
     return lax.dynamic_slice_in_dim(value, upper * half, half, axis=0)
 
@@ -71,7 +93,8 @@
 
 
 def sum_over_mesh(parts, divisor):
-    lat_bits, lon_bits = bits_of("lat"), bits_of("lon")
+    lat_bits = [("lat", bit) for bit in bits_of("lat")]
+    lon_bits = [("lon", bit) for bit in bits_of("lon")]
     halving = lat_bits[:2] + lon_bits[:1]
     whole = lon_bits[1:] + lat_bits[2:]
     parts = list(parts)
@@ -121,7 +144,7 @@
     hidden = gelu_tanh(preact).astype(jnp.bfloat16)
     mlp_out = jnp.dot(hidden, w_out, preferred_element_type=jnp.float32)
     output = student.reshape(-1, channel_count).astype(jnp.float32) + layer_scale * mlp_out
-    target = lax.all_to_all(teacher, "lat", split_axis=1, concat_axis=2, tiled=True)
+    target = to_bands(teacher, "lat")
     misfit = output - target.reshape(-1, channel_count).astype(jnp.float32)
     out_grad = (layer_scale * misfit).astype(jnp.bfloat16)
     part_out = lax.dot_general(

time: 91.3 us -> 83.7 us (0.917)
  waiting for transfers between devices: 39.3 us -> 34.6 us
  starting transfers between devices: 33.7 us -> 31 us
    ppermute x8, waiting for transfers between devices: 9.31 us -> 2.87 us  [the longest x4 2.86 us: with_halo(): from_outer = lax.ppermute(jnp.where(odd == 1, high, low), axis, outer)]
    ppermute x16 -> x18, starting transfers between devices: 13.3 us -> 17.7 us  [swap(): lax.ppermute(value, axis, [(i, i ^ bit) for i in range(lax.axis_size(axis...]
    all_to_all x1 -> x0, starting transfers between devices: 4.34 us -> none  [local(): lax.all_to_all(teacher, 'lat', split_axis=1, concat_axis=2, tiled=True)]
    ppermute x8, starting transfers between devices: 16.1 us -> 13.3 us  [the longest x4 8.66 us: with_halo(): from_outer = lax.ppermute(jnp.where(odd == 1, high, low), axis, outer)]
    ppermute x16 -> x18, waiting for transfers between devices: 29.9 us -> 31.7 us  [swap(): lax.ppermute(value, axis, [(i, i ^ bit) for i in range(lax.axis_size(axis...]
    unnamed x13 -> x12, local copies, waits for them, and re-layouts: 2.96 us -> 1.64 us
    dynamic_slice x0 -> x3, local copies, waits for them, and re-layouts: none -> 0.95 us  [the longest x2 0.95 us: to_bands(): lax.dynamic_index_in_dim(state, 1 - upper, axis=2, keepdims=False)]
  transfers between devices with their start and end apart: 25 -> 26, of which waited for: 14 -> 15; matrix products, arithmetic and copies ran while one was open for 6% -> 9% of each run, Pallas kernels for 0% -> 0%
where the time goes in v2:
time: 83.7 us; the launch traced here: 83.5 us
  waiting for transfers between devices  34.6 us (41%)
  starting transfers between devices  31 us (37%)
  other arithmetic  9.65 us (12%)
  local copies, waits for them, and re-layouts  3.94 us (5%)
  matrix products  2.94 us (4%)
  between operations  1.41 us (2%)
    ppermute x18, waiting for transfers between devices, swap(): lax.ppermute(value, axis, [(i, i ^ bit) for i in range(lax.axis_size(axis...  31.7 us
    ppermute x18, starting transfers between devices, swap(): lax.ppermute(value, axis, [(i, i ^ bit) for i in range(lax.axis_size(axis...  17.7 us
    ppermute x4, starting transfers between devices, with_halo(): from_outer = lax.ppermute(jnp.where(odd == 1, high, low), axis, outer)  8.66 us
    ppermute x4, starting transfers between devices, with_halo(): from_inner = lax.ppermute(jnp.where(odd == 1, low, high), axis, inner)  4.61 us
    ppermute x4, waiting for transfers between devices, with_halo(): from_outer = lax.ppermute(jnp.where(odd == 1, high, low), axis, outer)  2.86 us
    convert_element_type x1, other arithmetic, local(): (misfit.reshape(student.shape) + back_conv).astype(jnp.bfloat16)  2.49 us
    convert_element_type x2, other arithmetic, sum_over_mesh(): return [part.astype(jnp.float32) for part in parts]  2.19 us
    reduce_sum x1, other arithmetic, local(): average = jnp.mean(smoothed, axis=-1, keepdims=True)  1.84 us
  transfers between devices with their start and end apart: 26, of which 15 were waited for; matrix products, arithmetic and copies ran while one was open for 9% of the time, Pallas kernels for 0%

profile of v2, /device:TPU:0, one launch (start us, length us, event | category | flops | bytes accessed | tf_op | source)
XLA Modules:
  0.0 83.5 jit_solution(7265749752398075981)
XLA Ops:
  0.7 0.9 %constant_dynamic-slice_fusion.3 = (bf16[2,2,1,4,8,256]{5,4,3,2,1,0:T(8,128)(2,1)S(1)}, bf16[2,2,1,4,8,256]{5,4,3,2,1,0:T(8,128)(2,1)S(1)}) fusion(bf16[2,2,2,4,8,256]{5,4,3,2,1,0:T(8,128)(2,1)} %bitcast.186, s32[]{:T(128)S(6)} %select_n.290, s32[]{:T(128)S(6)} %select_n.291), kind=kLoop, calls=%fused_computation.285 | loop fusion | bytes 262152 | tf_op jit(solution)/shard_map/jit(dynamic_index_in_dim)/dynamic_slice | solution.py:47
  2.6 3.0 %collective-permute-start = (bf16[2,4,3,256]{3,2,1,0:T(4,128)(2,1)S(1)}, bf16[2,4,3,256]{3,2,1,0:T(4,128)(2,1)S(1)}, u32[]{:S(2)}, u32[]{:S(2)}) collective-permute-start(bf16[2,4,3,256]{3,2,1,0:T(4,128)(2,1)S(1)} %get-tuple-element.68), channel_id=1, source_target_pairs={{0,1},{1,0},{2,3},{3,2},{4,5},{5,4},{6,7},{7,6},{8,9},{9,8},{10,11... | collective-permute-start | bytes 36872 | tf_op jit(solution)/shard_map/ppermute | solution.py:31
  5.6 3.5 %collective-permute-start.1 = (bf16[2,4,3,256]{3,2,1,0:T(4,128)(2,1)S(1)}, bf16[2,4,3,256]{3,2,1,0:T(4,128)(2,1)S(1)}, u32[]{:S(2)}, u32[]{:S(2)}) collective-permute-start(bf16[2,4,3,256]{3,2,1,0:T(4,128)(2,1)S(1)} %get-tuple-element.69), channel_id=1, source_target_pairs={{1,2},{3,4},{5,6},{7,0},{2,1},{4,3},{6,5},{0,7},{9,10},{11,12},{13... | collective-permute-start | bytes 36872 | tf_op jit(solution)/shard_map/ppermute | solution.py:30
  9.3 2.7 %collective-permute-done.1 = bf16[2,4,3,256]{3,2,1,0:T(4,128)(2,1)S(1)} collective-permute-done((bf16[2,4,3,256]{3,2,1,0:T(4,128)(2,1)S(1)}, bf16[2,4,3,256]{3,2,1,0:T(4,128)(2,1)S(1)}, u32[]{:S(2)}, u32[]{:S(2)}) %collective-permute-start.1) | collective-permute-done | bytes 12320 | tf_op jit(solution)/shard_map/ppermute | solution.py:30
  13.0 3.4 %collective-permute-start.5 = (bf16[2,1,4,16,256]{4,3,2,0,1:T(8,128)(2,1)S(1)}, bf16[2,1,4,16,256]{4,3,2,0,1:T(8,128)(2,1)S(1)}, u32[]{:S(2)}, u32[]{:S(2)}) collective-permute-start(bf16[2,1,4,16,256]{4,3,2,0,1:T(8,128)(2,1)S(1)} %get-tuple-element.70), channel_id=1, source_target_pairs={{0,16},{8,24},{16,0},{24,8},{1,17},{9,25},{17,1},{25,9},{2,18},{10... | collective-permute-start | bytes 196616 | tf_op jit(solution)/shard_map/ppermute | solution.py:16
  16.5 1.8 %fusion.112 = (f32[2,4,32]{2,1,0:T(4,128)S(1)}, f32[2,4,32,256]{3,2,1,0:T(8,128)S(1)}) fusion(f32[2,10,38,256]{3,2,1,0:T(8,128)S(1)} %maximum_convert_fusion, f32[256]{0:T(256)S(1)} %bitcast.282, f32[256]{0:T(256)S(1)} %bitcast.284, f32[256]{0:T(256)S(1)} %bitcast.190, f32[256]{0:T(256)S(1)} %bitcast.192, f32[256]{0:T(256)S(1)} %bitcast.194, ...), kind=kLoop, calls=%fused_computation.292 | loop fusion | flops 6422272 | bytes 13158400 | tf_op jit(solution)/shard_map/reduce_sum | solution.py:137
  21.7 0.8 fusion
  25.6 3.6 %collective-permute-start.7 = (bf16[2,4,3,256]{3,2,1,0:T(4,128)(2,1)S(1)}, bf16[2,4,3,256]{3,2,1,0:T(4,128)(2,1)S(1)}, u32[]{:S(2)}, u32[]{:S(2)}) collective-permute-start(bf16[2,4,3,256]{3,2,1,0:T(4,128)(2,1)S(1)} %get-tuple-element.67), channel_id=1, source_target_pairs={{1,2},{3,4},{5,6},{7,0},{2,1},{4,3},{6,5},{0,7},{9,10},{11,12},{13... | collective-permute-start | bytes 36872 | tf_op jit(solution)/shard_map/ppermute | solution.py:30
  29.5 2.3 %collective-permute-start.10 = (bf16[136,1024]{1,0:T(8,128)(2,1)S(1)}, bf16[136,1024]{1,0:T(8,128)(2,1)S(1)}, u32[]{:S(2)}, u32[]{:S(2)}) collective-permute-start(bf16[136,1024]{1,0:T(8,128)(2,1)S(1)} %pad_maximum_fusion), channel_id=1, source_target_pairs={{0,8},{8,0},{16,24},{24,16},{1,9},{9,1},{17,25},{25,17},{2,10},{10... | collective-permute-start | bytes 835592 | tf_op jit(solution)/shard_map/ppermute | solution.py:16
  32.2 1.4 %collective-permute-start.8 = (bf16[2,3,38,256]{3,2,1,0:T(8,128)(2,1)S(1)}, bf16[2,3,38,256]{3,2,1,0:T(8,128)(2,1)S(1)}, u32[]{:S(2)}, u32[]{:S(2)}) collective-permute-start(bf16[2,3,38,256]{3,2,1,0:T(8,128)(2,1)S(1)} %get-tuple-element.62), channel_id=1, source_target_pairs={{0,8},{8,0},{16,24},{24,16},{1,9},{9,1},{17,25},{25,17},{2,10},{10... | collective-permute-start | bytes 350216 | tf_op jit(solution)/shard_map/ppermute | solution.py:31
  33.6 0.8 %collective-permute-start.9 = (bf16[2,3,38,256]{3,2,1,0:T(8,128)(2,1)S(1)}, bf16[2,3,38,256]{3,2,1,0:T(8,128)(2,1)S(1)}, u32[]{:S(2)}, u32[]{:S(2)}) collective-permute-start(bf16[2,3,38,256]{3,2,1,0:T(8,128)(2,1)S(1)} %get-tuple-element.63), channel_id=1, source_target_pairs={{8,16},{16,8},{9,17},{17,9},{10,18},{18,10},{11,19},{19,11},{12,20... | collective-permute-start | bytes 350216 | tf_op jit(solution)/shard_map/ppermute | solution.py:30
  34.6 3.0 %collective-permute-start.19 = (bf16[256,256]{1,0:T(8,128)(2,1)S(1)}, bf16[256,256]{1,0:T(8,128)(2,1)S(1)}, u32[]{:S(2)}, u32[]{:S(2)}) collective-permute-start(bf16[256,256]{1,0:T(8,128)(2,1)S(1)} %dynamic-slice_convert_fusion.2), channel_id=1, source_target_pairs={{0,16},{8,24},{16,0},{24,8},{1,17},{9,25},{17,1},{25,9},{2,18},{10... | collective-permute-start | bytes 393224 | tf_op jit(solution)/shard_map/ppermute | solution.py:16
  37.8 4.8 %collective-permute-done.19 = bf16[256,256]{1,0:T(8,128)(2,1)S(1)} collective-permute-done((bf16[256,256]{1,0:T(8,128)(2,1)S(1)}, bf16[256,256]{1,0:T(8,128)(2,1)S(1)}, u32[]{:S(2)}, u32[]{:S(2)}) %collective-permute-start.19) | collective-permute-done | bytes 131104 | tf_op jit(solution)/shard_map/ppermute | solution.py:16
  42.8 3.0 %collective-permute-done.11 = bf16[68,1024]{1,0:T(8,128)(2,1)S(1)} collective-permute-done((bf16[68,1024]{1,0:T(8,128)(2,1)S(1)}, bf16[68,1024]{1,0:T(8,128)(2,1)S(1)}, u32[]{:S(2)}, u32[]{:S(2)}) %collective-permute-start.11) | collective-permute-done | bytes 139296 | tf_op jit(solution)/shard_map/ppermute | solution.py:16
  46.0 1.2 %collective-permute-done.20 = bf16[128,256]{1,0:T(8,128)(2,1)S(1)} collective-permute-done((bf16[128,256]{1,0:T(8,128)(2,1)S(1)}, bf16[128,256]{1,0:T(8,128)(2,1)S(1)}, u32[]{:S(2)}, u32[]{:S(2)}) %collective-permute-start.20) | collective-permute-done | bytes 65568 | tf_op jit(solution)/shard_map/ppermute | solution.py:16
  47.3 3.1 %collective-permute-done.12 = bf16[34,1024]{1,0:T(8,128)(2,1)S(1)} collective-permute-done((bf16[34,1024]{1,0:T(8,128)(2,1)S(1)}, bf16[34,1024]{1,0:T(8,128)(2,1)S(1)}, u32[]{:S(2)}, u32[]{:S(2)}) %collective-permute-start.12) | collective-permute-done | bytes 69664 | tf_op jit(solution)/shard_map/ppermute | solution.py:16
  50.6 1.7 %collective-permute-done.21 = f32[128,256]{1,0:T(8,128)S(1)} collective-permute-done((f32[128,256]{1,0:T(8,128)S(1)}, f32[128,256]{1,0:T(8,128)S(1)}, u32[]{:S(2)}, u32[]{:S(2)}) %collective-permute-start.21) | collective-permute-done | bytes 131104 | tf_op jit(solution)/shard_map/ppermute | solution.py:16
  52.4 2.2 %collective-permute-start.22 = (f32[128,256]{1,0:T(8,128)S(1)}, f32[128,256]{1,0:T(8,128)S(1)}, u32[]{:S(2)}, u32[]{:S(2)}) collective-permute-start(f32[128,256]{1,0:T(8,128)S(1)} %add.589), channel_id=1, source_target_pairs={{0,4},{1,5},{2,6},{3,7},{4,0},{5,1},{6,2},{7,3},{8,12},{9,13},{10,... | collective-permute-start | bytes 393224 | tf_op jit(solution)/shard_map/ppermute | solution.py:16
  54.6 3.2 %collective-permute-done.13 = f32[34,1024]{1,0:T(8,128)S(1)} collective-permute-done((f32[34,1024]{1,0:T(8,128)S(1)}, f32[34,1024]{1,0:T(8,128)S(1)}, u32[]{:S(2)}, u32[]{:S(2)}) %collective-permute-start.13) | collective-permute-done | bytes 139296 | tf_op jit(solution)/shard_map/ppermute | solution.py:16
  57.8 0.9 %collective-permute-start.14 = (f32[34,1024]{1,0:T(8,128)S(1)}, f32[34,1024]{1,0:T(8,128)S(1)}, u32[]{:S(2)}, u32[]{:S(2)}) collective-permute-start(f32[34,1024]{1,0:T(8,128)S(1)} %fusion.110), channel_id=1, source_target_pairs={{0,4},{1,5},{2,6},{3,7},{4,0},{5,1},{6,2},{7,3},{8,12},{9,13},{10,... | collective-permute-start | bytes 417800 | tf_op jit(solution)/shard_map/ppermute | solution.py:16
  58.7 6.6 %collective-permute-done.22 = f32[128,256]{1,0:T(8,128)S(1)} collective-permute-done((f32[128,256]{1,0:T(8,128)S(1)}, f32[128,256]{1,0:T(8,128)S(1)}, u32[]{:S(2)}, u32[]{:S(2)}) %collective-permute-start.22) | collective-permute-done | bytes 131104 | tf_op jit(solution)/shard_map/ppermute | solution.py:16
  65.3 0.8 collective-permute-start.23
  66.0 1.9 %collective-permute-done.14 = f32[34,1024]{1,0:T(8,128)S(1)} collective-permute-done((f32[34,1024]{1,0:T(8,128)S(1)}, f32[34,1024]{1,0:T(8,128)S(1)}, u32[]{:S(2)}, u32[]{:S(2)}) %collective-permute-start.14) | collective-permute-done | bytes 139296 | tf_op jit(solution)/shard_map/ppermute | solution.py:16
  67.9 0.9 %collective-permute-start.15 = (bf16[34,1024]{1,0:T(8,128)(2,1)S(1)}, bf16[34,1024]{1,0:T(8,128)(2,1)S(1)}, u32[]{:S(2)}, u32[]{:S(2)}) collective-permute-start(bf16[34,1024]{1,0:T(8,128)(2,1)S(1)} %multiply_convert_fusion.4), channel_id=1, source_target_pairs={{0,1},{1,0},{2,3},{3,2},{4,5},{5,4},{6,7},{7,6},{8,9},{9,8},{10,11... | collective-permute-start | bytes 208904 | tf_op jit(solution)/shard_map/ppermute | solution.py:16
  69.6 1.7 %collective-permute-start.24 = (bf16[256,256]{1,0:T(8,128)(2,1)S(1)}, bf16[256,256]{1,0:T(8,128)(2,1)S(1)}, u32[]{:S(2)}, u32[]{:S(2)}) collective-permute-start(bf16[256,256]{1,0:T(8,128)(2,1)S(1)} %maximum_select_fusion.7), channel_id=1, source_target_pairs={{0,16},{8,24},{16,0},{24,8},{1,17},{9,25},{17,1},{25,9},{2,18},{10... | collective-permute-start | bytes 393224 | tf_op jit(solution)/shard_map/ppermute | solution.py:16
  71.3 1.1 %collective-permute-done.15 = bf16[34,1024]{1,0:T(8,128)(2,1)S(1)} collective-permute-done((bf16[34,1024]{1,0:T(8,128)(2,1)S(1)}, bf16[34,1024]{1,0:T(8,128)(2,1)S(1)}, u32[]{:S(2)}, u32[]{:S(2)}) %collective-permute-start.15) | collective-permute-done | bytes 69664 | tf_op jit(solution)/shard_map/ppermute | solution.py:16
  72.5 1.5 %collective-permute-start.16 = (bf16[68,1024]{1,0:T(8,128)(2,1)S(1)}, bf16[68,1024]{1,0:T(8,128)(2,1)S(1)}, u32[]{:S(2)}, u32[]{:S(2)}) collective-permute-start(bf16[68,1024]{1,0:T(8,128)(2,1)S(1)} %pad_maximum_fusion.6), channel_id=1, source_target_pairs={{0,16},{8,24},{16,0},{24,8},{1,17},{9,25},{17,1},{25,9},{2,18},{10... | collective-permute-start | bytes 417800 | tf_op jit(solution)/shard_map/ppermute | solution.py:16
  74.2 1.9 %collective-permute-done.24 = bf16[256,256]{1,0:T(8,128)(2,1)S(1)} collective-permute-done((bf16[256,256]{1,0:T(8,128)(2,1)S(1)}, bf16[256,256]{1,0:T(8,128)(2,1)S(1)}, u32[]{:S(2)}, u32[]{:S(2)}) %collective-permute-start.24) | collective-permute-done | bytes 131104 | tf_op jit(solution)/shard_map/ppermute | solution.py:16
  76.2 1.6 %collective-permute-done.16 = bf16[68,1024]{1,0:T(8,128)(2,1)S(1)} collective-permute-done((bf16[68,1024]{1,0:T(8,128)(2,1)S(1)}, bf16[68,1024]{1,0:T(8,128)(2,1)S(1)}, u32[]{:S(2)}, u32[]{:S(2)}) %collective-permute-start.16) | collective-permute-done | bytes 139296 | tf_op jit(solution)/shard_map/ppermute | solution.py:16
  78.0 2.5 %fusion.60 = bf16[2,4,32,256]{3,2,1,0:T(8,128)(2,1)} fusion(f32[2,4,32,256]{3,2,1,0:T(8,128)S(1)} %bitcast.185, f32[2,10,38,256]{3,2,1,0:T(8,128)S(1)} %maximum_convert_fusion.1, f32[256]{0:T(256)S(1)} %bitcast.283, f32[256]{0:T(256)S(1)} %bitcast.285, f32[256]{0:T(256)S(1)} %bitcast.191, f32[256]{0:T(256)S(1)} %bitcast.193, f32[256]{0:T(256)S(1)} %bitcast.195, ...), kind=kLoop, calls=%fused_computation.126 | loop fusion | flops 6488064 | bytes 13288448 | tf_op jit(solution)/shard_map/convert_element_type | solution.py:171
  80.5 1.1 %fusion.8 = f32[1024,256]{1,0:T(8,128)} fusion(bf16[512,256]{1,0:T(8,128)(2,1)S(1)} %maximum_select_fusion.3, bf16[512,256]{1,0:T(8,128)(2,1)S(1)} %collective-permute-done.25, pred[]{:T(512)S(6)} %eq.22), kind=kLoop, calls=%fused_computation.65 | loop fusion | flops 2621440 | bytes 1572865 | tf_op jit(solution)/shard_map/convert_element_type | solution.py:123
  81.7 1.1 %fusion.7 = f32[256,1024]{1,0:T(8,128)} fusion(bf16[128,1024]{1,0:T(8,128)(2,1)S(1)} %maximum_select_fusion.2, bf16[128,1024]{1,0:T(8,128)(2,1)S(1)} %slice.896, pred[]{:T(512)S(6)} %eq.22), kind=kLoop, calls=%fused_computation.63 | loop fusion | flops 2621440 | bytes 1572865 | tf_op jit(solution)/shard_map/convert_element_type | solution.py:123
  (122 shorter events, 11.8 us)
Async XLA Ops:
  0.6 18.8 %copy-start = (bf16[256,1024]{1,0:T(8,128)(2,1)S(1)}, bf16[256,1024]{1,0:T(8,128)(2,1)}, u32[]{:S(2)}) copy-start(bf16[256,1024]{1,0:T(8,128)(2,1)} %param.11) | copy-start | bytes 1572868
  1.6 0.9 %copy-start.1 = (bf16[2,4,32,256]{3,2,1,0:T(8,128)(2,1)S(1)}, bf16[2,4,32,256]{3,2,1,0:T(8,128)(2,1)}, u32[]{:S(2)}) copy-start(bf16[2,4,32,256]{3,2,1,0:T(8,128)(2,1)} %param.7) | copy-start | bytes 393220
  1.6 7.5 %copy-start.2 = (f32[7,7,256]{2,1,0:T(8,128)S(1)}, f32[7,7,256]{2,1,0:T(8,128)}, u32[]{:S(2)}) copy-start(f32[7,7,256]{2,1,0:T(8,128)} %param.9) | copy-start | bytes 150532
  1.7 11.2 %collective-permute-start.4 = (bf16[2,2,4,8,256]{4,3,2,0,1:T(8,128)(2,1)S(1)}, bf16[2,2,4,8,256]{4,3,2,0,1:T(8,128)(2,1)S(1)}, u32[]{:S(2)}, u32[]{:S(2)}) collective-permute-start(bf16[2,2,4,8,256]{4,3,2,0,1:T(8,128)(2,1)S(1)} %bitcast.187), channel_id=1, source_target_pairs={{0,8},{8,0},{16,24},{24,16},{1,9},{9,1},{17,25},{25,17},{2,10},{10... | collective-permute-start | bytes 196616 | tf_op jit(solution)/shard_map/ppermute | solution.py:16
  2.6 6.8 %collective-permute-start = (bf16[2,4,3,256]{3,2,1,0:T(4,128)(2,1)S(1)}, bf16[2,4,3,256]{3,2,1,0:T(4,128)(2,1)S(1)}, u32[]{:S(2)}, u32[]{:S(2)}) collective-permute-start(bf16[2,4,3,256]{3,2,1,0:T(4,128)(2,1)S(1)} %get-tuple-element.68), channel_id=1, source_target_pairs={{0,1},{1,0},{2,3},{3,2},{4,5},{5,4},{6,7},{7,6},{8,9},{9,8},{10,11... | collective-permute-start | bytes 36872 | tf_op jit(solution)/shard_map/ppermute | solution.py:31
  5.6 6.4 %collective-permute-start.1 = (bf16[2,4,3,256]{3,2,1,0:T(4,128)(2,1)S(1)}, bf16[2,4,3,256]{3,2,1,0:T(4,128)(2,1)S(1)}, u32[]{:S(2)}, u32[]{:S(2)}) collective-permute-start(bf16[2,4,3,256]{3,2,1,0:T(4,128)(2,1)S(1)} %get-tuple-element.69), channel_id=1, source_target_pairs={{1,2},{3,4},{5,6},{7,0},{2,1},{4,3},{6,5},{0,7},{9,10},{11,12},{13... | collective-permute-start | bytes 36872 | tf_op jit(solution)/shard_map/ppermute | solution.py:30
  12.1 4.3 %collective-permute-start.2 = (bf16[2,3,38,256]{3,2,1,0:T(8,128)(2,1)S(1)}, bf16[2,3,38,256]{3,2,1,0:T(8,128)(2,1)S(1)}, u32[]{:S(2)}, u32[]{:S(2)}) collective-permute-start(bf16[2,3,38,256]{3,2,1,0:T(8,128)(2,1)S(1)} %get-tuple-element.64), channel_id=1, source_target_pairs={{0,8},{8,0},{16,24},{24,16},{1,9},{9,1},{17,25},{25,17},{2,10},{10... | collective-permute-start | bytes 350216 | tf_op jit(solution)/shard_map/ppermute | solution.py:31
  12.2 4.2 %collective-permute-start.3 = (bf16[2,3,38,256]{3,2,1,0:T(8,128)(2,1)S(1)}, bf16[2,3,38,256]{3,2,1,0:T(8,128)(2,1)S(1)}, u32[]{:S(2)}, u32[]{:S(2)}) collective-permute-start(bf16[2,3,38,256]{3,2,1,0:T(8,128)(2,1)S(1)} %get-tuple-element.65), channel_id=1, source_target_pairs={{8,16},{16,8},{9,17},{17,9},{10,18},{18,10},{11,19},{19,11},{12,20... | collective-permute-start | bytes 350216 | tf_op jit(solution)/shard_map/ppermute | solution.py:30
  13.0 7.5 %collective-permute-start.5 = (bf16[2,1,4,16,256]{4,3,2,0,1:T(8,128)(2,1)S(1)}, bf16[2,1,4,16,256]{4,3,2,0,1:T(8,128)(2,1)S(1)}, u32[]{:S(2)}, u32[]{:S(2)}) collective-permute-start(bf16[2,1,4,16,256]{4,3,2,0,1:T(8,128)(2,1)S(1)} %get-tuple-element.70), channel_id=1, source_target_pairs={{0,16},{8,24},{16,0},{24,8},{1,17},{9,25},{17,1},{25,9},{2,18},{10... | collective-permute-start | bytes 196616 | tf_op jit(solution)/shard_map/ppermute | solution.py:16
  18.6 0.7 copy-start.3
  19.5 1.1 %copy-start.4 = (bf16[1024,256]{1,0:T(8,128)(2,1)S(1)}, bf16[1024,256]{1,0:T(8,128)(2,1)}, u32[]{:S(2)}) copy-start(bf16[1024,256]{1,0:T(8,128)(2,1)} %param.12) | copy-start | bytes 1572868
  20.5 0.7 copy-start.5
  25.5 6.4 %collective-permute-start.6 = (bf16[2,4,3,256]{3,2,1,0:T(4,128)(2,1)S(1)}, bf16[2,4,3,256]{3,2,1,0:T(4,128)(2,1)S(1)}, u32[]{:S(2)}, u32[]{:S(2)}) collective-permute-start(bf16[2,4,3,256]{3,2,1,0:T(4,128)(2,1)S(1)} %get-tuple-element.66), channel_id=1, source_target_pairs={{0,1},{1,0},{2,3},{3,2},{4,5},{5,4},{6,7},{7,6},{8,9},{9,8},{10,11... | collective-permute-start | bytes 36872 | tf_op jit(solution)/shard_map/ppermute | solution.py:31
  25.6 6.5 %collective-permute-start.7 = (bf16[2,4,3,256]{3,2,1,0:T(4,128)(2,1)S(1)}, bf16[2,4,3,256]{3,2,1,0:T(4,128)(2,1)S(1)}, u32[]{:S(2)}, u32[]{:S(2)}) collective-permute-start(bf16[2,4,3,256]{3,2,1,0:T(4,128)(2,1)S(1)} %get-tuple-element.67), channel_id=1, source_target_pairs={{1,2},{3,4},{5,6},{7,0},{2,1},{4,3},{6,5},{0,7},{9,10},{11,12},{13... | collective-permute-start | bytes 36872 | tf_op jit(solution)/shard_map/ppermute | solution.py:30
  29.5 8.1 %collective-permute-start.10 = (bf16[136,1024]{1,0:T(8,128)(2,1)S(1)}, bf16[136,1024]{1,0:T(8,128)(2,1)S(1)}, u32[]{:S(2)}, u32[]{:S(2)}) collective-permute-start(bf16[136,1024]{1,0:T(8,128)(2,1)S(1)} %pad_maximum_fusion), channel_id=1, source_target_pairs={{0,8},{8,0},{16,24},{24,16},{1,9},{9,1},{17,25},{25,17},{2,10},{10... | collective-permute-start | bytes 835592 | tf_op jit(solution)/shard_map/ppermute | solution.py:16
  31.8 2.7 %collective-permute-start.18 = (bf16[512,256]{1,0:T(8,128)(2,1)S(1)}, bf16[512,256]{1,0:T(8,128)(2,1)S(1)}, u32[]{:S(2)}, u32[]{:S(2)}) collective-permute-start(bf16[512,256]{1,0:T(8,128)(2,1)S(1)} %dynamic-slice_convert_fusion), channel_id=1, source_target_pairs={{0,8},{8,0},{16,24},{24,16},{1,9},{9,1},{17,25},{25,17},{2,10},{10... | collective-permute-start | bytes 786440 | tf_op jit(solution)/shard_map/ppermute | solution.py:16
  32.2 18.4 %collective-permute-start.8 = (bf16[2,3,38,256]{3,2,1,0:T(8,128)(2,1)S(1)}, bf16[2,3,38,256]{3,2,1,0:T(8,128)(2,1)S(1)}, u32[]{:S(2)}, u32[]{:S(2)}) collective-permute-start(bf16[2,3,38,256]{3,2,1,0:T(8,128)(2,1)S(1)} %get-tuple-element.62), channel_id=1, source_target_pairs={{0,8},{8,0},{16,24},{24,16},{1,9},{9,1},{17,25},{25,17},{2,10},{10... | collective-permute-start | bytes 350216 | tf_op jit(solution)/shard_map/ppermute | solution.py:31
  33.6 17.0 %collective-permute-start.9 = (bf16[2,3,38,256]{3,2,1,0:T(8,128)(2,1)S(1)}, bf16[2,3,38,256]{3,2,1,0:T(8,128)(2,1)S(1)}, u32[]{:S(2)}, u32[]{:S(2)}) collective-permute-start(bf16[2,3,38,256]{3,2,1,0:T(8,128)(2,1)S(1)} %get-tuple-element.63), channel_id=1, source_target_pairs={{8,16},{16,8},{9,17},{17,9},{10,18},{18,10},{11,19},{19,11},{12,20... | collective-permute-start | bytes 350216 | tf_op jit(solution)/shard_map/ppermute | solution.py:30
  34.6 8.1 %collective-permute-start.19 = (bf16[256,256]{1,0:T(8,128)(2,1)S(1)}, bf16[256,256]{1,0:T(8,128)(2,1)S(1)}, u32[]{:S(2)}, u32[]{:S(2)}) collective-permute-start(bf16[256,256]{1,0:T(8,128)(2,1)S(1)} %dynamic-slice_convert_fusion.2), channel_id=1, source_target_pairs={{0,16},{8,24},{16,0},{24,8},{1,17},{9,25},{17,1},{25,9},{2,18},{10... | collective-permute-start | bytes 393224 | tf_op jit(solution)/shard_map/ppermute | solution.py:16
  37.7 8.1 %collective-permute-start.11 = (bf16[68,1024]{1,0:T(8,128)(2,1)S(1)}, bf16[68,1024]{1,0:T(8,128)(2,1)S(1)}, u32[]{:S(2)}, u32[]{:S(2)}) collective-permute-start(bf16[68,1024]{1,0:T(8,128)(2,1)S(1)} %pad_maximum_fusion.5), channel_id=1, source_target_pairs={{0,16},{8,24},{16,0},{24,8},{1,17},{9,25},{17,1},{25,9},{2,18},{10... | collective-permute-start | bytes 417800 | tf_op jit(solution)/shard_map/ppermute | solution.py:16
  42.7 4.5 %collective-permute-start.20 = (bf16[128,256]{1,0:T(8,128)(2,1)S(1)}, bf16[128,256]{1,0:T(8,128)(2,1)S(1)}, u32[]{:S(2)}, u32[]{:S(2)}) collective-permute-start(bf16[128,256]{1,0:T(8,128)(2,1)S(1)} %dynamic-slice_convert_fusion.4), channel_id=1, source_target_pairs={{0,1},{1,0},{2,3},{3,2},{4,5},{5,4},{6,7},{7,6},{8,9},{9,8},{10,11... | collective-permute-start | bytes 196616 | tf_op jit(solution)/shard_map/ppermute | solution.py:16
  45.9 4.5 %collective-permute-start.12 = (bf16[34,1024]{1,0:T(8,128)(2,1)S(1)}, bf16[34,1024]{1,0:T(8,128)(2,1)S(1)}, u32[]{:S(2)}, u32[]{:S(2)}) collective-permute-start(bf16[34,1024]{1,0:T(8,128)(2,1)S(1)} %pad_maximum_fusion.7), channel_id=1, source_target_pairs={{0,1},{1,0},{2,3},{3,2},{4,5},{5,4},{6,7},{7,6},{8,9},{9,8},{10,11... | collective-permute-start | bytes 208904 | tf_op jit(solution)/shard_map/ppermute | solution.py:16
  47.2 5.1 %collective-permute-start.21 = (f32[128,256]{1,0:T(8,128)S(1)}, f32[128,256]{1,0:T(8,128)S(1)}, u32[]{:S(2)}, u32[]{:S(2)}) collective-permute-start(f32[128,256]{1,0:T(8,128)S(1)} %convert_add_fusion.4), channel_id=1, source_target_pairs={{0,2},{1,3},{2,0},{3,1},{4,6},{5,7},{6,4},{7,5},{8,10},{9,11},{10,... | collective-permute-start | bytes 393224 | tf_op jit(solution)/shard_map/ppermute | solution.py:16
  50.5 7.3 %collective-permute-start.13 = (f32[34,1024]{1,0:T(8,128)S(1)}, f32[34,1024]{1,0:T(8,128)S(1)}, u32[]{:S(2)}, u32[]{:S(2)}) collective-permute-start(f32[34,1024]{1,0:T(8,128)S(1)} %pad_maximum_fusion.4), channel_id=1, source_target_pairs={{0,2},{1,3},{2,0},{3,1},{4,6},{5,7},{6,4},{7,5},{8,10},{9,11},{10,... | collective-permute-start | bytes 417800 | tf_op jit(solution)/shard_map/ppermute | solution.py:16
  52.4 12.8 %collective-permute-start.22 = (f32[128,256]{1,0:T(8,128)S(1)}, f32[128,256]{1,0:T(8,128)S(1)}, u32[]{:S(2)}, u32[]{:S(2)}) collective-permute-start(f32[128,256]{1,0:T(8,128)S(1)} %add.589), channel_id=1, source_target_pairs={{0,4},{1,5},{2,6},{3,7},{4,0},{5,1},{6,2},{7,3},{8,12},{9,13},{10,... | collective-permute-start | bytes 393224 | tf_op jit(solution)/shard_map/ppermute | solution.py:16
  57.8 10.1 %collective-permute-start.14 = (f32[34,1024]{1,0:T(8,128)S(1)}, f32[34,1024]{1,0:T(8,128)S(1)}, u32[]{:S(2)}, u32[]{:S(2)}) collective-permute-start(f32[34,1024]{1,0:T(8,128)S(1)} %fusion.110), channel_id=1, source_target_pairs={{0,4},{1,5},{2,6},{3,7},{4,0},{5,1},{6,2},{7,3},{8,12},{9,13},{10,... | collective-permute-start | bytes 417800 | tf_op jit(solution)/shard_map/ppermute | solution.py:16
  65.3 4.3 %collective-permute-start.23 = (bf16[128,256]{1,0:T(8,128)(2,1)S(1)}, bf16[128,256]{1,0:T(8,128)(2,1)S(1)}, u32[]{:S(2)}, u32[]{:S(2)}) collective-permute-start(bf16[128,256]{1,0:T(8,128)(2,1)S(1)} %multiply_convert_fusion.5), channel_id=1, source_target_pairs={{0,1},{1,0},{2,3},{3,2},{4,5},{5,4},{6,7},{7,6},{8,9},{9,8},{10,11... | collective-permute-start | bytes 196616 | tf_op jit(solution)/shard_map/ppermute | solution.py:16
  67.9 4.5 %collective-permute-start.15 = (bf16[34,1024]{1,0:T(8,128)(2,1)S(1)}, bf16[34,1024]{1,0:T(8,128)(2,1)S(1)}, u32[]{:S(2)}, u32[]{:S(2)}) collective-permute-start(bf16[34,1024]{1,0:T(8,128)(2,1)S(1)} %multiply_convert_fusion.4), channel_id=1, source_target_pairs={{0,1},{1,0},{2,3},{3,2},{4,5},{5,4},{6,7},{7,6},{8,9},{9,8},{10,11... | collective-permute-start | bytes 208904 | tf_op jit(solution)/shard_map/ppermute | solution.py:16
  69.6 6.4 %collective-permute-start.24 = (bf16[256,256]{1,0:T(8,128)(2,1)S(1)}, bf16[256,256]{1,0:T(8,128)(2,1)S(1)}, u32[]{:S(2)}, u32[]{:S(2)}) collective-permute-start(bf16[256,256]{1,0:T(8,128)(2,1)S(1)} %maximum_select_fusion.7), channel_id=1, source_target_pairs={{0,16},{8,24},{16,0},{24,8},{1,17},{9,25},{17,1},{25,9},{2,18},{10... | collective-permute-start | bytes 393224 | tf_op jit(solution)/shard_map/ppermute | solution.py:16
  72.5 5.3 %collective-permute-start.16 = (bf16[68,1024]{1,0:T(8,128)(2,1)S(1)}, bf16[68,1024]{1,0:T(8,128)(2,1)S(1)}, u32[]{:S(2)}, u32[]{:S(2)}) collective-permute-start(bf16[68,1024]{1,0:T(8,128)(2,1)S(1)} %pad_maximum_fusion.6), channel_id=1, source_target_pairs={{0,16},{8,24},{16,0},{24,8},{1,17},{9,25},{17,1},{25,9},{2,18},{10... | collective-permute-start | bytes 417800 | tf_op jit(solution)/shard_map/ppermute | solution.py:16
  76.1 4.4 %collective-permute-start.25 = (bf16[512,256]{1,0:T(8,128)(2,1)S(1)}, bf16[512,256]{1,0:T(8,128)(2,1)S(1)}, u32[]{:S(2)}, u32[]{:S(2)}) collective-permute-start(bf16[512,256]{1,0:T(8,128)(2,1)S(1)} %maximum_select_fusion.3), channel_id=1, source_target_pairs={{0,8},{8,0},{16,24},{24,16},{1,9},{9,1},{17,25},{25,17},{2,10},{10... | collective-permute-start | bytes 786440 | tf_op jit(solution)/shard_map/ppermute | solution.py:16
  78.0 3.7 %collective-permute-start.17 = (bf16[136,1024]{1,0:T(8,128)(2,1)S(1)}, bf16[136,1024]{1,0:T(8,128)(2,1)S(1)}, u32[]{:S(2)}, u32[]{:S(2)}) collective-permute-start(bf16[136,1024]{1,0:T(8,128)(2,1)S(1)} %pad_maximum_fusion.1), channel_id=1, source_target_pairs={{0,8},{8,0},{16,24},{24,16},{1,9},{9,1},{17,25},{25,17},{2,10},{10... | collective-permute-start | bytes 835592 | tf_op jit(solution)/shard_map/ppermute | solution.py:16

commit v3 on v0

--- a/solution.py
+++ b/solution.py
@@ -8,19 +8,59 @@
 norm_eps = 1e-06
 
 
-def with_halo(block, sides, width, periodic):
-    for axis, dim in sides:
-        count = lax.axis_size(axis)
-        forward = [(i, i + 1) for i in range(count - 1)]
-        if periodic:
-            forward.append((count - 1, 0))
-        backward = [(target, source) for source, target in forward]
-        low = lax.ppermute(
-            lax.slice_in_dim(block, block.shape[dim] - width, None, axis=dim), axis, forward
+def bits_of(axis):
+    return [1 << k for k in range((lax.axis_size(axis) - 1).bit_length())]
+
+
+def swap(value, axis, bit):
+    return lax.ppermute(value, axis, [(i, i ^ bit) for i in range(lax.axis_size(axis))])
+
+
+def edges(block, axis, dim, width):
+    low = lax.slice_in_dim(block, 0, width, axis=dim)
+    high = lax.slice_in_dim(block, block.shape[dim] - width, None, axis=dim)
+    odd = lax.axis_index(axis) % 2 == 1
+    return jnp.where(odd, low, high), jnp.where(odd, high, low)
+
+
+def swap_outer(edge, axis, periodic):
+    count = lax.axis_size(axis)
+    pairs = [(i, (i + 1) % count) for i in range(1, count, 2)]
+    if not periodic:
+        pairs = [(i, j) for i, j in pairs if j]
+    return lax.ppermute(edge, axis, pairs + [(j, i) for i, j in pairs])
+
+
+def with_edges(block, from_inner, from_outer, axis, dim):
+    odd = lax.axis_index(axis) % 2 == 1
+    before = jnp.where(odd, from_inner, from_outer)
+    after = jnp.where(odd, from_outer, from_inner)
+    return jnp.concatenate([before, block, after], axis=dim)
+
+
+def with_halo(block, axis, dim, width, periodic):
+    to_inner, to_outer = edges(block, axis, dim, width)
+    from_outer = swap_outer(to_outer, axis, periodic)
+    from_inner = swap(to_inner, axis, 1)
+    return with_edges(block, from_inner, from_outer, axis, dim)
+
+
+def to_bands(teacher, axis):
+    batch_size, rows, cols, channel_count = teacher.shape
+    count = lax.axis_size(axis)
+    band = rows // count
+    state = teacher.reshape(batch_size, count, band, cols, channel_count)
+    for bit in bits_of(axis):
+        upper = (lax.axis_index(axis) // bit) % 2
+        state = state.reshape(batch_size, -1, 2, band, state.shape[3], channel_count)
+        mine = lax.dynamic_index_in_dim(state, upper, axis=2, keepdims=False)
+        got = swap(lax.dynamic_index_in_dim(state, 1 - upper, axis=2, keepdims=False), axis, bit)
+        state = jnp.where(
+            upper == 1,
+            jnp.concatenate([got, mine], axis=3),
+            jnp.concatenate([mine, got], axis=3),
         )
-        high = lax.ppermute(lax.slice_in_dim(block, 0, width, axis=dim), axis, backward)
-        block = jnp.concatenate([low, block, high], axis=dim)
-    return block
+    return state.reshape(batch_size, band, -1, channel_count)
 
 
 def gelu_tanh(values):
@@ -50,13 +90,128 @@
     return result
 
 
+def half_of(value, upper):
+    count = value.shape[0] // 2
+    return lax.dynamic_slice_in_dim(value, upper * count, count, axis=0)
+
+
+def total_of(terms):
+    total = terms[0].astype(jnp.float32)
+    for term in terms[1:]:
+        total = total + term.astype(jnp.float32)
+    return total
+
+
+def flat_rows(block):
+    return block.reshape(-1, block.shape[-1])
+
+
+def after(value, other):
+    return lax.optimization_barrier((value, other))[0]
+
+
+def exchange(parts, axis, bit, halved, sent_as, rider=None):
+    upper = (lax.axis_index(axis) // bit) % 2
+    if halved:
+        give = [total_of([half_of(t, 1 - upper) for t in terms]) for terms in parts]
+        keep = [total_of([half_of(t, upper) for t in terms]) for terms in parts]
+    else:
+        give = keep = [total_of(terms) for terms in parts]
+    give = [value.astype(sent_as) for value in give]
+    if not halved:
+        keep = [value.astype(jnp.float32) for value in give]
+    counts = [value.shape[0] for value in give]
+    if rider is not None:
+        give = give + [flat_rows(rider).astype(sent_as)]
+        counts = counts + [give[-1].shape[0]]
+    sent = jnp.concatenate(give, axis=0) if len(give) > 1 else give[0]
+    got = swap(sent, axis, bit)
+    got = split_rows(got, counts) if len(give) > 1 else [got]
+    parts = [[k, g] for k, g in zip(keep, got)]
+    ridden = None if rider is None else got[-1].astype(rider.dtype).reshape(rider.shape)
+    return parts, ridden, sent
+
+
+def split_rows(value, counts):
+    pieces, start = [], 0
+    for count in counts:
+        pieces.append(lax.slice_in_dim(value, start, start + count, axis=0))
+        start += count
+    return pieces
+
+
+def gather_halves(chunks, axis, bit):
+    upper = (lax.axis_index(axis) // bit) % 2
+    got = swap(chunks, axis, bit)
+    return jnp.where(
+        upper == 1, jnp.concatenate([got, chunks]), jnp.concatenate([chunks, got])
+    )
+
+
+def carried(axis, bit):
+    index = lax.axis_index(axis)
+    lower = index % bit // 2
+    return lower == jnp.where(index % 2 == 0, 0, bit // 2 - 1)
+
+
+def sum_stages():
+    lat_bits, lon_bits = bits_of("lat"), bits_of("lon")
+    lat_stages = [("lat", bit) for bit in lat_bits[1:]]
+    lon_stages = [("lon", bit) for bit in lon_bits]
+    return lat_stages, lon_stages, [lat_stages[0], lon_stages[0]]
+
+
+def sum_over_mesh(lead, trail, divisor, block, inner, outer, width):
+    lat_stages, lon_stages, halved = sum_stages()
+    last = (lat_stages + lon_stages)[-1]
+    for stages, dim, periodic in ((lat_stages, 1, False), (lon_stages, 2, True)):
+        for axis, bit in stages:
+            rider = jnp.stack(edges(block, axis, dim, width)) if bit == 1 else outer
+            is_halved = (axis, bit) in halved
+            sent_as = jnp.bfloat16 if is_halved or (axis, bit) == last else jnp.float32
+            lead, _, _ = exchange(lead, axis, bit, is_halved, sent_as)
+            trail, got, sent = exchange(trail, axis, bit, is_halved, sent_as, rider)
+            lead = after(lead, sent)
+            if bit == 1:
+                inner, outer = got[0], got[1]
+            else:
+                outer = jnp.where(carried(axis, bit), got, outer)
+        if not periodic:
+            index = lax.axis_index(axis)
+            at_end = (index == 0) | (index == lax.axis_size(axis) - 1)
+            outer = jnp.where(at_end, jnp.zeros_like(outer), outer)
+        block = with_edges(block, inner, outer, axis, dim)
+    lead = [(total_of(terms) / divisor).astype(jnp.bfloat16) for terms in lead]
+    trail = [(total_of(terms) / divisor).astype(jnp.bfloat16) for terms in trail]
+    return lead, trail, block
+
+
+def gather_sums(lead, trail):
+    for axis, bit in sum_stages()[2][::-1] + [("lat", 1)]:
+        lead = gather_halves(lead, axis, bit)
+        trail = gather_halves(trail, axis, bit)
+    return lead, trail
+
+
+def columns_half(value, upper):
+    count = value.shape[1] // 2
+    return lax.dynamic_slice_in_dim(value, upper * count, count, axis=1)
+
+
+def cell_products(left, right):
+    return lax.dot_general(
+        left, right, (((0,), (0,)), ((), ())), preferred_element_type=jnp.float32
+    )
+
+
 def local(student, teacher, dw_weight, norm_gain, w_in, w_out, layer_scale):
     batch_size, tile_rows, tile_cols, channel_count = student.shape
     kernel_size = dw_weight.shape[0]
     half_kernel = kernel_size // 2
     cell_total = batch_size * tile_rows * lax.axis_size("lat") * tile_cols * lax.axis_size("lon")
-    lon_padded = with_halo(student, (("lon", 2),), half_kernel, True)
-    padded_bf = with_halo(lon_padded, (("lat", 1),), half_kernel, False)
+    lon_padded = with_halo(student, "lon", 2, half_kernel, True)
+    lon_padded, teacher = lax.optimization_barrier((lon_padded, teacher))
+    padded_bf = with_halo(lon_padded, "lat", 1, half_kernel, False)
     padded = padded_bf.astype(jnp.float32)
     smoothed = apply_stencil(padded, dw_weight, tile_rows, tile_cols, False).reshape(
         -1, channel_count
@@ -71,19 +226,22 @@
     hidden = gelu_tanh(preact).astype(jnp.bfloat16)
     mlp_out = jnp.dot(hidden, w_out, preferred_element_type=jnp.float32)
     output = student.reshape(-1, channel_count).astype(jnp.float32) + layer_scale * mlp_out
-    target = lax.all_to_all(teacher, "lat", split_axis=1, concat_axis=2, tiled=True)
+    target = to_bands(teacher, "lat")
     misfit = output - target.reshape(-1, channel_count).astype(jnp.float32)
     out_grad = (layer_scale * misfit).astype(jnp.bfloat16)
-    part_out = lax.dot_general(
-        hidden, out_grad, (((0,), (0,)), ((), ())), preferred_element_type=jnp.float32
-    )
+    upper = lax.axis_index("lat") % 2
+    got_out = swap(
+        cell_products(columns_half(hidden, 1 - upper), out_grad).astype(jnp.bfloat16), "lat", 1
+    )
+    kept_out = cell_products(columns_half(hidden, upper), out_grad)
     hidden_grad = lax.dot_general(
         out_grad, w_out, (((1,), (1,)), ((), ())), preferred_element_type=jnp.float32
     )
     preact_grad = (hidden_grad * gelu_slope(preact)).astype(jnp.bfloat16)
-    part_in = lax.dot_general(
-        normed, preact_grad, (((0,), (0,)), ((), ())), preferred_element_type=jnp.float32
-    )
+    got_in = swap(
+        cell_products(columns_half(preact_grad, 1 - upper), normed).astype(jnp.bfloat16), "lat", 1
+    )
+    kept_in = cell_products(columns_half(preact_grad, upper), normed)
     normed_grad = lax.dot_general(
         preact_grad, w_in, (((1,), (1,)), ((), ())), preferred_element_type=jnp.float32
     )
@@ -92,10 +250,7 @@
     second_mean = jnp.mean(unit_grad * unit_norm, axis=-1, keepdims=True)
     conv_grad = (inv_std * (unit_grad - first_mean - unit_norm * second_mean)).astype(jnp.bfloat16)
     conv_grid = conv_grad.reshape(student.shape)
-    grad_lon = with_halo(conv_grid, (("lon", 2),), half_kernel, True)
-    padded_grad = with_halo(grad_lon, (("lat", 1),), half_kernel, False).astype(jnp.float32)
-    back_conv = apply_stencil(padded_grad, dw_weight, tile_rows, tile_cols, True)
-    grad_student = (misfit.reshape(student.shape) + back_conv).astype(jnp.bfloat16)
+    inner, outer = swap(jnp.stack(edges(conv_grid, "lat", 1, half_kernel)), "lat", 1)
     conv_grad_f = conv_grid.astype(jnp.float32)
     kernel_terms = []
     for row_off in range(kernel_size):
@@ -107,9 +262,35 @@
                     axis=(0, 1, 2),
                 )
             )
-    part_dw = jnp.stack(kernel_terms).reshape(kernel_size, kernel_size, channel_count)
-    sum_in, sum_out, sum_dw = lax.psum((part_in, part_out, part_dw), ("lat", "lon"))
-    return (grad_student, sum_in / cell_total, sum_out / cell_total, sum_dw / cell_total)
+    part_dw = jnp.stack(kernel_terms)
+    tap_count = kernel_size * kernel_size
+    part_dw = jnp.pad(part_dw, ((0, -tap_count % 64), (0, 0)))
+    got_dw = swap(half_of(part_dw, 1 - upper).astype(jnp.bfloat16), "lat", 1)
+    (out_chunk,), (in_chunk, dw_chunk), padded_grad = sum_over_mesh(
+        [[kept_out, got_out]],
+        [[kept_in, got_in], [half_of(part_dw, upper), got_dw]],
+        cell_total,
+        conv_grid,
+        inner,
+        outer,
+        half_kernel,
+    )
+    back_conv = apply_stencil(
+        padded_grad.astype(jnp.float32), dw_weight, tile_rows, tile_cols, True
+    )
+    grad_student = (misfit.reshape(student.shape) + back_conv).astype(jnp.bfloat16)
+    hidden_rows = in_chunk.shape[0]
+    mixed = jnp.concatenate([in_chunk.T, dw_chunk.reshape(-1, hidden_rows)])
+    out_chunks, in_chunks = gather_sums(out_chunk[None], mixed[None])
+    sum_out = out_chunks.astype(jnp.float32).reshape(w_out.shape)
+    sum_in = jnp.swapaxes(in_chunks[:, :channel_count], 0, 1).astype(jnp.float32)
+    sum_dw = in_chunks[:, channel_count:].astype(jnp.float32).reshape(-1, channel_count)
+    return (
+        grad_student,
+        sum_in.reshape(w_in.shape),
+        sum_out,
+        sum_dw[:tap_count].reshape(dw_weight.shape),
+    )
 
 
 def solution(mesh):

time: 186 us -> 77.8 us (0.42)
  waiting for transfers between devices: 91.3 us -> 27.3 us
  blocking collectives: 39.1 us -> 0 us
  between operations: 14.3 us -> 1.9 us
  starting transfers between devices: 20.6 us -> 27.6 us
  local copies, waits for them, and re-layouts: 4.22 us -> 7.12 us
    psum x1 -> x0, waiting for transfers between devices: 84.5 us -> none  [local(): lax.psum((part_in, part_out, part_dw), ('lat', 'lon'))]
    psum x1 -> x0, blocking collectives: 39.1 us -> none  [local(): lax.psum((part_in, part_out, part_dw), ('lat', 'lon'))]
    ppermute x8 -> x24, waiting for transfers between devices: 6.02 us -> 27.3 us  [the longest x22 24.8 us: swap(): lax.ppermute(value, axis, [(i, i ^ bit) for i in range(lax.axis_size(axis...]
    ppermute x8 -> x24, starting transfers between devices: 17.1 us -> 27.6 us  [the longest x22 23.4 us: swap(): lax.ppermute(value, axis, [(i, i ^ bit) for i in range(lax.axis_size(axis...]
    div x3 -> x0, other arithmetic: 4.07 us -> none  [the longest x1 2.35 us: local(): sum_out / cell_total]
    all_to_all x1 -> x0, starting transfers between devices: 3.46 us -> none  [local(): lax.all_to_all(teacher, 'lat', split_axis=1, concat_axis=2, tiled=True)]
    unnamed x15 -> x97, local copies, waits for them, and re-layouts: 2.9 us -> 5.6 us
  transfers between devices with their start and end apart: 10 -> 24, of which waited for: 4 -> 12; matrix products, arithmetic and copies ran while one was open for 3% -> 11% of each run, Pallas kernels for 0% -> 0%
where the time goes in v3:
time: 77.8 us; the launch traced here: 77.5 us
  starting transfers between devices  27.6 us (35%)
  waiting for transfers between devices  27.3 us (35%)
  other arithmetic  10.4 us (13%)
  local copies, waits for them, and re-layouts  7.12 us (9%)
  matrix products  3.16 us (4%)
  between operations  1.9 us (2%)
    ppermute x22, waiting for transfers between devices, swap(): lax.ppermute(value, axis, [(i, i ^ bit) for i in range(lax.axis_size(axis...  24.8 us
    ppermute x22, starting transfers between devices, swap(): lax.ppermute(value, axis, [(i, i ^ bit) for i in range(lax.axis_size(axis...  23.4 us
    unnamed x97, local copies, waits for them, and re-layouts  5.6 us
    ppermute x2, starting transfers between devices, swap_outer(): return lax.ppermute(edge, axis, pairs + [(j, i) for i, j in pairs])  4.2 us
    ppermute x2, waiting for transfers between devices, swap_outer(): return lax.ppermute(edge, axis, pairs + [(j, i) for i, j in pairs])  2.5 us
    convert_element_type x1, other arithmetic, local(): (misfit.reshape(student.shape) + back_conv).astype(jnp.bfloat16)  2.41 us
    reduce_sum x3, other arithmetic, local(): jnp.sum(padded[:, row_off:row_off + tile_rows, col_off:col_off + tile_col...  2.15 us
    reduce_sum x1, other arithmetic, local(): average = jnp.mean(smoothed, axis=-1, keepdims=True)  1.84 us
  transfers between devices with their start and end apart: 24, of which 12 were waited for; matrix products, arithmetic and copies ran while one was open for 11% of the time, Pallas kernels for 0%

profile of v3, /device:TPU:0, one launch (start us, length us, event | category | flops | bytes accessed | tf_op | source)
XLA Modules:
  0.0 77.5 jit_solution(15531055947309559514)
XLA Ops:
  0.7 0.9 %broadcast_select_fusion.11 = (bf16[2,4,3,256]{3,2,1,0:T(4,128)(2,1)S(1)}, bf16[2,4,3,256]{3,2,1,0:T(4,128)(2,1)S(1)}) fusion(pred[]{:T(512)S(6)} %eq.71, bf16[2,4,32,256]{3,2,1,0:T(8,128)(2,1)} %param.7), kind=kLoop, calls=%fused_computation.298 | loop fusion | flops 12288 | bytes 49153 | tf_op jit(solution)/shard_map/jit(_where)/select_n | solution.py:23
  1.5 3.0 %collective-permute-start = (bf16[2,4,3,256]{3,2,1,0:T(4,128)(2,1)S(1)}, bf16[2,4,3,256]{3,2,1,0:T(4,128)(2,1)S(1)}, u32[]{:S(2)}, u32[]{:S(2)}) collective-permute-start(bf16[2,4,3,256]{3,2,1,0:T(4,128)(2,1)S(1)} %get-tuple-element.111), channel_id=1, source_target_pairs={{0,1},{1,0},{2,3},{3,2},{4,5},{5,4},{6,7},{7,6},{8,9},{9,8},{10,11... | collective-permute-start | bytes 36872 | tf_op jit(solution)/shard_map/ppermute | solution.py:16
  4.6 3.5 %collective-permute-start.1 = (bf16[2,4,3,256]{3,2,1,0:T(4,128)(2,1)S(1)}, bf16[2,4,3,256]{3,2,1,0:T(4,128)(2,1)S(1)}, u32[]{:S(2)}, u32[]{:S(2)}) collective-permute-start(bf16[2,4,3,256]{3,2,1,0:T(4,128)(2,1)S(1)} %get-tuple-element.112), channel_id=1, source_target_pairs={{1,2},{3,4},{5,6},{7,0},{2,1},{4,3},{6,5},{0,7},{9,10},{11,12},{13... | collective-permute-start | bytes 36872 | tf_op jit(solution)/shard_map/ppermute | solution.py:31
  8.5 2.5 %collective-permute-done.1 = bf16[2,4,3,256]{3,2,1,0:T(4,128)(2,1)S(1)} collective-permute-done((bf16[2,4,3,256]{3,2,1,0:T(4,128)(2,1)S(1)}, bf16[2,4,3,256]{3,2,1,0:T(4,128)(2,1)S(1)}, u32[]{:S(2)}, u32[]{:S(2)}) %collective-permute-start.1) | collective-permute-done | bytes 12320 | tf_op jit(solution)/shard_map/ppermute | solution.py:31
  11.1 0.8 %copy-done.5 = bf16[2,16,8,256]{3,2,1,0:T(8,128)(2,1)S(1)} copy-done((bf16[2,16,8,256]{3,2,1,0:T(8,128)(2,1)S(1)}, bf16[2,16,8,256]{3,2,1,0:T(8,128)(2,1)}, u32[]{:S(2)}) %copy-start.5) | copy-done | bytes 131096
  12.6 0.7 collective-permute-start.3
  13.4 3.0 %collective-permute-start.5 = (bf16[2,1,4,16,256]{4,3,2,0,1:T(8,128)(2,1)S(1)}, bf16[2,1,4,16,256]{4,3,2,0,1:T(8,128)(2,1)S(1)}, u32[]{:S(2)}, u32[]{:S(2)}) collective-permute-start(bf16[2,1,4,16,256]{4,3,2,0,1:T(8,128)(2,1)S(1)} %get-tuple-element.107), channel_id=1, source_target_pairs={{0,16},{8,24},{16,0},{24,8},{1,17},{9,25},{17,1},{25,9},{2,18},{10... | collective-permute-start | bytes 196616 | tf_op jit(solution)/shard_map/ppermute | solution.py:16
  16.6 1.8 %fusion.133 = (f32[2,4,32]{2,1,0:T(4,128)S(1)}, f32[2,4,32,256]{3,2,1,0:T(8,128)S(1)}) fusion(f32[2,10,38,256]{3,2,1,0:T(8,128)S(1)} %maximum_convert_fusion, f32[256]{0:T(256)S(1)} %bitcast.325, f32[256]{0:T(256)S(1)} %bitcast.327, f32[256]{0:T(256)S(1)} %bitcast.233, f32[256]{0:T(256)S(1)} %bitcast.235, f32[256]{0:T(256)S(1)} %bitcast.237, ...), kind=kLoop, calls=%fused_computation.326 | loop fusion | flops 6422272 | bytes 13158400 | tf_op jit(solution)/shard_map/reduce_sum | solution.py:219
  21.5 0.8 %fusion = bf16[256,1024]{1,0:T(8,128)(2,1)S(1)} fusion(bf16[256,256]{1,0:T(8,128)(2,1)S(1)} %get-tuple-element.168, bf16[1024,256]{1,0:T(8,128)(2,1)S(1)} %copy-done.2, f32[256,1024]{1,0:T(8,128)S(1)} %get-tuple-element.167), kind=kOutput, calls=%fused_computation.52 | convolution fusion | flops 139198464 | bytes 2228224 | tf_op jit(solution)/shard_map/dot_general | solution.py:237
  23.4 1.2 %fusion.55 = (f32[256]{0:T(256)S(1)}, f32[256]{0:T(256)S(1)}, f32[256]{0:T(256)S(1)}, f32[256]{0:T(256)S(1)}, f32[256]{0:T(256)S(1)}, /*index=5*/f32[256]{0:T(25...) fusion(f32[2,10,38,256]{3,2,1,0:T(8,128)S(1)} %maximum_convert_, ...), kind=kLoop, calls=%fused_computation.119 | loop fusion | flops 2878976 | bytes 5396480 | tf_op jit(solution)/shard_map/reduce_sum | solution.py:259
  25.8 0.7 copy-done.46
  26.6 2.4 %collective-permute-start.7 = (bf16[32,256]{1,0:T(8,128)(2,1)S(1)}, bf16[32,256]{1,0:T(8,128)(2,1)S(1)}, u32[]{:S(2)}, u32[]{:S(2)}) collective-permute-start(bf16[32,256]{1,0:T(8,128)(2,1)S(1)} %fusion.118), channel_id=1, source_target_pairs={{0,8},{8,0},{16,24},{24,16},{1,9},{9,1},{17,25},{25,17},{2,10},{10... | collective-permute-start | bytes 49160 | tf_op jit(solution)/shard_map/ppermute | solution.py:16
  30.6 0.7 copy-done.3
  31.4 2.0 %collective-permute-start.17 = (bf16[256,256]{1,0:T(8,128)(2,1)S(1)}, bf16[256,256]{1,0:T(8,128)(2,1)S(1)}, u32[]{:S(2)}, u32[]{:S(2)}) collective-permute-start(bf16[256,256]{1,0:T(8,128)(2,1)S(1)} %get-tuple-element.91), channel_id=1, source_target_pairs={{0,16},{8,24},{16,0},{24,8},{1,17},{9,25},{17,1},{25,9},{2,18},{10... | collective-permute-start | bytes 393224 | tf_op jit(solution)/shard_map/ppermute | solution.py:16
  33.5 0.8 %collective-permute-start.9 = (bf16[464,256]{1,0:T(8,128)(2,1)S(1)}, bf16[464,256]{1,0:T(8,128)(2,1)S(1)}, u32[]{:S(2)}, u32[]{:S(2)}) collective-permute-start(bf16[464,256]{1,0:T(8,128)(2,1)S(1)} %pad_maximum_fusion), channel_id=1, source_target_pairs={{0,16},{8,24},{16,0},{24,8},{1,17},{9,25},{17,1},{25,9},{2,18},{10... | collective-permute-start | bytes 712712 | tf_op jit(solution)/shard_map/ppermute | solution.py:16
  34.3 3.5 %collective-permute-done.17 = bf16[256,256]{1,0:T(8,128)(2,1)S(1)} collective-permute-done((bf16[256,256]{1,0:T(8,128)(2,1)S(1)}, bf16[256,256]{1,0:T(8,128)(2,1)S(1)}, u32[]{:S(2)}, u32[]{:S(2)}) %collective-permute-start.17) | collective-permute-done | bytes 131104 | tf_op jit(solution)/shard_map/ppermute | solution.py:16
  37.8 4.6 %collective-permute-done.9 = bf16[464,256]{1,0:T(8,128)(2,1)S(1)} collective-permute-done((bf16[464,256]{1,0:T(8,128)(2,1)S(1)}, bf16[464,256]{1,0:T(8,128)(2,1)S(1)}, u32[]{:S(2)}, u32[]{:S(2)}) %collective-permute-start.9) | collective-permute-done | bytes 237600 | tf_op jit(solution)/shard_map/ppermute | solution.py:16
  43.3 4.8 %collective-permute-done.10 = bf16[256,256]{1,0:T(8,128)(2,1)S(1)} collective-permute-done((bf16[256,256]{1,0:T(8,128)(2,1)S(1)}, bf16[256,256]{1,0:T(8,128)(2,1)S(1)}, u32[]{:S(2)}, u32[]{:S(2)}) %collective-permute-start.10) | collective-permute-done | bytes 131104 | tf_op jit(solution)/shard_map/ppermute | solution.py:16
  48.3 3.0 %collective-permute-start.20 = (bf16[128,256]{1,0:T(8,128)(2,1)S(1)}, bf16[128,256]{1,0:T(8,128)(2,1)S(1)}, u32[]{:S(2)}, u32[]{:S(2)}) collective-permute-start(bf16[128,256]{1,0:T(8,128)(2,1)S(1)} %get-tuple-element.84), channel_id=1, source_target_pairs={{0,4},{1,5},{2,6},{3,7},{4,0},{5,1},{6,2},{7,3},{8,12},{9,13},{10,... | collective-permute-start | bytes 196616 | tf_op jit(solution)/shard_map/ppermute | solution.py:16
  51.3 4.2 %collective-permute-done.11 = f32[196,256]{1,0:T(8,128)S(1)} collective-permute-done((f32[196,256]{1,0:T(8,128)S(1)}, f32[196,256]{1,0:T(8,128)S(1)}, u32[]{:S(2)}, u32[]{:S(2)}) %collective-permute-start.11) | collective-permute-done | bytes 200736 | tf_op jit(solution)/shard_map/ppermute | solution.py:16
  55.6 0.7 collective-permute-start.21
  56.3 2.0 %collective-permute-start.12 = (bf16[196,256]{1,0:T(8,128)(2,1)S(1)}, bf16[196,256]{1,0:T(8,128)(2,1)S(1)}, u32[]{:S(2)}, u32[]{:S(2)}) collective-permute-start(bf16[196,256]{1,0:T(8,128)(2,1)S(1)} %pad_maximum_fusion.5), channel_id=1, source_target_pairs={{0,4},{1,5},{2,6},{3,7},{4,0},{5,1},{6,2},{7,3},{8,12},{9,13},{10,... | collective-permute-start | bytes 301064 | tf_op jit(solution)/shard_map/ppermute | solution.py:16
  58.3 1.7 %collective-permute-done.21 = bf16[1,128,256]{2,1,0:T(8,128)(2,1)S(1)} collective-permute-done((bf16[1,128,256]{2,1,0:T(8,128)(2,1)S(1)}, bf16[1,128,256]{2,1,0:T(8,128)(2,1)S(1)}, u32[]{:S(2)}, u32[]{:S(2)}) %collective-permute-start.21) | collective-permute-done | bytes 65568 | tf_op jit(solution)/shard_map/ppermute | solution.py:16
  60.0 1.1 %collective-permute-start.22 = (bf16[2,128,256]{2,1,0:T(8,128)(2,1)S(1)}, bf16[2,128,256]{2,1,0:T(8,128)(2,1)S(1)}, u32[]{:S(2)}, u32[]{:S(2)}) collective-permute-start(bf16[2,128,256]{2,1,0:T(8,128)(2,1)S(1)} %maximum_select_fusion.7), channel_id=1, source_target_pairs={{0,16},{8,24},{16,0},{24,8},{1,17},{9,25},{17,1},{25,9},{2,18},{10... | collective-permute-start | bytes 393224 | tf_op jit(solution)/shard_map/ppermute | solution.py:16
  61.1 0.8 collective-permute-done.12
  62.1 2.6 %collective-permute-start.13 = (bf16[1,272,128]{1,2,0:T(8,128)(2,1)S(1)}, bf16[1,272,128]{1,2,0:T(8,128)(2,1)S(1)}, u32[]{:S(2)}, u32[]{:S(2)}) collective-permute-start(bf16[1,272,128]{1,2,0:T(8,128)(2,1)S(1)} %maximum_bitcast_fusion), channel_id=1, source_target_pairs={{0,1},{1,0},{2,3},{3,2},{4,5},{5,4},{6,7},{7,6},{8,9},{9,8},{10,11... | collective-permute-start | bytes 208904 | tf_op jit(solution)/shard_map/ppermute | solution.py:16
  64.8 2.5 %collective-permute-done.13 = bf16[1,272,128]{1,2,0:T(8,128)(2,1)S(1)} collective-permute-done((bf16[1,272,128]{1,2,0:T(8,128)(2,1)S(1)}, bf16[1,272,128]{1,2,0:T(8,128)(2,1)S(1)}, u32[]{:S(2)}, u32[]{:S(2)}) %collective-permute-start.13) | collective-permute-done | bytes 69664 | tf_op jit(solution)/shard_map/ppermute | solution.py:16
  67.4 1.0 %collective-permute-start.14 = (bf16[2,272,128]{1,2,0:T(8,128)(2,1)S(1)}, bf16[2,272,128]{1,2,0:T(8,128)(2,1)S(1)}, u32[]{:S(2)}, u32[]{:S(2)}) collective-permute-start(bf16[2,272,128]{1,2,0:T(8,128)(2,1)S(1)} %maximum_select_fusion.4), channel_id=1, source_target_pairs={{0,16},{8,24},{16,0},{24,8},{1,17},{9,25},{17,1},{25,9},{2,18},{10... | collective-permute-start | bytes 417800 | tf_op jit(solution)/shard_map/ppermute | solution.py:16
  69.3 2.4 %fusion.58 = bf16[2,4,32,256]{3,2,1,0:T(8,128)(2,1)} fusion(f32[2,4,32,256]{3,2,1,0:T(8,128)S(1)} %bitcast.224, f32[2,10,38,256]{3,2,1,0:T(8,128)S(1)} %maximum_convert_fusion.1, f32[256]{0:T(256)S(1)} %bitcast.326, f32[256]{0:T(256)S(1)} %bitcast.328, f32[256]{0:T(256)S(1)} %bitcast.234, f32[256]{0:T(256)S(1)} %bitcast.236, f32[256]{0:T(256)S(1)} %bitcast.238, ...), kind=kLoop, calls=%fused_computation.123 | loop fusion | flops 6488064 | bytes 13288448 | tf_op jit(solution)/shard_map/convert_element_type | solution.py:281
  71.7 1.4 %collective-permute-done.14 = bf16[2,272,128]{1,2,0:T(8,128)(2,1)S(1)} collective-permute-done((bf16[2,272,128]{1,2,0:T(8,128)(2,1)S(1)}, bf16[2,272,128]{1,2,0:T(8,128)(2,1)S(1)}, u32[]{:S(2)}, u32[]{:S(2)}) %collective-permute-start.14) | collective-permute-done | bytes 139296 | tf_op jit(solution)/shard_map/ppermute | solution.py:16
  73.4 1.1 %bitcast_convert_fusion = f32[1024,256]{1,0:T(8,128)} fusion(bf16[8,128,256]{2,1,0:T(8,128)(2,1)S(1)} %maximum_select_fusion.1), kind=kLoop, calls=%fused_computation.67 | loop fusion | flops 262144 | bytes 1572864 | tf_op jit(solution)/shard_map/convert_element_type | solution.py:285
  76.2 1.3 %copy.19 = f32[256,1024]{1,0:T(8,128)} copy(f32[256,1024]{0,1:T(8,128)S(1)} %bitcast.223) | data formatting | bytes 2097152
  (203 shorter events, 12.4 us)
Async XLA Ops:
  0.6 19.0 %copy-start = (bf16[256,1024]{1,0:T(8,128)(2,1)S(1)}, bf16[256,1024]{1,0:T(8,128)(2,1)}, u32[]{:S(2)}) copy-start(bf16[256,1024]{1,0:T(8,128)(2,1)} %param.11) | copy-start | bytes 1572868
  1.5 7.0 %collective-permute-start = (bf16[2,4,3,256]{3,2,1,0:T(4,128)(2,1)S(1)}, bf16[2,4,3,256]{3,2,1,0:T(4,128)(2,1)S(1)}, u32[]{:S(2)}, u32[]{:S(2)}) collective-permute-start(bf16[2,4,3,256]{3,2,1,0:T(4,128)(2,1)S(1)} %get-tuple-element.111), channel_id=1, source_target_pairs={{0,1},{1,0},{2,3},{3,2},{4,5},{5,4},{6,7},{7,6},{8,9},{9,8},{10,11... | collective-permute-start | bytes 36872 | tf_op jit(solution)/shard_map/ppermute | solution.py:16
  4.6 6.4 %collective-permute-start.1 = (bf16[2,4,3,256]{3,2,1,0:T(4,128)(2,1)S(1)}, bf16[2,4,3,256]{3,2,1,0:T(4,128)(2,1)S(1)}, u32[]{:S(2)}, u32[]{:S(2)}) collective-permute-start(bf16[2,4,3,256]{3,2,1,0:T(4,128)(2,1)S(1)} %get-tuple-element.112), channel_id=1, source_target_pairs={{1,2},{3,4},{5,6},{7,0},{2,1},{4,3},{6,5},{0,7},{9,10},{11,12},{13... | collective-permute-start | bytes 36872 | tf_op jit(solution)/shard_map/ppermute | solution.py:31
  8.2 8.3 %copy-start.7 = (f32[1,1,256]{2,1,0:T(1,128)}, f32[1,1,256]{2,1,0:T(1,128)S(1)}, u32[]{:S(2)}) copy-start(f32[1,1,256]{2,1,0:T(1,128)S(1)} %get-tuple-element.145) | copy-start | bytes 3076
  8.2 8.3 %copy-start.9 = (f32[1,1,256]{2,1,0:T(1,128)}, f32[1,1,256]{2,1,0:T(1,128)S(1)}, u32[]{:S(2)}) copy-start(f32[1,1,256]{2,1,0:T(1,128)S(1)} %get-tuple-element.146) | copy-start | bytes 3076
  8.2 8.3 %copy-start.11 = (f32[1,1,256]{2,1,0:T(1,128)}, f32[1,1,256]{2,1,0:T(1,128)S(1)}, u32[]{:S(2)}) copy-start(f32[1,1,256]{2,1,0:T(1,128)S(1)} %get-tuple-element.147) | copy-start | bytes 3076
  8.2 8.3 %copy-start.13 = (f32[1,1,256]{2,1,0:T(1,128)}, f32[1,1,256]{2,1,0:T(1,128)S(1)}, u32[]{:S(2)}) copy-start(f32[1,1,256]{2,1,0:T(1,128)S(1)} %get-tuple-element.148) | copy-start | bytes 3076
  8.2 8.3 %copy-start.15 = (f32[1,1,256]{2,1,0:T(1,128)}, f32[1,1,256]{2,1,0:T(1,128)S(1)}, u32[]{:S(2)}) copy-start(f32[1,1,256]{2,1,0:T(1,128)S(1)} %get-tuple-element.149) | copy-start | bytes 3076
  8.2 8.3 %copy-start.17 = (f32[1,1,256]{2,1,0:T(1,128)}, f32[1,1,256]{2,1,0:T(1,128)S(1)}, u32[]{:S(2)}) copy-start(f32[1,1,256]{2,1,0:T(1,128)S(1)} %get-tuple-element.150) | copy-start | bytes 3076
  8.2 8.3 %copy-start.19 = (f32[1,1,256]{2,1,0:T(1,128)}, f32[1,1,256]{2,1,0:T(1,128)S(1)}, u32[]{:S(2)}) copy-start(f32[1,1,256]{2,1,0:T(1,128)S(1)} %get-tuple-element.151) | copy-start | bytes 3076
  12.0 1.3 %collective-permute-start.4 = (bf16[2,2,4,8,256]{4,3,2,0,1:T(8,128)(2,1)S(1)}, bf16[2,2,4,8,256]{4,3,2,0,1:T(8,128)(2,1)S(1)}, u32[]{:S(2)}, u32[]{:S(2)}) collective-permute-start(bf16[2,2,4,8,256]{4,3,2,0,1:T(8,128)(2,1)S(1)} %bitcast.230), channel_id=1, source_target_pairs={{0,8},{8,0},{16,24},{24,16},{1,9},{9,1},{17,25},{25,17},{2,10},{10... | collective-permute-start | bytes 196616 | tf_op jit(solution)/shard_map/ppermute | solution.py:16
  12.1 4.3 %collective-permute-start.2 = (bf16[2,3,38,256]{3,2,1,0:T(8,128)(2,1)S(1)}, bf16[2,3,38,256]{3,2,1,0:T(8,128)(2,1)S(1)}, u32[]{:S(2)}, u32[]{:S(2)}) collective-permute-start(bf16[2,3,38,256]{3,2,1,0:T(8,128)(2,1)S(1)} %get-tuple-element.103), channel_id=1, source_target_pairs={{0,8},{8,0},{16,24},{24,16},{1,9},{9,1},{17,25},{25,17},{2,10},{10... | collective-permute-start | bytes 350216 | tf_op jit(solution)/shard_map/ppermute | solution.py:16
  12.6 3.7 %collective-permute-start.3 = (bf16[2,3,38,256]{3,2,1,0:T(8,128)(2,1)S(1)}, bf16[2,3,38,256]{3,2,1,0:T(8,128)(2,1)S(1)}, u32[]{:S(2)}, u32[]{:S(2)}) collective-permute-start(bf16[2,3,38,256]{3,2,1,0:T(8,128)(2,1)S(1)} %get-tuple-element.104), channel_id=1, source_target_pairs={{8,16},{16,8},{9,17},{17,9},{10,18},{18,10},{11,19},{19,11},{12,20... | collective-permute-start | bytes 350216 | tf_op jit(solution)/shard_map/ppermute | solution.py:31
  13.4 7.1 %collective-permute-start.5 = (bf16[2,1,4,16,256]{4,3,2,0,1:T(8,128)(2,1)S(1)}, bf16[2,1,4,16,256]{4,3,2,0,1:T(8,128)(2,1)S(1)}, u32[]{:S(2)}, u32[]{:S(2)}) collective-permute-start(bf16[2,1,4,16,256]{4,3,2,0,1:T(8,128)(2,1)S(1)} %get-tuple-element.107), channel_id=1, source_target_pairs={{0,16},{8,24},{16,0},{24,8},{1,17},{9,25},{17,1},{25,9},{2,18},{10... | collective-permute-start | bytes 196616 | tf_op jit(solution)/shard_map/ppermute | solution.py:16
  26.6 3.4 %collective-permute-start.7 = (bf16[32,256]{1,0:T(8,128)(2,1)S(1)}, bf16[32,256]{1,0:T(8,128)(2,1)S(1)}, u32[]{:S(2)}, u32[]{:S(2)}) collective-permute-start(bf16[32,256]{1,0:T(8,128)(2,1)S(1)} %fusion.118), channel_id=1, source_target_pairs={{0,8},{8,0},{16,24},{24,16},{1,9},{9,1},{17,25},{25,17},{2,10},{10... | collective-permute-start | bytes 49160 | tf_op jit(solution)/shard_map/ppermute | solution.py:16
  29.1 1.5 %collective-permute-start.8 = (bf16[2,2,3,32,256]{4,3,2,1,0:T(8,128)(2,1)S(1)}, bf16[2,2,3,32,256]{4,3,2,1,0:T(8,128)(2,1)S(1)}, u32[]{:S(2)}, u32[]{:S(2)}) collective-permute-start(bf16[2,2,3,32,256]{4,3,2,1,0:T(8,128)(2,1)S(1)} %pad_maximum_fusion.2), channel_id=1, source_target_pairs={{0,8},{8,0},{16,24},{24,16},{1,9},{9,1},{17,25},{25,17},{2,10},{10... | collective-permute-start | bytes 589832 | tf_op jit(solution)/shard_map/ppermute | solution.py:16
  29.2 2.1 %collective-permute-start.16 = (bf16[512,256]{1,0:T(8,128)(2,1)S(1)}, bf16[512,256]{1,0:T(8,128)(2,1)S(1)}, u32[]{:S(2)}, u32[]{:S(2)}) collective-permute-start(bf16[512,256]{1,0:T(8,128)(2,1)S(1)} %convolution_convert_fusion), channel_id=1, source_target_pairs={{0,8},{8,0},{16,24},{24,16},{1,9},{9,1},{17,25},{25,17},{2,10},{10... | collective-permute-start | bytes 786440 | tf_op jit(solution)/shard_map/ppermute | solution.py:16
  29.7 3.7 %collective-permute-start.6 = (bf16[512,256]{1,0:T(8,128)(2,1)S(1)}, bf16[512,256]{1,0:T(8,128)(2,1)S(1)}, u32[]{:S(2)}, u32[]{:S(2)}) collective-permute-start(bf16[512,256]{1,0:T(8,128)(2,1)S(1)} %convolution_convert_fusion.1), channel_id=1, source_target_pairs={{0,8},{8,0},{16,24},{24,16},{1,9},{9,1},{17,25},{25,17},{2,10},{10... | collective-permute-start | bytes 786440 | tf_op jit(solution)/shard_map/ppermute | solution.py:16
  31.4 6.4 %collective-permute-start.17 = (bf16[256,256]{1,0:T(8,128)(2,1)S(1)}, bf16[256,256]{1,0:T(8,128)(2,1)S(1)}, u32[]{:S(2)}, u32[]{:S(2)}) collective-permute-start(bf16[256,256]{1,0:T(8,128)(2,1)S(1)} %get-tuple-element.91), channel_id=1, source_target_pairs={{0,16},{8,24},{16,0},{24,8},{1,17},{9,25},{17,1},{25,9},{2,18},{10... | collective-permute-start | bytes 393224 | tf_op jit(solution)/shard_map/ppermute | solution.py:16
  33.5 9.0 %collective-permute-start.9 = (bf16[464,256]{1,0:T(8,128)(2,1)S(1)}, bf16[464,256]{1,0:T(8,128)(2,1)S(1)}, u32[]{:S(2)}, u32[]{:S(2)}) collective-permute-start(bf16[464,256]{1,0:T(8,128)(2,1)S(1)} %pad_maximum_fusion), channel_id=1, source_target_pairs={{0,16},{8,24},{16,0},{24,8},{1,17},{9,25},{17,1},{25,9},{2,18},{10... | collective-permute-start | bytes 712712 | tf_op jit(solution)/shard_map/ppermute | solution.py:16
  37.8 5.2 %collective-permute-start.18 = (bf16[128,256]{1,0:T(8,128)(2,1)S(1)}, bf16[128,256]{1,0:T(8,128)(2,1)S(1)}, u32[]{:S(2)}, u32[]{:S(2)}) collective-permute-start(bf16[128,256]{1,0:T(8,128)(2,1)S(1)} %get-tuple-element.95), channel_id=1, source_target_pairs={{0,1},{1,0},{2,3},{3,2},{4,5},{5,4},{6,7},{7,6},{8,9},{9,8},{10,11... | collective-permute-start | bytes 196616 | tf_op jit(solution)/shard_map/ppermute | solution.py:16
  42.8 5.2 %collective-permute-start.10 = (bf16[256,256]{1,0:T(8,128)(2,1)S(1)}, bf16[256,256]{1,0:T(8,128)(2,1)S(1)}, u32[]{:S(2)}, u32[]{:S(2)}) collective-permute-start(bf16[256,256]{1,0:T(8,128)(2,1)S(1)} %pad_maximum_fusion.4), channel_id=1, source_target_pairs={{0,1},{1,0},{2,3},{3,2},{4,5},{5,4},{6,7},{7,6},{8,9},{9,8},{10,11... | collective-permute-start | bytes 393224 | tf_op jit(solution)/shard_map/ppermute | solution.py:16
  43.0 5.3 %collective-permute-start.19 = (f32[128,256]{1,0:T(8,128)S(1)}, f32[128,256]{1,0:T(8,128)S(1)}, u32[]{:S(2)}, u32[]{:S(2)}) collective-permute-start(f32[128,256]{1,0:T(8,128)S(1)} %convert_add_fusion.2), channel_id=1, source_target_pairs={{0,2},{1,3},{2,0},{3,1},{4,6},{5,7},{6,4},{7,5},{8,10},{9,11},{10,... | collective-permute-start | bytes 393224 | tf_op jit(solution)/shard_map/ppermute | solution.py:16
  48.2 7.3 %collective-permute-start.11 = (f32[196,256]{1,0:T(8,128)S(1)}, f32[196,256]{1,0:T(8,128)S(1)}, u32[]{:S(2)}, u32[]{:S(2)}) collective-permute-start(f32[196,256]{1,0:T(8,128)S(1)} %pad_maximum_fusion.1), channel_id=1, source_target_pairs={{0,2},{1,3},{2,0},{3,1},{4,6},{5,7},{6,4},{7,5},{8,10},{9,11},{10,... | collective-permute-start | bytes 602120 | tf_op jit(solution)/shard_map/ppermute | solution.py:16
  48.3 7.3 %collective-permute-start.20 = (bf16[128,256]{1,0:T(8,128)(2,1)S(1)}, bf16[128,256]{1,0:T(8,128)(2,1)S(1)}, u32[]{:S(2)}, u32[]{:S(2)}) collective-permute-start(bf16[128,256]{1,0:T(8,128)(2,1)S(1)} %get-tuple-element.84), channel_id=1, source_target_pairs={{0,4},{1,5},{2,6},{3,7},{4,0},{5,1},{6,2},{7,3},{8,12},{9,13},{10,... | collective-permute-start | bytes 196616 | tf_op jit(solution)/shard_map/ppermute | solution.py:16
  55.6 4.3 %collective-permute-start.21 = (bf16[1,128,256]{2,1,0:T(8,128)(2,1)S(1)}, bf16[1,128,256]{2,1,0:T(8,128)(2,1)S(1)}, u32[]{:S(2)}, u32[]{:S(2)}) collective-permute-start(bf16[1,128,256]{2,1,0:T(8,128)(2,1)S(1)} %fusion.116), channel_id=1, source_target_pairs={{0,1},{1,0},{2,3},{3,2},{4,5},{5,4},{6,7},{7,6},{8,9},{9,8},{10,11... | collective-permute-start | bytes 196616 | tf_op jit(solution)/shard_map/ppermute | solution.py:16
  56.3 5.6 %collective-permute-start.12 = (bf16[196,256]{1,0:T(8,128)(2,1)S(1)}, bf16[196,256]{1,0:T(8,128)(2,1)S(1)}, u32[]{:S(2)}, u32[]{:S(2)}) collective-permute-start(bf16[196,256]{1,0:T(8,128)(2,1)S(1)} %pad_maximum_fusion.5), channel_id=1, source_target_pairs={{0,4},{1,5},{2,6},{3,7},{4,0},{5,1},{6,2},{7,3},{8,12},{9,13},{10,... | collective-permute-start | bytes 301064 | tf_op jit(solution)/shard_map/ppermute | solution.py:16
  60.0 8.4 %collective-permute-start.22 = (bf16[2,128,256]{2,1,0:T(8,128)(2,1)S(1)}, bf16[2,128,256]{2,1,0:T(8,128)(2,1)S(1)}, u32[]{:S(2)}, u32[]{:S(2)}) collective-permute-start(bf16[2,128,256]{2,1,0:T(8,128)(2,1)S(1)} %maximum_select_fusion.7), channel_id=1, source_target_pairs={{0,16},{8,24},{16,0},{24,8},{1,17},{9,25},{17,1},{25,9},{2,18},{10... | collective-permute-start | bytes 393224 | tf_op jit(solution)/shard_map/ppermute | solution.py:16
  62.1 5.2 %collective-permute-start.13 = (bf16[1,272,128]{1,2,0:T(8,128)(2,1)S(1)}, bf16[1,272,128]{1,2,0:T(8,128)(2,1)S(1)}, u32[]{:S(2)}, u32[]{:S(2)}) collective-permute-start(bf16[1,272,128]{1,2,0:T(8,128)(2,1)S(1)} %maximum_bitcast_fusion), channel_id=1, source_target_pairs={{0,1},{1,0},{2,3},{3,2},{4,5},{5,4},{6,7},{7,6},{8,9},{9,8},{10,11... | collective-permute-start | bytes 208904 | tf_op jit(solution)/shard_map/ppermute | solution.py:16
  67.4 5.7 %collective-permute-start.14 = (bf16[2,272,128]{1,2,0:T(8,128)(2,1)S(1)}, bf16[2,272,128]{1,2,0:T(8,128)(2,1)S(1)}, u32[]{:S(2)}, u32[]{:S(2)}) collective-permute-start(bf16[2,272,128]{1,2,0:T(8,128)(2,1)S(1)} %maximum_select_fusion.4), channel_id=1, source_target_pairs={{0,16},{8,24},{16,0},{24,8},{1,17},{9,25},{17,1},{25,9},{2,18},{10... | collective-permute-start | bytes 417800 | tf_op jit(solution)/shard_map/ppermute | solution.py:16
  68.5 4.8 %collective-permute-start.23 = (bf16[4,128,256]{2,1,0:T(8,128)(2,1)S(1)}, bf16[4,128,256]{2,1,0:T(8,128)(2,1)S(1)}, u32[]{:S(2)}, u32[]{:S(2)}) collective-permute-start(bf16[4,128,256]{2,1,0:T(8,128)(2,1)S(1)} %maximum_select_fusion.3), channel_id=1, source_target_pairs={{0,8},{8,0},{16,24},{24,16},{1,9},{9,1},{17,25},{25,17},{2,10},{10... | collective-permute-start | bytes 786440 | tf_op jit(solution)/shard_map/ppermute | solution.py:16
  73.2 1.8 %collective-permute-start.15 = (bf16[4,272,128]{1,2,0:T(8,128)(2,1)S(1)}, bf16[4,272,128]{1,2,0:T(8,128)(2,1)S(1)}, u32[]{:S(2)}, u32[]{:S(2)}) collective-permute-start(bf16[4,272,128]{1,2,0:T(8,128)(2,1)S(1)} %maximum_select_fusion.2), channel_id=1, source_target_pairs={{0,8},{8,0},{16,24},{24,16},{1,9},{9,1},{17,25},{25,17},{2,10},{10... | collective-permute-start | bytes 835592 | tf_op jit(solution)/shard_map/ppermute | solution.py:16
  (41 other events, 133.8 us)

commit v4 on v3

--- a/solution.py
+++ b/solution.py
@@ -1,6 +1,8 @@
 import jax
 import jax.numpy as jnp
 from jax import lax
+from jax.experimental import pallas as pl
+from jax.experimental.pallas import tpu as pltpu
 from jax.sharding import PartitionSpec as P
 
 slope_coef = 0.7978845608028654
@@ -73,21 +75,6 @@
     return 0.5 * (1.0 + tangent) + 0.5 * values * (1.0 - tangent * tangent) * slope_coef * (
         1.0 + 3.0 * cubic_coef * values * values
     )
-
-
-def apply_stencil(padded, dw_weight, tile_rows, tile_cols, flipped):
-    kernel_size = dw_weight.shape[0]
-    result = jnp.zeros((padded.shape[0], tile_rows, tile_cols, padded.shape[3]), jnp.float32)
-    for row_off in range(kernel_size):
-        for col_off in range(kernel_size):
-            row_start = kernel_size - 1 - row_off if flipped else row_off
-            col_start = kernel_size - 1 - col_off if flipped else col_off
-            result = (
-                result
-                + dw_weight[row_off, col_off]
-                * padded[:, row_start : row_start + tile_rows, col_start : col_start + tile_cols]
-            )
-    return result
 
 
 def half_of(value, upper):
@@ -187,7 +174,7 @@
 
 
 def gather_sums(lead, trail):
-    for axis, bit in sum_stages()[2][::-1] + [("lat", 1)]:
+    for axis, bit in sum_stages()[2][::-1]:
         lead = gather_halves(lead, axis, bit)
         trail = gather_halves(trail, axis, bit)
     return lead, trail
@@ -202,6 +189,237 @@
     return lax.dot_general(
         left, right, (((0,), (0,)), ((), ())), preferred_element_type=jnp.float32
     )
+
+
+lane_count = 128
+
+
+def spread(padded_ref, wide):
+    batch_size, rows, cols, channel_count = padded_ref.shape
+    for group in range(channel_count // lane_count):
+        lanes = slice(group * lane_count, (group + 1) * lane_count)
+        for b in range(batch_size):
+            wide[group, b, :, :cols, :] = padded_ref[b, :, :, lanes].astype(jnp.float32)
+
+
+def stencil(wide, weights, group, b, tile_rows, tile_cols, flipped):
+    kernel_size = weights.shape[1]
+    rows = [None] * tile_rows
+    for q in range(kernel_size):
+        for r in range(tile_rows + kernel_size - 1):
+            shifted = wide[group, b, r, q : q + tile_cols, :]
+            for i in range(max(0, r - kernel_size + 1), min(tile_rows, r + 1)):
+                p = r - i
+                tap = (kernel_size - 1 - p, kernel_size - 1 - q) if flipped else (p, q)
+                term = weights[group, tap[0], pl.ds(tap[1], 1), :] * shifted
+                rows[i] = term if rows[i] is None else rows[i] + term
+    return rows
+
+
+def conv_norm_kernel(padded_ref, weights_ref, gain_ref, normed_ref, unit_ref, inv_ref, wide, smooth):
+    batch_size, pad_rows, pad_cols, channel_count = padded_ref.shape
+    kernel_size = weights_ref.shape[1]
+    tile_rows, tile_cols = pad_rows - kernel_size + 1, pad_cols - kernel_size + 1
+    spread(padded_ref, wide)
+
+    def one(step, _):
+        group, b = step // batch_size, step % batch_size
+        rows = stencil(wide, weights_ref, group, b, tile_rows, tile_cols, False)
+        for i, row in enumerate(rows):
+            smooth[group, pl.ds((b * tile_rows + i) * tile_cols, tile_cols), :] = row
+        return 0
+
+    lax.fori_loop(0, wide.shape[0] * batch_size, one, 0)
+    groups = range(wide.shape[0])
+    cells = smooth.shape[1]
+    block = 32
+
+    def norm(step, _):
+        at = pl.ds(pl.multiple_of(step * block, block), block)
+        values = jnp.concatenate([smooth[g, at, :] for g in groups], axis=1)
+        average = jnp.mean(values, axis=-1, keepdims=True)
+        centred = values - average
+        variance = jnp.mean(centred * centred, axis=-1, keepdims=True)
+        inv_std = lax.rsqrt(variance + norm_eps)
+        unit = centred * inv_std
+        unit_ref[at, :] = unit
+        inv_ref[at, :] = inv_std
+        normed_ref[at, :] = (unit * gain_ref[...]).astype(jnp.bfloat16)
+        return 0
+
+    lax.fori_loop(0, cells // block, norm, 0, unroll=True)
+
+
+def lane_groups(weights):
+    groups = weights.shape[-1] // lane_count
+    return jnp.moveaxis(weights.reshape(weights.shape[:2] + (groups, lane_count)), 2, 0)
+
+
+def round_up(value, unit):
+    return -(-value // unit) * unit
+
+
+def conv_norm(padded, weights, gain):
+    batch_size, pad_rows, pad_cols, channel_count = padded.shape
+    kernel_size = weights.shape[0]
+    cells = batch_size * (pad_rows - kernel_size + 1) * (pad_cols - kernel_size + 1)
+    groups = channel_count // lane_count
+    return pl.pallas_call(
+        conv_norm_kernel,
+        out_shape=(
+            jax.ShapeDtypeStruct((cells, channel_count), jnp.bfloat16),
+            jax.ShapeDtypeStruct((cells, channel_count), jnp.float32),
+            jax.ShapeDtypeStruct((cells, 1), jnp.float32),
+        ),
+        scratch_shapes=[
+            pltpu.VMEM((groups, batch_size, pad_rows, round_up(pad_cols, 8), lane_count), jnp.float32),
+            pltpu.VMEM((groups, cells, lane_count), jnp.float32),
+        ],
+        compiler_params=pltpu.CompilerParams(vmem_limit_bytes=16 << 20),
+        cost_estimate=pl.CostEstimate(flops=2 * 49 * cells * channel_count, bytes_accessed=1 << 20, transcendentals=0),
+        name="conv_norm",
+    )(padded, lane_groups(weights), gain.reshape(1, -1))
+
+
+def conv_back_kernel(padded_ref, weights_ref, misfit_ref, out_ref, wide):
+    batch_size, tile_rows, tile_cols, channel_count = out_ref.shape
+    spread(padded_ref, wide)
+    for group in range(wide.shape[0]):
+        lanes = slice(group * lane_count, (group + 1) * lane_count)
+
+        def one(b, _):
+            rows = stencil(wide, weights_ref, group, b, tile_rows, tile_cols, True)
+            for i, row in enumerate(rows):
+                out_ref[b, i, :, lanes] = (misfit_ref[b, i, :, lanes] + row).astype(out_ref.dtype)
+            return 0
+
+        lax.fori_loop(0, batch_size, one, 0)
+
+
+def conv_back(padded, weights, misfit):
+    batch_size, pad_rows, pad_cols, channel_count = padded.shape
+    groups = channel_count // lane_count
+    return pl.pallas_call(
+        conv_back_kernel,
+        out_shape=jax.ShapeDtypeStruct(misfit.shape, jnp.bfloat16),
+        scratch_shapes=[
+            pltpu.VMEM((groups, batch_size, pad_rows, round_up(pad_cols, 8), lane_count), jnp.float32),
+        ],
+        compiler_params=pltpu.CompilerParams(vmem_limit_bytes=16 << 20),
+        cost_estimate=pl.CostEstimate(flops=2 * 49 * misfit.size, bytes_accessed=1 << 20, transcendentals=0),
+        name="conv_back",
+    )(padded, lane_groups(weights), misfit)
+
+
+def tap_sums_kernel(padded_ref, grad_ref, out_ref, wide, partial):
+    batch_size, tile_rows, tile_cols, channel_count = grad_ref.shape
+    kernel_size = padded_ref.shape[1] - tile_rows + 1
+    spread(padded_ref, wide)
+    out_ref[...] = jnp.zeros_like(out_ref)
+    for group in range(wide.shape[0]):
+        lanes = slice(group * lane_count, (group + 1) * lane_count)
+
+        def one(b, _):
+            grads = [grad_ref[b, i, :, lanes].astype(jnp.float32) for i in range(tile_rows)]
+            for q in range(kernel_size):
+                sums = [None] * kernel_size
+                for r in range(tile_rows + kernel_size - 1):
+                    shifted = wide[group, b, r, q : q + tile_cols, :]
+                    for i in range(max(0, r - kernel_size + 1), min(tile_rows, r + 1)):
+                        product = shifted * grads[i]
+                        term = product.reshape(tile_cols // 8, 8, lane_count).sum(axis=0)
+                        p = r - i
+                        sums[p] = term if sums[p] is None else sums[p] + term
+                for p in range(kernel_size):
+                    at = pl.ds((p * kernel_size + q) * 8, 8)
+                    partial[group, b, at, :] = sums[p]
+            return 0
+
+        lax.fori_loop(0, batch_size, one, 0)
+        taps = kernel_size * kernel_size
+        total = partial[group, 0]
+        for b in range(1, batch_size):
+            total = total + partial[group, b]
+        out_ref[:taps, lanes] = total.reshape(taps, 8, lane_count).sum(axis=1)
+
+
+def tap_sums(padded, grads, row_count):
+    batch_size, pad_rows, pad_cols, channel_count = padded.shape
+    kernel_size = pad_rows - grads.shape[1] + 1
+    groups = channel_count // lane_count
+    return pl.pallas_call(
+        tap_sums_kernel,
+        out_shape=jax.ShapeDtypeStruct((row_count, channel_count), jnp.float32),
+        scratch_shapes=[
+            pltpu.VMEM((groups, batch_size, pad_rows, round_up(pad_cols, 8), lane_count), jnp.float32),
+            pltpu.VMEM((groups, batch_size, kernel_size * kernel_size * 8, lane_count), jnp.float32),
+        ],
+        compiler_params=pltpu.CompilerParams(vmem_limit_bytes=16 << 20),
+        cost_estimate=pl.CostEstimate(flops=2 * 49 * grads.size, bytes_accessed=1 << 20, transcendentals=0),
+        name="tap_sums",
+    )(padded, grads)
+
+
+def assemble_kernel(side_ref, out_mine, out_got, in_mine, in_got, out_ref, in_ref, taps_ref):
+    half = pl.program_id(0)
+    own = half == side_ref[0]
+    count, rows, _ = out_mine.shape
+    channel_count = in_ref.shape[0]
+
+    def write(out_chunks, in_chunks):
+        for k in range(count):
+            out_ref[k * rows : (k + 1) * rows, :] = out_chunks[k].astype(jnp.float32)
+            in_ref[:, k * rows : (k + 1) * rows] = in_chunks[k, :channel_count].astype(jnp.float32)
+
+    @pl.when(own)
+    def _():
+        write(out_mine, in_mine)
+
+    @pl.when(jnp.logical_not(own))
+    def _():
+        write(out_got, in_got)
+
+    @pl.when(half == 0)
+    def _():
+        first = side_ref[0] == 0
+        tail = slice(channel_count, in_mine.shape[1])
+        mine, got = in_mine[:, tail].astype(jnp.float32), in_got[:, tail].astype(jnp.float32)
+        halves = [jnp.where(first, mine, got), jnp.where(first, got, mine)]
+        rows_of = (channel_count // in_mine.shape[2], mine.shape[1])
+        step = rows_of[1] // rows_of[0]
+        pieces = []
+        for chunks in halves:
+            for k in range(count):
+                groups = [chunks[k, n * step : (n + 1) * step] for n in range(rows_of[0])]
+                pieces.append(jnp.concatenate(groups, axis=1))
+        taps = jnp.concatenate(pieces, axis=0)
+        width = taps_ref.shape[1]
+        for p in range(taps_ref.shape[0]):
+            taps_ref[p] = taps[p * width : (p + 1) * width]
+
+
+def assemble(side, out_mine, out_got, in_mine, in_got, channel_count, kernel_size):
+    count, rows, _ = out_mine.shape
+    whole = lambda value: pl.BlockSpec(value.shape, lambda i: (0,) * value.ndim)
+    operands = (out_mine, out_got, in_mine, in_got)
+    return pl.pallas_call(
+        assemble_kernel,
+        grid=(2,),
+        in_specs=[pl.BlockSpec(memory_space=pltpu.SMEM)] + [whole(v) for v in operands],
+        out_specs=(
+            pl.BlockSpec((count * rows, channel_count), lambda i: (i, 0)),
+            pl.BlockSpec((channel_count, count * rows), lambda i: (0, i)),
+            pl.BlockSpec((kernel_size, kernel_size, channel_count), lambda i: (0, 0, 0)),
+        ),
+        out_shape=(
+            jax.ShapeDtypeStruct((2 * count * rows, channel_count), jnp.float32),
+            jax.ShapeDtypeStruct((channel_count, 2 * count * rows), jnp.float32),
+            jax.ShapeDtypeStruct((kernel_size, kernel_size, channel_count), jnp.float32),
+        ),
+        compiler_params=pltpu.CompilerParams(vmem_limit_bytes=16 << 20),
+        cost_estimate=pl.CostEstimate(flops=0, bytes_accessed=3 << 20, transcendentals=0),
+        name="assemble",
+    )(side, *operands)
 
 
 def local(student, teacher, dw_weight, norm_gain, w_in, w_out, layer_scale):
@@ -212,16 +430,7 @@
     lon_padded = with_halo(student, "lon", 2, half_kernel, True)
     lon_padded, teacher = lax.optimization_barrier((lon_padded, teacher))
     padded_bf = with_halo(lon_padded, "lat", 1, half_kernel, False)
-    padded = padded_bf.astype(jnp.float32)
-    smoothed = apply_stencil(padded, dw_weight, tile_rows, tile_cols, False).reshape(
-        -1, channel_count
-    )
-    average = jnp.mean(smoothed, axis=-1, keepdims=True)
-    centred = smoothed - average
-    variance = jnp.mean(centred * centred, axis=-1, keepdims=True)
-    inv_std = lax.rsqrt(variance + norm_eps)
-    unit_norm = centred * inv_std
-    normed = (unit_norm * norm_gain).astype(jnp.bfloat16)
+    normed, unit_norm, inv_std = conv_norm(padded_bf, dw_weight, norm_gain)
     preact = jnp.dot(normed, w_in, preferred_element_type=jnp.float32)
     hidden = gelu_tanh(preact).astype(jnp.bfloat16)
     mlp_out = jnp.dot(hidden, w_out, preferred_element_type=jnp.float32)
@@ -251,20 +460,8 @@
     conv_grad = (inv_std * (unit_grad - first_mean - unit_norm * second_mean)).astype(jnp.bfloat16)
     conv_grid = conv_grad.reshape(student.shape)
     inner, outer = swap(jnp.stack(edges(conv_grid, "lat", 1, half_kernel)), "lat", 1)
-    conv_grad_f = conv_grid.astype(jnp.float32)
-    kernel_terms = []
-    for row_off in range(kernel_size):
-        for col_off in range(kernel_size):
-            kernel_terms.append(
-                jnp.sum(
-                    padded[:, row_off : row_off + tile_rows, col_off : col_off + tile_cols]
-                    * conv_grad_f,
-                    axis=(0, 1, 2),
-                )
-            )
-    part_dw = jnp.stack(kernel_terms)
     tap_count = kernel_size * kernel_size
-    part_dw = jnp.pad(part_dw, ((0, -tap_count % 64), (0, 0)))
+    part_dw = tap_sums(padded_bf, conv_grid, round_up(tap_count, 64))
     got_dw = swap(half_of(part_dw, 1 - upper).astype(jnp.bfloat16), "lat", 1)
     (out_chunk,), (in_chunk, dw_chunk), padded_grad = sum_over_mesh(
         [[kept_out, got_out]],
@@ -275,22 +472,21 @@
         outer,
         half_kernel,
     )
-    back_conv = apply_stencil(
-        padded_grad.astype(jnp.float32), dw_weight, tile_rows, tile_cols, True
-    )
-    grad_student = (misfit.reshape(student.shape) + back_conv).astype(jnp.bfloat16)
+    grad_student = conv_back(padded_grad, dw_weight, misfit.reshape(student.shape))
     hidden_rows = in_chunk.shape[0]
-    mixed = jnp.concatenate([in_chunk.T, dw_chunk.reshape(-1, hidden_rows)])
+    dw_groups = [dw_chunk[:, k : k + hidden_rows] for k in range(0, channel_count, hidden_rows)]
+    mixed = jnp.concatenate([in_chunk.T] + dw_groups)
     out_chunks, in_chunks = gather_sums(out_chunk[None], mixed[None])
-    sum_out = out_chunks.astype(jnp.float32).reshape(w_out.shape)
-    sum_in = jnp.swapaxes(in_chunks[:, :channel_count], 0, 1).astype(jnp.float32)
-    sum_dw = in_chunks[:, channel_count:].astype(jnp.float32).reshape(-1, channel_count)
-    return (
-        grad_student,
-        sum_in.reshape(w_in.shape),
-        sum_out,
-        sum_dw[:tap_count].reshape(dw_weight.shape),
-    )
+    sum_out, sum_in, sum_dw = assemble(
+        upper.astype(jnp.int32).reshape(1),
+        out_chunks,
+        swap(out_chunks, "lat", 1),
+        in_chunks,
+        swap(in_chunks, "lat", 1),
+        channel_count,
+        kernel_size,
+    )
+    return (grad_student, sum_in, sum_out, sum_dw)
 
 
 def solution(mesh):

time: 77.8 us -> 73.2 us (0.941)
  other arithmetic: 10.4 us -> 2.34 us
  Pallas kernels: 0 us -> 5.9 us
  local copies, waits for them, and re-layouts: 7.12 us -> 4.26 us
  matrix products: 3.16 us -> 4.05 us
    pallas_call x0 -> x4, Pallas kernels: none -> 5.9 us  [the longest x1 1.94 us: conv_back(): pl.pallas_call(conv_back_kernel, out_shape=jax.ShapeDtypeStruct(misfit.sh...]
    reduce_sum x5 -> x0, other arithmetic: 4.18 us -> none  [the longest x3 2.15 us: local(): jnp.sum(padded[:, row_off:row_off + tile_rows, col_off:col_off + tile_col...]
    convert_element_type x5 -> x1, other arithmetic: 3.83 us -> 0.18 us  [local(): (inv_std * (unit_grad - first_mean - unit_norm * second_mean)).astype(jnp...]
    unnamed x97 -> x20, local copies, waits for them, and re-layouts: 5.6 us -> 3.93 us
    ppermute x22, waiting for transfers between devices: 24.8 us -> 25.8 us  [swap(): lax.ppermute(value, axis, [(i, i ^ bit) for i in range(lax.axis_size(axis...]
    dot_general x1, matrix products: 0.5 us -> 1.39 us  [local(): preact = jnp.dot(normed, w_in, preferred_element_type=jnp.float32)]
  transfers between devices with their start and end apart: 24 -> 24, of which waited for: 12 -> 11; matrix products, arithmetic and copies ran while one was open for 11% -> 5% of each run, Pallas kernels for 0% -> 5%
where the time goes in v4:
time: 73.2 us; the launch traced here: 72.9 us
  waiting for transfers between devices  27.8 us (38%)
  starting transfers between devices  27.3 us (37%)
  Pallas kernels  5.9 us (8%)
  local copies, waits for them, and re-layouts  4.26 us (6%)
  matrix products  4.05 us (6%)
  other arithmetic  2.34 us (3%)
  between operations  1.34 us (2%)
    ppermute x22, waiting for transfers between devices, swap(): lax.ppermute(value, axis, [(i, i ^ bit) for i in range(lax.axis_size(axis...  25.8 us
    ppermute x22, starting transfers between devices, swap(): lax.ppermute(value, axis, [(i, i ^ bit) for i in range(lax.axis_size(axis...  23.1 us
    ppermute x2, starting transfers between devices, swap_outer(): return lax.ppermute(edge, axis, pairs + [(j, i) for i, j in pairs])  4.2 us
    unnamed x20, local copies, waits for them, and re-layouts  3.93 us
    pallas_call x1, Pallas kernels, conv_back(): pl.pallas_call(conv_back_kernel, out_shape=jax.ShapeDtypeStruct(misfit.sh...  1.94 us
    ppermute x2, waiting for transfers between devices, swap_outer(): return lax.ppermute(edge, axis, pairs + [(j, i) for i, j in pairs])  1.93 us
    pallas_call x1, Pallas kernels, conv_norm(): pl.pallas_call(conv_norm_kernel, out_shape=(jax.ShapeDtypeStruct((cells,...  1.5 us
  transfers between devices with their start and end apart: 24, of which 11 were waited for; matrix products, arithmetic and copies ran while one was open for 5% of the time, Pallas kernels for 5%

profile of v4, /device:TPU:0, one launch (start us, length us, event | category | flops | bytes accessed | tf_op | source)
XLA Modules:
  0.0 72.9 jit_solution(954582089207241656)
XLA Ops:
  0.7 0.9 %broadcast_select_fusion.11 = (bf16[2,4,3,256]{3,2,1,0:T(4,128)(2,1)S(1)}, bf16[2,4,3,256]{3,2,1,0:T(4,128)(2,1)S(1)}) fusion(pred[]{:T(512)S(6)} %eq.66, bf16[2,4,32,256]{3,2,1,0:T(8,128)(2,1)} %param.7), kind=kLoop, calls=%fused_computation.88 | loop fusion | flops 12288 | bytes 49153 | tf_op jit(solution)/shard_map/jit(_where)/select_n | solution.py:25
  1.5 3.0 %collective-permute-start = (bf16[2,4,3,256]{3,2,1,0:T(4,128)(2,1)S(1)}, bf16[2,4,3,256]{3,2,1,0:T(4,128)(2,1)S(1)}, u32[]{:S(2)}, u32[]{:S(2)}) collective-permute-start(bf16[2,4,3,256]{3,2,1,0:T(4,128)(2,1)S(1)} %get-tuple-element.63), channel_id=1, source_target_pairs={{0,1},{1,0},{2,3},{3,2},{4,5},{5,4},{6,7},{7,6},{8,9},{9,8},{10,11... | collective-permute-start | bytes 36872 | tf_op jit(solution)/shard_map/ppermute | solution.py:18
  4.5 3.5 %collective-permute-start.1 = (bf16[2,4,3,256]{3,2,1,0:T(4,128)(2,1)S(1)}, bf16[2,4,3,256]{3,2,1,0:T(4,128)(2,1)S(1)}, u32[]{:S(2)}, u32[]{:S(2)}) collective-permute-start(bf16[2,4,3,256]{3,2,1,0:T(4,128)(2,1)S(1)} %get-tuple-element.64), channel_id=1, source_target_pairs={{1,2},{3,4},{5,6},{7,0},{2,1},{4,3},{6,5},{0,7},{9,10},{11,12},{13... | collective-permute-start | bytes 36872 | tf_op jit(solution)/shard_map/ppermute | solution.py:33
  8.1 0.8 %copy-done.7 = f32[7,7,256]{2,1,0:T(8,128)S(1)} copy-done((f32[7,7,256]{2,1,0:T(8,128)S(1)}, f32[7,7,256]{2,1,0:T(8,128)}, u32[]{:S(2)}) %copy-start.7) | copy-done | bytes 50200
  9.1 1.9 %collective-permute-done.1 = bf16[2,4,3,256]{3,2,1,0:T(4,128)(2,1)S(1)} collective-permute-done((bf16[2,4,3,256]{3,2,1,0:T(4,128)(2,1)S(1)}, bf16[2,4,3,256]{3,2,1,0:T(4,128)(2,1)S(1)}, u32[]{:S(2)}, u32[]{:S(2)}) %collective-permute-start.1) | collective-permute-done | bytes 12320 | tf_op jit(solution)/shard_map/ppermute | solution.py:33
  11.1 0.8 %copy-done.6 = bf16[2,16,8,256]{3,2,1,0:T(8,128)(2,1)S(1)} copy-done((bf16[2,16,8,256]{3,2,1,0:T(8,128)(2,1)S(1)}, bf16[2,16,8,256]{3,2,1,0:T(8,128)(2,1)}, u32[]{:S(2)}) %copy-start.6) | copy-done | bytes 131096
  12.6 0.7 collective-permute-start.3
  13.4 3.0 %collective-permute-start.5 = (bf16[2,1,4,16,256]{4,3,2,0,1:T(8,128)(2,1)S(1)}, bf16[2,1,4,16,256]{4,3,2,0,1:T(8,128)(2,1)S(1)}, u32[]{:S(2)}, u32[]{:S(2)}) collective-permute-start(bf16[2,1,4,16,256]{4,3,2,0,1:T(8,128)(2,1)S(1)} %get-tuple-element.59), channel_id=1, source_target_pairs={{0,16},{8,24},{16,0},{24,8},{1,17},{9,25},{17,1},{25,9},{2,18},{10... | collective-permute-start | bytes 196616 | tf_op jit(solution)/shard_map/ppermute | solution.py:18
  16.4 0.7 copy-done.1
  17.1 1.5 %conv_norm.1 = (bf16[256,256]{1,0:T(8,128)(2,1)S(1)}, f32[256,256]{1,0:T(8,128)S(1)}, f32[256,1]{1,0:T(8,128)S(1)}) custom-call(bf16[2,10,38,256]{3,2,1,0:T(8,128)(2,1)S(1)} %pad_maximum_fusion.padded_ref, f32[2,7,7,128]{3,2,1,0:T(8,128)S(1)} %bitcast.66, f32[1,256]{1,0:T(1,128)S(1)} %bitcast.68), custom_call_target="tpu_custom_call" | custom-call | flops 6422528 | bytes 1048576 | tf_op jit(solution)/shard_map/conv_norm/pallas_call | solution.py:267
  18.6 1.4 %multiply_convert_fusion = (bf16[256,1024]{1,0:T(8,128)(2,1)S(1)}, f32[256,1024]{1,0:T(8,128)}) fusion(bf16[256,256]{1,0:T(8,128)(2,1)S(1)} %get-tuple-element.21, bf16[256,1024]{1,0:T(8,128)(2,1)S(1)} %copy-done), kind=kOutput, calls=%fused_computation.14 | convolution fusion | flops 136577024 | bytes 2228224 | tf_op jit(solution)/shard_map/dot_general | solution.py:434
  21.7 0.8 %fusion = bf16[256,1024]{1,0:T(8,128)(2,1)S(1)} fusion(bf16[256,256]{1,0:T(8,128)(2,1)S(1)} %get-tuple-element.73, bf16[1024,256]{1,0:T(8,128)(2,1)S(1)} %copy-done.3, f32[256,1024]{1,0:T(8,128)S(1)} %copy-done.9), kind=kOutput, calls=%fused_computation.3 | convolution fusion | flops 139198464 | bytes 2228224 | tf_op jit(solution)/shard_map/dot_general | solution.py:446
  23.2 1.0 %tap_sums.1 = f32[64,256]{1,0:T(8,128)S(1)} custom-call(bf16[2,10,38,256]{3,2,1,0:T(8,128)(2,1)S(1)} %pad_maximum_fusion.padded_ref, bf16[2,4,32,256]{3,2,1,0:T(8,128)(2,1)S(1)} %bitcast.62), custom_call_target="tpu_custom_call" | custom-call | flops 6422528 | bytes 1048576 | tf_op jit(solution)/shard_map/tap_sums/pallas_call | solution.py:350
  24.8 2.4 %collective-permute-start.8 = (bf16[2,2,3,32,256]{4,3,2,1,0:T(8,128)(2,1)S(1)}, bf16[2,2,3,32,256]{4,3,2,1,0:T(8,128)(2,1)S(1)}, u32[]{:S(2)}, u32[]{:S(2)}) collective-permute-start(bf16[2,2,3,32,256]{4,3,2,1,0:T(8,128)(2,1)S(1)} %pad_maximum_fusion.4), channel_id=1, source_target_pairs={{0,8},{8,0},{16,24},{24,16},{1,9},{9,1},{17,25},{25,17},{2,10},{10... | collective-permute-start | bytes 589832 | tf_op jit(solution)/shard_map/ppermute | solution.py:18
  28.5 0.7 copy-done.4
  29.7 2.2 %collective-permute-start.14 = (bf16[256,256]{1,0:T(8,128)(2,1)S(1)}, bf16[256,256]{1,0:T(8,128)(2,1)S(1)}, u32[]{:S(2)}, u32[]{:S(2)}) collective-permute-start(bf16[256,256]{1,0:T(8,128)(2,1)S(1)} %get-tuple-element.43), channel_id=1, source_target_pairs={{0,16},{8,24},{16,0},{24,8},{1,17},{9,25},{17,1},{25,9},{2,18},{10... | collective-permute-start | bytes 393224 | tf_op jit(solution)/shard_map/ppermute | solution.py:18
  32.0 0.8 %collective-permute-start.9 = (bf16[464,256]{1,0:T(8,128)(2,1)S(1)}, bf16[464,256]{1,0:T(8,128)(2,1)S(1)}, u32[]{:S(2)}, u32[]{:S(2)}) collective-permute-start(bf16[464,256]{1,0:T(8,128)(2,1)S(1)} %pad_maximum_fusion.2), channel_id=1, source_target_pairs={{0,16},{8,24},{16,0},{24,8},{1,17},{9,25},{17,1},{25,9},{2,18},{10... | collective-permute-start | bytes 712712 | tf_op jit(solution)/shard_map/ppermute | solution.py:18
  32.8 3.4 %collective-permute-done.14 = bf16[256,256]{1,0:T(8,128)(2,1)S(1)} collective-permute-done((bf16[256,256]{1,0:T(8,128)(2,1)S(1)}, bf16[256,256]{1,0:T(8,128)(2,1)S(1)}, u32[]{:S(2)}, u32[]{:S(2)}) %collective-permute-start.14) | collective-permute-done | bytes 131104 | tf_op jit(solution)/shard_map/ppermute | solution.py:18
  36.3 4.5 %collective-permute-done.9 = bf16[464,256]{1,0:T(8,128)(2,1)S(1)} collective-permute-done((bf16[464,256]{1,0:T(8,128)(2,1)S(1)}, bf16[464,256]{1,0:T(8,128)(2,1)S(1)}, u32[]{:S(2)}, u32[]{:S(2)}) %collective-permute-start.9) | collective-permute-done | bytes 237600 | tf_op jit(solution)/shard_map/ppermute | solution.py:18
  41.6 4.7 %collective-permute-done.10 = bf16[256,256]{1,0:T(8,128)(2,1)S(1)} collective-permute-done((bf16[256,256]{1,0:T(8,128)(2,1)S(1)}, bf16[256,256]{1,0:T(8,128)(2,1)S(1)}, u32[]{:S(2)}, u32[]{:S(2)}) %collective-permute-start.10) | collective-permute-done | bytes 131104 | tf_op jit(solution)/shard_map/ppermute | solution.py:18
  46.4 3.0 %collective-permute-start.17 = (bf16[128,256]{1,0:T(8,128)(2,1)S(1)}, bf16[128,256]{1,0:T(8,128)(2,1)S(1)}, u32[]{:S(2)}, u32[]{:S(2)}) collective-permute-start(bf16[128,256]{1,0:T(8,128)(2,1)S(1)} %get-tuple-element.39), channel_id=1, source_target_pairs={{0,4},{1,5},{2,6},{3,7},{4,0},{5,1},{6,2},{7,3},{8,12},{9,13},{10,... | collective-permute-start | bytes 196616 | tf_op jit(solution)/shard_map/ppermute | solution.py:18
  49.4 4.1 %collective-permute-done.11 = f32[196,256]{1,0:T(8,128)S(1)} collective-permute-done((f32[196,256]{1,0:T(8,128)S(1)}, f32[196,256]{1,0:T(8,128)S(1)}, u32[]{:S(2)}, u32[]{:S(2)}) %collective-permute-start.11) | collective-permute-done | bytes 200736 | tf_op jit(solution)/shard_map/ppermute | solution.py:18
  53.5 0.9 %collective-permute-start.12 = (bf16[196,256]{1,0:T(8,128)(2,1)S(1)}, bf16[196,256]{1,0:T(8,128)(2,1)S(1)}, u32[]{:S(2)}, u32[]{:S(2)}) collective-permute-start(bf16[196,256]{1,0:T(8,128)(2,1)S(1)} %pad_maximum_fusion.7), channel_id=1, source_target_pairs={{0,4},{1,5},{2,6},{3,7},{4,0},{5,1},{6,2},{7,3},{8,12},{9,13},{10,... | collective-permute-start | bytes 301064 | tf_op jit(solution)/shard_map/ppermute | solution.py:18
  54.4 1.5 %collective-permute-start.18 = (bf16[1,128,256]{2,1,0:T(8,128)(2,1)S(1)}, bf16[1,128,256]{2,1,0:T(8,128)(2,1)S(1)}, u32[]{:S(2)}, u32[]{:S(2)}) collective-permute-start(bf16[1,128,256]{2,1,0:T(8,128)(2,1)S(1)} %fusion.15), channel_id=1, source_target_pairs={{0,1},{1,0},{2,3},{3,2},{4,5},{5,4},{6,7},{7,6},{8,9},{9,8},{10,11... | collective-permute-start | bytes 196616 | tf_op jit(solution)/shard_map/ppermute | solution.py:18
  55.9 3.5 %collective-permute-done.12 = bf16[196,256]{1,0:T(8,128)(2,1)S(1)} collective-permute-done((bf16[196,256]{1,0:T(8,128)(2,1)S(1)}, bf16[196,256]{1,0:T(8,128)(2,1)S(1)}, u32[]{:S(2)}, u32[]{:S(2)}) %collective-permute-start.12) | collective-permute-done | bytes 100384 | tf_op jit(solution)/shard_map/ppermute | solution.py:18
  59.6 1.4 %collective-permute-start.21 = (bf16[1,272,128]{2,1,0:T(8,128)(2,1)S(1)}, bf16[1,272,128]{2,1,0:T(8,128)(2,1)S(1)}, u32[]{:S(2)}, u32[]{:S(2)}) collective-permute-start(bf16[1,272,128]{2,1,0:T(8,128)(2,1)S(1)} %maximum_bitcast_fusion), channel_id=1, source_target_pairs={{0,1},{1,0},{2,3},{3,2},{4,5},{5,4},{6,7},{7,6},{8,9},{9,8},{10,11... | collective-permute-start | bytes 208904 | tf_op jit(solution)/shard_map/ppermute | solution.py:18
  60.9 1.3 %collective-permute-start.19 = (bf16[2,128,256]{2,1,0:T(8,128)(2,1)S(1)}, bf16[2,128,256]{2,1,0:T(8,128)(2,1)S(1)}, u32[]{:S(2)}, u32[]{:S(2)}) collective-permute-start(bf16[2,128,256]{2,1,0:T(8,128)(2,1)S(1)} %maximum_select_fusion.5), channel_id=1, source_target_pairs={{0,16},{8,24},{16,0},{24,8},{1,17},{9,25},{17,1},{25,9},{2,18},{10... | collective-permute-start | bytes 393224 | tf_op jit(solution)/shard_map/ppermute | solution.py:18
  62.2 1.7 %collective-permute-done.21 = bf16[1,272,128]{2,1,0:T(8,128)(2,1)S(1)} collective-permute-done((bf16[1,272,128]{2,1,0:T(8,128)(2,1)S(1)}, bf16[1,272,128]{2,1,0:T(8,128)(2,1)S(1)}, u32[]{:S(2)}, u32[]{:S(2)}) %collective-permute-start.21) | collective-permute-done | bytes 69664 | tf_op jit(solution)/shard_map/ppermute | solution.py:18
  64.0 1.7 %collective-permute-start.22 = (bf16[2,272,128]{2,1,0:T(8,128)(2,1)S(1)}, bf16[2,272,128]{2,1,0:T(8,128)(2,1)S(1)}, u32[]{:S(2)}, u32[]{:S(2)}) collective-permute-start(bf16[2,272,128]{2,1,0:T(8,128)(2,1)S(1)} %maximum_select_fusion.2), channel_id=1, source_target_pairs={{0,16},{8,24},{16,0},{24,8},{1,17},{9,25},{17,1},{25,9},{2,18},{10... | collective-permute-start | bytes 417800 | tf_op jit(solution)/shard_map/ppermute | solution.py:18
  66.1 3.0 %collective-permute-done.22 = bf16[2,272,128]{2,1,0:T(8,128)(2,1)S(1)} collective-permute-done((bf16[2,272,128]{2,1,0:T(8,128)(2,1)S(1)}, bf16[2,272,128]{2,1,0:T(8,128)(2,1)S(1)}, u32[]{:S(2)}, u32[]{:S(2)}) %collective-permute-start.22) | collective-permute-done | bytes 139296 | tf_op jit(solution)/shard_map/ppermute | solution.py:18
  69.5 1.9 %conv_back.1 = bf16[2,4,32,256]{3,2,1,0:T(8,128)(2,1)} custom-call(bf16[2,10,38,256]{3,2,1,0:T(8,128)(2,1)S(1)} %pad_maximum_fusion.1.padded_ref, f32[2,7,7,128]{3,2,1,0:T(8,128)S(1)} %bitcast.67, f32[2,4,32,256]{3,2,1,0:T(8,128)S(1)} %bitcast.65), custom_call_target="tpu_custom_call" | custom-call | flops 6422528 | bytes 1048576 | tf_op jit(solution)/shard_map/conv_back/pallas_call | solution.py:302
  71.5 1.5 %assemble.1 = (f32[1024,256]{1,0:T(8,128)}, f32[256,1024]{1,0:T(8,128)}, f32[7,7,256]{2,1,0:T(8,128)}) custom-call(s32[1]{0:T(128)} %bitcast.17.side_ref, bf16[4,128,256]{2,1,0:T(8,128)(2,1)S(1)} %maximum_select_fusion.1.out_mine, bf16[4,128,256]{2,1,0:T(8,128)(2,1)S(1)} %collective-permute-done.20.out_got, ...), custom_call_target="tpu_custom_call" | custom-call | bytes 3145728 | tf_op jit(solution)/shard_map/assemble/pallas_call | solution.py:405
  (110 shorter events, 7.7 us)
Async XLA Ops:
  0.6 18.0 %copy-start = (bf16[256,1024]{1,0:T(8,128)(2,1)S(1)}, bf16[256,1024]{1,0:T(8,128)(2,1)}, u32[]{:S(2)}) copy-start(bf16[256,1024]{1,0:T(8,128)(2,1)} %param.11) | copy-start | bytes 1572868
  1.5 7.5 %collective-permute-start = (bf16[2,4,3,256]{3,2,1,0:T(4,128)(2,1)S(1)}, bf16[2,4,3,256]{3,2,1,0:T(4,128)(2,1)S(1)}, u32[]{:S(2)}, u32[]{:S(2)}) collective-permute-start(bf16[2,4,3,256]{3,2,1,0:T(4,128)(2,1)S(1)} %get-tuple-element.63), channel_id=1, source_target_pairs={{0,1},{1,0},{2,3},{3,2},{4,5},{5,4},{6,7},{7,6},{8,9},{9,8},{10,11... | collective-permute-start | bytes 36872 | tf_op jit(solution)/shard_map/ppermute | solution.py:18
  4.5 6.4 %collective-permute-start.1 = (bf16[2,4,3,256]{3,2,1,0:T(4,128)(2,1)S(1)}, bf16[2,4,3,256]{3,2,1,0:T(4,128)(2,1)S(1)}, u32[]{:S(2)}, u32[]{:S(2)}) collective-permute-start(bf16[2,4,3,256]{3,2,1,0:T(4,128)(2,1)S(1)} %get-tuple-element.64), channel_id=1, source_target_pairs={{1,2},{3,4},{5,6},{7,0},{2,1},{4,3},{6,5},{0,7},{9,10},{11,12},{13... | collective-permute-start | bytes 36872 | tf_op jit(solution)/shard_map/ppermute | solution.py:33
  8.1 0.8 %copy-start.7 = (f32[7,7,256]{2,1,0:T(8,128)S(1)}, f32[7,7,256]{2,1,0:T(8,128)}, u32[]{:S(2)}) copy-start(f32[7,7,256]{2,1,0:T(8,128)} %param.9) | copy-start | bytes 150532
  8.9 2.1 %copy-start.2 = (bf16[2,4,32,256]{3,2,1,0:T(8,128)(2,1)S(1)}, bf16[2,4,32,256]{3,2,1,0:T(8,128)(2,1)}, u32[]{:S(2)}) copy-start(bf16[2,4,32,256]{3,2,1,0:T(8,128)(2,1)} %param.7) | copy-start | bytes 393220
  11.0 0.9 %copy-start.6 = (bf16[2,16,8,256]{3,2,1,0:T(8,128)(2,1)S(1)}, bf16[2,16,8,256]{3,2,1,0:T(8,128)(2,1)}, u32[]{:S(2)}) copy-start(bf16[2,16,8,256]{3,2,1,0:T(8,128)(2,1)} %param.8) | copy-start | bytes 393220
  12.0 1.3 %collective-permute-start.4 = (bf16[2,2,4,8,256]{4,3,2,0,1:T(8,128)(2,1)S(1)}, bf16[2,2,4,8,256]{4,3,2,0,1:T(8,128)(2,1)S(1)}, u32[]{:S(2)}, u32[]{:S(2)}) collective-permute-start(bf16[2,2,4,8,256]{4,3,2,0,1:T(8,128)(2,1)S(1)} %bitcast.74), channel_id=1, source_target_pairs={{0,8},{8,0},{16,24},{24,16},{1,9},{9,1},{17,25},{25,17},{2,10},{10... | collective-permute-start | bytes 196616 | tf_op jit(solution)/shard_map/ppermute | solution.py:18
  12.1 4.3 %collective-permute-start.2 = (bf16[2,3,38,256]{3,2,1,0:T(8,128)(2,1)S(1)}, bf16[2,3,38,256]{3,2,1,0:T(8,128)(2,1)S(1)}, u32[]{:S(2)}, u32[]{:S(2)}) collective-permute-start(bf16[2,3,38,256]{3,2,1,0:T(8,128)(2,1)S(1)} %get-tuple-element.55), channel_id=1, source_target_pairs={{0,8},{8,0},{16,24},{24,16},{1,9},{9,1},{17,25},{25,17},{2,10},{10... | collective-permute-start | bytes 350216 | tf_op jit(solution)/shard_map/ppermute | solution.py:18
  12.6 3.7 %collective-permute-start.3 = (bf16[2,3,38,256]{3,2,1,0:T(8,128)(2,1)S(1)}, bf16[2,3,38,256]{3,2,1,0:T(8,128)(2,1)S(1)}, u32[]{:S(2)}, u32[]{:S(2)}) collective-permute-start(bf16[2,3,38,256]{3,2,1,0:T(8,128)(2,1)S(1)} %get-tuple-element.56), channel_id=1, source_target_pairs={{8,16},{16,8},{9,17},{17,9},{10,18},{18,10},{11,19},{19,11},{12,20... | collective-permute-start | bytes 350216 | tf_op jit(solution)/shard_map/ppermute | solution.py:33
  13.4 7.0 %collective-permute-start.5 = (bf16[2,1,4,16,256]{4,3,2,0,1:T(8,128)(2,1)S(1)}, bf16[2,1,4,16,256]{4,3,2,0,1:T(8,128)(2,1)S(1)}, u32[]{:S(2)}, u32[]{:S(2)}) collective-permute-start(bf16[2,1,4,16,256]{4,3,2,0,1:T(8,128)(2,1)S(1)} %get-tuple-element.59), channel_id=1, source_target_pairs={{0,16},{8,24},{16,0},{24,8},{1,17},{9,25},{17,1},{25,9},{2,18},{10... | collective-permute-start | bytes 196616 | tf_op jit(solution)/shard_map/ppermute | solution.py:18
  18.6 1.8 %copy-start.3 = (bf16[1024,256]{1,0:T(8,128)(2,1)S(1)}, bf16[1024,256]{1,0:T(8,128)(2,1)}, u32[]{:S(2)}) copy-start(bf16[1024,256]{1,0:T(8,128)(2,1)} %param.12) | copy-start | bytes 1572868
  20.5 1.2 %copy-start.9 = (f32[256,1024]{1,0:T(8,128)S(1)}, f32[256,1024]{1,0:T(8,128)}, u32[]{:S(2)}) copy-start(f32[256,1024]{1,0:T(8,128)} %get-tuple-element.72) | copy-start | bytes 3145732
  24.8 3.7 %collective-permute-start.8 = (bf16[2,2,3,32,256]{4,3,2,1,0:T(8,128)(2,1)S(1)}, bf16[2,2,3,32,256]{4,3,2,1,0:T(8,128)(2,1)S(1)}, u32[]{:S(2)}, u32[]{:S(2)}) collective-permute-start(bf16[2,2,3,32,256]{4,3,2,1,0:T(8,128)(2,1)S(1)} %pad_maximum_fusion.4), channel_id=1, source_target_pairs={{0,8},{8,0},{16,24},{24,16},{1,9},{9,1},{17,25},{25,17},{2,10},{10... | collective-permute-start | bytes 589832 | tf_op jit(solution)/shard_map/ppermute | solution.py:18
  27.2 1.2 %collective-permute-start.7 = (bf16[32,256]{1,0:T(8,128)(2,1)S(1)}, bf16[32,256]{1,0:T(8,128)(2,1)S(1)}, u32[]{:S(2)}, u32[]{:S(2)}) collective-permute-start(bf16[32,256]{1,0:T(8,128)(2,1)S(1)} %dynamic-slice_convert_fusion), channel_id=1, source_target_pairs={{0,8},{8,0},{16,24},{24,16},{1,9},{9,1},{17,25},{25,17},{2,10},{10... | collective-permute-start | bytes 49160 | tf_op jit(solution)/shard_map/ppermute | solution.py:18
  27.6 4.3 %collective-permute-start.6 = (bf16[512,256]{1,0:T(8,128)(2,1)S(1)}, bf16[512,256]{1,0:T(8,128)(2,1)S(1)}, u32[]{:S(2)}, u32[]{:S(2)}) collective-permute-start(bf16[512,256]{1,0:T(8,128)(2,1)S(1)} %convolution_convert_fusion.1), channel_id=1, source_target_pairs={{0,8},{8,0},{16,24},{24,16},{1,9},{9,1},{17,25},{25,17},{2,10},{10... | collective-permute-start | bytes 786440 | tf_op jit(solution)/shard_map/ppermute | solution.py:18
  28.0 1.5 %collective-permute-start.13 = (bf16[512,256]{1,0:T(8,128)(2,1)S(1)}, bf16[512,256]{1,0:T(8,128)(2,1)S(1)}, u32[]{:S(2)}, u32[]{:S(2)}) collective-permute-start(bf16[512,256]{1,0:T(8,128)(2,1)S(1)} %convolution_convert_fusion), channel_id=1, source_target_pairs={{0,8},{8,0},{16,24},{24,16},{1,9},{9,1},{17,25},{25,17},{2,10},{10... | collective-permute-start | bytes 786440 | tf_op jit(solution)/shard_map/ppermute | solution.py:18
  29.6 2.3 %slice-start = ((bf16[2,2,3,32,256]{4,3,2,1,0:T(8,128)(2,1)}), bf16[1,2,3,32,256]{4,3,2,1,0:T(8,128)(2,1)S(1)}, s32[]{:S(2)}) async-start(bf16[2,2,3,32,256]{4,3,2,1,0:T(8,128)(2,1)} %copy-done.4), calls=%async_computation | async-start | bytes 196608 | tf_op jit(solution)/shard_map/unstack | solution.py:462
  29.7 6.5 %collective-permute-start.14 = (bf16[256,256]{1,0:T(8,128)(2,1)S(1)}, bf16[256,256]{1,0:T(8,128)(2,1)S(1)}, u32[]{:S(2)}, u32[]{:S(2)}) collective-permute-start(bf16[256,256]{1,0:T(8,128)(2,1)S(1)} %get-tuple-element.43), channel_id=1, source_target_pairs={{0,16},{8,24},{16,0},{24,8},{1,17},{9,25},{17,1},{25,9},{2,18},{10... | collective-permute-start | bytes 393224 | tf_op jit(solution)/shard_map/ppermute | solution.py:18
  32.0 8.8 %collective-permute-start.9 = (bf16[464,256]{1,0:T(8,128)(2,1)S(1)}, bf16[464,256]{1,0:T(8,128)(2,1)S(1)}, u32[]{:S(2)}, u32[]{:S(2)}) collective-permute-start(bf16[464,256]{1,0:T(8,128)(2,1)S(1)} %pad_maximum_fusion.2), channel_id=1, source_target_pairs={{0,16},{8,24},{16,0},{24,8},{1,17},{9,25},{17,1},{25,9},{2,18},{10... | collective-permute-start | bytes 712712 | tf_op jit(solution)/shard_map/ppermute | solution.py:18
  36.2 4.6 %copy-start.5 = (bf16[2,2,3,32,256]{4,3,2,1,0:T(8,128)(2,1)S(1)}, bf16[2,2,3,32,256]{4,3,2,1,0:T(8,128)(2,1)}, u32[]{:S(2)}) copy-start(bf16[2,2,3,32,256]{4,3,2,1,0:T(8,128)(2,1)} %copy-done.4) | copy-start | bytes 589828
  36.2 5.0 %collective-permute-start.15 = (bf16[128,256]{1,0:T(8,128)(2,1)S(1)}, bf16[128,256]{1,0:T(8,128)(2,1)S(1)}, u32[]{:S(2)}, u32[]{:S(2)}) collective-permute-start(bf16[128,256]{1,0:T(8,128)(2,1)S(1)} %get-tuple-element.47), channel_id=1, source_target_pairs={{0,1},{1,0},{2,3},{3,2},{4,5},{5,4},{6,7},{7,6},{8,9},{9,8},{10,11... | collective-permute-start | bytes 196616 | tf_op jit(solution)/shard_map/ppermute | solution.py:18
  41.1 5.1 %collective-permute-start.10 = (bf16[256,256]{1,0:T(8,128)(2,1)S(1)}, bf16[256,256]{1,0:T(8,128)(2,1)S(1)}, u32[]{:S(2)}, u32[]{:S(2)}) collective-permute-start(bf16[256,256]{1,0:T(8,128)(2,1)S(1)} %pad_maximum_fusion.6), channel_id=1, source_target_pairs={{0,1},{1,0},{2,3},{3,2},{4,5},{5,4},{6,7},{7,6},{8,9},{9,8},{10,11... | collective-permute-start | bytes 393224 | tf_op jit(solution)/shard_map/ppermute | solution.py:18
  41.2 5.2 %collective-permute-start.16 = (f32[128,256]{1,0:T(8,128)S(1)}, f32[128,256]{1,0:T(8,128)S(1)}, u32[]{:S(2)}, u32[]{:S(2)}) collective-permute-start(f32[128,256]{1,0:T(8,128)S(1)} %convert_add_fusion.2), channel_id=1, source_target_pairs={{0,2},{1,3},{2,0},{3,1},{4,6},{5,7},{6,4},{7,5},{8,10},{9,11},{10,... | collective-permute-start | bytes 393224 | tf_op jit(solution)/shard_map/ppermute | solution.py:18
  46.3 7.2 %collective-permute-start.11 = (f32[196,256]{1,0:T(8,128)S(1)}, f32[196,256]{1,0:T(8,128)S(1)}, u32[]{:S(2)}, u32[]{:S(2)}) collective-permute-start(f32[196,256]{1,0:T(8,128)S(1)} %pad_maximum_fusion.3), channel_id=1, source_target_pairs={{0,2},{1,3},{2,0},{3,1},{4,6},{5,7},{6,4},{7,5},{8,10},{9,11},{10,... | collective-permute-start | bytes 602120 | tf_op jit(solution)/shard_map/ppermute | solution.py:18
  46.4 8.0 %collective-permute-start.17 = (bf16[128,256]{1,0:T(8,128)(2,1)S(1)}, bf16[128,256]{1,0:T(8,128)(2,1)S(1)}, u32[]{:S(2)}, u32[]{:S(2)}) collective-permute-start(bf16[128,256]{1,0:T(8,128)(2,1)S(1)} %get-tuple-element.39), channel_id=1, source_target_pairs={{0,4},{1,5},{2,6},{3,7},{4,0},{5,1},{6,2},{7,3},{8,12},{9,13},{10,... | collective-permute-start | bytes 196616 | tf_op jit(solution)/shard_map/ppermute | solution.py:18
  53.5 5.8 %collective-permute-start.12 = (bf16[196,256]{1,0:T(8,128)(2,1)S(1)}, bf16[196,256]{1,0:T(8,128)(2,1)S(1)}, u32[]{:S(2)}, u32[]{:S(2)}) collective-permute-start(bf16[196,256]{1,0:T(8,128)(2,1)S(1)} %pad_maximum_fusion.7), channel_id=1, source_target_pairs={{0,4},{1,5},{2,6},{3,7},{4,0},{5,1},{6,2},{7,3},{8,12},{9,13},{10,... | collective-permute-start | bytes 301064 | tf_op jit(solution)/shard_map/ppermute | solution.py:18
  54.4 6.5 %collective-permute-start.18 = (bf16[1,128,256]{2,1,0:T(8,128)(2,1)S(1)}, bf16[1,128,256]{2,1,0:T(8,128)(2,1)S(1)}, u32[]{:S(2)}, u32[]{:S(2)}) collective-permute-start(bf16[1,128,256]{2,1,0:T(8,128)(2,1)S(1)} %fusion.15), channel_id=1, source_target_pairs={{0,1},{1,0},{2,3},{3,2},{4,5},{5,4},{6,7},{7,6},{8,9},{9,8},{10,11... | collective-permute-start | bytes 196616 | tf_op jit(solution)/shard_map/ppermute | solution.py:18
  59.6 4.4 %collective-permute-start.21 = (bf16[1,272,128]{2,1,0:T(8,128)(2,1)S(1)}, bf16[1,272,128]{2,1,0:T(8,128)(2,1)S(1)}, u32[]{:S(2)}, u32[]{:S(2)}) collective-permute-start(bf16[1,272,128]{2,1,0:T(8,128)(2,1)S(1)} %maximum_bitcast_fusion), channel_id=1, source_target_pairs={{0,1},{1,0},{2,3},{3,2},{4,5},{5,4},{6,7},{7,6},{8,9},{9,8},{10,11... | collective-permute-start | bytes 208904 | tf_op jit(solution)/shard_map/ppermute | solution.py:18
  60.9 5.0 %collective-permute-start.19 = (bf16[2,128,256]{2,1,0:T(8,128)(2,1)S(1)}, bf16[2,128,256]{2,1,0:T(8,128)(2,1)S(1)}, u32[]{:S(2)}, u32[]{:S(2)}) collective-permute-start(bf16[2,128,256]{2,1,0:T(8,128)(2,1)S(1)} %maximum_select_fusion.5), channel_id=1, source_target_pairs={{0,16},{8,24},{16,0},{24,8},{1,17},{9,25},{17,1},{25,9},{2,18},{10... | collective-permute-start | bytes 393224 | tf_op jit(solution)/shard_map/ppermute | solution.py:18
  64.0 5.1 %collective-permute-start.22 = (bf16[2,272,128]{2,1,0:T(8,128)(2,1)S(1)}, bf16[2,272,128]{2,1,0:T(8,128)(2,1)S(1)}, u32[]{:S(2)}, u32[]{:S(2)}) collective-permute-start(bf16[2,272,128]{2,1,0:T(8,128)(2,1)S(1)} %maximum_select_fusion.2), channel_id=1, source_target_pairs={{0,16},{8,24},{16,0},{24,8},{1,17},{9,25},{17,1},{25,9},{2,18},{10... | collective-permute-start | bytes 417800 | tf_op jit(solution)/shard_map/ppermute | solution.py:18
  66.0 5.4 %collective-permute-start.20 = (bf16[4,128,256]{2,1,0:T(8,128)(2,1)S(1)}, bf16[4,128,256]{2,1,0:T(8,128)(2,1)S(1)}, u32[]{:S(2)}, u32[]{:S(2)}) collective-permute-start(bf16[4,128,256]{2,1,0:T(8,128)(2,1)S(1)} %maximum_select_fusion.1.out_mine), channel_id=1, source_target_pairs={{0,8},{8,0},{16,24},{24,16},{1,9},{9,1},{17,25},{25,17},{2,10},{10... | collective-permute-start | bytes 786440 | tf_op jit(solution)/shard_map/ppermute | solution.py:18
  69.1 2.3 %collective-permute-start.23 = (bf16[4,272,128]{2,1,0:T(8,128)(2,1)S(1)}, bf16[4,272,128]{2,1,0:T(8,128)(2,1)S(1)}, u32[]{:S(2)}, u32[]{:S(2)}) collective-permute-start(bf16[4,272,128]{2,1,0:T(8,128)(2,1)S(1)} %maximum_select_fusion.in_mine), channel_id=1, source_target_pairs={{0,8},{8,0},{16,24},{24,16},{1,9},{9,1},{17,25},{25,17},{2,10},{10... | collective-permute-start | bytes 835592 | tf_op jit(solution)/shard_map/ppermute | solution.py:18
  (3 other events, 2.0 us)

commit v5 on v4

--- a/solution.py
+++ b/solution.py
@@ -63,18 +63,6 @@
             jnp.concatenate([mine, got], axis=3),
         )
     return state.reshape(batch_size, band, -1, channel_count)
-
-
-def gelu_tanh(values):
-    tanh_arg = slope_coef * (values + cubic_coef * values * values * values)
-    return 0.5 * values * (1.0 + jnp.tanh(tanh_arg))
-
-
-def gelu_slope(values):
-    tangent = jnp.tanh(slope_coef * (values + cubic_coef * values * values * values))
-    return 0.5 * (1.0 + tangent) + 0.5 * values * (1.0 - tangent * tangent) * slope_coef * (
-        1.0 + 3.0 * cubic_coef * values * values
-    )
 
 
 def half_of(value, upper):
@@ -142,56 +130,58 @@
 
 
 def sum_stages():
-    lat_bits, lon_bits = bits_of("lat"), bits_of("lon")
-    lat_stages = [("lat", bit) for bit in lat_bits[1:]]
-    lon_stages = [("lon", bit) for bit in lon_bits]
-    return lat_stages, lon_stages, [lat_stages[0], lon_stages[0]]
+    lat_stages = [("lat", bit) for bit in bits_of("lat")[1:]]
+    lon_stages = [("lon", bit) for bit in bits_of("lon")]
+    trail = lat_stages + lon_stages
+    lead = lon_stages[1:3] + lat_stages + lon_stages[:1] + lon_stages[3:]
+    return (lead, lead[:2]), (trail, [lat_stages[0], lon_stages[0]])
+
+
+def sent_type(stage, stages, halved):
+    return jnp.bfloat16 if stage in halved or stage == stages[-1] else jnp.float32
 
 
 def sum_over_mesh(lead, trail, divisor, block, inner, outer, width):
-    lat_stages, lon_stages, halved = sum_stages()
-    last = (lat_stages + lon_stages)[-1]
-    for stages, dim, periodic in ((lat_stages, 1, False), (lon_stages, 2, True)):
-        for axis, bit in stages:
-            rider = jnp.stack(edges(block, axis, dim, width)) if bit == 1 else outer
-            is_halved = (axis, bit) in halved
-            sent_as = jnp.bfloat16 if is_halved or (axis, bit) == last else jnp.float32
-            lead, _, _ = exchange(lead, axis, bit, is_halved, sent_as)
-            trail, got, sent = exchange(trail, axis, bit, is_halved, sent_as, rider)
-            lead = after(lead, sent)
-            if bit == 1:
-                inner, outer = got[0], got[1]
-            else:
-                outer = jnp.where(carried(axis, bit), got, outer)
-        if not periodic:
-            index = lax.axis_index(axis)
-            at_end = (index == 0) | (index == lax.axis_size(axis) - 1)
-            outer = jnp.where(at_end, jnp.zeros_like(outer), outer)
-        block = with_edges(block, inner, outer, axis, dim)
+    (lead_stages, lead_halved), (stages, halved) = sum_stages()
+    dim_of = {"lat": 1, "lon": 2}
+    for k, (axis, bit) in enumerate(stages):
+        dim = dim_of[axis]
+        stage = lead_stages[k]
+        lead, _, _ = exchange(
+            lead, *stage, stage in lead_halved, sent_type(stage, lead_stages, lead_halved)
+        )
+        rider = jnp.stack(edges(block, axis, dim, width)) if bit == 1 else outer
+        trail, got, sent = exchange(
+            trail, axis, bit, (axis, bit) in halved, sent_type((axis, bit), stages, halved), rider
+        )
+        lead = after(lead, sent)
+        if bit == 1:
+            inner, outer = got[0], got[1]
+        else:
+            outer = jnp.where(carried(axis, bit), got, outer)
+        if k + 1 == len(stages) or stages[k + 1][0] != axis:
+            if axis == "lat":
+                index = lax.axis_index(axis)
+                at_end = (index == 0) | (index == lax.axis_size(axis) - 1)
+                outer = jnp.where(at_end, jnp.zeros_like(outer), outer)
+            block = with_edges(block, inner, outer, axis, dim)
     lead = [(total_of(terms) / divisor).astype(jnp.bfloat16) for terms in lead]
     trail = [(total_of(terms) / divisor).astype(jnp.bfloat16) for terms in trail]
     return lead, trail, block
 
 
 def gather_sums(lead, trail):
-    for axis, bit in sum_stages()[2][::-1]:
-        lead = gather_halves(lead, axis, bit)
-        trail = gather_halves(trail, axis, bit)
+    (_, lead_halved), (_, halved) = sum_stages()
+    for lead_stage, stage in zip(lead_halved[::-1], halved[::-1]):
+        lead = gather_halves(lead, *lead_stage)
+        trail = gather_halves(trail, *stage)
     return lead, trail
 
 
-def columns_half(value, upper):
-    count = value.shape[1] // 2
-    return lax.dynamic_slice_in_dim(value, upper * count, count, axis=1)
-
-
-def cell_products(left, right):
-    return lax.dot_general(
-        left, right, (((0,), (0,)), ((), ())), preferred_element_type=jnp.float32
-    )
-
-
 lane_count = 128
+kernel_side = 7
+gain_row = kernel_side * kernel_side
+scale_row = gain_row + 1
 
 
 def spread(padded_ref, wide):
@@ -202,8 +192,9 @@
             wide[group, b, :, :cols, :] = padded_ref[b, :, :, lanes].astype(jnp.float32)
 
 
-def stencil(wide, weights, group, b, tile_rows, tile_cols, flipped):
-    kernel_size = weights.shape[1]
+def stencil(wide, params, group, b, tile_rows, tile_cols, flipped):
+    kernel_size = wide.shape[2] - tile_rows + 1
+    lanes = slice(group * lane_count, (group + 1) * lane_count)
     rows = [None] * tile_rows
     for q in range(kernel_size):
         for r in range(tile_rows + kernel_size - 1):
@@ -211,32 +202,32 @@
             for i in range(max(0, r - kernel_size + 1), min(tile_rows, r + 1)):
                 p = r - i
                 tap = (kernel_size - 1 - p, kernel_size - 1 - q) if flipped else (p, q)
-                term = weights[group, tap[0], pl.ds(tap[1], 1), :] * shifted
+                term = params[pl.ds(tap[0] * kernel_size + tap[1], 1), lanes] * shifted
                 rows[i] = term if rows[i] is None else rows[i] + term
     return rows
 
 
-def conv_norm_kernel(padded_ref, weights_ref, gain_ref, normed_ref, unit_ref, inv_ref, wide, smooth):
+def conv_norm_kernel(padded_ref, params_ref, normed_ref, unit_ref, inv_ref, wide, smooth):
     batch_size, pad_rows, pad_cols, channel_count = padded_ref.shape
-    kernel_size = weights_ref.shape[1]
-    tile_rows, tile_cols = pad_rows - kernel_size + 1, pad_cols - kernel_size + 1
+    cells = smooth.shape[1]
+    tile_rows = pad_rows - kernel_side + 1
+    tile_cols = pad_cols - kernel_side + 1
     spread(padded_ref, wide)
-
-    def one(step, _):
-        group, b = step // batch_size, step % batch_size
-        rows = stencil(wide, weights_ref, group, b, tile_rows, tile_cols, False)
-        for i, row in enumerate(rows):
-            smooth[group, pl.ds((b * tile_rows + i) * tile_cols, tile_cols), :] = row
-        return 0
-
-    lax.fori_loop(0, wide.shape[0] * batch_size, one, 0)
-    groups = range(wide.shape[0])
-    cells = smooth.shape[1]
+    for group in range(wide.shape[0]):
+
+        def one(b, _):
+            rows = stencil(wide, params_ref, group, b, tile_rows, tile_cols, False)
+            for i, row in enumerate(rows):
+                smooth[group, pl.ds((b * tile_rows + i) * tile_cols, tile_cols), :] = row
+            return 0
+
+        lax.fori_loop(0, batch_size, one, 0)
+    gain = params_ref[gain_row : gain_row + 1, :]
     block = 32
 
     def norm(step, _):
         at = pl.ds(pl.multiple_of(step * block, block), block)
-        values = jnp.concatenate([smooth[g, at, :] for g in groups], axis=1)
+        values = jnp.concatenate([smooth[g, at, :] for g in range(wide.shape[0])], axis=1)
         average = jnp.mean(values, axis=-1, keepdims=True)
         centred = values - average
         variance = jnp.mean(centred * centred, axis=-1, keepdims=True)
@@ -244,25 +235,19 @@
         unit = centred * inv_std
         unit_ref[at, :] = unit
         inv_ref[at, :] = inv_std
-        normed_ref[at, :] = (unit * gain_ref[...]).astype(jnp.bfloat16)
+        normed_ref[at, :] = (unit * gain).astype(jnp.bfloat16)
         return 0
 
     lax.fori_loop(0, cells // block, norm, 0, unroll=True)
-
-
-def lane_groups(weights):
-    groups = weights.shape[-1] // lane_count
-    return jnp.moveaxis(weights.reshape(weights.shape[:2] + (groups, lane_count)), 2, 0)
 
 
 def round_up(value, unit):
     return -(-value // unit) * unit
 
 
-def conv_norm(padded, weights, gain):
+def conv_norm(padded, params):
     batch_size, pad_rows, pad_cols, channel_count = padded.shape
-    kernel_size = weights.shape[0]
-    cells = batch_size * (pad_rows - kernel_size + 1) * (pad_cols - kernel_size + 1)
+    cells = batch_size * (pad_rows - kernel_side + 1) * (pad_cols - kernel_side + 1)
     groups = channel_count // lane_count
     return pl.pallas_call(
         conv_norm_kernel,
@@ -278,17 +263,17 @@
         compiler_params=pltpu.CompilerParams(vmem_limit_bytes=16 << 20),
         cost_estimate=pl.CostEstimate(flops=2 * 49 * cells * channel_count, bytes_accessed=1 << 20, transcendentals=0),
         name="conv_norm",
-    )(padded, lane_groups(weights), gain.reshape(1, -1))
-
-
-def conv_back_kernel(padded_ref, weights_ref, misfit_ref, out_ref, wide):
+    )(padded, params)
+
+
+def conv_back_kernel(padded_ref, params_ref, misfit_ref, out_ref, wide):
     batch_size, tile_rows, tile_cols, channel_count = out_ref.shape
     spread(padded_ref, wide)
     for group in range(wide.shape[0]):
         lanes = slice(group * lane_count, (group + 1) * lane_count)
 
         def one(b, _):
-            rows = stencil(wide, weights_ref, group, b, tile_rows, tile_cols, True)
+            rows = stencil(wide, params_ref, group, b, tile_rows, tile_cols, True)
             for i, row in enumerate(rows):
                 out_ref[b, i, :, lanes] = (misfit_ref[b, i, :, lanes] + row).astype(out_ref.dtype)
             return 0
@@ -296,7 +281,7 @@
         lax.fori_loop(0, batch_size, one, 0)
 
 
-def conv_back(padded, weights, misfit):
+def conv_back(padded, params, misfit):
     batch_size, pad_rows, pad_cols, channel_count = padded.shape
     groups = channel_count // lane_count
     return pl.pallas_call(
@@ -308,7 +293,7 @@
         compiler_params=pltpu.CompilerParams(vmem_limit_bytes=16 << 20),
         cost_estimate=pl.CostEstimate(flops=2 * 49 * misfit.size, bytes_accessed=1 << 20, transcendentals=0),
         name="conv_back",
-    )(padded, lane_groups(weights), misfit)
+    )(padded, params, misfit)
 
 
 def tap_sums_kernel(padded_ref, grad_ref, out_ref, wide, partial):
@@ -381,17 +366,14 @@
 
     @pl.when(half == 0)
     def _():
-        first = side_ref[0] == 0
         tail = slice(channel_count, in_mine.shape[1])
-        mine, got = in_mine[:, tail].astype(jnp.float32), in_got[:, tail].astype(jnp.float32)
-        halves = [jnp.where(first, mine, got), jnp.where(first, got, mine)]
-        rows_of = (channel_count // in_mine.shape[2], mine.shape[1])
-        step = rows_of[1] // rows_of[0]
-        pieces = []
-        for chunks in halves:
-            for k in range(count):
-                groups = [chunks[k, n * step : (n + 1) * step] for n in range(rows_of[0])]
-                pieces.append(jnp.concatenate(groups, axis=1))
+        chunks = in_mine[:, tail].astype(jnp.float32) + in_got[:, tail].astype(jnp.float32)
+        groups = channel_count // in_mine.shape[2]
+        step = chunks.shape[1] // groups
+        pieces = [
+            jnp.concatenate([chunks[k, n * step : (n + 1) * step] for n in range(groups)], axis=1)
+            for k in range(count)
+        ]
         taps = jnp.concatenate(pieces, axis=0)
         width = taps_ref.shape[1]
         for p in range(taps_ref.shape[0]):
@@ -422,69 +404,188 @@
     )(side, *operands)
 
 
+def product(left, right, left_dim, right_dim):
+    return lax.dot_general(
+        left, right, (((left_dim,), (right_dim,)), ((), ())), preferred_element_type=jnp.float32
+    )
+
+
+def half_columns(ref, half):
+    count = ref.shape[1] // 2
+    return ref[:, pl.ds(pl.multiple_of(half * count, count), count)]
+
+
+def forward_kernel(
+    side_ref, normed_ref, student_ref, target_ref, w_in_ref, w_out_ref, params_ref,
+    slope_ref, misfit_ref, out_grad_ref, sent_ref, kept_ref, hidden,
+):
+    cells, hidden_size = slope_ref.shape
+    scale = params_ref[scale_row : scale_row + 1, :]
+    slope_ref[...] = product(normed_ref[...], w_in_ref[...], 1, 0)
+    rows, cols = 16, min(512, hidden_size)
+
+    def gelu(step, _):
+        at = pl.ds(pl.multiple_of(step * rows, rows), rows)
+        for k in range(0, hidden_size, cols):
+            values = slope_ref[at, k : k + cols]
+            squares = values * values
+            tangent = jnp.tanh(slope_coef * (values + cubic_coef * (squares * values)))
+            gate = 0.5 * (1.0 + tangent)
+            hidden[at, k : k + cols] = (values * gate).astype(jnp.bfloat16)
+            bend = (1.0 - tangent * tangent) * (slope_coef + 3.0 * slope_coef * cubic_coef * squares)
+            slope_ref[at, k : k + cols] = gate + 0.5 * values * bend
+        return 0
+
+    lax.fori_loop(0, cells // rows, gelu, 0, unroll=2)
+    mlp_out = product(hidden[...], w_out_ref[...], 1, 0)
+    misfit = student_ref[...].astype(jnp.float32) + scale * mlp_out
+    misfit = misfit - target_ref[...].astype(jnp.float32)
+    misfit_ref[...] = misfit
+    out_grad_ref[...] = (scale * misfit).astype(jnp.bfloat16)
+    side = side_ref[0]
+    sent_ref[...] = product(half_columns(hidden, 1 - side), out_grad_ref[...], 0, 0).astype(
+        jnp.bfloat16
+    )
+    kept_ref[...] = product(half_columns(hidden, side), out_grad_ref[...], 0, 0)
+
+
+def vmem_specs(count):
+    return [pl.BlockSpec(memory_space=pltpu.VMEM)] * count
+
+
+def forward(side, normed, student, target, w_in, w_out, params):
+    cells, channel_count = normed.shape
+    hidden_size = w_in.shape[1]
+    shape = jax.ShapeDtypeStruct
+    return pl.pallas_call(
+        forward_kernel,
+        in_specs=[pl.BlockSpec(memory_space=pltpu.SMEM)] + vmem_specs(6),
+        out_specs=vmem_specs(5),
+        out_shape=(
+            shape((cells, hidden_size), jnp.float32),
+            shape((cells, channel_count), jnp.float32),
+            shape((cells, channel_count), jnp.bfloat16),
+            shape((hidden_size // 2, channel_count), jnp.bfloat16),
+            shape((hidden_size // 2, channel_count), jnp.float32),
+        ),
+        scratch_shapes=[pltpu.VMEM((cells, hidden_size), jnp.bfloat16)],
+        compiler_params=pltpu.CompilerParams(vmem_limit_bytes=16 << 20),
+        cost_estimate=pl.CostEstimate(
+            flops=6 * cells * channel_count * hidden_size,
+            bytes_accessed=4 << 20,
+            transcendentals=cells * hidden_size,
+        ),
+        name="forward",
+    )(side, normed, student, target, w_in, w_out, params)
+
+
+def backward_kernel(
+    side_ref, slope_ref, out_grad_ref, normed_ref, unit_ref, inv_ref, w_in_ref, w_out_ref, params_ref,
+    conv_grad_ref, sent_ref, kept_ref, hidden_grad, preact_grad,
+):
+    cells, hidden_size = slope_ref.shape
+    hidden_grad[...] = product(out_grad_ref[...], w_out_ref[...], 1, 1)
+    rows = 16
+
+    def scale_by_slope(step, _):
+        at = pl.ds(pl.multiple_of(step * rows, rows), rows)
+        preact_grad[at, :] = (hidden_grad[at, :] * slope_ref[at, :]).astype(jnp.bfloat16)
+        return 0
+
+    lax.fori_loop(0, cells // rows, scale_by_slope, 0, unroll=2)
+    unit_grad = product(preact_grad[...], w_in_ref[...], 1, 1) * params_ref[gain_row : gain_row + 1, :]
+    unit = unit_ref[...]
+    first_mean = jnp.mean(unit_grad, axis=-1, keepdims=True)
+    second_mean = jnp.mean(unit_grad * unit, axis=-1, keepdims=True)
+    conv_grad_ref[...] = (inv_ref[...] * (unit_grad - first_mean - unit * second_mean)).astype(
+        jnp.bfloat16
+    )
+    side = side_ref[0]
+    sent_ref[...] = product(half_columns(preact_grad, 1 - side), normed_ref[...], 0, 0).astype(
+        jnp.bfloat16
+    )
+    kept_ref[...] = product(half_columns(preact_grad, side), normed_ref[...], 0, 0)
+
+
+def backward(side, slope, out_grad, normed, unit_norm, inv_std, w_in, w_out, params):
+    cells, channel_count = normed.shape
+    hidden_size = w_in.shape[1]
+    shape = jax.ShapeDtypeStruct
+    return pl.pallas_call(
+        backward_kernel,
+        in_specs=[pl.BlockSpec(memory_space=pltpu.SMEM)] + vmem_specs(8),
+        out_specs=vmem_specs(3),
+        out_shape=(
+            shape((cells, channel_count), jnp.bfloat16),
+            shape((hidden_size // 2, channel_count), jnp.bfloat16),
+            shape((hidden_size // 2, channel_count), jnp.float32),
+        ),
+        scratch_shapes=[
+            pltpu.VMEM((cells, hidden_size), jnp.float32),
+            pltpu.VMEM((cells, hidden_size), jnp.bfloat16),
+        ],
+        compiler_params=pltpu.CompilerParams(vmem_limit_bytes=16 << 20),
+        cost_estimate=pl.CostEstimate(
+            flops=6 * cells * channel_count * hidden_size, bytes_accessed=4 << 20, transcendentals=0
+        ),
+        name="backward",
+    )(side, slope, out_grad, normed, unit_norm, inv_std, w_in, w_out, params)
+
+
 def local(student, teacher, dw_weight, norm_gain, w_in, w_out, layer_scale):
     batch_size, tile_rows, tile_cols, channel_count = student.shape
-    kernel_size = dw_weight.shape[0]
-    half_kernel = kernel_size // 2
+    half_kernel = kernel_side // 2
     cell_total = batch_size * tile_rows * lax.axis_size("lat") * tile_cols * lax.axis_size("lon")
-    lon_padded = with_halo(student, "lon", 2, half_kernel, True)
-    lon_padded, teacher = lax.optimization_barrier((lon_padded, teacher))
+    tap_count = kernel_side * kernel_side
+    params = jnp.concatenate(
+        [dw_weight.reshape(tap_count, channel_count), norm_gain[None], layer_scale[None]]
+    )
+    to_inner, to_outer = edges(student, "lon", 2, half_kernel)
+    from_outer = swap_outer(to_outer, "lon", True)
+    from_inner = swap(to_inner, "lon", 1)
+    teacher, params = after((teacher, params), (to_inner, to_outer))
+    lon_padded = with_edges(student, from_inner, from_outer, "lon", 2)
+    lon_padded = after(lon_padded, params)
     padded_bf = with_halo(lon_padded, "lat", 1, half_kernel, False)
-    normed, unit_norm, inv_std = conv_norm(padded_bf, dw_weight, norm_gain)
-    preact = jnp.dot(normed, w_in, preferred_element_type=jnp.float32)
-    hidden = gelu_tanh(preact).astype(jnp.bfloat16)
-    mlp_out = jnp.dot(hidden, w_out, preferred_element_type=jnp.float32)
-    output = student.reshape(-1, channel_count).astype(jnp.float32) + layer_scale * mlp_out
+    normed, unit_norm, inv_std = conv_norm(padded_bf, params)
     target = to_bands(teacher, "lat")
-    misfit = output - target.reshape(-1, channel_count).astype(jnp.float32)
-    out_grad = (layer_scale * misfit).astype(jnp.bfloat16)
     upper = lax.axis_index("lat") % 2
-    got_out = swap(
-        cell_products(columns_half(hidden, 1 - upper), out_grad).astype(jnp.bfloat16), "lat", 1
-    )
-    kept_out = cell_products(columns_half(hidden, upper), out_grad)
-    hidden_grad = lax.dot_general(
-        out_grad, w_out, (((1,), (1,)), ((), ())), preferred_element_type=jnp.float32
-    )
-    preact_grad = (hidden_grad * gelu_slope(preact)).astype(jnp.bfloat16)
-    got_in = swap(
-        cell_products(columns_half(preact_grad, 1 - upper), normed).astype(jnp.bfloat16), "lat", 1
-    )
-    kept_in = cell_products(columns_half(preact_grad, upper), normed)
-    normed_grad = lax.dot_general(
-        preact_grad, w_in, (((1,), (1,)), ((), ())), preferred_element_type=jnp.float32
-    )
-    unit_grad = normed_grad * norm_gain
-    first_mean = jnp.mean(unit_grad, axis=-1, keepdims=True)
-    second_mean = jnp.mean(unit_grad * unit_norm, axis=-1, keepdims=True)
-    conv_grad = (inv_std * (unit_grad - first_mean - unit_norm * second_mean)).astype(jnp.bfloat16)
+    side = upper.astype(jnp.int32).reshape(1)
+    rows = lambda block: block.reshape(-1, channel_count)
+    slope, misfit, out_grad, sent, kept_out = forward(
+        side, normed, rows(student), rows(target), w_in, w_out, params
+    )
+    got_out = swap(sent, "lat", 1)
+    conv_grad, sent, kept_in = backward(
+        side, slope, out_grad, normed, unit_norm, inv_std, w_in, w_out, params
+    )
+    got_in = swap(sent, "lat", 1)
     conv_grid = conv_grad.reshape(student.shape)
-    inner, outer = swap(jnp.stack(edges(conv_grid, "lat", 1, half_kernel)), "lat", 1)
-    tap_count = kernel_size * kernel_size
+    inner, outer = [swap(edge, "lat", 1) for edge in edges(conv_grid, "lat", 1, half_kernel)]
     part_dw = tap_sums(padded_bf, conv_grid, round_up(tap_count, 64))
-    got_dw = swap(half_of(part_dw, 1 - upper).astype(jnp.bfloat16), "lat", 1)
     (out_chunk,), (in_chunk, dw_chunk), padded_grad = sum_over_mesh(
         [[kept_out, got_out]],
-        [[kept_in, got_in], [half_of(part_dw, upper), got_dw]],
+        [[kept_in, got_in], [part_dw]],
         cell_total,
         conv_grid,
         inner,
         outer,
         half_kernel,
     )
-    grad_student = conv_back(padded_grad, dw_weight, misfit.reshape(student.shape))
+    grad_student = conv_back(padded_grad, params, misfit.reshape(student.shape))
     hidden_rows = in_chunk.shape[0]
     dw_groups = [dw_chunk[:, k : k + hidden_rows] for k in range(0, channel_count, hidden_rows)]
     mixed = jnp.concatenate([in_chunk.T] + dw_groups)
     out_chunks, in_chunks = gather_sums(out_chunk[None], mixed[None])
+    in_chunks = after(in_chunks, grad_student)
     sum_out, sum_in, sum_dw = assemble(
-        upper.astype(jnp.int32).reshape(1),
+        side,
         out_chunks,
         swap(out_chunks, "lat", 1),
         in_chunks,
         swap(in_chunks, "lat", 1),
         channel_count,
-        kernel_size,
+        kernel_side,
     )
     return (grad_student, sum_in, sum_out, sum_dw)
 

time: 73.2 us -> 65.2 us (0.89)
  matrix products: 4.05 us -> 0 us
  local copies, waits for them, and re-layouts: 4.26 us -> 1.21 us
  Pallas kernels: 5.9 us -> 8.62 us
  starting transfers between devices: 27.3 us -> 25.1 us
  waiting for transfers between devices: 27.8 us -> 26.6 us
    dot_general x8 -> x0, matrix products: 4.05 us -> none  [the longest x1 1.39 us: local(): preact = jnp.dot(normed, w_in, preferred_element_type=jnp.float32)]
    unnamed x20 -> x14, local copies, waits for them, and re-layouts: 3.93 us -> 0.91 us
    pallas_call x0 -> x2, Pallas kernels: none -> 2.83 us  [the longest x1 1.81 us: forward(): pl.pallas_call(forward_kernel, in_specs=[pl.BlockSpec(memory_space=pltpu....]
    ppermute x22, starting transfers between devices: 23.1 us -> 20.9 us  [swap(): lax.ppermute(value, axis, [(i, i ^ bit) for i in range(lax.axis_size(axis...]
    ppermute x22, waiting for transfers between devices: 25.8 us -> 24.9 us  [swap(): lax.ppermute(value, axis, [(i, i ^ bit) for i in range(lax.axis_size(axis...]
  transfers between devices with their start and end apart: 24 -> 24, of which waited for: 11 -> 12; matrix products, arithmetic and copies ran while one was open for 5% -> 2% of each run, Pallas kernels for 5% -> 7%
where the time goes in v5:
time: 65.2 us; the launch traced here: 64.9 us
  waiting for transfers between devices  26.6 us (41%)
  starting transfers between devices  25.1 us (38%)
  Pallas kernels  8.62 us (13%)
  other arithmetic  2.02 us (3%)
  between operations  1.3 us (2%)
  local copies, waits for them, and re-layouts  1.21 us (2%)
    ppermute x22, waiting for transfers between devices, swap(): lax.ppermute(value, axis, [(i, i ^ bit) for i in range(lax.axis_size(axis...  24.9 us
    ppermute x22, starting transfers between devices, swap(): lax.ppermute(value, axis, [(i, i ^ bit) for i in range(lax.axis_size(axis...  20.9 us
    ppermute x2, starting transfers between devices, swap_outer(): return lax.ppermute(edge, axis, pairs + [(j, i) for i, j in pairs])  4.21 us
    pallas_call x1, Pallas kernels, conv_back(): pl.pallas_call(conv_back_kernel, out_shape=jax.ShapeDtypeStruct(misfit.sh...  1.93 us
    pallas_call x1, Pallas kernels, forward(): pl.pallas_call(forward_kernel, in_specs=[pl.BlockSpec(memory_space=pltpu....  1.81 us
    ppermute x2, waiting for transfers between devices, swap_outer(): return lax.ppermute(edge, axis, pairs + [(j, i) for i, j in pairs])  1.68 us
    pallas_call x1, Pallas kernels, assemble(): pl.pallas_call(assemble_kernel, grid=(2,), in_specs=[pl.BlockSpec(memory_...  1.44 us
    pallas_call x1, Pallas kernels, conv_norm(): pl.pallas_call(conv_norm_kernel, out_shape=(jax.ShapeDtypeStruct((cells,...  1.42 us
  transfers between devices with their start and end apart: 24, of which 12 were waited for; matrix products, arithmetic and copies ran while one was open for 2% of the time, Pallas kernels for 7%

profile of v5, /device:TPU:0, one launch (start us, length us, event | category | flops | bytes accessed | tf_op | source)
XLA Modules:
  0.0 64.9 jit_solution(6010297277009144187)
XLA Ops:
  0.7 0.8 %broadcast_select_fusion.13 = (bf16[2,4,3,256]{3,2,1,0:T(4,128)(2,1)S(1)}, bf16[2,4,3,256]{3,2,1,0:T(4,128)(2,1)S(1)}) fusion(pred[]{:T(512)S(6)} %eq.70, bf16[2,4,32,256]{3,2,1,0:T(8,128)(2,1)} %param.7), kind=kLoop, calls=%fused_computation.63 | loop fusion | flops 12288 | bytes 49153 | tf_op jit(solution)/shard_map/jit(_where)/select_n | solution.py:25
  1.5 3.0 %collective-permute-start = (bf16[2,4,3,256]{3,2,1,0:T(4,128)(2,1)S(1)}, bf16[2,4,3,256]{3,2,1,0:T(4,128)(2,1)S(1)}, u32[]{:S(2)}, u32[]{:S(2)}) collective-permute-start(bf16[2,4,3,256]{3,2,1,0:T(4,128)(2,1)S(1)} %get-tuple-element.81), channel_id=1, source_target_pairs={{0,1},{1,0},{2,3},{3,2},{4,5},{5,4},{6,7},{7,6},{8,9},{9,8},{10,11... | collective-permute-start | bytes 36872 | tf_op jit(solution)/shard_map/ppermute | solution.py:18
  4.5 3.5 %collective-permute-start.1 = (bf16[2,4,3,256]{3,2,1,0:T(4,128)(2,1)S(1)}, bf16[2,4,3,256]{3,2,1,0:T(4,128)(2,1)S(1)}, u32[]{:S(2)}, u32[]{:S(2)}) collective-permute-start(bf16[2,4,3,256]{3,2,1,0:T(4,128)(2,1)S(1)} %get-tuple-element.82), channel_id=1, source_target_pairs={{1,2},{3,4},{5,6},{7,0},{2,1},{4,3},{6,5},{0,7},{9,10},{11,12},{13... | collective-permute-start | bytes 36872 | tf_op jit(solution)/shard_map/ppermute | solution.py:33
  8.1 0.7 %copy-done.6 = f32[256]{0:T(256)S(1)} copy-done((f32[256]{0:T(256)S(1)}, f32[256]{0:T(256)}, u32[]{:S(2)}) %copy-start.6) | copy-done | bytes 1048
  9.3 1.7 %collective-permute-done.1 = bf16[2,4,3,256]{3,2,1,0:T(4,128)(2,1)S(1)} collective-permute-done((bf16[2,4,3,256]{3,2,1,0:T(4,128)(2,1)S(1)}, bf16[2,4,3,256]{3,2,1,0:T(4,128)(2,1)S(1)}, u32[]{:S(2)}, u32[]{:S(2)}) %collective-permute-start.1) | collective-permute-done | bytes 12320 | tf_op jit(solution)/shard_map/ppermute | solution.py:33
  11.1 0.7 %collective-permute-start.3 = (bf16[2,3,38,256]{3,2,1,0:T(8,128)(2,1)S(1)}, bf16[2,3,38,256]{3,2,1,0:T(8,128)(2,1)S(1)}, u32[]{:S(2)}, u32[]{:S(2)}) collective-permute-start(bf16[2,3,38,256]{3,2,1,0:T(8,128)(2,1)S(1)} %get-tuple-element.74), channel_id=1, source_target_pairs={{8,16},{16,8},{9,17},{17,9},{10,18},{18,10},{11,19},{19,11},{12,20... | collective-permute-start | bytes 350216 | tf_op jit(solution)/shard_map/ppermute | solution.py:33
  11.9 3.4 %collective-permute-start.5 = (bf16[2,1,4,16,256]{4,3,2,0,1:T(8,128)(2,1)S(1)}, bf16[2,1,4,16,256]{4,3,2,0,1:T(8,128)(2,1)S(1)}, u32[]{:S(2)}, u32[]{:S(2)}) collective-permute-start(bf16[2,1,4,16,256]{4,3,2,0,1:T(8,128)(2,1)S(1)} %get-tuple-element.77), channel_id=1, source_target_pairs={{0,16},{8,24},{16,0},{24,8},{1,17},{9,25},{17,1},{25,9},{2,18},{10... | collective-permute-start | bytes 196616 | tf_op jit(solution)/shard_map/ppermute | solution.py:18
  15.4 1.4 %conv_norm.1 = (bf16[256,256]{1,0:T(8,128)(2,1)S(1)}, f32[256,256]{1,0:T(8,128)S(1)}, f32[256,1]{1,0:T(8,128)S(1)}) custom-call(bf16[2,10,38,256]{3,2,1,0:T(8,128)(2,1)S(1)} %pad_maximum_fusion.padded_ref, f32[51,256]{1,0:T(8,128)S(1)} %pad_maximum_fusion.8.params_ref), custom_call_target="tpu_custom_call" | custom-call | flops 6422528 | bytes 1048576 | tf_op jit(solution)/shard_map/conv_norm/pallas_call | solution.py:252
  16.9 2.5 %collective-permute-done.5 = bf16[2,1,4,16,256]{4,3,2,0,1:T(8,128)(2,1)S(1)} collective-permute-done((bf16[2,1,4,16,256]{4,3,2,0,1:T(8,128)(2,1)S(1)}, bf16[2,1,4,16,256]{4,3,2,0,1:T(8,128)(2,1)S(1)}, u32[]{:S(2)}, u32[]{:S(2)}) %collective-permute-start.5) | collective-permute-done | bytes 65568 | tf_op jit(solution)/shard_map/ppermute | solution.py:18
  19.5 1.8 %forward.1 = (f32[256,1024]{1,0:T(8,128)S(1)}, f32[256,256]{1,0:T(8,128)S(1)}, bf16[256,256]{1,0:T(8,128)(2,1)S(1)}, bf16[512,256]{1,0:T(8,128)(2,1)S(1)}, f32[512,256]{1,0:T(8,128)S(1)}) custom-call(s32[1]{0:T(128)} %bitcast.side_ref, bf16[256,256]{1,0:T(8,128)(2,1)S(1)} %get-tuple-element.32.normed_ref, bf16[256,256]{1,0:T(8,128)(2,1)S(1)} %bitcast.30, ...), custom_call_target="tpu_custom_call" | custom-call | flops 402653184 | bytes 4194304 | tf_op jit(solution)/shard_map/forward/pallas_call | solution.py:460
  21.3 1.0 %backward.1 = (bf16[256,256]{1,0:T(8,128)(2,1)S(1)}, bf16[512,256]{1,0:T(8,128)(2,1)S(1)}, f32[512,256]{1,0:T(8,128)S(1)}) custom-call(s32[1]{0:T(128)} %bitcast.side_ref, f32[256,1024]{1,0:T(8,128)S(1)} %get-tuple-element.34.slope_ref, bf16[256,256]{1,0:T(8,128)(2,1)S(1)} %get-tuple-element.35.out_grad_ref, ...), custom_call_target="tpu_custom_call" | custom-call | flops 402653184 | bytes 4194304 | tf_op jit(solution)/shard_map/backward/pallas_call | solution.py:514
  22.3 0.7 %collective-permute-start.6 = (bf16[512,256]{1,0:T(8,128)(2,1)S(1)}, bf16[512,256]{1,0:T(8,128)(2,1)S(1)}, u32[]{:S(2)}, u32[]{:S(2)}) collective-permute-start(bf16[512,256]{1,0:T(8,128)(2,1)S(1)} %get-tuple-element.39), channel_id=1, source_target_pairs={{0,8},{8,0},{16,24},{24,16},{1,9},{9,1},{17,25},{25,17},{2,10},{10... | collective-permute-start | bytes 786440 | tf_op jit(solution)/shard_map/ppermute | solution.py:18
  23.6 1.0 %tap_sums.1 = f32[64,256]{1,0:T(8,128)S(1)} custom-call(bf16[2,10,38,256]{3,2,1,0:T(8,128)(2,1)S(1)} %pad_maximum_fusion.padded_ref, bf16[2,4,32,256]{3,2,1,0:T(8,128)(2,1)S(1)} %bitcast.27), custom_call_target="tpu_custom_call" | custom-call | flops 6422528 | bytes 1048576 | tf_op jit(solution)/shard_map/tap_sums/pallas_call | solution.py:335
  24.9 0.7 %collective-permute-start.8 = (bf16[480,256]{1,0:T(8,128)(2,1)S(1)}, bf16[480,256]{1,0:T(8,128)(2,1)S(1)}, u32[]{:S(2)}, u32[]{:S(2)}) collective-permute-start(bf16[480,256]{1,0:T(8,128)(2,1)S(1)} %pad_maximum_fusion.2), channel_id=1, source_target_pairs={{0,16},{8,24},{16,0},{24,8},{1,17},{9,25},{17,1},{25,9},{2,18},{10... | collective-permute-start | bytes 737288 | tf_op jit(solution)/shard_map/ppermute | solution.py:18
  25.6 4.8 %collective-permute-done.14 = bf16[256,256]{1,0:T(8,128)(2,1)S(1)} collective-permute-done((bf16[256,256]{1,0:T(8,128)(2,1)S(1)}, bf16[256,256]{1,0:T(8,128)(2,1)S(1)}, u32[]{:S(2)}, u32[]{:S(2)}) %collective-permute-start.14) | collective-permute-done | bytes 131104 | tf_op jit(solution)/shard_map/ppermute | solution.py:18
  30.4 0.9 %collective-permute-start.15 = (bf16[128,256]{1,0:T(8,128)(2,1)S(1)}, bf16[128,256]{1,0:T(8,128)(2,1)S(1)}, u32[]{:S(2)}, u32[]{:S(2)}) collective-permute-start(bf16[128,256]{1,0:T(8,128)(2,1)S(1)} %get-tuple-element.65), channel_id=1, source_target_pairs={{0,4},{1,5},{2,6},{3,7},{4,0},{5,1},{6,2},{7,3},{8,12},{9,13},{10,... | collective-permute-start | bytes 196616 | tf_op jit(solution)/shard_map/ppermute | solution.py:18
  31.3 1.8 %collective-permute-done.8 = bf16[480,256]{1,0:T(8,128)(2,1)S(1)} collective-permute-done((bf16[480,256]{1,0:T(8,128)(2,1)S(1)}, bf16[480,256]{1,0:T(8,128)(2,1)S(1)}, u32[]{:S(2)}, u32[]{:S(2)}) %collective-permute-start.8) | collective-permute-done | bytes 245792 | tf_op jit(solution)/shard_map/ppermute | solution.py:18
  33.9 2.4 %collective-permute-done.15 = bf16[128,256]{1,0:T(8,128)(2,1)S(1)} collective-permute-done((bf16[128,256]{1,0:T(8,128)(2,1)S(1)}, bf16[128,256]{1,0:T(8,128)(2,1)S(1)}, u32[]{:S(2)}, u32[]{:S(2)}) %collective-permute-start.15) | collective-permute-done | bytes 65568 | tf_op jit(solution)/shard_map/ppermute | solution.py:18
  36.3 0.6 collective-permute-start.16
  36.9 1.6 %collective-permute-done.10 = bf16[264,256]{1,0:T(8,128)(2,1)S(1)} collective-permute-done((bf16[264,256]{1,0:T(8,128)(2,1)S(1)}, bf16[264,256]{1,0:T(8,128)(2,1)S(1)}, u32[]{:S(2)}, u32[]{:S(2)}) %collective-permute-start.10) | collective-permute-done | bytes 135200 | tf_op jit(solution)/shard_map/ppermute | solution.py:18
  38.6 1.8 %collective-permute-start.11 = (f32[204,256]{1,0:T(8,128)S(1)}, f32[204,256]{1,0:T(8,128)S(1)}, u32[]{:S(2)}, u32[]{:S(2)}) collective-permute-start(f32[204,256]{1,0:T(8,128)S(1)} %pad_maximum_fusion.3), channel_id=1, source_target_pairs={{0,2},{1,3},{2,0},{3,1},{4,6},{5,7},{6,4},{7,5},{8,10},{9,11},{10,... | collective-permute-start | bytes 626696 | tf_op jit(solution)/shard_map/ppermute | solution.py:18
  40.4 0.9 %collective-permute-done.16 = f32[128,256]{1,0:T(8,128)S(1)} collective-permute-done((f32[128,256]{1,0:T(8,128)S(1)}, f32[128,256]{1,0:T(8,128)S(1)}, u32[]{:S(2)}, u32[]{:S(2)}) %collective-permute-start.16) | collective-permute-done | bytes 131104 | tf_op jit(solution)/shard_map/ppermute | solution.py:18
  41.3 0.8 %collective-permute-start.17 = (bf16[128,256]{1,0:T(8,128)(2,1)S(1)}, bf16[128,256]{1,0:T(8,128)(2,1)S(1)}, u32[]{:S(2)}, u32[]{:S(2)}) collective-permute-start(bf16[128,256]{1,0:T(8,128)(2,1)S(1)} %get-tuple-element.57), channel_id=1, source_target_pairs={{0,1},{1,0},{2,3},{3,2},{4,5},{5,4},{6,7},{7,6},{8,9},{9,8},{10,11... | collective-permute-start | bytes 196616 | tf_op jit(solution)/shard_map/ppermute | solution.py:18
  42.2 2.4 %collective-permute-done.11 = f32[204,256]{1,0:T(8,128)S(1)} collective-permute-done((f32[204,256]{1,0:T(8,128)S(1)}, f32[204,256]{1,0:T(8,128)S(1)}, u32[]{:S(2)}, u32[]{:S(2)}) %collective-permute-start.11) | collective-permute-done | bytes 208928 | tf_op jit(solution)/shard_map/ppermute | solution.py:18
  44.6 2.5 %collective-permute-start.12 = (bf16[204,256]{1,0:T(8,128)(2,1)S(1)}, bf16[204,256]{1,0:T(8,128)(2,1)S(1)}, u32[]{:S(2)}, u32[]{:S(2)}) collective-permute-start(bf16[204,256]{1,0:T(8,128)(2,1)S(1)} %pad_maximum_fusion.6), channel_id=1, source_target_pairs={{0,4},{1,5},{2,6},{3,7},{4,0},{5,1},{6,2},{7,3},{8,12},{9,13},{10,... | collective-permute-start | bytes 313352 | tf_op jit(solution)/shard_map/ppermute | solution.py:18
  47.7 2.6 %collective-permute-done.12 = bf16[204,256]{1,0:T(8,128)(2,1)S(1)} collective-permute-done((bf16[204,256]{1,0:T(8,128)(2,1)S(1)}, bf16[204,256]{1,0:T(8,128)(2,1)S(1)}, u32[]{:S(2)}, u32[]{:S(2)}) %collective-permute-start.12) | collective-permute-done | bytes 104480 | tf_op jit(solution)/shard_map/ppermute | solution.py:18
  50.5 3.3 %collective-permute-start.21 = (bf16[1,288,128]{2,1,0:T(8,128)(2,1)S(1)}, bf16[1,288,128]{2,1,0:T(8,128)(2,1)S(1)}, u32[]{:S(2)}, u32[]{:S(2)}) collective-permute-start(bf16[1,288,128]{2,1,0:T(8,128)(2,1)S(1)} %maximum_bitcast_fusion), channel_id=1, source_target_pairs={{0,1},{1,0},{2,3},{3,2},{4,5},{5,4},{6,7},{7,6},{8,9},{9,8},{10,11... | collective-permute-start | bytes 221192 | tf_op jit(solution)/shard_map/ppermute | solution.py:18
  53.9 2.2 %collective-permute-done.21 = bf16[1,288,128]{2,1,0:T(8,128)(2,1)S(1)} collective-permute-done((bf16[1,288,128]{2,1,0:T(8,128)(2,1)S(1)}, bf16[1,288,128]{2,1,0:T(8,128)(2,1)S(1)}, u32[]{:S(2)}, u32[]{:S(2)}) %collective-permute-start.21) | collective-permute-done | bytes 73760 | tf_op jit(solution)/shard_map/ppermute | solution.py:18
  57.1 1.9 %conv_back.1 = bf16[2,4,32,256]{3,2,1,0:T(8,128)(2,1)} custom-call(bf16[2,10,38,256]{3,2,1,0:T(8,128)(2,1)S(1)} %pad_maximum_fusion.1.padded_ref, f32[51,256]{1,0:T(8,128)S(1)} %pad_maximum_fusion.8.params_ref, f32[2,4,32,256]{3,2,1,0:T(8,128)S(1)} %bitcast.32), custom_call_target="tpu_custom_call" | custom-call | flops 6422528 | bytes 1048576 | tf_op jit(solution)/shard_map/conv_back/pallas_call | solution.py:287
  59.0 2.4 %collective-permute-done.22 = bf16[2,288,128]{2,1,0:T(8,128)(2,1)S(1)} collective-permute-done((bf16[2,288,128]{2,1,0:T(8,128)(2,1)S(1)}, bf16[2,288,128]{2,1,0:T(8,128)(2,1)S(1)}, u32[]{:S(2)}, u32[]{:S(2)}) %collective-permute-start.22) | collective-permute-done | bytes 147488 | tf_op jit(solution)/shard_map/ppermute | solution.py:18
  62.1 1.3 %collective-permute-done.20.out_got = bf16[4,128,256]{2,1,0:T(8,128)(2,1)S(1)} collective-permute-done((bf16[4,128,256]{2,1,0:T(8,128)(2,1)S(1)}, bf16[4,128,256]{2,1,0:T(8,128)(2,1)S(1)}, u32[]{:S(2)}, u32[]{:S(2)}) %collective-permute-start.20) | collective-permute-done | bytes 262176 | tf_op jit(solution)/shard_map/ppermute | solution.py:18
  63.4 1.4 %assemble.1 = (f32[1024,256]{1,0:T(8,128)}, f32[256,1024]{1,0:T(8,128)}, f32[7,7,256]{2,1,0:T(8,128)}) custom-call(s32[1]{0:T(128)} %bitcast.side_ref, bf16[4,128,256]{2,1,0:T(8,128)(2,1)S(1)} %maximum_select_fusion.1.out_mine, bf16[4,128,256]{2,1,0:T(8,128)(2,1)S(1)} %collective-permute-done.20.out_got, ...), custom_call_target="tpu_custom_call" | custom-call | bytes 3145728 | tf_op jit(solution)/shard_map/assemble/pallas_call | solution.py:387
  (91 shorter events, 4.9 us)
Async XLA Ops:
  0.6 7.4 %copy-start.4 = (f32[7,7,256]{2,1,0:T(8,128)S(1)}, f32[7,7,256]{2,1,0:T(8,128)}, u32[]{:S(2)}) copy-start(f32[7,7,256]{2,1,0:T(8,128)} %param.9) | copy-start | bytes 150532
  1.5 7.8 %collective-permute-start = (bf16[2,4,3,256]{3,2,1,0:T(4,128)(2,1)S(1)}, bf16[2,4,3,256]{3,2,1,0:T(4,128)(2,1)S(1)}, u32[]{:S(2)}, u32[]{:S(2)}) collective-permute-start(bf16[2,4,3,256]{3,2,1,0:T(4,128)(2,1)S(1)} %get-tuple-element.81), channel_id=1, source_target_pairs={{0,1},{1,0},{2,3},{3,2},{4,5},{5,4},{6,7},{7,6},{8,9},{9,8},{10,11... | collective-permute-start | bytes 36872 | tf_op jit(solution)/shard_map/ppermute | solution.py:18
  4.5 6.4 %collective-permute-start.1 = (bf16[2,4,3,256]{3,2,1,0:T(4,128)(2,1)S(1)}, bf16[2,4,3,256]{3,2,1,0:T(4,128)(2,1)S(1)}, u32[]{:S(2)}, u32[]{:S(2)}) collective-permute-start(bf16[2,4,3,256]{3,2,1,0:T(4,128)(2,1)S(1)} %get-tuple-element.82), channel_id=1, source_target_pairs={{1,2},{3,4},{5,6},{7,0},{2,1},{4,3},{6,5},{0,7},{9,10},{11,12},{13... | collective-permute-start | bytes 36872 | tf_op jit(solution)/shard_map/ppermute | solution.py:33
  8.0 0.9 %copy-start.3 = (bf16[2,16,8,256]{3,2,1,0:T(8,128)(2,1)S(1)}, bf16[2,16,8,256]{3,2,1,0:T(8,128)(2,1)}, u32[]{:S(2)}) copy-start(bf16[2,16,8,256]{3,2,1,0:T(8,128)(2,1)} %param.8) | copy-start | bytes 393220
  8.0 0.7 %copy-start.6 = (f32[256]{0:T(256)S(1)}, f32[256]{0:T(256)}, u32[]{:S(2)}) copy-start(f32[256]{0:T(256)} %param.10) | copy-start | bytes 3076
  8.1 0.7 %copy-start.5 = (f32[256]{0:T(256)S(1)}, f32[256]{0:T(256)}, u32[]{:S(2)}) copy-start(f32[256]{0:T(256)} %param.13) | copy-start | bytes 3076
  9.0 2.8 %collective-permute-start.4 = (bf16[2,2,4,8,256]{4,3,2,0,1:T(8,128)(2,1)S(1)}, bf16[2,2,4,8,256]{4,3,2,0,1:T(8,128)(2,1)S(1)}, u32[]{:S(2)}, u32[]{:S(2)}) collective-permute-start(bf16[2,2,4,8,256]{4,3,2,0,1:T(8,128)(2,1)S(1)} %bitcast.37), channel_id=1, source_target_pairs={{0,8},{8,0},{16,24},{24,16},{1,9},{9,1},{17,25},{25,17},{2,10},{10... | collective-permute-start | bytes 196616 | tf_op jit(solution)/shard_map/ppermute | solution.py:18
  9.1 1.8 %copy-start.2 = (bf16[2,4,32,256]{3,2,1,0:T(8,128)(2,1)S(1)}, bf16[2,4,32,256]{3,2,1,0:T(8,128)(2,1)}, u32[]{:S(2)}) copy-start(bf16[2,4,32,256]{3,2,1,0:T(8,128)(2,1)} %param.7) | copy-start | bytes 393220
  11.1 4.3 %collective-permute-start.2 = (bf16[2,3,38,256]{3,2,1,0:T(8,128)(2,1)S(1)}, bf16[2,3,38,256]{3,2,1,0:T(8,128)(2,1)S(1)}, u32[]{:S(2)}, u32[]{:S(2)}) collective-permute-start(bf16[2,3,38,256]{3,2,1,0:T(8,128)(2,1)S(1)} %get-tuple-element.73), channel_id=1, source_target_pairs={{0,8},{8,0},{16,24},{24,16},{1,9},{9,1},{17,25},{25,17},{2,10},{10... | collective-permute-start | bytes 350216 | tf_op jit(solution)/shard_map/ppermute | solution.py:18
  11.1 4.2 %collective-permute-start.3 = (bf16[2,3,38,256]{3,2,1,0:T(8,128)(2,1)S(1)}, bf16[2,3,38,256]{3,2,1,0:T(8,128)(2,1)S(1)}, u32[]{:S(2)}, u32[]{:S(2)}) collective-permute-start(bf16[2,3,38,256]{3,2,1,0:T(8,128)(2,1)S(1)} %get-tuple-element.74), channel_id=1, source_target_pairs={{8,16},{16,8},{9,17},{17,9},{10,18},{18,10},{11,19},{19,11},{12,20... | collective-permute-start | bytes 350216 | tf_op jit(solution)/shard_map/ppermute | solution.py:33
  11.9 7.5 %collective-permute-start.5 = (bf16[2,1,4,16,256]{4,3,2,0,1:T(8,128)(2,1)S(1)}, bf16[2,1,4,16,256]{4,3,2,0,1:T(8,128)(2,1)S(1)}, u32[]{:S(2)}, u32[]{:S(2)}) collective-permute-start(bf16[2,1,4,16,256]{4,3,2,0,1:T(8,128)(2,1)S(1)} %get-tuple-element.77), channel_id=1, source_target_pairs={{0,16},{8,24},{16,0},{24,8},{1,17},{9,25},{17,1},{25,9},{2,18},{10... | collective-permute-start | bytes 196616 | tf_op jit(solution)/shard_map/ppermute | solution.py:18
  15.3 4.1 %copy-start.1 = (bf16[1024,256]{1,0:T(8,128)(2,1)S(1)}, bf16[1024,256]{1,0:T(8,128)(2,1)}, u32[]{:S(2)}) copy-start(bf16[1024,256]{1,0:T(8,128)(2,1)} %w_out_ref.3) | copy-start | bytes 1572868
  15.4 4.0 %copy-start = (bf16[256,1024]{1,0:T(8,128)(2,1)S(1)}, bf16[256,1024]{1,0:T(8,128)(2,1)}, u32[]{:S(2)}) copy-start(bf16[256,1024]{1,0:T(8,128)(2,1)} %w_in_ref.3) | copy-start | bytes 1572868
  22.3 2.5 %collective-permute-start.6 = (bf16[512,256]{1,0:T(8,128)(2,1)S(1)}, bf16[512,256]{1,0:T(8,128)(2,1)S(1)}, u32[]{:S(2)}, u32[]{:S(2)}) collective-permute-start(bf16[512,256]{1,0:T(8,128)(2,1)S(1)} %get-tuple-element.39), channel_id=1, source_target_pairs={{0,8},{8,0},{16,24},{24,16},{1,9},{9,1},{17,25},{25,17},{2,10},{10... | collective-permute-start | bytes 786440 | tf_op jit(solution)/shard_map/ppermute | solution.py:18
  23.0 1.6 %collective-permute-start.13 = (bf16[512,256]{1,0:T(8,128)(2,1)S(1)}, bf16[512,256]{1,0:T(8,128)(2,1)S(1)}, u32[]{:S(2)}, u32[]{:S(2)}) collective-permute-start(bf16[512,256]{1,0:T(8,128)(2,1)S(1)} %get-tuple-element.43), channel_id=1, source_target_pairs={{0,8},{8,0},{16,24},{24,16},{1,9},{9,1},{17,25},{25,17},{2,10},{10... | collective-permute-start | bytes 786440 | tf_op jit(solution)/shard_map/ppermute | solution.py:18
  23.1 1.8 %collective-permute-start.7 = (bf16[2,3,32,256]{3,2,1,0:T(8,128)(2,1)S(1)}, bf16[2,3,32,256]{3,2,1,0:T(8,128)(2,1)S(1)}, u32[]{:S(2)}, u32[]{:S(2)}) collective-permute-start(bf16[2,3,32,256]{3,2,1,0:T(8,128)(2,1)S(1)} %get-tuple-element.75), channel_id=1, source_target_pairs={{0,8},{8,0},{16,24},{24,16},{1,9},{9,1},{17,25},{25,17},{2,10},{10... | collective-permute-start | bytes 294920 | tf_op jit(solution)/shard_map/ppermute | solution.py:18
  24.7 5.7 %collective-permute-start.14 = (bf16[256,256]{1,0:T(8,128)(2,1)S(1)}, bf16[256,256]{1,0:T(8,128)(2,1)S(1)}, u32[]{:S(2)}, u32[]{:S(2)}) collective-permute-start(bf16[256,256]{1,0:T(8,128)(2,1)S(1)} %get-tuple-element.61), channel_id=1, source_target_pairs={{0,2},{1,3},{2,0},{3,1},{4,6},{5,7},{6,4},{7,5},{8,10},{9,11},{10,... | collective-permute-start | bytes 393224 | tf_op jit(solution)/shard_map/ppermute | solution.py:18
  24.9 8.2 %collective-permute-start.8 = (bf16[480,256]{1,0:T(8,128)(2,1)S(1)}, bf16[480,256]{1,0:T(8,128)(2,1)S(1)}, u32[]{:S(2)}, u32[]{:S(2)}) collective-permute-start(bf16[480,256]{1,0:T(8,128)(2,1)S(1)} %pad_maximum_fusion.2), channel_id=1, source_target_pairs={{0,16},{8,24},{16,0},{24,8},{1,17},{9,25},{17,1},{25,9},{2,18},{10... | collective-permute-start | bytes 737288 | tf_op jit(solution)/shard_map/ppermute | solution.py:18
  25.6 7.5 %collective-permute-start.9 = (bf16[2,3,32,256]{3,2,1,0:T(8,128)(2,1)S(1)}, bf16[2,3,32,256]{3,2,1,0:T(8,128)(2,1)S(1)}, u32[]{:S(2)}, u32[]{:S(2)}) collective-permute-start(bf16[2,3,32,256]{3,2,1,0:T(8,128)(2,1)S(1)} %get-tuple-element.76), channel_id=1, source_target_pairs={{0,8},{8,0},{16,24},{24,16},{1,9},{9,1},{17,25},{25,17},{2,10},{10... | collective-permute-start | bytes 294920 | tf_op jit(solution)/shard_map/ppermute | solution.py:18
  30.4 5.8 %collective-permute-start.15 = (bf16[128,256]{1,0:T(8,128)(2,1)S(1)}, bf16[128,256]{1,0:T(8,128)(2,1)S(1)}, u32[]{:S(2)}, u32[]{:S(2)}) collective-permute-start(bf16[128,256]{1,0:T(8,128)(2,1)S(1)} %get-tuple-element.65), channel_id=1, source_target_pairs={{0,4},{1,5},{2,6},{3,7},{4,0},{5,1},{6,2},{7,3},{8,12},{9,13},{10,... | collective-permute-start | bytes 196616 | tf_op jit(solution)/shard_map/ppermute | solution.py:18
  33.5 5.1 %collective-permute-start.10 = (bf16[264,256]{1,0:T(8,128)(2,1)S(1)}, bf16[264,256]{1,0:T(8,128)(2,1)S(1)}, u32[]{:S(2)}, u32[]{:S(2)}) collective-permute-start(bf16[264,256]{1,0:T(8,128)(2,1)S(1)} %pad_maximum_fusion.5), channel_id=1, source_target_pairs={{0,1},{1,0},{2,3},{3,2},{4,5},{5,4},{6,7},{7,6},{8,9},{9,8},{10,11... | collective-permute-start | bytes 405512 | tf_op jit(solution)/shard_map/ppermute | solution.py:18
  36.3 5.0 %collective-permute-start.16 = (f32[128,256]{1,0:T(8,128)S(1)}, f32[128,256]{1,0:T(8,128)S(1)}, u32[]{:S(2)}, u32[]{:S(2)}) collective-permute-start(f32[128,256]{1,0:T(8,128)S(1)} %convert_add_fusion.2), channel_id=1, source_target_pairs={{0,16},{8,24},{16,0},{24,8},{1,17},{9,25},{17,1},{25,9},{2,18},{10... | collective-permute-start | bytes 393224 | tf_op jit(solution)/shard_map/ppermute | solution.py:18
  38.6 5.9 %collective-permute-start.11 = (f32[204,256]{1,0:T(8,128)S(1)}, f32[204,256]{1,0:T(8,128)S(1)}, u32[]{:S(2)}, u32[]{:S(2)}) collective-permute-start(f32[204,256]{1,0:T(8,128)S(1)} %pad_maximum_fusion.3), channel_id=1, source_target_pairs={{0,2},{1,3},{2,0},{3,1},{4,6},{5,7},{6,4},{7,5},{8,10},{9,11},{10,... | collective-permute-start | bytes 626696 | tf_op jit(solution)/shard_map/ppermute | solution.py:18
  41.3 5.8 %collective-permute-start.17 = (bf16[128,256]{1,0:T(8,128)(2,1)S(1)}, bf16[128,256]{1,0:T(8,128)(2,1)S(1)}, u32[]{:S(2)}, u32[]{:S(2)}) collective-permute-start(bf16[128,256]{1,0:T(8,128)(2,1)S(1)} %get-tuple-element.57), channel_id=1, source_target_pairs={{0,1},{1,0},{2,3},{3,2},{4,5},{5,4},{6,7},{7,6},{8,9},{9,8},{10,11... | collective-permute-start | bytes 196616 | tf_op jit(solution)/shard_map/ppermute | solution.py:18
  44.6 5.7 %collective-permute-start.12 = (bf16[204,256]{1,0:T(8,128)(2,1)S(1)}, bf16[204,256]{1,0:T(8,128)(2,1)S(1)}, u32[]{:S(2)}, u32[]{:S(2)}) collective-permute-start(bf16[204,256]{1,0:T(8,128)(2,1)S(1)} %pad_maximum_fusion.6), channel_id=1, source_target_pairs={{0,4},{1,5},{2,6},{3,7},{4,0},{5,1},{6,2},{7,3},{8,12},{9,13},{10,... | collective-permute-start | bytes 313352 | tf_op jit(solution)/shard_map/ppermute | solution.py:18
  47.1 6.7 %collective-permute-start.18 = (bf16[1,128,256]{2,1,0:T(8,128)(2,1)S(1)}, bf16[1,128,256]{2,1,0:T(8,128)(2,1)S(1)}, u32[]{:S(2)}, u32[]{:S(2)}) collective-permute-start(bf16[1,128,256]{2,1,0:T(8,128)(2,1)S(1)} %fusion.1), channel_id=1, source_target_pairs={{0,4},{1,5},{2,6},{3,7},{4,0},{5,1},{6,2},{7,3},{8,12},{9,13},{10,... | collective-permute-start | bytes 196616 | tf_op jit(solution)/shard_map/ppermute | solution.py:18
  50.5 5.7 %collective-permute-start.21 = (bf16[1,288,128]{2,1,0:T(8,128)(2,1)S(1)}, bf16[1,288,128]{2,1,0:T(8,128)(2,1)S(1)}, u32[]{:S(2)}, u32[]{:S(2)}) collective-permute-start(bf16[1,288,128]{2,1,0:T(8,128)(2,1)S(1)} %maximum_bitcast_fusion), channel_id=1, source_target_pairs={{0,1},{1,0},{2,3},{3,2},{4,5},{5,4},{6,7},{7,6},{8,9},{9,8},{10,11... | collective-permute-start | bytes 221192 | tf_op jit(solution)/shard_map/ppermute | solution.py:18
  53.8 7.7 %collective-permute-start.19 = (bf16[2,128,256]{2,1,0:T(8,128)(2,1)S(1)}, bf16[2,128,256]{2,1,0:T(8,128)(2,1)S(1)}, u32[]{:S(2)}, u32[]{:S(2)}) collective-permute-start(bf16[2,128,256]{2,1,0:T(8,128)(2,1)S(1)} %maximum_select_fusion.5), channel_id=1, source_target_pairs={{0,2},{1,3},{2,0},{3,1},{4,6},{5,7},{6,4},{7,5},{8,10},{9,11},{10,... | collective-permute-start | bytes 393224 | tf_op jit(solution)/shard_map/ppermute | solution.py:18
  56.2 5.2 %collective-permute-start.22 = (bf16[2,288,128]{2,1,0:T(8,128)(2,1)S(1)}, bf16[2,288,128]{2,1,0:T(8,128)(2,1)S(1)}, u32[]{:S(2)}, u32[]{:S(2)}) collective-permute-start(bf16[2,288,128]{2,1,0:T(8,128)(2,1)S(1)} %maximum_select_fusion.2), channel_id=1, source_target_pairs={{0,16},{8,24},{16,0},{24,8},{1,17},{9,25},{17,1},{25,9},{2,18},{10... | collective-permute-start | bytes 442376 | tf_op jit(solution)/shard_map/ppermute | solution.py:18
  61.4 2.0 %collective-permute-start.23 = (bf16[4,288,128]{2,1,0:T(8,128)(2,1)S(1)}, bf16[4,288,128]{2,1,0:T(8,128)(2,1)S(1)}, u32[]{:S(2)}, u32[]{:S(2)}) collective-permute-start(bf16[4,288,128]{2,1,0:T(8,128)(2,1)S(1)} %maximum_select_fusion.in_mine), channel_id=1, source_target_pairs={{0,8},{8,0},{16,24},{24,16},{1,9},{9,1},{17,25},{25,17},{2,10},{10... | collective-permute-start | bytes 884744 | tf_op jit(solution)/shard_map/ppermute | solution.py:18
  61.5 1.9 %collective-permute-start.20 = (bf16[4,128,256]{2,1,0:T(8,128)(2,1)S(1)}, bf16[4,128,256]{2,1,0:T(8,128)(2,1)S(1)}, u32[]{:S(2)}, u32[]{:S(2)}) collective-permute-start(bf16[4,128,256]{2,1,0:T(8,128)(2,1)S(1)} %maximum_select_fusion.1.out_mine), channel_id=1, source_target_pairs={{0,8},{8,0},{16,24},{24,16},{1,9},{9,1},{17,25},{25,17},{2,10},{10... | collective-permute-start | bytes 786440 | tf_op jit(solution)/shard_map/ppermute | solution.py:18

commit v6 on v5

--- a/solution.py
+++ b/solution.py
@@ -1,3 +1,5 @@
+import functools
+
 import jax
 import jax.numpy as jnp
 from jax import lax
@@ -28,9 +30,14 @@
 def swap_outer(edge, axis, periodic):
     count = lax.axis_size(axis)
     pairs = [(i, (i + 1) % count) for i in range(1, count, 2)]
-    if not periodic:
-        pairs = [(i, j) for i, j in pairs if j]
-    return lax.ppermute(edge, axis, pairs + [(j, i) for i, j in pairs])
+    got = lax.ppermute(edge, axis, pairs + [(j, i) for i, j in pairs])
+    return got if periodic else inside(got, axis)
+
+
+def inside(edge, axis):
+    index = lax.axis_index(axis)
+    at_end = (index == 0) | (index == lax.axis_size(axis) - 1)
+    return jnp.where(at_end, jnp.zeros_like(edge), edge)
 
 
 def with_edges(block, from_inner, from_outer, axis, dim):
@@ -49,19 +56,17 @@
 
 def to_bands(teacher, axis):
     batch_size, rows, cols, channel_count = teacher.shape
-    count = lax.axis_size(axis)
-    band = rows // count
-    state = teacher.reshape(batch_size, count, band, cols, channel_count)
-    for bit in bits_of(axis):
+    band = rows // lax.axis_size(axis)
+    state = teacher.reshape(batch_size, -1, band, 1, cols, channel_count)
+    for bit in bits_of(axis)[::-1]:
         upper = (lax.axis_index(axis) // bit) % 2
-        state = state.reshape(batch_size, -1, 2, band, state.shape[3], channel_count)
-        mine = lax.dynamic_index_in_dim(state, upper, axis=2, keepdims=False)
-        got = swap(lax.dynamic_index_in_dim(state, 1 - upper, axis=2, keepdims=False), axis, bit)
+        state = state.reshape(batch_size, 2, -1, *state.shape[2:])
+        mine = lax.dynamic_index_in_dim(state, upper, axis=1, keepdims=False)
+        got = swap(lax.dynamic_index_in_dim(state, 1 - upper, axis=1, keepdims=False), axis, bit)
         state = jnp.where(
-            upper == 1,
-            jnp.concatenate([got, mine], axis=3),
-            jnp.concatenate([mine, got], axis=3),
+            upper == 1, jnp.stack([got, mine], axis=4), jnp.stack([mine, got], axis=4)
         )
+        state = state.reshape(batch_size, -1, band, 2 * state.shape[3], cols, channel_count)
     return state.reshape(batch_size, band, -1, channel_count)
 
 
@@ -100,11 +105,11 @@
         give = give + [flat_rows(rider).astype(sent_as)]
         counts = counts + [give[-1].shape[0]]
     sent = jnp.concatenate(give, axis=0) if len(give) > 1 else give[0]
-    got = swap(sent, axis, bit)
-    got = split_rows(got, counts) if len(give) > 1 else [got]
+    raw = swap(sent, axis, bit)
+    got = split_rows(raw, counts) if len(give) > 1 else [raw]
     parts = [[k, g] for k, g in zip(keep, got)]
     ridden = None if rider is None else got[-1].astype(rider.dtype).reshape(rider.shape)
-    return parts, ridden, sent
+    return parts, ridden, sent, raw
 
 
 def split_rows(value, counts):
@@ -115,12 +120,37 @@
     return pieces
 
 
-def gather_halves(chunks, axis, bit):
+def in_order(chunks, got, axis, bit):
     upper = (lax.axis_index(axis) // bit) % 2
-    got = swap(chunks, axis, bit)
     return jnp.where(
         upper == 1, jnp.concatenate([got, chunks]), jnp.concatenate([chunks, got])
     )
+
+
+def gather_halves(chunks, axis, bit):
+    return in_order(chunks, swap(chunks, axis, bit), axis, bit)
+
+
+def join_kernel(place_ref, mine, got, _, out_ref):
+    count = mine.shape[0]
+    place = place_ref[0]
+    out_ref[pl.ds(place * count, count)] = mine[...]
+    out_ref[pl.ds((1 - place) * count, count)] = got[...]
+
+
+def join(place, mine, got, earlier):
+    shape = (2 * mine.shape[0],) + mine.shape[1:]
+    return pl.pallas_call(
+        join_kernel,
+        in_specs=[pl.BlockSpec(memory_space=pltpu.SMEM)]
+        + vmem_specs(2)
+        + [pl.BlockSpec(memory_space=pl.ANY)],
+        out_specs=pl.BlockSpec(memory_space=pltpu.VMEM),
+        out_shape=jax.ShapeDtypeStruct(shape, mine.dtype),
+        compiler_params=pltpu.CompilerParams(vmem_limit_bytes=4 << 20),
+        cost_estimate=pl.CostEstimate(flops=0, bytes_accessed=1 << 18, transcendentals=0),
+        name="join",
+    )(place, mine, got, earlier)
 
 
 def carried(axis, bit):
@@ -141,17 +171,43 @@
     return jnp.bfloat16 if stage in halved or stage == stages[-1] else jnp.float32
 
 
+def finish_columns_kernel(divisor, main_ref, taps_ref, got_ref, out_ref):
+    rows, channel_count = main_ref.shape
+    tap_rows = taps_ref.shape[0]
+    main = main_ref[...] + got_ref[:rows].astype(jnp.float32)
+    out_ref[0, :channel_count] = (main / divisor).T.astype(jnp.bfloat16)
+    taps = taps_ref[...] + got_ref[rows : rows + tap_rows].astype(jnp.float32)
+    taps = (taps / divisor).astype(jnp.bfloat16)
+    for k in range(channel_count // rows):
+        at = channel_count + k * tap_rows
+        out_ref[0, at : at + tap_rows] = taps[:, k * rows : (k + 1) * rows]
+
+
+def finish_columns(main, taps, got, divisor):
+    rows, channel_count = main.shape
+    height = channel_count + channel_count // rows * taps.shape[0]
+    return pl.pallas_call(
+        functools.partial(finish_columns_kernel, float(divisor)),
+        out_shape=jax.ShapeDtypeStruct((1, height, rows), jnp.bfloat16),
+        in_specs=vmem_specs(3),
+        out_specs=pl.BlockSpec(memory_space=pltpu.VMEM),
+        compiler_params=pltpu.CompilerParams(vmem_limit_bytes=4 << 20),
+        cost_estimate=pl.CostEstimate(flops=main.size, bytes_accessed=1 << 18, transcendentals=0),
+        name="finish_columns",
+    )(main, taps, got)
+
+
 def sum_over_mesh(lead, trail, divisor, block, inner, outer, width):
     (lead_stages, lead_halved), (stages, halved) = sum_stages()
     dim_of = {"lat": 1, "lon": 2}
     for k, (axis, bit) in enumerate(stages):
         dim = dim_of[axis]
         stage = lead_stages[k]
-        lead, _, _ = exchange(
+        lead, _, _, _ = exchange(
             lead, *stage, stage in lead_halved, sent_type(stage, lead_stages, lead_halved)
         )
         rider = jnp.stack(edges(block, axis, dim, width)) if bit == 1 else outer
-        trail, got, sent = exchange(
+        trail, got, sent, raw = exchange(
             trail, axis, bit, (axis, bit) in halved, sent_type((axis, bit), stages, halved), rider
         )
         lead = after(lead, sent)
@@ -161,21 +217,10 @@
             outer = jnp.where(carried(axis, bit), got, outer)
         if k + 1 == len(stages) or stages[k + 1][0] != axis:
             if axis == "lat":
-                index = lax.axis_index(axis)
-                at_end = (index == 0) | (index == lax.axis_size(axis) - 1)
-                outer = jnp.where(at_end, jnp.zeros_like(outer), outer)
+                outer = inside(outer, axis)
             block = with_edges(block, inner, outer, axis, dim)
     lead = [(total_of(terms) / divisor).astype(jnp.bfloat16) for terms in lead]
-    trail = [(total_of(terms) / divisor).astype(jnp.bfloat16) for terms in trail]
-    return lead, trail, block
-
-
-def gather_sums(lead, trail):
-    (_, lead_halved), (_, halved) = sum_stages()
-    for lead_stage, stage in zip(lead_halved[::-1], halved[::-1]):
-        lead = gather_halves(lead, *lead_stage)
-        trail = gather_halves(trail, *stage)
-    return lead, trail
+    return lead, finish_columns(trail[0][0], trail[1][0], raw, divisor), block
 
 
 lane_count = 128
@@ -260,13 +305,14 @@
             pltpu.VMEM((groups, batch_size, pad_rows, round_up(pad_cols, 8), lane_count), jnp.float32),
             pltpu.VMEM((groups, cells, lane_count), jnp.float32),
         ],
-        compiler_params=pltpu.CompilerParams(vmem_limit_bytes=16 << 20),
+        compiler_params=pltpu.CompilerParams(vmem_limit_bytes=6 << 20),
         cost_estimate=pl.CostEstimate(flops=2 * 49 * cells * channel_count, bytes_accessed=1 << 20, transcendentals=0),
         name="conv_norm",
     )(padded, params)
 
 
-def conv_back_kernel(padded_ref, params_ref, misfit_ref, out_ref, wide):
+def conv_back_kernel(padded_ref, params_ref, misfit_ref, _, out_ref, mark_ref, wide):
+    mark_ref[...] = jnp.zeros_like(mark_ref)
     batch_size, tile_rows, tile_cols, channel_count = out_ref.shape
     spread(padded_ref, wide)
     for group in range(wide.shape[0]):
@@ -281,19 +327,21 @@
         lax.fori_loop(0, batch_size, one, 0)
 
 
-def conv_back(padded, params, misfit):
+def conv_back(padded, params, misfit, earlier):
     batch_size, pad_rows, pad_cols, channel_count = padded.shape
     groups = channel_count // lane_count
     return pl.pallas_call(
         conv_back_kernel,
-        out_shape=jax.ShapeDtypeStruct(misfit.shape, jnp.bfloat16),
+        out_shape=(jax.ShapeDtypeStruct(misfit.shape, jnp.bfloat16), mark_shape),
+        in_specs=vmem_specs(3) + [pl.BlockSpec(memory_space=pl.ANY)],
+        out_specs=vmem_specs(2),
         scratch_shapes=[
             pltpu.VMEM((groups, batch_size, pad_rows, round_up(pad_cols, 8), lane_count), jnp.float32),
         ],
-        compiler_params=pltpu.CompilerParams(vmem_limit_bytes=16 << 20),
+        compiler_params=pltpu.CompilerParams(vmem_limit_bytes=6 << 20),
         cost_estimate=pl.CostEstimate(flops=2 * 49 * misfit.size, bytes_accessed=1 << 20, transcendentals=0),
         name="conv_back",
-    )(padded, params, misfit)
+    )(padded, params, misfit, earlier)
 
 
 def tap_sums_kernel(padded_ref, grad_ref, out_ref, wide, partial):
@@ -339,36 +387,39 @@
             pltpu.VMEM((groups, batch_size, pad_rows, round_up(pad_cols, 8), lane_count), jnp.float32),
             pltpu.VMEM((groups, batch_size, kernel_size * kernel_size * 8, lane_count), jnp.float32),
         ],
-        compiler_params=pltpu.CompilerParams(vmem_limit_bytes=16 << 20),
+        compiler_params=pltpu.CompilerParams(vmem_limit_bytes=6 << 20),
         cost_estimate=pl.CostEstimate(flops=2 * 49 * grads.size, bytes_accessed=1 << 20, transcendentals=0),
         name="tap_sums",
     )(padded, grads)
 
 
-def assemble_kernel(side_ref, out_mine, out_got, in_mine, in_got, out_ref, in_ref, taps_ref):
+def assemble_rows_kernel(side_ref, mine, got, _, out_ref, mark_ref):
+    mark_ref[...] = jnp.zeros_like(mark_ref)
+    own = pl.program_id(0) == side_ref[0]
+    count, rows, _ = mine.shape
+    for k in range(count):
+        chunk = jnp.where(own, mine[k].astype(jnp.float32), got[k].astype(jnp.float32))
+        out_ref[k * rows : (k + 1) * rows, :] = chunk
+
+
+def assemble_columns_kernel(side_ref, mine, got, out_ref, taps_ref):
     half = pl.program_id(0)
     own = half == side_ref[0]
-    count, rows, _ = out_mine.shape
-    channel_count = in_ref.shape[0]
-
-    def write(out_chunks, in_chunks):
-        for k in range(count):
-            out_ref[k * rows : (k + 1) * rows, :] = out_chunks[k].astype(jnp.float32)
-            in_ref[:, k * rows : (k + 1) * rows] = in_chunks[k, :channel_count].astype(jnp.float32)
-
-    @pl.when(own)
-    def _():
-        write(out_mine, in_mine)
-
-    @pl.when(jnp.logical_not(own))
-    def _():
-        write(out_got, in_got)
+    count, _, cols = mine.shape
+    channel_count = out_ref.shape[0]
+    for k in range(count):
+        chunk = jnp.where(
+            own,
+            mine[k, :channel_count].astype(jnp.float32),
+            got[k, :channel_count].astype(jnp.float32),
+        )
+        out_ref[:, k * cols : (k + 1) * cols] = chunk
 
     @pl.when(half == 0)
     def _():
-        tail = slice(channel_count, in_mine.shape[1])
-        chunks = in_mine[:, tail].astype(jnp.float32) + in_got[:, tail].astype(jnp.float32)
-        groups = channel_count // in_mine.shape[2]
+        tail = slice(channel_count, mine.shape[1])
+        chunks = mine[:, tail].astype(jnp.float32) + got[:, tail].astype(jnp.float32)
+        groups = channel_count // cols
         step = chunks.shape[1] // groups
         pieces = [
             jnp.concatenate([chunks[k, n * step : (n + 1) * step] for n in range(groups)], axis=1)
@@ -380,28 +431,46 @@
             taps_ref[p] = taps[p * width : (p + 1) * width]
 
 
-def assemble(side, out_mine, out_got, in_mine, in_got, channel_count, kernel_size):
-    count, rows, _ = out_mine.shape
-    whole = lambda value: pl.BlockSpec(value.shape, lambda i: (0,) * value.ndim)
-    operands = (out_mine, out_got, in_mine, in_got)
-    return pl.pallas_call(
-        assemble_kernel,
+mark_shape = jax.ShapeDtypeStruct((8, 128), jnp.float32)
+
+
+def whole_block(value):
+    return pl.BlockSpec(value.shape, lambda i: (0,) * len(value.shape))
+
+
+def assemble_rows(side, mine, got, earlier):
+    count, rows, cols = mine.shape
+    return pl.pallas_call(
+        assemble_rows_kernel,
         grid=(2,),
-        in_specs=[pl.BlockSpec(memory_space=pltpu.SMEM)] + [whole(v) for v in operands],
+        in_specs=[pl.BlockSpec(memory_space=pltpu.SMEM), whole_block(mine), whole_block(got)]
+        + [pl.BlockSpec(memory_space=pl.ANY)],
+        out_specs=(pl.BlockSpec((count * rows, cols), lambda i: (i, 0)), whole_block(mark_shape)),
+        out_shape=(jax.ShapeDtypeStruct((2 * count * rows, cols), jnp.float32), mark_shape),
+        compiler_params=pltpu.CompilerParams(vmem_limit_bytes=6 << 20),
+        cost_estimate=pl.CostEstimate(flops=0, bytes_accessed=3 << 19, transcendentals=0),
+        name="assemble_rows",
+    )(side, mine, got, earlier)
+
+
+def assemble_columns(side, mine, got, channel_count):
+    count, _, cols = mine.shape
+    return pl.pallas_call(
+        assemble_columns_kernel,
+        grid=(2,),
+        in_specs=[pl.BlockSpec(memory_space=pltpu.SMEM), whole_block(mine), whole_block(got)],
         out_specs=(
-            pl.BlockSpec((count * rows, channel_count), lambda i: (i, 0)),
-            pl.BlockSpec((channel_count, count * rows), lambda i: (0, i)),
-            pl.BlockSpec((kernel_size, kernel_size, channel_count), lambda i: (0, 0, 0)),
+            pl.BlockSpec((channel_count, count * cols), lambda i: (0, i)),
+            pl.BlockSpec((kernel_side, kernel_side, channel_count), lambda i: (0, 0, 0)),
         ),
         out_shape=(
-            jax.ShapeDtypeStruct((2 * count * rows, channel_count), jnp.float32),
-            jax.ShapeDtypeStruct((channel_count, 2 * count * rows), jnp.float32),
-            jax.ShapeDtypeStruct((kernel_size, kernel_size, channel_count), jnp.float32),
+            jax.ShapeDtypeStruct((channel_count, 2 * count * cols), jnp.float32),
+            jax.ShapeDtypeStruct((kernel_side, kernel_side, channel_count), jnp.float32),
         ),
-        compiler_params=pltpu.CompilerParams(vmem_limit_bytes=16 << 20),
-        cost_estimate=pl.CostEstimate(flops=0, bytes_accessed=3 << 20, transcendentals=0),
-        name="assemble",
-    )(side, *operands)
+        compiler_params=pltpu.CompilerParams(vmem_limit_bytes=6 << 20),
+        cost_estimate=pl.CostEstimate(flops=0, bytes_accessed=3 << 19, transcendentals=0),
+        name="assemble_columns",
+    )(side, mine, got)
 
 
 def product(left, right, left_dim, right_dim):
@@ -469,7 +538,7 @@
             shape((hidden_size // 2, channel_count), jnp.float32),
         ),
         scratch_shapes=[pltpu.VMEM((cells, hidden_size), jnp.bfloat16)],
-        compiler_params=pltpu.CompilerParams(vmem_limit_bytes=16 << 20),
+        compiler_params=pltpu.CompilerParams(vmem_limit_bytes=6 << 20),
         cost_estimate=pl.CostEstimate(
             flops=6 * cells * channel_count * hidden_size,
             bytes_accessed=4 << 20,
@@ -524,7 +593,7 @@
             pltpu.VMEM((cells, hidden_size), jnp.float32),
             pltpu.VMEM((cells, hidden_size), jnp.bfloat16),
         ],
-        compiler_params=pltpu.CompilerParams(vmem_limit_bytes=16 << 20),
+        compiler_params=pltpu.CompilerParams(vmem_limit_bytes=6 << 20),
         cost_estimate=pl.CostEstimate(
             flops=6 * cells * channel_count * hidden_size, bytes_accessed=4 << 20, transcendentals=0
         ),
@@ -563,7 +632,7 @@
     conv_grid = conv_grad.reshape(student.shape)
     inner, outer = [swap(edge, "lat", 1) for edge in edges(conv_grid, "lat", 1, half_kernel)]
     part_dw = tap_sums(padded_bf, conv_grid, round_up(tap_count, 64))
-    (out_chunk,), (in_chunk, dw_chunk), padded_grad = sum_over_mesh(
+    (out_chunk,), in_chunk, padded_grad = sum_over_mesh(
         [[kept_out, got_out]],
         [[kept_in, got_in], [part_dw]],
         cell_total,
@@ -572,21 +641,19 @@
         outer,
         half_kernel,
     )
-    grad_student = conv_back(padded_grad, params, misfit.reshape(student.shape))
-    hidden_rows = in_chunk.shape[0]
-    dw_groups = [dw_chunk[:, k : k + hidden_rows] for k in range(0, channel_count, hidden_rows)]
-    mixed = jnp.concatenate([in_chunk.T] + dw_groups)
-    out_chunks, in_chunks = gather_sums(out_chunk[None], mixed[None])
-    in_chunks = after(in_chunks, grad_student)
-    sum_out, sum_in, sum_dw = assemble(
-        side,
-        out_chunks,
-        swap(out_chunks, "lat", 1),
-        in_chunks,
-        swap(in_chunks, "lat", 1),
-        channel_count,
-        kernel_side,
-    )
+    out_chunks, in_chunks = out_chunk[None], in_chunk
+    (_, out_halved), (_, in_halved) = sum_stages()
+    for out_stage, in_stage in zip(out_halved[::-1], in_halved[::-1]):
+        out_chunks = gather_halves(out_chunks, *out_stage)
+        in_mine, in_got = in_chunks, swap(in_chunks, *in_stage)
+        if in_stage != in_halved[0]:
+            in_chunks = in_order(in_mine, in_got, *in_stage)
+    grad_student, mark = conv_back(padded_grad, params, misfit.reshape(student.shape), out_chunks)
+    sum_out, mark = assemble_rows(side, out_chunks, swap(out_chunks, "lat", 1), mark)
+    axis, bit = in_halved[0]
+    place = ((lax.axis_index(axis) // bit) % 2).astype(jnp.int32).reshape(1)
+    in_chunks = join(place, in_mine, in_got, mark)
+    sum_in, sum_dw = assemble_columns(side, in_chunks, swap(in_chunks, "lat", 1), channel_count)
     return (grad_student, sum_in, sum_out, sum_dw)
 
 

time: 65.2 us -> 63.1 us (0.968)
  waiting for transfers between devices: 26.6 us -> 23.5 us
  Pallas kernels: 8.62 us -> 9.37 us
  starting transfers between devices: 25.1 us -> 25.8 us
    ppermute x22, waiting for transfers between devices: 24.9 us -> 20.4 us  [swap(): lax.ppermute(value, axis, [(i, i ^ bit) for i in range(lax.axis_size(axis...]
    ppermute x2, waiting for transfers between devices: 1.68 us -> 3.13 us  [swap_outer(): got = lax.ppermute(edge, axis, pairs + [(j, i) for i, j in pairs])]
    ppermute x2, starting transfers between devices: 4.21 us -> 5.15 us  [swap_outer(): got = lax.ppermute(edge, axis, pairs + [(j, i) for i, j in pairs])]
    pallas_call x2 -> x5, Pallas kernels: 3.36 us -> 4.13 us  [the longest x1 1.93 us: conv_back(): pl.pallas_call(conv_back_kernel, out_shape=(jax.ShapeDtypeStruct(misfit.s...]
  transfers between devices with their start and end apart: 24 -> 24, of which waited for: 12 -> 13; matrix products, arithmetic and copies ran while one was open for 2% -> 2% of each run, Pallas kernels for 7% -> 10%
where the time goes in v6:
time: 63.1 us; the launch traced here: 62.9 us
  starting transfers between devices  25.8 us (41%)
  waiting for transfers between devices  23.5 us (37%)
  Pallas kernels  9.37 us (15%)
  other arithmetic  1.94 us (3%)
  between operations  1.18 us (2%)
  local copies, waits for them, and re-layouts  1.1 us (2%)
    ppermute x22, starting transfers between devices, swap(): lax.ppermute(value, axis, [(i, i ^ bit) for i in range(lax.axis_size(axis...  20.7 us
    ppermute x22, waiting for transfers between devices, swap(): lax.ppermute(value, axis, [(i, i ^ bit) for i in range(lax.axis_size(axis...  20.4 us
    ppermute x2, starting transfers between devices, swap_outer(): got = lax.ppermute(edge, axis, pairs + [(j, i) for i, j in pairs])  5.15 us
    ppermute x2, waiting for transfers between devices, swap_outer(): got = lax.ppermute(edge, axis, pairs + [(j, i) for i, j in pairs])  3.13 us
    pallas_call x1, Pallas kernels, conv_back(): pl.pallas_call(conv_back_kernel, out_shape=(jax.ShapeDtypeStruct(misfit.s...  1.93 us
    pallas_call x1, Pallas kernels, forward(): pl.pallas_call(forward_kernel, in_specs=[pl.BlockSpec(memory_space=pltpu....  1.81 us
    pallas_call x1, Pallas kernels, conv_norm(): pl.pallas_call(conv_norm_kernel, out_shape=(jax.ShapeDtypeStruct((cells,...  1.42 us
  transfers between devices with their start and end apart: 24, of which 13 were waited for; matrix products, arithmetic and copies ran while one was open for 2% of the time, Pallas kernels for 10%

profile of v6, /device:TPU:0, one launch (start us, length us, event | category | flops | bytes accessed | tf_op | source)
XLA Modules:
  0.0 62.9 jit_solution(2316232404090120338)
XLA Ops:
  0.7 0.8 %broadcast_select_fusion.14 = (bf16[2,4,3,256]{3,2,1,0:T(4,128)(2,1)S(1)}, bf16[2,4,3,256]{3,2,1,0:T(4,128)(2,1)S(1)}) fusion(pred[]{:T(512)S(6)} %eq.71, bf16[2,4,32,256]{3,2,1,0:T(8,128)(2,1)} %param.7), kind=kLoop, calls=%fused_computation.61 | loop fusion | flops 12288 | bytes 49153 | tf_op jit(solution)/shard_map/jit(_where)/select_n | solution.py:27
  1.5 3.0 %collective-permute-start = (bf16[2,4,3,256]{3,2,1,0:T(4,128)(2,1)S(1)}, bf16[2,4,3,256]{3,2,1,0:T(4,128)(2,1)S(1)}, u32[]{:S(2)}, u32[]{:S(2)}) collective-permute-start(bf16[2,4,3,256]{3,2,1,0:T(4,128)(2,1)S(1)} %get-tuple-element.89), channel_id=1, source_target_pairs={{0,1},{1,0},{2,3},{3,2},{4,5},{5,4},{6,7},{7,6},{8,9},{9,8},{10,11... | collective-permute-start | bytes 36872 | tf_op jit(solution)/shard_map/ppermute | solution.py:20
  4.5 3.5 %collective-permute-start.1 = (bf16[2,4,3,256]{3,2,1,0:T(4,128)(2,1)S(1)}, bf16[2,4,3,256]{3,2,1,0:T(4,128)(2,1)S(1)}, u32[]{:S(2)}, u32[]{:S(2)}) collective-permute-start(bf16[2,4,3,256]{3,2,1,0:T(4,128)(2,1)S(1)} %get-tuple-element.90), channel_id=1, source_target_pairs={{1,2},{3,4},{5,6},{7,0},{2,1},{4,3},{6,5},{0,7},{9,10},{11,12},{13... | collective-permute-start | bytes 36872 | tf_op jit(solution)/shard_map/ppermute | solution.py:33
  8.1 0.7 %copy-done.6 = f32[256]{0:T(256)S(1)} copy-done((f32[256]{0:T(256)S(1)}, f32[256]{0:T(256)}, u32[]{:S(2)}) %copy-start.6) | copy-done | bytes 1048
  9.0 1.6 %collective-permute-start.4 = (bf16[2,2,4,1,8,256]{5,4,2,1,0,3:T(8,128)(2,1)S(1)}, bf16[2,2,4,1,8,256]{5,4,2,1,0,3:T(8,128)(2,1)S(1)}, u32[]{:S(2)}, u32[]{:S(2)}) collective-permute-start(bf16[2,2,4,1,8,256]{5,4,2,1,0,3:T(8,128)(2,1)S(1)} %get-tuple-element.87), channel_id=1, source_target_pairs={{0,16},{8,24},{16,0},{24,8},{1,17},{9,25},{17,1},{25,9},{2,18},{10... | collective-permute-start | bytes 196616 | tf_op jit(solution)/shard_map/ppermute | solution.py:20
  11.2 1.6 %collective-permute-start.3 = (bf16[2,3,38,256]{3,2,1,0:T(8,128)(2,1)S(1)}, bf16[2,3,38,256]{3,2,1,0:T(8,128)(2,1)S(1)}, u32[]{:S(2)}, u32[]{:S(2)}) collective-permute-start(bf16[2,3,38,256]{3,2,1,0:T(8,128)(2,1)S(1)} %get-tuple-element.81), channel_id=1, source_target_pairs={{8,16},{24,0},{16,8},{0,24},{9,17},{25,1},{17,9},{1,25},{10,18},{2... | collective-permute-start | bytes 350216 | tf_op jit(solution)/shard_map/ppermute | solution.py:33
  12.8 0.6 collective-permute-done.4
  13.5 2.8 %collective-permute-done.3 = bf16[2,3,38,256]{3,2,1,0:T(8,128)(2,1)S(1)} collective-permute-done((bf16[2,3,38,256]{3,2,1,0:T(8,128)(2,1)S(1)}, bf16[2,3,38,256]{3,2,1,0:T(8,128)(2,1)S(1)}, u32[]{:S(2)}, u32[]{:S(2)}) %collective-permute-start.3) | collective-permute-done | bytes 116768 | tf_op jit(solution)/shard_map/ppermute | solution.py:33
  16.4 1.4 %conv_norm.1 = (bf16[256,256]{1,0:T(8,128)(2,1)S(1)}, f32[256,256]{1,0:T(8,128)S(1)}, f32[256,1]{1,0:T(8,128)S(1)}) custom-call(bf16[2,10,38,256]{3,2,1,0:T(8,128)(2,1)S(1)} %pad_maximum_fusion.padded_ref, f32[51,256]{1,0:T(8,128)S(1)} %pad_maximum_fusion.8.params_ref), custom_call_target="tpu_custom_call" | custom-call | flops 6422528 | bytes 1048576 | tf_op jit(solution)/shard_map/conv_norm/pallas_call | solution.py:297
  17.9 1.8 %forward.1 = (f32[256,1024]{1,0:T(8,128)S(1)}, f32[256,256]{1,0:T(8,128)S(1)}, bf16[256,256]{1,0:T(8,128)(2,1)S(1)}, bf16[512,256]{1,0:T(8,128)(2,1)S(1)}, f32[512,256]{1,0:T(8,128)S(1)}) custom-call(s32[1]{0:T(128)} %bitcast.side_ref, bf16[256,256]{1,0:T(8,128)(2,1)S(1)} %get-tuple-element.34.normed_ref, bf16[256,256]{1,0:T(8,128)(2,1)S(1)} %bitcast.33, ...), custom_call_target="tpu_custom_call" | custom-call | flops 402653184 | bytes 4194304 | tf_op jit(solution)/shard_map/forward/pallas_call | solution.py:529
  20.1 1.0 %backward.1 = (bf16[256,256]{1,0:T(8,128)(2,1)S(1)}, bf16[512,256]{1,0:T(8,128)(2,1)S(1)}, f32[512,256]{1,0:T(8,128)S(1)}) custom-call(s32[1]{0:T(128)} %bitcast.side_ref, f32[256,1024]{1,0:T(8,128)S(1)} %get-tuple-element.36.slope_ref, bf16[256,256]{1,0:T(8,128)(2,1)S(1)} %get-tuple-element.37.out_grad_ref, ...), custom_call_target="tpu_custom_call" | custom-call | flops 402653184 | bytes 4194304 | tf_op jit(solution)/shard_map/backward/pallas_call | solution.py:583
  21.8 1.0 %tap_sums.1 = f32[64,256]{1,0:T(8,128)S(1)} custom-call(bf16[2,10,38,256]{3,2,1,0:T(8,128)(2,1)S(1)} %pad_maximum_fusion.padded_ref, bf16[2,4,32,256]{3,2,1,0:T(8,128)(2,1)S(1)} %bitcast.30), custom_call_target="tpu_custom_call" | custom-call | flops 6422528 | bytes 1048576 | tf_op jit(solution)/shard_map/tap_sums/pallas_call | solution.py:383
  23.1 1.6 %collective-permute-start.8 = (bf16[480,256]{1,0:T(8,128)(2,1)S(1)}, bf16[480,256]{1,0:T(8,128)(2,1)S(1)}, u32[]{:S(2)}, u32[]{:S(2)}) collective-permute-start(bf16[480,256]{1,0:T(8,128)(2,1)S(1)} %pad_maximum_fusion.2), channel_id=1, source_target_pairs={{0,16},{8,24},{16,0},{24,8},{1,17},{9,25},{17,1},{25,9},{2,18},{10... | collective-permute-start | bytes 737288 | tf_op jit(solution)/shard_map/ppermute | solution.py:20
  24.7 3.8 %collective-permute-done.14 = bf16[256,256]{1,0:T(8,128)(2,1)S(1)} collective-permute-done((bf16[256,256]{1,0:T(8,128)(2,1)S(1)}, bf16[256,256]{1,0:T(8,128)(2,1)S(1)}, u32[]{:S(2)}, u32[]{:S(2)}) %collective-permute-start.14) | collective-permute-done | bytes 131104 | tf_op jit(solution)/shard_map/ppermute | solution.py:20
  28.6 0.9 %collective-permute-start.15 = (bf16[128,256]{1,0:T(8,128)(2,1)S(1)}, bf16[128,256]{1,0:T(8,128)(2,1)S(1)}, u32[]{:S(2)}, u32[]{:S(2)}) collective-permute-start(bf16[128,256]{1,0:T(8,128)(2,1)S(1)} %get-tuple-element.73), channel_id=1, source_target_pairs={{0,4},{1,5},{2,6},{3,7},{4,0},{5,1},{6,2},{7,3},{8,12},{9,13},{10,... | collective-permute-start | bytes 196616 | tf_op jit(solution)/shard_map/ppermute | solution.py:20
  29.4 1.8 %collective-permute-done.8 = bf16[480,256]{1,0:T(8,128)(2,1)S(1)} collective-permute-done((bf16[480,256]{1,0:T(8,128)(2,1)S(1)}, bf16[480,256]{1,0:T(8,128)(2,1)S(1)}, u32[]{:S(2)}, u32[]{:S(2)}) %collective-permute-start.8) | collective-permute-done | bytes 245792 | tf_op jit(solution)/shard_map/ppermute | solution.py:20
  32.0 2.2 %collective-permute-done.15 = bf16[128,256]{1,0:T(8,128)(2,1)S(1)} collective-permute-done((bf16[128,256]{1,0:T(8,128)(2,1)S(1)}, bf16[128,256]{1,0:T(8,128)(2,1)S(1)}, u32[]{:S(2)}, u32[]{:S(2)}) %collective-permute-start.15) | collective-permute-done | bytes 65568 | tf_op jit(solution)/shard_map/ppermute | solution.py:20
  34.2 1.6 %collective-permute-start.16 = (f32[128,256]{1,0:T(8,128)S(1)}, f32[128,256]{1,0:T(8,128)S(1)}, u32[]{:S(2)}, u32[]{:S(2)}) collective-permute-start(f32[128,256]{1,0:T(8,128)S(1)} %convert_add_fusion.2), channel_id=1, source_target_pairs={{0,16},{8,24},{16,0},{24,8},{1,17},{9,25},{17,1},{25,9},{2,18},{10... | collective-permute-start | bytes 393224 | tf_op jit(solution)/shard_map/ppermute | solution.py:20
  35.8 0.8 %collective-permute-done.10 = bf16[264,256]{1,0:T(8,128)(2,1)S(1)} collective-permute-done((bf16[264,256]{1,0:T(8,128)(2,1)S(1)}, bf16[264,256]{1,0:T(8,128)(2,1)S(1)}, u32[]{:S(2)}, u32[]{:S(2)}) %collective-permute-start.10) | collective-permute-done | bytes 135200 | tf_op jit(solution)/shard_map/ppermute | solution.py:20
  36.7 1.8 %collective-permute-start.11 = (f32[204,256]{1,0:T(8,128)S(1)}, f32[204,256]{1,0:T(8,128)S(1)}, u32[]{:S(2)}, u32[]{:S(2)}) collective-permute-start(f32[204,256]{1,0:T(8,128)S(1)} %pad_maximum_fusion.3), channel_id=1, source_target_pairs={{0,2},{1,3},{2,0},{3,1},{4,6},{5,7},{6,4},{7,5},{8,10},{9,11},{10,... | collective-permute-start | bytes 626696 | tf_op jit(solution)/shard_map/ppermute | solution.py:20
  38.5 0.8 %collective-permute-done.16 = f32[128,256]{1,0:T(8,128)S(1)} collective-permute-done((f32[128,256]{1,0:T(8,128)S(1)}, f32[128,256]{1,0:T(8,128)S(1)}, u32[]{:S(2)}, u32[]{:S(2)}) %collective-permute-start.16) | collective-permute-done | bytes 131104 | tf_op jit(solution)/shard_map/ppermute | solution.py:20
  39.4 3.2 %collective-permute-done.11 = f32[204,256]{1,0:T(8,128)S(1)} collective-permute-done((f32[204,256]{1,0:T(8,128)S(1)}, f32[204,256]{1,0:T(8,128)S(1)}, u32[]{:S(2)}, u32[]{:S(2)}) %collective-permute-start.11) | collective-permute-done | bytes 208928 | tf_op jit(solution)/shard_map/ppermute | solution.py:20
  42.7 2.7 %collective-permute-start.12 = (bf16[204,256]{1,0:T(8,128)(2,1)S(1)}, bf16[204,256]{1,0:T(8,128)(2,1)S(1)}, u32[]{:S(2)}, u32[]{:S(2)}) collective-permute-start(bf16[204,256]{1,0:T(8,128)(2,1)S(1)} %pad_maximum_fusion.6), channel_id=1, source_target_pairs={{0,4},{1,5},{2,6},{3,7},{4,0},{5,1},{6,2},{7,3},{8,12},{9,13},{10,... | collective-permute-start | bytes 313352 | tf_op jit(solution)/shard_map/ppermute | solution.py:20
  45.8 2.6 %collective-permute-done.12.got_ref = bf16[204,256]{1,0:T(8,128)(2,1)S(1)} collective-permute-done((bf16[204,256]{1,0:T(8,128)(2,1)S(1)}, bf16[204,256]{1,0:T(8,128)(2,1)S(1)}, u32[]{:S(2)}, u32[]{:S(2)}) %collective-permute-start.12) | collective-permute-done | bytes 104480 | tf_op jit(solution)/shard_map/ppermute | solution.py:20
  48.5 3.1 %collective-permute-start.20 = (bf16[1,288,128]{2,1,0:T(8,128)(2,1)S(1)}, bf16[1,288,128]{2,1,0:T(8,128)(2,1)S(1)}, u32[]{:S(2)}, u32[]{:S(2)}) collective-permute-start(bf16[1,288,128]{2,1,0:T(8,128)(2,1)S(1)} %finish_columns.1), channel_id=1, source_target_pairs={{0,1},{1,0},{2,3},{3,2},{4,5},{5,4},{6,7},{7,6},{8,9},{9,8},{10,11... | collective-permute-start | bytes 221192 | tf_op jit(solution)/shard_map/ppermute | solution.py:20
  51.8 2.2 %collective-permute-done.20 = bf16[1,288,128]{2,1,0:T(8,128)(2,1)S(1)} collective-permute-done((bf16[1,288,128]{2,1,0:T(8,128)(2,1)S(1)}, bf16[1,288,128]{2,1,0:T(8,128)(2,1)S(1)}, u32[]{:S(2)}, u32[]{:S(2)}) %collective-permute-start.20) | collective-permute-done | bytes 73760 | tf_op jit(solution)/shard_map/ppermute | solution.py:20
  54.0 1.6 %collective-permute-start.21 = (bf16[2,288,128]{2,1,0:T(8,128)(2,1)S(1)}, bf16[2,288,128]{2,1,0:T(8,128)(2,1)S(1)}, u32[]{:S(2)}, u32[]{:S(2)}) collective-permute-start(bf16[2,288,128]{2,1,0:T(8,128)(2,1)S(1)} %maximum_select_fusion.1.mine), channel_id=1, source_target_pairs={{0,16},{8,24},{16,0},{24,8},{1,17},{9,25},{17,1},{25,9},{2,18},{10... | collective-permute-start | bytes 442376 | tf_op jit(solution)/shard_map/ppermute | solution.py:20
  55.5 1.1 %collective-permute-done.19 = bf16[2,128,256]{2,1,0:T(8,128)(2,1)S(1)} collective-permute-done((bf16[2,128,256]{2,1,0:T(8,128)(2,1)S(1)}, bf16[2,128,256]{2,1,0:T(8,128)(2,1)S(1)}, u32[]{:S(2)}, u32[]{:S(2)}) %collective-permute-start.19) | collective-permute-done | bytes 131104 | tf_op jit(solution)/shard_map/ppermute | solution.py:20
  57.1 1.9 %conv_back.1 = (bf16[2,4,32,256]{3,2,1,0:T(8,128)(2,1)}, f32[8,128]{1,0:T(8,128)S(1)}) custom-call(bf16[2,10,38,256]{3,2,1,0:T(8,128)(2,1)S(1)} %pad_maximum_fusion.1.padded_ref, f32[51,256]{1,0:T(8,128)S(1)} %pad_maximum_fusion.8.params_ref, f32[2,4,32,256]{3,2,1,0:T(8,128)S(1)} %bitcast.35, bf16[4,128,256]{2,1,0:T(8,128)(2,1)S(1)} %maximum_select_fusion._.mine), custom_call_target="tpu_custom_call" | custom-call | flops 6422528 | bytes 1048576 | tf_op jit(solution)/shard_map/conv_back/pallas_call | solution.py:333
  59.0 1.0 %assemble_rows.1 = (f32[1024,256]{1,0:T(8,128)}, f32[8,128]{1,0:T(8,128)S(1)}) custom-call(s32[1]{0:T(128)} %bitcast.side_ref, bf16[4,128,256]{2,1,0:T(8,128)(2,1)S(1)} %maximum_select_fusion._.mine, bf16[4,128,256]{2,1,0:T(8,128)(2,1)S(1)} %collective-permute-done.22.got, f32[8,128]{1,0:T(8,128)S(1)} %get-tuple-element.55._), custom_call_target="tpu_custom_call" | custom-call | bytes 1572864 | tf_op jit(solution)/shard_map/assemble_rows/pallas_call | solution.py:443
  60.6 1.2 %collective-permute-done.23.got = bf16[4,288,128]{2,1,0:T(8,128)(2,1)S(1)} collective-permute-done((bf16[4,288,128]{2,1,0:T(8,128)(2,1)S(1)}, bf16[4,288,128]{2,1,0:T(8,128)(2,1)S(1)}, u32[]{:S(2)}, u32[]{:S(2)}) %collective-permute-start.23) | collective-permute-done | bytes 294944 | tf_op jit(solution)/shard_map/ppermute | solution.py:20
  61.8 1.1 %assemble_columns.1 = (f32[256,1024]{1,0:T(8,128)}, f32[7,7,256]{2,1,0:T(8,128)}) custom-call(s32[1]{0:T(128)} %bitcast.side_ref, bf16[4,288,128]{2,1,0:T(8,128)(2,1)S(1)} %join.1.mine, bf16[4,288,128]{2,1,0:T(8,128)(2,1)S(1)} %collective-permute-done.23.got), custom_call_target="tpu_custom_call" | custom-call | bytes 1572864 | tf_op jit(solution)/shard_map/assemble_columns/pallas_call | solution.py:458
  (89 shorter events, 5.0 us)
Async XLA Ops:
  0.6 7.4 %copy-start.4 = (f32[7,7,256]{2,1,0:T(8,128)S(1)}, f32[7,7,256]{2,1,0:T(8,128)}, u32[]{:S(2)}) copy-start(f32[7,7,256]{2,1,0:T(8,128)} %param.9) | copy-start | bytes 150532
  1.5 9.1 %collective-permute-start = (bf16[2,4,3,256]{3,2,1,0:T(4,128)(2,1)S(1)}, bf16[2,4,3,256]{3,2,1,0:T(4,128)(2,1)S(1)}, u32[]{:S(2)}, u32[]{:S(2)}) collective-permute-start(bf16[2,4,3,256]{3,2,1,0:T(4,128)(2,1)S(1)} %get-tuple-element.89), channel_id=1, source_target_pairs={{0,1},{1,0},{2,3},{3,2},{4,5},{5,4},{6,7},{7,6},{8,9},{9,8},{10,11... | collective-permute-start | bytes 36872 | tf_op jit(solution)/shard_map/ppermute | solution.py:20
  4.5 6.4 %collective-permute-start.1 = (bf16[2,4,3,256]{3,2,1,0:T(4,128)(2,1)S(1)}, bf16[2,4,3,256]{3,2,1,0:T(4,128)(2,1)S(1)}, u32[]{:S(2)}, u32[]{:S(2)}) collective-permute-start(bf16[2,4,3,256]{3,2,1,0:T(4,128)(2,1)S(1)} %get-tuple-element.90), channel_id=1, source_target_pairs={{1,2},{3,4},{5,6},{7,0},{2,1},{4,3},{6,5},{0,7},{9,10},{11,12},{13... | collective-permute-start | bytes 36872 | tf_op jit(solution)/shard_map/ppermute | solution.py:33
  8.1 0.9 %copy-start.3 = (bf16[2,16,8,256]{3,2,1,0:T(8,128)(2,1)S(1)}, bf16[2,16,8,256]{3,2,1,0:T(8,128)(2,1)}, u32[]{:S(2)}) copy-start(bf16[2,16,8,256]{3,2,1,0:T(8,128)(2,1)} %param.8) | copy-start | bytes 393220
  8.1 0.7 %copy-start.6 = (f32[256]{0:T(256)S(1)}, f32[256]{0:T(256)}, u32[]{:S(2)}) copy-start(f32[256]{0:T(256)} %param.10) | copy-start | bytes 3076
  8.1 0.7 %copy-start.5 = (f32[256]{0:T(256)S(1)}, f32[256]{0:T(256)}, u32[]{:S(2)}) copy-start(f32[256]{0:T(256)} %param.13) | copy-start | bytes 3076
  9.0 2.0 %copy-start.2 = (bf16[2,4,32,256]{3,2,1,0:T(8,128)(2,1)S(1)}, bf16[2,4,32,256]{3,2,1,0:T(8,128)(2,1)}, u32[]{:S(2)}) copy-start(bf16[2,4,32,256]{3,2,1,0:T(8,128)(2,1)} %param.7) | copy-start | bytes 393220
  9.0 4.3 %collective-permute-start.4 = (bf16[2,2,4,1,8,256]{5,4,2,1,0,3:T(8,128)(2,1)S(1)}, bf16[2,2,4,1,8,256]{5,4,2,1,0,3:T(8,128)(2,1)S(1)}, u32[]{:S(2)}, u32[]{:S(2)}) collective-permute-start(bf16[2,2,4,1,8,256]{5,4,2,1,0,3:T(8,128)(2,1)S(1)} %get-tuple-element.87), channel_id=1, source_target_pairs={{0,16},{8,24},{16,0},{24,8},{1,17},{9,25},{17,1},{25,9},{2,18},{10... | collective-permute-start | bytes 196616 | tf_op jit(solution)/shard_map/ppermute | solution.py:20
  11.1 2.4 %collective-permute-start.2 = (bf16[2,3,38,256]{3,2,1,0:T(8,128)(2,1)S(1)}, bf16[2,3,38,256]{3,2,1,0:T(8,128)(2,1)S(1)}, u32[]{:S(2)}, u32[]{:S(2)}) collective-permute-start(bf16[2,3,38,256]{3,2,1,0:T(8,128)(2,1)S(1)} %get-tuple-element.82), channel_id=1, source_target_pairs={{0,8},{8,0},{16,24},{24,16},{1,9},{9,1},{17,25},{25,17},{2,10},{10... | collective-permute-start | bytes 350216 | tf_op jit(solution)/shard_map/ppermute | solution.py:20
  11.2 5.1 %collective-permute-start.3 = (bf16[2,3,38,256]{3,2,1,0:T(8,128)(2,1)S(1)}, bf16[2,3,38,256]{3,2,1,0:T(8,128)(2,1)S(1)}, u32[]{:S(2)}, u32[]{:S(2)}) collective-permute-start(bf16[2,3,38,256]{3,2,1,0:T(8,128)(2,1)S(1)} %get-tuple-element.81), channel_id=1, source_target_pairs={{8,16},{24,0},{16,8},{0,24},{9,17},{25,1},{17,9},{1,25},{10,18},{2... | collective-permute-start | bytes 350216 | tf_op jit(solution)/shard_map/ppermute | solution.py:33
  13.4 4.4 %collective-permute-start.5 = (bf16[2,1,4,2,8,256]{5,4,3,2,0,1:T(8,128)(2,1)S(1)}, bf16[2,1,4,2,8,256]{5,4,3,2,0,1:T(8,128)(2,1)S(1)}, u32[]{:S(2)}, u32[]{:S(2)}) collective-permute-start(bf16[2,1,4,2,8,256]{5,4,3,2,0,1:T(8,128)(2,1)S(1)} %bitcast.40), channel_id=1, source_target_pairs={{0,8},{8,0},{16,24},{24,16},{1,9},{9,1},{17,25},{25,17},{2,10},{10... | collective-permute-start | bytes 196616 | tf_op jit(solution)/shard_map/ppermute | solution.py:20
  16.3 1.6 %copy-start.1 = (bf16[1024,256]{1,0:T(8,128)(2,1)S(1)}, bf16[1024,256]{1,0:T(8,128)(2,1)}, u32[]{:S(2)}) copy-start(bf16[1024,256]{1,0:T(8,128)(2,1)} %w_out_ref.3) | copy-start | bytes 1572868
  16.4 1.5 %copy-start = (bf16[256,1024]{1,0:T(8,128)(2,1)S(1)}, bf16[256,1024]{1,0:T(8,128)(2,1)}, u32[]{:S(2)}) copy-start(bf16[256,1024]{1,0:T(8,128)(2,1)} %w_in_ref.3) | copy-start | bytes 1572868
  19.7 3.2 %collective-permute-start.13 = (bf16[512,256]{1,0:T(8,128)(2,1)S(1)}, bf16[512,256]{1,0:T(8,128)(2,1)S(1)}, u32[]{:S(2)}, u32[]{:S(2)}) collective-permute-start(bf16[512,256]{1,0:T(8,128)(2,1)S(1)} %get-tuple-element.45), channel_id=1, source_target_pairs={{0,8},{8,0},{16,24},{24,16},{1,9},{9,1},{17,25},{25,17},{2,10},{10... | collective-permute-start | bytes 786440 | tf_op jit(solution)/shard_map/ppermute | solution.py:20
  21.2 1.9 %collective-permute-start.6 = (bf16[512,256]{1,0:T(8,128)(2,1)S(1)}, bf16[512,256]{1,0:T(8,128)(2,1)S(1)}, u32[]{:S(2)}, u32[]{:S(2)}) collective-permute-start(bf16[512,256]{1,0:T(8,128)(2,1)S(1)} %get-tuple-element.41), channel_id=1, source_target_pairs={{0,8},{8,0},{16,24},{24,16},{1,9},{9,1},{17,25},{25,17},{2,10},{10... | collective-permute-start | bytes 786440 | tf_op jit(solution)/shard_map/ppermute | solution.py:20
  21.4 1.7 %collective-permute-start.7 = (bf16[2,3,32,256]{3,2,1,0:T(8,128)(2,1)S(1)}, bf16[2,3,32,256]{3,2,1,0:T(8,128)(2,1)S(1)}, u32[]{:S(2)}, u32[]{:S(2)}) collective-permute-start(bf16[2,3,32,256]{3,2,1,0:T(8,128)(2,1)S(1)} %get-tuple-element.83), channel_id=1, source_target_pairs={{0,8},{8,0},{16,24},{24,16},{1,9},{9,1},{17,25},{25,17},{2,10},{10... | collective-permute-start | bytes 294920 | tf_op jit(solution)/shard_map/ppermute | solution.py:20
  22.9 5.6 %collective-permute-start.14 = (bf16[256,256]{1,0:T(8,128)(2,1)S(1)}, bf16[256,256]{1,0:T(8,128)(2,1)S(1)}, u32[]{:S(2)}, u32[]{:S(2)}) collective-permute-start(bf16[256,256]{1,0:T(8,128)(2,1)S(1)} %get-tuple-element.69), channel_id=1, source_target_pairs={{0,2},{1,3},{2,0},{3,1},{4,6},{5,7},{6,4},{7,5},{8,10},{9,11},{10,... | collective-permute-start | bytes 393224 | tf_op jit(solution)/shard_map/ppermute | solution.py:20
  23.1 8.0 %collective-permute-start.8 = (bf16[480,256]{1,0:T(8,128)(2,1)S(1)}, bf16[480,256]{1,0:T(8,128)(2,1)S(1)}, u32[]{:S(2)}, u32[]{:S(2)}) collective-permute-start(bf16[480,256]{1,0:T(8,128)(2,1)S(1)} %pad_maximum_fusion.2), channel_id=1, source_target_pairs={{0,16},{8,24},{16,0},{24,8},{1,17},{9,25},{17,1},{25,9},{2,18},{10... | collective-permute-start | bytes 737288 | tf_op jit(solution)/shard_map/ppermute | solution.py:20
  24.7 6.5 %collective-permute-start.9 = (bf16[2,3,32,256]{3,2,1,0:T(8,128)(2,1)S(1)}, bf16[2,3,32,256]{3,2,1,0:T(8,128)(2,1)S(1)}, u32[]{:S(2)}, u32[]{:S(2)}) collective-permute-start(bf16[2,3,32,256]{3,2,1,0:T(8,128)(2,1)S(1)} %get-tuple-element.84), channel_id=1, source_target_pairs={{0,8},{8,0},{16,24},{24,16},{1,9},{9,1},{17,25},{25,17},{2,10},{10... | collective-permute-start | bytes 294920 | tf_op jit(solution)/shard_map/ppermute | solution.py:20
  28.6 5.7 %collective-permute-start.15 = (bf16[128,256]{1,0:T(8,128)(2,1)S(1)}, bf16[128,256]{1,0:T(8,128)(2,1)S(1)}, u32[]{:S(2)}, u32[]{:S(2)}) collective-permute-start(bf16[128,256]{1,0:T(8,128)(2,1)S(1)} %get-tuple-element.73), channel_id=1, source_target_pairs={{0,4},{1,5},{2,6},{3,7},{4,0},{5,1},{6,2},{7,3},{8,12},{9,13},{10,... | collective-permute-start | bytes 196616 | tf_op jit(solution)/shard_map/ppermute | solution.py:20
  31.6 5.1 %collective-permute-start.10 = (bf16[264,256]{1,0:T(8,128)(2,1)S(1)}, bf16[264,256]{1,0:T(8,128)(2,1)S(1)}, u32[]{:S(2)}, u32[]{:S(2)}) collective-permute-start(bf16[264,256]{1,0:T(8,128)(2,1)S(1)} %pad_maximum_fusion.5), channel_id=1, source_target_pairs={{0,1},{1,0},{2,3},{3,2},{4,5},{5,4},{6,7},{7,6},{8,9},{9,8},{10,11... | collective-permute-start | bytes 405512 | tf_op jit(solution)/shard_map/ppermute | solution.py:20
  34.2 5.0 %collective-permute-start.16 = (f32[128,256]{1,0:T(8,128)S(1)}, f32[128,256]{1,0:T(8,128)S(1)}, u32[]{:S(2)}, u32[]{:S(2)}) collective-permute-start(f32[128,256]{1,0:T(8,128)S(1)} %convert_add_fusion.2), channel_id=1, source_target_pairs={{0,16},{8,24},{16,0},{24,8},{1,17},{9,25},{17,1},{25,9},{2,18},{10... | collective-permute-start | bytes 393224 | tf_op jit(solution)/shard_map/ppermute | solution.py:20
  36.7 5.9 %collective-permute-start.11 = (f32[204,256]{1,0:T(8,128)S(1)}, f32[204,256]{1,0:T(8,128)S(1)}, u32[]{:S(2)}, u32[]{:S(2)}) collective-permute-start(f32[204,256]{1,0:T(8,128)S(1)} %pad_maximum_fusion.3), channel_id=1, source_target_pairs={{0,2},{1,3},{2,0},{3,1},{4,6},{5,7},{6,4},{7,5},{8,10},{9,11},{10,... | collective-permute-start | bytes 626696 | tf_op jit(solution)/shard_map/ppermute | solution.py:20
  39.3 6.1 %collective-permute-start.17 = (bf16[128,256]{1,0:T(8,128)(2,1)S(1)}, bf16[128,256]{1,0:T(8,128)(2,1)S(1)}, u32[]{:S(2)}, u32[]{:S(2)}) collective-permute-start(bf16[128,256]{1,0:T(8,128)(2,1)S(1)} %get-tuple-element.65), channel_id=1, source_target_pairs={{0,1},{1,0},{2,3},{3,2},{4,5},{5,4},{6,7},{7,6},{8,9},{9,8},{10,11... | collective-permute-start | bytes 196616 | tf_op jit(solution)/shard_map/ppermute | solution.py:20
  42.7 5.7 %collective-permute-start.12 = (bf16[204,256]{1,0:T(8,128)(2,1)S(1)}, bf16[204,256]{1,0:T(8,128)(2,1)S(1)}, u32[]{:S(2)}, u32[]{:S(2)}) collective-permute-start(bf16[204,256]{1,0:T(8,128)(2,1)S(1)} %pad_maximum_fusion.6), channel_id=1, source_target_pairs={{0,4},{1,5},{2,6},{3,7},{4,0},{5,1},{6,2},{7,3},{8,12},{9,13},{10,... | collective-permute-start | bytes 313352 | tf_op jit(solution)/shard_map/ppermute | solution.py:20
  45.4 6.2 %collective-permute-start.18 = (bf16[1,128,256]{2,1,0:T(8,128)(2,1)S(1)}, bf16[1,128,256]{2,1,0:T(8,128)(2,1)S(1)}, u32[]{:S(2)}, u32[]{:S(2)}) collective-permute-start(bf16[1,128,256]{2,1,0:T(8,128)(2,1)S(1)} %fusion.1), channel_id=1, source_target_pairs={{0,4},{1,5},{2,6},{3,7},{4,0},{5,1},{6,2},{7,3},{8,12},{9,13},{10,... | collective-permute-start | bytes 196616 | tf_op jit(solution)/shard_map/ppermute | solution.py:20
  48.5 5.5 %collective-permute-start.20 = (bf16[1,288,128]{2,1,0:T(8,128)(2,1)S(1)}, bf16[1,288,128]{2,1,0:T(8,128)(2,1)S(1)}, u32[]{:S(2)}, u32[]{:S(2)}) collective-permute-start(bf16[1,288,128]{2,1,0:T(8,128)(2,1)S(1)} %finish_columns.1), channel_id=1, source_target_pairs={{0,1},{1,0},{2,3},{3,2},{4,5},{5,4},{6,7},{7,6},{8,9},{9,8},{10,11... | collective-permute-start | bytes 221192 | tf_op jit(solution)/shard_map/ppermute | solution.py:20
  51.7 5.0 %collective-permute-start.19 = (bf16[2,128,256]{2,1,0:T(8,128)(2,1)S(1)}, bf16[2,128,256]{2,1,0:T(8,128)(2,1)S(1)}, u32[]{:S(2)}, u32[]{:S(2)}) collective-permute-start(bf16[2,128,256]{2,1,0:T(8,128)(2,1)S(1)} %maximum_select_fusion.4), channel_id=1, source_target_pairs={{0,2},{1,3},{2,0},{3,1},{4,6},{5,7},{6,4},{7,5},{8,10},{9,11},{10,... | collective-permute-start | bytes 393224 | tf_op jit(solution)/shard_map/ppermute | solution.py:20
  54.0 6.1 %collective-permute-start.21 = (bf16[2,288,128]{2,1,0:T(8,128)(2,1)S(1)}, bf16[2,288,128]{2,1,0:T(8,128)(2,1)S(1)}, u32[]{:S(2)}, u32[]{:S(2)}) collective-permute-start(bf16[2,288,128]{2,1,0:T(8,128)(2,1)S(1)} %maximum_select_fusion.1.mine), channel_id=1, source_target_pairs={{0,16},{8,24},{16,0},{24,8},{1,17},{9,25},{17,1},{25,9},{2,18},{10... | collective-permute-start | bytes 442376 | tf_op jit(solution)/shard_map/ppermute | solution.py:20
  56.7 2.3 %collective-permute-start.22 = (bf16[4,128,256]{2,1,0:T(8,128)(2,1)S(1)}, bf16[4,128,256]{2,1,0:T(8,128)(2,1)S(1)}, u32[]{:S(2)}, u32[]{:S(2)}) collective-permute-start(bf16[4,128,256]{2,1,0:T(8,128)(2,1)S(1)} %maximum_select_fusion._.mine), channel_id=1, source_target_pairs={{0,8},{8,0},{16,24},{24,16},{1,9},{9,1},{17,25},{25,17},{2,10},{10... | collective-permute-start | bytes 786440 | tf_op jit(solution)/shard_map/ppermute | solution.py:20
  60.1 1.8 %collective-permute-start.23 = (bf16[4,288,128]{2,1,0:T(8,128)(2,1)S(1)}, bf16[4,288,128]{2,1,0:T(8,128)(2,1)S(1)}, u32[]{:S(2)}, u32[]{:S(2)}) collective-permute-start(bf16[4,288,128]{2,1,0:T(8,128)(2,1)S(1)} %join.1.mine), channel_id=1, source_target_pairs={{0,8},{8,0},{16,24},{24,16},{1,9},{9,1},{17,25},{25,17},{2,10},{10... | collective-permute-start | bytes 884744 | tf_op jit(solution)/shard_map/ppermute | solution.py:20

commit v7 on v6

--- a/solution.py
+++ b/solution.py
@@ -266,7 +266,8 @@
                 smooth[group, pl.ds((b * tile_rows + i) * tile_cols, tile_cols), :] = row
             return 0
 
-        lax.fori_loop(0, batch_size, one, 0)
+        for b in range(batch_size):
+            one(b, 0)
     gain = params_ref[gain_row : gain_row + 1, :]
     block = 32
 
@@ -324,7 +325,8 @@
                 out_ref[b, i, :, lanes] = (misfit_ref[b, i, :, lanes] + row).astype(out_ref.dtype)
             return 0
 
-        lax.fori_loop(0, batch_size, one, 0)
+        for b in range(batch_size):
+            one(b, 0)
 
 
 def conv_back(padded, params, misfit, earlier):
@@ -368,7 +370,8 @@
                     partial[group, b, at, :] = sums[p]
             return 0
 
-        lax.fori_loop(0, batch_size, one, 0)
+        for b in range(batch_size):
+            one(b, 0)
         taps = kernel_size * kernel_size
         total = partial[group, 0]
         for b in range(1, batch_size):
@@ -473,6 +476,9 @@
     )(side, mine, got)
 
 
+block_cols = 256
+
+
 def product(left, right, left_dim, right_dim):
     return lax.dot_general(
         left, right, (((left_dim,), (right_dim,)), ((), ())), preferred_element_type=jnp.float32
@@ -490,23 +496,24 @@
 ):
     cells, hidden_size = slope_ref.shape
     scale = params_ref[scale_row : scale_row + 1, :]
-    slope_ref[...] = product(normed_ref[...], w_in_ref[...], 1, 0)
-    rows, cols = 16, min(512, hidden_size)
-
-    def gelu(step, _):
-        at = pl.ds(pl.multiple_of(step * rows, rows), rows)
-        for k in range(0, hidden_size, cols):
-            values = slope_ref[at, k : k + cols]
+    rows = 16
+    mlp_out = None
+    for k in range(0, hidden_size, block_cols):
+        cols = slice(k, k + block_cols)
+        slope_ref[:, cols] = product(normed_ref[...], w_in_ref[:, cols], 1, 0)
+        for r in range(0, cells, rows):
+            at = slice(r, r + rows)
+            values = slope_ref[at, cols]
             squares = values * values
-            tangent = jnp.tanh(slope_coef * (values + cubic_coef * (squares * values)))
-            gate = 0.5 * (1.0 + tangent)
-            hidden[at, k : k + cols] = (values * gate).astype(jnp.bfloat16)
-            bend = (1.0 - tangent * tangent) * (slope_coef + 3.0 * slope_coef * cubic_coef * squares)
-            slope_ref[at, k : k + cols] = gate + 0.5 * values * bend
-        return 0
-
-    lax.fori_loop(0, cells // rows, gelu, 0, unroll=2)
-    mlp_out = product(hidden[...], w_out_ref[...], 1, 0)
+            tangent = jnp.tanh(values * (slope_coef + slope_coef * cubic_coef * squares))
+            gate = 0.5 + 0.5 * tangent
+            bend = (0.5 - 0.5 * (tangent * tangent)) * (
+                slope_coef + 3.0 * slope_coef * cubic_coef * squares
+            )
+            hidden[at, cols] = (values * gate).astype(jnp.bfloat16)
+            slope_ref[at, cols] = gate + values * bend
+        part = product(hidden[:, cols], w_out_ref[cols, :], 1, 0)
+        mlp_out = part if mlp_out is None else mlp_out + part
     misfit = student_ref[...].astype(jnp.float32) + scale * mlp_out
     misfit = misfit - target_ref[...].astype(jnp.float32)
     misfit_ref[...] = misfit
@@ -550,19 +557,17 @@
 
 def backward_kernel(
     side_ref, slope_ref, out_grad_ref, normed_ref, unit_ref, inv_ref, w_in_ref, w_out_ref, params_ref,
-    conv_grad_ref, sent_ref, kept_ref, hidden_grad, preact_grad,
+    conv_grad_ref, sent_ref, kept_ref, preact_grad,
 ):
     cells, hidden_size = slope_ref.shape
-    hidden_grad[...] = product(out_grad_ref[...], w_out_ref[...], 1, 1)
-    rows = 16
-
-    def scale_by_slope(step, _):
-        at = pl.ds(pl.multiple_of(step * rows, rows), rows)
-        preact_grad[at, :] = (hidden_grad[at, :] * slope_ref[at, :]).astype(jnp.bfloat16)
-        return 0
-
-    lax.fori_loop(0, cells // rows, scale_by_slope, 0, unroll=2)
-    unit_grad = product(preact_grad[...], w_in_ref[...], 1, 1) * params_ref[gain_row : gain_row + 1, :]
+    normed_grad = None
+    for k in range(0, hidden_size, block_cols):
+        cols = slice(k, k + block_cols)
+        hidden_grad = product(out_grad_ref[...], w_out_ref[cols, :], 1, 1)
+        preact_grad[:, cols] = (hidden_grad * slope_ref[:, cols]).astype(jnp.bfloat16)
+        part = product(preact_grad[:, cols], w_in_ref[:, cols], 1, 1)
+        normed_grad = part if normed_grad is None else normed_grad + part
+    unit_grad = normed_grad * params_ref[gain_row : gain_row + 1, :]
     unit = unit_ref[...]
     first_mean = jnp.mean(unit_grad, axis=-1, keepdims=True)
     second_mean = jnp.mean(unit_grad * unit, axis=-1, keepdims=True)
@@ -589,10 +594,7 @@
             shape((hidden_size // 2, channel_count), jnp.bfloat16),
             shape((hidden_size // 2, channel_count), jnp.float32),
         ),
-        scratch_shapes=[
-            pltpu.VMEM((cells, hidden_size), jnp.float32),
-            pltpu.VMEM((cells, hidden_size), jnp.bfloat16),
-        ],
+        scratch_shapes=[pltpu.VMEM((cells, hidden_size), jnp.bfloat16)],
         compiler_params=pltpu.CompilerParams(vmem_limit_bytes=6 << 20),
         cost_estimate=pl.CostEstimate(
             flops=6 * cells * channel_count * hidden_size, bytes_accessed=4 << 20, transcendentals=0

time: 63.1 us -> 61.9 us (0.981)
  Pallas kernels: 9.37 us -> 8.19 us
  transfers between devices with their start and end apart: 24 -> 24, of which waited for: 13 -> 13; matrix products, arithmetic and copies ran while one was open for 2% -> 2% of each run, Pallas kernels for 10% -> 9%
where the time goes in v7:
time: 61.9 us; the launch traced here: 61.7 us
  starting transfers between devices  25.8 us (42%)
  waiting for transfers between devices  23.5 us (38%)
  Pallas kernels  8.19 us (13%)
  other arithmetic  1.95 us (3%)
  between operations  1.17 us (2%)
  local copies, waits for them, and re-layouts  1.1 us (2%)
    ppermute x22, starting transfers between devices, swap(): lax.ppermute(value, axis, [(i, i ^ bit) for i in range(lax.axis_size(axis...  20.7 us
    ppermute x22, waiting for transfers between devices, swap(): lax.ppermute(value, axis, [(i, i ^ bit) for i in range(lax.axis_size(axis...  20.4 us
    ppermute x2, starting transfers between devices, swap_outer(): got = lax.ppermute(edge, axis, pairs + [(j, i) for i, j in pairs])  5.15 us
    ppermute x2, waiting for transfers between devices, swap_outer(): got = lax.ppermute(edge, axis, pairs + [(j, i) for i, j in pairs])  3.13 us
    pallas_call x1, Pallas kernels, conv_back(): pl.pallas_call(conv_back_kernel, out_shape=(jax.ShapeDtypeStruct(misfit.s...  1.55 us
    pallas_call x1, Pallas kernels, conv_norm(): pl.pallas_call(conv_norm_kernel, out_shape=(jax.ShapeDtypeStruct((cells,...  1.3 us
    pallas_call x1, Pallas kernels, forward(): pl.pallas_call(forward_kernel, in_specs=[pl.BlockSpec(memory_space=pltpu....  1.26 us
  transfers between devices with their start and end apart: 24, of which 13 were waited for; matrix products, arithmetic and copies ran while one was open for 2% of the time, Pallas kernels for 9%

profile of v7, /device:TPU:0, one launch (start us, length us, event | category | flops | bytes accessed | tf_op | source)
XLA Modules:
  0.0 61.7 jit_solution(8510302879542427901)
XLA Ops:
  0.7 0.8 %broadcast_select_fusion.14 = (bf16[2,4,3,256]{3,2,1,0:T(4,128)(2,1)S(1)}, bf16[2,4,3,256]{3,2,1,0:T(4,128)(2,1)S(1)}) fusion(pred[]{:T(512)S(6)} %eq.71, bf16[2,4,32,256]{3,2,1,0:T(8,128)(2,1)} %param.7), kind=kLoop, calls=%fused_computation.61 | loop fusion | flops 12288 | bytes 49153 | tf_op jit(solution)/shard_map/jit(_where)/select_n | solution.py:27
  1.5 3.0 %collective-permute-start = (bf16[2,4,3,256]{3,2,1,0:T(4,128)(2,1)S(1)}, bf16[2,4,3,256]{3,2,1,0:T(4,128)(2,1)S(1)}, u32[]{:S(2)}, u32[]{:S(2)}) collective-permute-start(bf16[2,4,3,256]{3,2,1,0:T(4,128)(2,1)S(1)} %get-tuple-element.89), channel_id=1, source_target_pairs={{0,1},{1,0},{2,3},{3,2},{4,5},{5,4},{6,7},{7,6},{8,9},{9,8},{10,11... | collective-permute-start | bytes 36872 | tf_op jit(solution)/shard_map/ppermute | solution.py:20
  4.5 3.5 %collective-permute-start.1 = (bf16[2,4,3,256]{3,2,1,0:T(4,128)(2,1)S(1)}, bf16[2,4,3,256]{3,2,1,0:T(4,128)(2,1)S(1)}, u32[]{:S(2)}, u32[]{:S(2)}) collective-permute-start(bf16[2,4,3,256]{3,2,1,0:T(4,128)(2,1)S(1)} %get-tuple-element.90), channel_id=1, source_target_pairs={{1,2},{3,4},{5,6},{7,0},{2,1},{4,3},{6,5},{0,7},{9,10},{11,12},{13... | collective-permute-start | bytes 36872 | tf_op jit(solution)/shard_map/ppermute | solution.py:33
  8.1 0.7 %copy-done.6 = f32[256]{0:T(256)S(1)} copy-done((f32[256]{0:T(256)S(1)}, f32[256]{0:T(256)}, u32[]{:S(2)}) %copy-start.6) | copy-done | bytes 1048
  9.0 1.6 %collective-permute-start.4 = (bf16[2,2,4,1,8,256]{5,4,2,1,0,3:T(8,128)(2,1)S(1)}, bf16[2,2,4,1,8,256]{5,4,2,1,0,3:T(8,128)(2,1)S(1)}, u32[]{:S(2)}, u32[]{:S(2)}) collective-permute-start(bf16[2,2,4,1,8,256]{5,4,2,1,0,3:T(8,128)(2,1)S(1)} %get-tuple-element.87), channel_id=1, source_target_pairs={{0,16},{8,24},{16,0},{24,8},{1,17},{9,25},{17,1},{25,9},{2,18},{10... | collective-permute-start | bytes 196616 | tf_op jit(solution)/shard_map/ppermute | solution.py:20
  11.2 1.6 %collective-permute-start.3 = (bf16[2,3,38,256]{3,2,1,0:T(8,128)(2,1)S(1)}, bf16[2,3,38,256]{3,2,1,0:T(8,128)(2,1)S(1)}, u32[]{:S(2)}, u32[]{:S(2)}) collective-permute-start(bf16[2,3,38,256]{3,2,1,0:T(8,128)(2,1)S(1)} %get-tuple-element.81), channel_id=1, source_target_pairs={{8,16},{24,0},{16,8},{0,24},{9,17},{25,1},{17,9},{1,25},{10,18},{2... | collective-permute-start | bytes 350216 | tf_op jit(solution)/shard_map/ppermute | solution.py:33
  12.8 0.6 collective-permute-done.4
  13.5 2.8 %collective-permute-done.3 = bf16[2,3,38,256]{3,2,1,0:T(8,128)(2,1)S(1)} collective-permute-done((bf16[2,3,38,256]{3,2,1,0:T(8,128)(2,1)S(1)}, bf16[2,3,38,256]{3,2,1,0:T(8,128)(2,1)S(1)}, u32[]{:S(2)}, u32[]{:S(2)}) %collective-permute-start.3) | collective-permute-done | bytes 116768 | tf_op jit(solution)/shard_map/ppermute | solution.py:33
  16.4 1.3 %conv_norm.1 = (bf16[256,256]{1,0:T(8,128)(2,1)S(1)}, f32[256,256]{1,0:T(8,128)S(1)}, f32[256,1]{1,0:T(8,128)S(1)}) custom-call(bf16[2,10,38,256]{3,2,1,0:T(8,128)(2,1)S(1)} %pad_maximum_fusion.padded_ref, f32[51,256]{1,0:T(8,128)S(1)} %pad_maximum_fusion.8.params_ref), custom_call_target="tpu_custom_call" | custom-call | flops 6422528 | bytes 1048576 | tf_op jit(solution)/shard_map/conv_norm/pallas_call | solution.py:298
  17.8 1.3 %forward.1 = (f32[256,1024]{1,0:T(8,128)S(1)}, f32[256,256]{1,0:T(8,128)S(1)}, bf16[256,256]{1,0:T(8,128)(2,1)S(1)}, bf16[512,256]{1,0:T(8,128)(2,1)S(1)}, f32[512,256]{1,0:T(8,128)S(1)}) custom-call(s32[1]{0:T(128)} %bitcast.side_ref, bf16[256,256]{1,0:T(8,128)(2,1)S(1)} %get-tuple-element.34.normed_ref, bf16[256,256]{1,0:T(8,128)(2,1)S(1)} %bitcast.33, ...), custom_call_target="tpu_custom_call" | custom-call | flops 402653184 | bytes 4194304 | tf_op jit(solution)/shard_map/forward/pallas_call | solution.py:536
  19.5 0.9 %backward.1 = (bf16[256,256]{1,0:T(8,128)(2,1)S(1)}, bf16[512,256]{1,0:T(8,128)(2,1)S(1)}, f32[512,256]{1,0:T(8,128)S(1)}) custom-call(s32[1]{0:T(128)} %bitcast.side_ref, f32[256,1024]{1,0:T(8,128)S(1)} %get-tuple-element.36.slope_ref, bf16[256,256]{1,0:T(8,128)(2,1)S(1)} %get-tuple-element.37.out_grad_ref, ...), custom_call_target="tpu_custom_call" | custom-call | flops 402653184 | bytes 4194304 | tf_op jit(solution)/shard_map/backward/pallas_call | solution.py:588
  21.1 1.0 %tap_sums.1 = f32[64,256]{1,0:T(8,128)S(1)} custom-call(bf16[2,10,38,256]{3,2,1,0:T(8,128)(2,1)S(1)} %pad_maximum_fusion.padded_ref, bf16[2,4,32,256]{3,2,1,0:T(8,128)(2,1)S(1)} %bitcast.30), custom_call_target="tpu_custom_call" | custom-call | flops 6422528 | bytes 1048576 | tf_op jit(solution)/shard_map/tap_sums/pallas_call | solution.py:386
  22.3 1.6 %collective-permute-start.8 = (bf16[480,256]{1,0:T(8,128)(2,1)S(1)}, bf16[480,256]{1,0:T(8,128)(2,1)S(1)}, u32[]{:S(2)}, u32[]{:S(2)}) collective-permute-start(bf16[480,256]{1,0:T(8,128)(2,1)S(1)} %pad_maximum_fusion.2), channel_id=1, source_target_pairs={{0,16},{8,24},{16,0},{24,8},{1,17},{9,25},{17,1},{25,9},{2,18},{10... | collective-permute-start | bytes 737288 | tf_op jit(solution)/shard_map/ppermute | solution.py:20
  23.9 3.8 %collective-permute-done.14 = bf16[256,256]{1,0:T(8,128)(2,1)S(1)} collective-permute-done((bf16[256,256]{1,0:T(8,128)(2,1)S(1)}, bf16[256,256]{1,0:T(8,128)(2,1)S(1)}, u32[]{:S(2)}, u32[]{:S(2)}) %collective-permute-start.14) | collective-permute-done | bytes 131104 | tf_op jit(solution)/shard_map/ppermute | solution.py:20
  27.7 0.9 %collective-permute-start.15 = (bf16[128,256]{1,0:T(8,128)(2,1)S(1)}, bf16[128,256]{1,0:T(8,128)(2,1)S(1)}, u32[]{:S(2)}, u32[]{:S(2)}) collective-permute-start(bf16[128,256]{1,0:T(8,128)(2,1)S(1)} %get-tuple-element.73), channel_id=1, source_target_pairs={{0,4},{1,5},{2,6},{3,7},{4,0},{5,1},{6,2},{7,3},{8,12},{9,13},{10,... | collective-permute-start | bytes 196616 | tf_op jit(solution)/shard_map/ppermute | solution.py:20
  28.6 1.8 %collective-permute-done.8 = bf16[480,256]{1,0:T(8,128)(2,1)S(1)} collective-permute-done((bf16[480,256]{1,0:T(8,128)(2,1)S(1)}, bf16[480,256]{1,0:T(8,128)(2,1)S(1)}, u32[]{:S(2)}, u32[]{:S(2)}) %collective-permute-start.8) | collective-permute-done | bytes 245792 | tf_op jit(solution)/shard_map/ppermute | solution.py:20
  31.2 2.2 %collective-permute-done.15 = bf16[128,256]{1,0:T(8,128)(2,1)S(1)} collective-permute-done((bf16[128,256]{1,0:T(8,128)(2,1)S(1)}, bf16[128,256]{1,0:T(8,128)(2,1)S(1)}, u32[]{:S(2)}, u32[]{:S(2)}) %collective-permute-start.15) | collective-permute-done | bytes 65568 | tf_op jit(solution)/shard_map/ppermute | solution.py:20
  33.4 1.6 %collective-permute-start.16 = (f32[128,256]{1,0:T(8,128)S(1)}, f32[128,256]{1,0:T(8,128)S(1)}, u32[]{:S(2)}, u32[]{:S(2)}) collective-permute-start(f32[128,256]{1,0:T(8,128)S(1)} %convert_add_fusion.2), channel_id=1, source_target_pairs={{0,16},{8,24},{16,0},{24,8},{1,17},{9,25},{17,1},{25,9},{2,18},{10... | collective-permute-start | bytes 393224 | tf_op jit(solution)/shard_map/ppermute | solution.py:20
  35.0 0.8 %collective-permute-done.10 = bf16[264,256]{1,0:T(8,128)(2,1)S(1)} collective-permute-done((bf16[264,256]{1,0:T(8,128)(2,1)S(1)}, bf16[264,256]{1,0:T(8,128)(2,1)S(1)}, u32[]{:S(2)}, u32[]{:S(2)}) %collective-permute-start.10) | collective-permute-done | bytes 135200 | tf_op jit(solution)/shard_map/ppermute | solution.py:20
  35.9 1.8 %collective-permute-start.11 = (f32[204,256]{1,0:T(8,128)S(1)}, f32[204,256]{1,0:T(8,128)S(1)}, u32[]{:S(2)}, u32[]{:S(2)}) collective-permute-start(f32[204,256]{1,0:T(8,128)S(1)} %pad_maximum_fusion.3), channel_id=1, source_target_pairs={{0,2},{1,3},{2,0},{3,1},{4,6},{5,7},{6,4},{7,5},{8,10},{9,11},{10,... | collective-permute-start | bytes 626696 | tf_op jit(solution)/shard_map/ppermute | solution.py:20
  37.7 0.8 %collective-permute-done.16 = f32[128,256]{1,0:T(8,128)S(1)} collective-permute-done((f32[128,256]{1,0:T(8,128)S(1)}, f32[128,256]{1,0:T(8,128)S(1)}, u32[]{:S(2)}, u32[]{:S(2)}) %collective-permute-start.16) | collective-permute-done | bytes 131104 | tf_op jit(solution)/shard_map/ppermute | solution.py:20
  38.6 3.2 %collective-permute-done.11 = f32[204,256]{1,0:T(8,128)S(1)} collective-permute-done((f32[204,256]{1,0:T(8,128)S(1)}, f32[204,256]{1,0:T(8,128)S(1)}, u32[]{:S(2)}, u32[]{:S(2)}) %collective-permute-start.11) | collective-permute-done | bytes 208928 | tf_op jit(solution)/shard_map/ppermute | solution.py:20
  41.9 2.7 %collective-permute-start.12 = (bf16[204,256]{1,0:T(8,128)(2,1)S(1)}, bf16[204,256]{1,0:T(8,128)(2,1)S(1)}, u32[]{:S(2)}, u32[]{:S(2)}) collective-permute-start(bf16[204,256]{1,0:T(8,128)(2,1)S(1)} %pad_maximum_fusion.6), channel_id=1, source_target_pairs={{0,4},{1,5},{2,6},{3,7},{4,0},{5,1},{6,2},{7,3},{8,12},{9,13},{10,... | collective-permute-start | bytes 313352 | tf_op jit(solution)/shard_map/ppermute | solution.py:20
  45.0 2.6 %collective-permute-done.12.got_ref = bf16[204,256]{1,0:T(8,128)(2,1)S(1)} collective-permute-done((bf16[204,256]{1,0:T(8,128)(2,1)S(1)}, bf16[204,256]{1,0:T(8,128)(2,1)S(1)}, u32[]{:S(2)}, u32[]{:S(2)}) %collective-permute-start.12) | collective-permute-done | bytes 104480 | tf_op jit(solution)/shard_map/ppermute | solution.py:20
  47.7 3.1 %collective-permute-start.20 = (bf16[1,288,128]{2,1,0:T(8,128)(2,1)S(1)}, bf16[1,288,128]{2,1,0:T(8,128)(2,1)S(1)}, u32[]{:S(2)}, u32[]{:S(2)}) collective-permute-start(bf16[1,288,128]{2,1,0:T(8,128)(2,1)S(1)} %finish_columns.1), channel_id=1, source_target_pairs={{0,1},{1,0},{2,3},{3,2},{4,5},{5,4},{6,7},{7,6},{8,9},{9,8},{10,11... | collective-permute-start | bytes 221192 | tf_op jit(solution)/shard_map/ppermute | solution.py:20
  51.0 2.2 %collective-permute-done.20 = bf16[1,288,128]{2,1,0:T(8,128)(2,1)S(1)} collective-permute-done((bf16[1,288,128]{2,1,0:T(8,128)(2,1)S(1)}, bf16[1,288,128]{2,1,0:T(8,128)(2,1)S(1)}, u32[]{:S(2)}, u32[]{:S(2)}) %collective-permute-start.20) | collective-permute-done | bytes 73760 | tf_op jit(solution)/shard_map/ppermute | solution.py:20
  53.2 1.6 %collective-permute-start.21 = (bf16[2,288,128]{2,1,0:T(8,128)(2,1)S(1)}, bf16[2,288,128]{2,1,0:T(8,128)(2,1)S(1)}, u32[]{:S(2)}, u32[]{:S(2)}) collective-permute-start(bf16[2,288,128]{2,1,0:T(8,128)(2,1)S(1)} %maximum_select_fusion.1.mine), channel_id=1, source_target_pairs={{0,16},{8,24},{16,0},{24,8},{1,17},{9,25},{17,1},{25,9},{2,18},{10... | collective-permute-start | bytes 442376 | tf_op jit(solution)/shard_map/ppermute | solution.py:20
  54.7 1.1 %collective-permute-done.19 = bf16[2,128,256]{2,1,0:T(8,128)(2,1)S(1)} collective-permute-done((bf16[2,128,256]{2,1,0:T(8,128)(2,1)S(1)}, bf16[2,128,256]{2,1,0:T(8,128)(2,1)S(1)}, u32[]{:S(2)}, u32[]{:S(2)}) %collective-permute-start.19) | collective-permute-done | bytes 131104 | tf_op jit(solution)/shard_map/ppermute | solution.py:20
  56.3 1.6 %conv_back.1 = (bf16[2,4,32,256]{3,2,1,0:T(8,128)(2,1)}, f32[8,128]{1,0:T(8,128)S(1)}) custom-call(bf16[2,10,38,256]{3,2,1,0:T(8,128)(2,1)S(1)} %pad_maximum_fusion.1.padded_ref, f32[51,256]{1,0:T(8,128)S(1)} %pad_maximum_fusion.8.params_ref, f32[2,4,32,256]{3,2,1,0:T(8,128)S(1)} %bitcast.35, bf16[4,128,256]{2,1,0:T(8,128)(2,1)S(1)} %maximum_select_fusion._.mine), custom_call_target="tpu_custom_call" | custom-call | flops 6422528 | bytes 1048576 | tf_op jit(solution)/shard_map/conv_back/pallas_call | solution.py:335
  57.8 1.0 %assemble_rows.1 = (f32[1024,256]{1,0:T(8,128)}, f32[8,128]{1,0:T(8,128)S(1)}) custom-call(s32[1]{0:T(128)} %bitcast.side_ref, bf16[4,128,256]{2,1,0:T(8,128)(2,1)S(1)} %maximum_select_fusion._.mine, bf16[4,128,256]{2,1,0:T(8,128)(2,1)S(1)} %collective-permute-done.22.got, f32[8,128]{1,0:T(8,128)S(1)} %get-tuple-element.55._), custom_call_target="tpu_custom_call" | custom-call | bytes 1572864 | tf_op jit(solution)/shard_map/assemble_rows/pallas_call | solution.py:446
  59.4 1.2 %collective-permute-done.23.got = bf16[4,288,128]{2,1,0:T(8,128)(2,1)S(1)} collective-permute-done((bf16[4,288,128]{2,1,0:T(8,128)(2,1)S(1)}, bf16[4,288,128]{2,1,0:T(8,128)(2,1)S(1)}, u32[]{:S(2)}, u32[]{:S(2)}) %collective-permute-start.23) | collective-permute-done | bytes 294944 | tf_op jit(solution)/shard_map/ppermute | solution.py:20
  60.7 1.1 %assemble_columns.1 = (f32[256,1024]{1,0:T(8,128)}, f32[7,7,256]{2,1,0:T(8,128)}) custom-call(s32[1]{0:T(128)} %bitcast.side_ref, bf16[4,288,128]{2,1,0:T(8,128)(2,1)S(1)} %join.1.mine, bf16[4,288,128]{2,1,0:T(8,128)(2,1)S(1)} %collective-permute-done.23.got), custom_call_target="tpu_custom_call" | custom-call | bytes 1572864 | tf_op jit(solution)/shard_map/assemble_columns/pallas_call | solution.py:461
  (89 shorter events, 5.1 us)
Async XLA Ops:
  0.6 7.4 %copy-start.4 = (f32[7,7,256]{2,1,0:T(8,128)S(1)}, f32[7,7,256]{2,1,0:T(8,128)}, u32[]{:S(2)}) copy-start(f32[7,7,256]{2,1,0:T(8,128)} %param.9) | copy-start | bytes 150532
  1.5 9.1 %collective-permute-start = (bf16[2,4,3,256]{3,2,1,0:T(4,128)(2,1)S(1)}, bf16[2,4,3,256]{3,2,1,0:T(4,128)(2,1)S(1)}, u32[]{:S(2)}, u32[]{:S(2)}) collective-permute-start(bf16[2,4,3,256]{3,2,1,0:T(4,128)(2,1)S(1)} %get-tuple-element.89), channel_id=1, source_target_pairs={{0,1},{1,0},{2,3},{3,2},{4,5},{5,4},{6,7},{7,6},{8,9},{9,8},{10,11... | collective-permute-start | bytes 36872 | tf_op jit(solution)/shard_map/ppermute | solution.py:20
  4.5 6.4 %collective-permute-start.1 = (bf16[2,4,3,256]{3,2,1,0:T(4,128)(2,1)S(1)}, bf16[2,4,3,256]{3,2,1,0:T(4,128)(2,1)S(1)}, u32[]{:S(2)}, u32[]{:S(2)}) collective-permute-start(bf16[2,4,3,256]{3,2,1,0:T(4,128)(2,1)S(1)} %get-tuple-element.90), channel_id=1, source_target_pairs={{1,2},{3,4},{5,6},{7,0},{2,1},{4,3},{6,5},{0,7},{9,10},{11,12},{13... | collective-permute-start | bytes 36872 | tf_op jit(solution)/shard_map/ppermute | solution.py:33
  8.1 0.9 %copy-start.3 = (bf16[2,16,8,256]{3,2,1,0:T(8,128)(2,1)S(1)}, bf16[2,16,8,256]{3,2,1,0:T(8,128)(2,1)}, u32[]{:S(2)}) copy-start(bf16[2,16,8,256]{3,2,1,0:T(8,128)(2,1)} %param.8) | copy-start | bytes 393220
  8.1 0.7 %copy-start.6 = (f32[256]{0:T(256)S(1)}, f32[256]{0:T(256)}, u32[]{:S(2)}) copy-start(f32[256]{0:T(256)} %param.10) | copy-start | bytes 3076
  8.1 0.7 %copy-start.5 = (f32[256]{0:T(256)S(1)}, f32[256]{0:T(256)}, u32[]{:S(2)}) copy-start(f32[256]{0:T(256)} %param.13) | copy-start | bytes 3076
  9.0 2.0 %copy-start.2 = (bf16[2,4,32,256]{3,2,1,0:T(8,128)(2,1)S(1)}, bf16[2,4,32,256]{3,2,1,0:T(8,128)(2,1)}, u32[]{:S(2)}) copy-start(bf16[2,4,32,256]{3,2,1,0:T(8,128)(2,1)} %param.7) | copy-start | bytes 393220
  9.0 4.3 %collective-permute-start.4 = (bf16[2,2,4,1,8,256]{5,4,2,1,0,3:T(8,128)(2,1)S(1)}, bf16[2,2,4,1,8,256]{5,4,2,1,0,3:T(8,128)(2,1)S(1)}, u32[]{:S(2)}, u32[]{:S(2)}) collective-permute-start(bf16[2,2,4,1,8,256]{5,4,2,1,0,3:T(8,128)(2,1)S(1)} %get-tuple-element.87), channel_id=1, source_target_pairs={{0,16},{8,24},{16,0},{24,8},{1,17},{9,25},{17,1},{25,9},{2,18},{10... | collective-permute-start | bytes 196616 | tf_op jit(solution)/shard_map/ppermute | solution.py:20
  11.1 2.4 %collective-permute-start.2 = (bf16[2,3,38,256]{3,2,1,0:T(8,128)(2,1)S(1)}, bf16[2,3,38,256]{3,2,1,0:T(8,128)(2,1)S(1)}, u32[]{:S(2)}, u32[]{:S(2)}) collective-permute-start(bf16[2,3,38,256]{3,2,1,0:T(8,128)(2,1)S(1)} %get-tuple-element.82), channel_id=1, source_target_pairs={{0,8},{8,0},{16,24},{24,16},{1,9},{9,1},{17,25},{25,17},{2,10},{10... | collective-permute-start | bytes 350216 | tf_op jit(solution)/shard_map/ppermute | solution.py:20
  11.2 5.1 %collective-permute-start.3 = (bf16[2,3,38,256]{3,2,1,0:T(8,128)(2,1)S(1)}, bf16[2,3,38,256]{3,2,1,0:T(8,128)(2,1)S(1)}, u32[]{:S(2)}, u32[]{:S(2)}) collective-permute-start(bf16[2,3,38,256]{3,2,1,0:T(8,128)(2,1)S(1)} %get-tuple-element.81), channel_id=1, source_target_pairs={{8,16},{24,0},{16,8},{0,24},{9,17},{25,1},{17,9},{1,25},{10,18},{2... | collective-permute-start | bytes 350216 | tf_op jit(solution)/shard_map/ppermute | solution.py:33
  13.4 4.3 %collective-permute-start.5 = (bf16[2,1,4,2,8,256]{5,4,3,2,0,1:T(8,128)(2,1)S(1)}, bf16[2,1,4,2,8,256]{5,4,3,2,0,1:T(8,128)(2,1)S(1)}, u32[]{:S(2)}, u32[]{:S(2)}) collective-permute-start(bf16[2,1,4,2,8,256]{5,4,3,2,0,1:T(8,128)(2,1)S(1)} %bitcast.40), channel_id=1, source_target_pairs={{0,8},{8,0},{16,24},{24,16},{1,9},{9,1},{17,25},{25,17},{2,10},{10... | collective-permute-start | bytes 196616 | tf_op jit(solution)/shard_map/ppermute | solution.py:20
  16.3 1.4 %copy-start.1 = (bf16[1024,256]{1,0:T(8,128)(2,1)S(1)}, bf16[1024,256]{1,0:T(8,128)(2,1)}, u32[]{:S(2)}) copy-start(bf16[1024,256]{1,0:T(8,128)(2,1)} %w_out_ref.3) | copy-start | bytes 1572868
  16.4 1.4 %copy-start = (bf16[256,1024]{1,0:T(8,128)(2,1)S(1)}, bf16[256,1024]{1,0:T(8,128)(2,1)}, u32[]{:S(2)}) copy-start(bf16[256,1024]{1,0:T(8,128)(2,1)} %w_in_ref.3) | copy-start | bytes 1572868
  19.0 3.0 %collective-permute-start.13 = (bf16[512,256]{1,0:T(8,128)(2,1)S(1)}, bf16[512,256]{1,0:T(8,128)(2,1)S(1)}, u32[]{:S(2)}, u32[]{:S(2)}) collective-permute-start(bf16[512,256]{1,0:T(8,128)(2,1)S(1)} %get-tuple-element.45), channel_id=1, source_target_pairs={{0,8},{8,0},{16,24},{24,16},{1,9},{9,1},{17,25},{25,17},{2,10},{10... | collective-permute-start | bytes 786440 | tf_op jit(solution)/shard_map/ppermute | solution.py:20
  20.4 1.8 %collective-permute-start.6 = (bf16[512,256]{1,0:T(8,128)(2,1)S(1)}, bf16[512,256]{1,0:T(8,128)(2,1)S(1)}, u32[]{:S(2)}, u32[]{:S(2)}) collective-permute-start(bf16[512,256]{1,0:T(8,128)(2,1)S(1)} %get-tuple-element.41), channel_id=1, source_target_pairs={{0,8},{8,0},{16,24},{24,16},{1,9},{9,1},{17,25},{25,17},{2,10},{10... | collective-permute-start | bytes 786440 | tf_op jit(solution)/shard_map/ppermute | solution.py:20
  20.6 1.7 %collective-permute-start.7 = (bf16[2,3,32,256]{3,2,1,0:T(8,128)(2,1)S(1)}, bf16[2,3,32,256]{3,2,1,0:T(8,128)(2,1)S(1)}, u32[]{:S(2)}, u32[]{:S(2)}) collective-permute-start(bf16[2,3,32,256]{3,2,1,0:T(8,128)(2,1)S(1)} %get-tuple-element.83), channel_id=1, source_target_pairs={{0,8},{8,0},{16,24},{24,16},{1,9},{9,1},{17,25},{25,17},{2,10},{10... | collective-permute-start | bytes 294920 | tf_op jit(solution)/shard_map/ppermute | solution.py:20
  22.1 5.6 %collective-permute-start.14 = (bf16[256,256]{1,0:T(8,128)(2,1)S(1)}, bf16[256,256]{1,0:T(8,128)(2,1)S(1)}, u32[]{:S(2)}, u32[]{:S(2)}) collective-permute-start(bf16[256,256]{1,0:T(8,128)(2,1)S(1)} %get-tuple-element.69), channel_id=1, source_target_pairs={{0,2},{1,3},{2,0},{3,1},{4,6},{5,7},{6,4},{7,5},{8,10},{9,11},{10,... | collective-permute-start | bytes 393224 | tf_op jit(solution)/shard_map/ppermute | solution.py:20
  22.3 8.0 %collective-permute-start.8 = (bf16[480,256]{1,0:T(8,128)(2,1)S(1)}, bf16[480,256]{1,0:T(8,128)(2,1)S(1)}, u32[]{:S(2)}, u32[]{:S(2)}) collective-permute-start(bf16[480,256]{1,0:T(8,128)(2,1)S(1)} %pad_maximum_fusion.2), channel_id=1, source_target_pairs={{0,16},{8,24},{16,0},{24,8},{1,17},{9,25},{17,1},{25,9},{2,18},{10... | collective-permute-start | bytes 737288 | tf_op jit(solution)/shard_map/ppermute | solution.py:20
  23.9 6.5 %collective-permute-start.9 = (bf16[2,3,32,256]{3,2,1,0:T(8,128)(2,1)S(1)}, bf16[2,3,32,256]{3,2,1,0:T(8,128)(2,1)S(1)}, u32[]{:S(2)}, u32[]{:S(2)}) collective-permute-start(bf16[2,3,32,256]{3,2,1,0:T(8,128)(2,1)S(1)} %get-tuple-element.84), channel_id=1, source_target_pairs={{0,8},{8,0},{16,24},{24,16},{1,9},{9,1},{17,25},{25,17},{2,10},{10... | collective-permute-start | bytes 294920 | tf_op jit(solution)/shard_map/ppermute | solution.py:20
  27.7 5.7 %collective-permute-start.15 = (bf16[128,256]{1,0:T(8,128)(2,1)S(1)}, bf16[128,256]{1,0:T(8,128)(2,1)S(1)}, u32[]{:S(2)}, u32[]{:S(2)}) collective-permute-start(bf16[128,256]{1,0:T(8,128)(2,1)S(1)} %get-tuple-element.73), channel_id=1, source_target_pairs={{0,4},{1,5},{2,6},{3,7},{4,0},{5,1},{6,2},{7,3},{8,12},{9,13},{10,... | collective-permute-start | bytes 196616 | tf_op jit(solution)/shard_map/ppermute | solution.py:20
  30.7 5.1 %collective-permute-start.10 = (bf16[264,256]{1,0:T(8,128)(2,1)S(1)}, bf16[264,256]{1,0:T(8,128)(2,1)S(1)}, u32[]{:S(2)}, u32[]{:S(2)}) collective-permute-start(bf16[264,256]{1,0:T(8,128)(2,1)S(1)} %pad_maximum_fusion.5), channel_id=1, source_target_pairs={{0,1},{1,0},{2,3},{3,2},{4,5},{5,4},{6,7},{7,6},{8,9},{9,8},{10,11... | collective-permute-start | bytes 405512 | tf_op jit(solution)/shard_map/ppermute | solution.py:20
  33.4 5.0 %collective-permute-start.16 = (f32[128,256]{1,0:T(8,128)S(1)}, f32[128,256]{1,0:T(8,128)S(1)}, u32[]{:S(2)}, u32[]{:S(2)}) collective-permute-start(f32[128,256]{1,0:T(8,128)S(1)} %convert_add_fusion.2), channel_id=1, source_target_pairs={{0,16},{8,24},{16,0},{24,8},{1,17},{9,25},{17,1},{25,9},{2,18},{10... | collective-permute-start | bytes 393224 | tf_op jit(solution)/shard_map/ppermute | solution.py:20
  35.9 5.9 %collective-permute-start.11 = (f32[204,256]{1,0:T(8,128)S(1)}, f32[204,256]{1,0:T(8,128)S(1)}, u32[]{:S(2)}, u32[]{:S(2)}) collective-permute-start(f32[204,256]{1,0:T(8,128)S(1)} %pad_maximum_fusion.3), channel_id=1, source_target_pairs={{0,2},{1,3},{2,0},{3,1},{4,6},{5,7},{6,4},{7,5},{8,10},{9,11},{10,... | collective-permute-start | bytes 626696 | tf_op jit(solution)/shard_map/ppermute | solution.py:20
  38.5 6.1 %collective-permute-start.17 = (bf16[128,256]{1,0:T(8,128)(2,1)S(1)}, bf16[128,256]{1,0:T(8,128)(2,1)S(1)}, u32[]{:S(2)}, u32[]{:S(2)}) collective-permute-start(bf16[128,256]{1,0:T(8,128)(2,1)S(1)} %get-tuple-element.65), channel_id=1, source_target_pairs={{0,1},{1,0},{2,3},{3,2},{4,5},{5,4},{6,7},{7,6},{8,9},{9,8},{10,11... | collective-permute-start | bytes 196616 | tf_op jit(solution)/shard_map/ppermute | solution.py:20
  41.9 5.7 %collective-permute-start.12 = (bf16[204,256]{1,0:T(8,128)(2,1)S(1)}, bf16[204,256]{1,0:T(8,128)(2,1)S(1)}, u32[]{:S(2)}, u32[]{:S(2)}) collective-permute-start(bf16[204,256]{1,0:T(8,128)(2,1)S(1)} %pad_maximum_fusion.6), channel_id=1, source_target_pairs={{0,4},{1,5},{2,6},{3,7},{4,0},{5,1},{6,2},{7,3},{8,12},{9,13},{10,... | collective-permute-start | bytes 313352 | tf_op jit(solution)/shard_map/ppermute | solution.py:20
  44.6 6.2 %collective-permute-start.18 = (bf16[1,128,256]{2,1,0:T(8,128)(2,1)S(1)}, bf16[1,128,256]{2,1,0:T(8,128)(2,1)S(1)}, u32[]{:S(2)}, u32[]{:S(2)}) collective-permute-start(bf16[1,128,256]{2,1,0:T(8,128)(2,1)S(1)} %fusion.1), channel_id=1, source_target_pairs={{0,4},{1,5},{2,6},{3,7},{4,0},{5,1},{6,2},{7,3},{8,12},{9,13},{10,... | collective-permute-start | bytes 196616 | tf_op jit(solution)/shard_map/ppermute | solution.py:20
  47.7 5.5 %collective-permute-start.20 = (bf16[1,288,128]{2,1,0:T(8,128)(2,1)S(1)}, bf16[1,288,128]{2,1,0:T(8,128)(2,1)S(1)}, u32[]{:S(2)}, u32[]{:S(2)}) collective-permute-start(bf16[1,288,128]{2,1,0:T(8,128)(2,1)S(1)} %finish_columns.1), channel_id=1, source_target_pairs={{0,1},{1,0},{2,3},{3,2},{4,5},{5,4},{6,7},{7,6},{8,9},{9,8},{10,11... | collective-permute-start | bytes 221192 | tf_op jit(solution)/shard_map/ppermute | solution.py:20
  50.8 5.0 %collective-permute-start.19 = (bf16[2,128,256]{2,1,0:T(8,128)(2,1)S(1)}, bf16[2,128,256]{2,1,0:T(8,128)(2,1)S(1)}, u32[]{:S(2)}, u32[]{:S(2)}) collective-permute-start(bf16[2,128,256]{2,1,0:T(8,128)(2,1)S(1)} %maximum_select_fusion.4), channel_id=1, source_target_pairs={{0,2},{1,3},{2,0},{3,1},{4,6},{5,7},{6,4},{7,5},{8,10},{9,11},{10,... | collective-permute-start | bytes 393224 | tf_op jit(solution)/shard_map/ppermute | solution.py:20
  53.2 5.7 %collective-permute-start.21 = (bf16[2,288,128]{2,1,0:T(8,128)(2,1)S(1)}, bf16[2,288,128]{2,1,0:T(8,128)(2,1)S(1)}, u32[]{:S(2)}, u32[]{:S(2)}) collective-permute-start(bf16[2,288,128]{2,1,0:T(8,128)(2,1)S(1)} %maximum_select_fusion.1.mine), channel_id=1, source_target_pairs={{0,16},{8,24},{16,0},{24,8},{1,17},{9,25},{17,1},{25,9},{2,18},{10... | collective-permute-start | bytes 442376 | tf_op jit(solution)/shard_map/ppermute | solution.py:20
  55.9 1.9 %collective-permute-start.22 = (bf16[4,128,256]{2,1,0:T(8,128)(2,1)S(1)}, bf16[4,128,256]{2,1,0:T(8,128)(2,1)S(1)}, u32[]{:S(2)}, u32[]{:S(2)}) collective-permute-start(bf16[4,128,256]{2,1,0:T(8,128)(2,1)S(1)} %maximum_select_fusion._.mine), channel_id=1, source_target_pairs={{0,8},{8,0},{16,24},{24,16},{1,9},{9,1},{17,25},{25,17},{2,10},{10... | collective-permute-start | bytes 786440 | tf_op jit(solution)/shard_map/ppermute | solution.py:20
  58.9 1.8 %collective-permute-start.23 = (bf16[4,288,128]{2,1,0:T(8,128)(2,1)S(1)}, bf16[4,288,128]{2,1,0:T(8,128)(2,1)S(1)}, u32[]{:S(2)}, u32[]{:S(2)}) collective-permute-start(bf16[4,288,128]{2,1,0:T(8,128)(2,1)S(1)} %join.1.mine), channel_id=1, source_target_pairs={{0,8},{8,0},{16,24},{24,16},{1,9},{9,1},{17,25},{25,17},{2,10},{10... | collective-permute-start | bytes 884744 | tf_op jit(solution)/shard_map/ppermute | solution.py:20

commit v8 on v7

--- a/solution.py
+++ b/solution.py
@@ -237,37 +237,72 @@
             wide[group, b, :, :cols, :] = padded_ref[b, :, :, lanes].astype(jnp.float32)
 
 
-def stencil(wide, params, group, b, tile_rows, tile_cols, flipped):
-    kernel_size = wide.shape[2] - tile_rows + 1
+def stencil(wide, params, group, b, rows, tile_cols, used, first, flipped):
     lanes = slice(group * lane_count, (group + 1) * lane_count)
-    rows = [None] * tile_rows
-    for q in range(kernel_size):
-        for r in range(tile_rows + kernel_size - 1):
-            shifted = wide[group, b, r, q : q + tile_cols, :]
-            for i in range(max(0, r - kernel_size + 1), min(tile_rows, r + 1)):
+    rows = list(rows)
+    for q in range(kernel_side):
+        for r in used:
+            shifted = wide[group, b, r - first, q : q + tile_cols, :]
+            for i in range(max(0, r - kernel_side + 1), min(len(rows), r + 1)):
                 p = r - i
-                tap = (kernel_size - 1 - p, kernel_size - 1 - q) if flipped else (p, q)
-                term = params[pl.ds(tap[0] * kernel_size + tap[1], 1), lanes] * shifted
+                tap = (kernel_side - 1 - p, kernel_side - 1 - q) if flipped else (p, q)
+                term = params[pl.ds(tap[0] * kernel_side + tap[1], 1), lanes] * shifted
                 rows[i] = term if rows[i] is None else rows[i] + term
     return rows
 
 
-def conv_norm_kernel(padded_ref, params_ref, normed_ref, unit_ref, inv_ref, wide, smooth):
+def conv_own_kernel(block_ref, params_ref, _w_in_ref, _w_out_ref, out_ref, wide):
+    batch_size, tile_rows, pad_cols, _ = block_ref.shape
+    tile_cols = pad_cols - kernel_side + 1
+    first = kernel_side // 2
+    spread(block_ref, wide)
+    for group in range(wide.shape[0]):
+        for b in range(batch_size):
+            rows = stencil(
+                wide, params_ref, group, b, [None] * tile_rows, tile_cols,
+                range(first, first + tile_rows), first, False,
+            )
+            for i, row in enumerate(rows):
+                at = (b * tile_rows + i) * tile_cols
+                out_ref[group, at : at + tile_cols, :] = row
+
+
+def conv_own(block, params, w_in, w_out):
+    batch_size, tile_rows, pad_cols, channel_count = block.shape
+    cells = batch_size * tile_rows * (pad_cols - kernel_side + 1)
+    groups = channel_count // lane_count
+    return pl.pallas_call(
+        conv_own_kernel,
+        out_shape=jax.ShapeDtypeStruct((groups, cells, lane_count), jnp.float32),
+        in_specs=vmem_specs(4),
+        out_specs=pl.BlockSpec(memory_space=pltpu.VMEM),
+        scratch_shapes=[
+            pltpu.VMEM((groups, batch_size, tile_rows, round_up(pad_cols, 8), lane_count), jnp.float32)
+        ],
+        compiler_params=pltpu.CompilerParams(vmem_limit_bytes=6 << 20),
+        cost_estimate=pl.CostEstimate(flops=64 * cells * channel_count, bytes_accessed=1 << 20, transcendentals=0),
+        name="conv_own",
+    )(block, params, w_in, w_out)
+
+
+def conv_norm_kernel(own_ref, padded_ref, params_ref, normed_ref, unit_ref, inv_ref, wide, smooth):
     batch_size, pad_rows, pad_cols, channel_count = padded_ref.shape
     cells = smooth.shape[1]
     tile_rows = pad_rows - kernel_side + 1
     tile_cols = pad_cols - kernel_side + 1
     spread(padded_ref, wide)
+    first = kernel_side // 2
+    used = [r for r in range(pad_rows) if r < first or r >= first + tile_rows]
     for group in range(wide.shape[0]):
-
-        def one(b, _):
-            rows = stencil(wide, params_ref, group, b, tile_rows, tile_cols, False)
-            for i, row in enumerate(rows):
-                smooth[group, pl.ds((b * tile_rows + i) * tile_cols, tile_cols), :] = row
-            return 0
-
         for b in range(batch_size):
-            one(b, 0)
+            places = [
+                slice(at, at + tile_cols)
+                for at in range(b * tile_rows * tile_cols, (b + 1) * tile_rows * tile_cols, tile_cols)
+            ]
+            rows = [own_ref[group, at, :] for at in places]
+            rows = stencil(wide, params_ref, group, b, rows, tile_cols, used, 0, False)
+            for at, row in zip(places, rows):
+                smooth[group, at, :] = row
     gain = params_ref[gain_row : gain_row + 1, :]
     block = 32
 
@@ -291,7 +326,7 @@
     return -(-value // unit) * unit
 
 
-def conv_norm(padded, params):
+def conv_norm(own, padded, params):
     batch_size, pad_rows, pad_cols, channel_count = padded.shape
     cells = batch_size * (pad_rows - kernel_side + 1) * (pad_cols - kernel_side + 1)
     groups = channel_count // lane_count
@@ -309,7 +344,7 @@
         compiler_params=pltpu.CompilerParams(vmem_limit_bytes=6 << 20),
         cost_estimate=pl.CostEstimate(flops=2 * 49 * cells * channel_count, bytes_accessed=1 << 20, transcendentals=0),
         name="conv_norm",
-    )(padded, params)
+    )(own, padded, params)
 
 
 def conv_back_kernel(padded_ref, params_ref, misfit_ref, _, out_ref, mark_ref, wide):
@@ -320,7 +355,10 @@
         lanes = slice(group * lane_count, (group + 1) * lane_count)
 
         def one(b, _):
-            rows = stencil(wide, params_ref, group, b, tile_rows, tile_cols, True)
+            rows = stencil(
+                wide, params_ref, group, b, [None] * tile_rows, tile_cols,
+                range(wide.shape[2]), 0, True,
+            )
             for i, row in enumerate(rows):
                 out_ref[b, i, :, lanes] = (misfit_ref[b, i, :, lanes] + row).astype(out_ref.dtype)
             return 0
@@ -618,7 +656,7 @@
     lon_padded = with_edges(student, from_inner, from_outer, "lon", 2)
     lon_padded = after(lon_padded, params)
     padded_bf = with_halo(lon_padded, "lat", 1, half_kernel, False)
-    normed, unit_norm, inv_std = conv_norm(padded_bf, params)
+    normed, unit_norm, inv_std = conv_norm(conv_own(lon_padded, params, w_in, w_out), padded_bf, params)
     target = to_bands(teacher, "lat")
     upper = lax.axis_index("lat") % 2
     side = upper.astype(jnp.int32).reshape(1)
@@ -650,7 +688,7 @@
         in_mine, in_got = in_chunks, swap(in_chunks, *in_stage)
         if in_stage != in_halved[0]:
             in_chunks = in_order(in_mine, in_got, *in_stage)
-    grad_student, mark = conv_back(padded_grad, params, misfit.reshape(student.shape), out_chunks)
+    grad_student, mark = conv_back(padded_grad, params, misfit.reshape(student.shape), in_chunk)
     sum_out, mark = assemble_rows(side, out_chunks, swap(out_chunks, "lat", 1), mark)
     axis, bit = in_halved[0]
     place = ((lax.axis_index(axis) // bit) % 2).astype(jnp.int32).reshape(1)

time: 61.9 us -> 61.2 us (0.989)
    pallas_call x1, Pallas kernels: 1.3 us -> 0.62 us  [conv_norm(): pl.pallas_call(conv_norm_kernel, out_shape=(jax.ShapeDtypeStruct((cells,...]
where the time goes in v8:
time: 61.2 us; the launch traced here: 61 us
  starting transfers between devices  25.8 us (42%)
  waiting for transfers between devices  23 us (38%)
  Pallas kernels  7.96 us (13%)
  other arithmetic  1.93 us (3%)
  between operations  1.16 us (2%)
  local copies, waits for them, and re-layouts  1.09 us (2%)
    ppermute x22, starting transfers between devices, swap(): lax.ppermute(value, axis, [(i, i ^ bit) for i in range(lax.axis_size(axis...  20.7 us
    ppermute x22, waiting for transfers between devices, swap(): lax.ppermute(value, axis, [(i, i ^ bit) for i in range(lax.axis_size(axis...  19.9 us
    ppermute x2, starting transfers between devices, swap_outer(): got = lax.ppermute(edge, axis, pairs + [(j, i) for i, j in pairs])  5.15 us
    ppermute x2, waiting for transfers between devices, swap_outer(): got = lax.ppermute(edge, axis, pairs + [(j, i) for i, j in pairs])  3.13 us
    pallas_call x1, Pallas kernels, conv_back(): pl.pallas_call(conv_back_kernel, out_shape=(jax.ShapeDtypeStruct(misfit.s...  1.55 us
    pallas_call x1, Pallas kernels, forward(): pl.pallas_call(forward_kernel, in_specs=[pl.BlockSpec(memory_space=pltpu....  1.26 us
  transfers between devices with their start and end apart: 24, of which 13 were waited for; matrix products, arithmetic and copies ran while one was open for 2% of the time, Pallas kernels for 9%

profile of v8, /device:TPU:0, one launch (start us, length us, event | category | flops | bytes accessed | tf_op | source)
XLA Modules:
  0.0 61.0 jit_solution(15351184980703618829)
XLA Ops:
  0.7 0.8 %broadcast_select_fusion.14 = (bf16[2,4,3,256]{3,2,1,0:T(4,128)(2,1)S(1)}, bf16[2,4,3,256]{3,2,1,0:T(4,128)(2,1)S(1)}) fusion(pred[]{:T(512)S(6)} %eq.71, bf16[2,4,32,256]{3,2,1,0:T(8,128)(2,1)} %param.7), kind=kLoop, calls=%fused_computation.61 | loop fusion | flops 12288 | bytes 49153 | tf_op jit(solution)/shard_map/jit(_where)/select_n | solution.py:27
  1.5 3.0 %collective-permute-start = (bf16[2,4,3,256]{3,2,1,0:T(4,128)(2,1)S(1)}, bf16[2,4,3,256]{3,2,1,0:T(4,128)(2,1)S(1)}, u32[]{:S(2)}, u32[]{:S(2)}) collective-permute-start(bf16[2,4,3,256]{3,2,1,0:T(4,128)(2,1)S(1)} %get-tuple-element.89), channel_id=1, source_target_pairs={{0,1},{1,0},{2,3},{3,2},{4,5},{5,4},{6,7},{7,6},{8,9},{9,8},{10,11... | collective-permute-start | bytes 36872 | tf_op jit(solution)/shard_map/ppermute | solution.py:20
  4.5 3.5 %collective-permute-start.1 = (bf16[2,4,3,256]{3,2,1,0:T(4,128)(2,1)S(1)}, bf16[2,4,3,256]{3,2,1,0:T(4,128)(2,1)S(1)}, u32[]{:S(2)}, u32[]{:S(2)}) collective-permute-start(bf16[2,4,3,256]{3,2,1,0:T(4,128)(2,1)S(1)} %get-tuple-element.90), channel_id=1, source_target_pairs={{1,2},{3,4},{5,6},{7,0},{2,1},{4,3},{6,5},{0,7},{9,10},{11,12},{13... | collective-permute-start | bytes 36872 | tf_op jit(solution)/shard_map/ppermute | solution.py:33
  8.1 0.7 %copy-done.6 = f32[256]{0:T(256)S(1)} copy-done((f32[256]{0:T(256)S(1)}, f32[256]{0:T(256)}, u32[]{:S(2)}) %copy-start.6) | copy-done | bytes 1048
  9.0 1.6 %collective-permute-start.4 = (bf16[2,2,4,1,8,256]{5,4,2,1,0,3:T(8,128)(2,1)S(1)}, bf16[2,2,4,1,8,256]{5,4,2,1,0,3:T(8,128)(2,1)S(1)}, u32[]{:S(2)}, u32[]{:S(2)}) collective-permute-start(bf16[2,2,4,1,8,256]{5,4,2,1,0,3:T(8,128)(2,1)S(1)} %get-tuple-element.87), channel_id=1, source_target_pairs={{0,16},{8,24},{16,0},{24,8},{1,17},{9,25},{17,1},{25,9},{2,18},{10... | collective-permute-start | bytes 196616 | tf_op jit(solution)/shard_map/ppermute | solution.py:20
  11.2 1.6 %collective-permute-start.3 = (bf16[2,3,38,256]{3,2,1,0:T(8,128)(2,1)S(1)}, bf16[2,3,38,256]{3,2,1,0:T(8,128)(2,1)S(1)}, u32[]{:S(2)}, u32[]{:S(2)}) collective-permute-start(bf16[2,3,38,256]{3,2,1,0:T(8,128)(2,1)S(1)} %get-tuple-element.81), channel_id=1, source_target_pairs={{8,16},{24,0},{16,8},{0,24},{9,17},{25,1},{17,9},{1,25},{10,18},{2... | collective-permute-start | bytes 350216 | tf_op jit(solution)/shard_map/ppermute | solution.py:33
  13.5 2.8 %collective-permute-done.3 = bf16[2,3,38,256]{3,2,1,0:T(8,128)(2,1)S(1)} collective-permute-done((bf16[2,3,38,256]{3,2,1,0:T(8,128)(2,1)S(1)}, bf16[2,3,38,256]{3,2,1,0:T(8,128)(2,1)S(1)}, u32[]{:S(2)}, u32[]{:S(2)}) %collective-permute-start.3) | collective-permute-done | bytes 116768 | tf_op jit(solution)/shard_map/ppermute | solution.py:33
  16.4 0.6 %conv_norm.1 = (bf16[256,256]{1,0:T(8,128)(2,1)S(1)}, f32[256,256]{1,0:T(8,128)S(1)}, f32[256,1]{1,0:T(8,128)S(1)}) custom-call(f32[2,256,128]{2,1,0:T(8,128)S(1)} %conv_own.1.own_ref, bf16[2,10,38,256]{3,2,1,0:T(8,128)(2,1)S(1)} %pad_maximum_fusion.padded_ref, f32[51,256]{1,0:T(8,128)S(1)} %pad_maximum_fusion.8.params_ref), custom_call_target="tpu_custom_call" | custom-call | flops 6422528 | bytes 1048576 | tf_op jit(solution)/shard_map/conv_norm/pallas_call | solution.py:333
  17.0 1.3 %forward.1 = (f32[256,1024]{1,0:T(8,128)S(1)}, f32[256,256]{1,0:T(8,128)S(1)}, bf16[256,256]{1,0:T(8,128)(2,1)S(1)}, bf16[512,256]{1,0:T(8,128)(2,1)S(1)}, f32[512,256]{1,0:T(8,128)S(1)}) custom-call(s32[1]{0:T(128)} %bitcast.side_ref, bf16[256,256]{1,0:T(8,128)(2,1)S(1)} %get-tuple-element.34.normed_ref, bf16[256,256]{1,0:T(8,128)(2,1)S(1)} %bitcast.33, ...), custom_call_target="tpu_custom_call" | custom-call | flops 402653184 | bytes 4194304 | tf_op jit(solution)/shard_map/forward/pallas_call | solution.py:574
  18.8 0.9 %backward.1 = (bf16[256,256]{1,0:T(8,128)(2,1)S(1)}, bf16[512,256]{1,0:T(8,128)(2,1)S(1)}, f32[512,256]{1,0:T(8,128)S(1)}) custom-call(s32[1]{0:T(128)} %bitcast.side_ref, f32[256,1024]{1,0:T(8,128)S(1)} %get-tuple-element.36.slope_ref, bf16[256,256]{1,0:T(8,128)(2,1)S(1)} %get-tuple-element.37.out_grad_ref, ...), custom_call_target="tpu_custom_call" | custom-call | flops 402653184 | bytes 4194304 | tf_op jit(solution)/shard_map/backward/pallas_call | solution.py:626
  20.3 1.0 %tap_sums.1 = f32[64,256]{1,0:T(8,128)S(1)} custom-call(bf16[2,10,38,256]{3,2,1,0:T(8,128)(2,1)S(1)} %pad_maximum_fusion.padded_ref, bf16[2,4,32,256]{3,2,1,0:T(8,128)(2,1)S(1)} %bitcast.30), custom_call_target="tpu_custom_call" | custom-call | flops 6422528 | bytes 1048576 | tf_op jit(solution)/shard_map/tap_sums/pallas_call | solution.py:424
  21.6 1.6 %collective-permute-start.8 = (bf16[480,256]{1,0:T(8,128)(2,1)S(1)}, bf16[480,256]{1,0:T(8,128)(2,1)S(1)}, u32[]{:S(2)}, u32[]{:S(2)}) collective-permute-start(bf16[480,256]{1,0:T(8,128)(2,1)S(1)} %pad_maximum_fusion.2), channel_id=1, source_target_pairs={{0,16},{8,24},{16,0},{24,8},{1,17},{9,25},{17,1},{25,9},{2,18},{10... | collective-permute-start | bytes 737288 | tf_op jit(solution)/shard_map/ppermute | solution.py:20
  23.1 3.8 %collective-permute-done.16 = bf16[256,256]{1,0:T(8,128)(2,1)S(1)} collective-permute-done((bf16[256,256]{1,0:T(8,128)(2,1)S(1)}, bf16[256,256]{1,0:T(8,128)(2,1)S(1)}, u32[]{:S(2)}, u32[]{:S(2)}) %collective-permute-start.16) | collective-permute-done | bytes 131104 | tf_op jit(solution)/shard_map/ppermute | solution.py:20
  27.0 0.9 %collective-permute-start.17 = (bf16[128,256]{1,0:T(8,128)(2,1)S(1)}, bf16[128,256]{1,0:T(8,128)(2,1)S(1)}, u32[]{:S(2)}, u32[]{:S(2)}) collective-permute-start(bf16[128,256]{1,0:T(8,128)(2,1)S(1)} %get-tuple-element.73), channel_id=1, source_target_pairs={{0,4},{1,5},{2,6},{3,7},{4,0},{5,1},{6,2},{7,3},{8,12},{9,13},{10,... | collective-permute-start | bytes 196616 | tf_op jit(solution)/shard_map/ppermute | solution.py:20
  27.8 1.8 %collective-permute-done.8 = bf16[480,256]{1,0:T(8,128)(2,1)S(1)} collective-permute-done((bf16[480,256]{1,0:T(8,128)(2,1)S(1)}, bf16[480,256]{1,0:T(8,128)(2,1)S(1)}, u32[]{:S(2)}, u32[]{:S(2)}) %collective-permute-start.8) | collective-permute-done | bytes 245792 | tf_op jit(solution)/shard_map/ppermute | solution.py:20
  30.5 2.2 %collective-permute-done.17 = bf16[128,256]{1,0:T(8,128)(2,1)S(1)} collective-permute-done((bf16[128,256]{1,0:T(8,128)(2,1)S(1)}, bf16[128,256]{1,0:T(8,128)(2,1)S(1)}, u32[]{:S(2)}, u32[]{:S(2)}) %collective-permute-start.17) | collective-permute-done | bytes 65568 | tf_op jit(solution)/shard_map/ppermute | solution.py:20
  32.7 1.6 %collective-permute-start.18 = (f32[128,256]{1,0:T(8,128)S(1)}, f32[128,256]{1,0:T(8,128)S(1)}, u32[]{:S(2)}, u32[]{:S(2)}) collective-permute-start(f32[128,256]{1,0:T(8,128)S(1)} %convert_add_fusion.2), channel_id=1, source_target_pairs={{0,16},{8,24},{16,0},{24,8},{1,17},{9,25},{17,1},{25,9},{2,18},{10... | collective-permute-start | bytes 393224 | tf_op jit(solution)/shard_map/ppermute | solution.py:20
  34.2 0.9 %collective-permute-done.10 = bf16[264,256]{1,0:T(8,128)(2,1)S(1)} collective-permute-done((bf16[264,256]{1,0:T(8,128)(2,1)S(1)}, bf16[264,256]{1,0:T(8,128)(2,1)S(1)}, u32[]{:S(2)}, u32[]{:S(2)}) %collective-permute-start.10) | collective-permute-done | bytes 135200 | tf_op jit(solution)/shard_map/ppermute | solution.py:20
  35.2 1.8 %collective-permute-start.11 = (f32[204,256]{1,0:T(8,128)S(1)}, f32[204,256]{1,0:T(8,128)S(1)}, u32[]{:S(2)}, u32[]{:S(2)}) collective-permute-start(f32[204,256]{1,0:T(8,128)S(1)} %pad_maximum_fusion.3), channel_id=1, source_target_pairs={{0,2},{1,3},{2,0},{3,1},{4,6},{5,7},{6,4},{7,5},{8,10},{9,11},{10,... | collective-permute-start | bytes 626696 | tf_op jit(solution)/shard_map/ppermute | solution.py:20
  36.9 0.8 %collective-permute-done.18 = f32[128,256]{1,0:T(8,128)S(1)} collective-permute-done((f32[128,256]{1,0:T(8,128)S(1)}, f32[128,256]{1,0:T(8,128)S(1)}, u32[]{:S(2)}, u32[]{:S(2)}) %collective-permute-start.18) | collective-permute-done | bytes 131104 | tf_op jit(solution)/shard_map/ppermute | solution.py:20
  37.9 3.2 %collective-permute-done.11 = f32[204,256]{1,0:T(8,128)S(1)} collective-permute-done((f32[204,256]{1,0:T(8,128)S(1)}, f32[204,256]{1,0:T(8,128)S(1)}, u32[]{:S(2)}, u32[]{:S(2)}) %collective-permute-start.11) | collective-permute-done | bytes 208928 | tf_op jit(solution)/shard_map/ppermute | solution.py:20
  41.2 2.7 %collective-permute-start.12 = (bf16[204,256]{1,0:T(8,128)(2,1)S(1)}, bf16[204,256]{1,0:T(8,128)(2,1)S(1)}, u32[]{:S(2)}, u32[]{:S(2)}) collective-permute-start(bf16[204,256]{1,0:T(8,128)(2,1)S(1)} %pad_maximum_fusion.6), channel_id=1, source_target_pairs={{0,4},{1,5},{2,6},{3,7},{4,0},{5,1},{6,2},{7,3},{8,12},{9,13},{10,... | collective-permute-start | bytes 313352 | tf_op jit(solution)/shard_map/ppermute | solution.py:20
  44.2 2.6 %collective-permute-done.12.got_ref = bf16[204,256]{1,0:T(8,128)(2,1)S(1)} collective-permute-done((bf16[204,256]{1,0:T(8,128)(2,1)S(1)}, bf16[204,256]{1,0:T(8,128)(2,1)S(1)}, u32[]{:S(2)}, u32[]{:S(2)}) %collective-permute-start.12) | collective-permute-done | bytes 104480 | tf_op jit(solution)/shard_map/ppermute | solution.py:20
  46.9 3.1 %collective-permute-start.13 = (bf16[1,288,128]{2,1,0:T(8,128)(2,1)S(1)}, bf16[1,288,128]{2,1,0:T(8,128)(2,1)S(1)}, u32[]{:S(2)}, u32[]{:S(2)}) collective-permute-start(bf16[1,288,128]{2,1,0:T(8,128)(2,1)S(1)} %finish_columns.1._), channel_id=1, source_target_pairs={{0,1},{1,0},{2,3},{3,2},{4,5},{5,4},{6,7},{7,6},{8,9},{9,8},{10,11... | collective-permute-start | bytes 221192 | tf_op jit(solution)/shard_map/ppermute | solution.py:20
  50.2 2.2 %collective-permute-done.13 = bf16[1,288,128]{2,1,0:T(8,128)(2,1)S(1)} collective-permute-done((bf16[1,288,128]{2,1,0:T(8,128)(2,1)S(1)}, bf16[1,288,128]{2,1,0:T(8,128)(2,1)S(1)}, u32[]{:S(2)}, u32[]{:S(2)}) %collective-permute-start.13) | collective-permute-done | bytes 73760 | tf_op jit(solution)/shard_map/ppermute | solution.py:20
  52.4 1.6 %collective-permute-start.14 = (bf16[2,288,128]{2,1,0:T(8,128)(2,1)S(1)}, bf16[2,288,128]{2,1,0:T(8,128)(2,1)S(1)}, u32[]{:S(2)}, u32[]{:S(2)}) collective-permute-start(bf16[2,288,128]{2,1,0:T(8,128)(2,1)S(1)} %maximum_select_fusion.1.mine), channel_id=1, source_target_pairs={{0,16},{8,24},{16,0},{24,8},{1,17},{9,25},{17,1},{25,9},{2,18},{10... | collective-permute-start | bytes 442376 | tf_op jit(solution)/shard_map/ppermute | solution.py:20
  54.0 1.1 %collective-permute-done.21 = bf16[2,128,256]{2,1,0:T(8,128)(2,1)S(1)} collective-permute-done((bf16[2,128,256]{2,1,0:T(8,128)(2,1)S(1)}, bf16[2,128,256]{2,1,0:T(8,128)(2,1)S(1)}, u32[]{:S(2)}, u32[]{:S(2)}) %collective-permute-start.21) | collective-permute-done | bytes 131104 | tf_op jit(solution)/shard_map/ppermute | solution.py:20
  55.5 1.6 %conv_back.1 = (bf16[2,4,32,256]{3,2,1,0:T(8,128)(2,1)}, f32[8,128]{1,0:T(8,128)S(1)}) custom-call(bf16[2,10,38,256]{3,2,1,0:T(8,128)(2,1)S(1)} %pad_maximum_fusion.1.padded_ref, f32[51,256]{1,0:T(8,128)S(1)} %pad_maximum_fusion.8.params_ref, f32[2,4,32,256]{3,2,1,0:T(8,128)S(1)} %bitcast.35, bf16[1,288,128]{2,1,0:T(8,128)(2,1)S(1)} %finish_columns.1._), custom_call_target="tpu_custom_call" | custom-call | flops 6422528 | bytes 1048576 | tf_op jit(solution)/shard_map/conv_back/pallas_call | solution.py:373
  57.1 1.0 %assemble_rows.1 = (f32[1024,256]{1,0:T(8,128)}, f32[8,128]{1,0:T(8,128)S(1)}) custom-call(s32[1]{0:T(128)} %bitcast.side_ref, bf16[4,128,256]{2,1,0:T(8,128)(2,1)S(1)} %maximum_select_fusion.mine, bf16[4,128,256]{2,1,0:T(8,128)(2,1)S(1)} %collective-permute-done.22.got, f32[8,128]{1,0:T(8,128)S(1)} %get-tuple-element.55._), custom_call_target="tpu_custom_call" | custom-call | bytes 1572864 | tf_op jit(solution)/shard_map/assemble_rows/pallas_call | solution.py:484
  58.1 0.6 collective-permute-start.23
  58.7 1.2 %collective-permute-done.23.got = bf16[4,288,128]{2,1,0:T(8,128)(2,1)S(1)} collective-permute-done((bf16[4,288,128]{2,1,0:T(8,128)(2,1)S(1)}, bf16[4,288,128]{2,1,0:T(8,128)(2,1)S(1)}, u32[]{:S(2)}, u32[]{:S(2)}) %collective-permute-start.23) | collective-permute-done | bytes 294944 | tf_op jit(solution)/shard_map/ppermute | solution.py:20
  59.9 1.1 %assemble_columns.1 = (f32[256,1024]{1,0:T(8,128)}, f32[7,7,256]{2,1,0:T(8,128)}) custom-call(s32[1]{0:T(128)} %bitcast.side_ref, bf16[4,288,128]{2,1,0:T(8,128)(2,1)S(1)} %join.1.mine, bf16[4,288,128]{2,1,0:T(8,128)(2,1)S(1)} %collective-permute-done.23.got), custom_call_target="tpu_custom_call" | custom-call | bytes 1572864 | tf_op jit(solution)/shard_map/assemble_columns/pallas_call | solution.py:499
  (90 shorter events, 5.1 us)
Async XLA Ops:
  0.6 7.4 %copy-start.4 = (f32[7,7,256]{2,1,0:T(8,128)S(1)}, f32[7,7,256]{2,1,0:T(8,128)}, u32[]{:S(2)}) copy-start(f32[7,7,256]{2,1,0:T(8,128)} %param.9) | copy-start | bytes 150532
  1.5 9.1 %collective-permute-start = (bf16[2,4,3,256]{3,2,1,0:T(4,128)(2,1)S(1)}, bf16[2,4,3,256]{3,2,1,0:T(4,128)(2,1)S(1)}, u32[]{:S(2)}, u32[]{:S(2)}) collective-permute-start(bf16[2,4,3,256]{3,2,1,0:T(4,128)(2,1)S(1)} %get-tuple-element.89), channel_id=1, source_target_pairs={{0,1},{1,0},{2,3},{3,2},{4,5},{5,4},{6,7},{7,6},{8,9},{9,8},{10,11... | collective-permute-start | bytes 36872 | tf_op jit(solution)/shard_map/ppermute | solution.py:20
  4.5 6.4 %collective-permute-start.1 = (bf16[2,4,3,256]{3,2,1,0:T(4,128)(2,1)S(1)}, bf16[2,4,3,256]{3,2,1,0:T(4,128)(2,1)S(1)}, u32[]{:S(2)}, u32[]{:S(2)}) collective-permute-start(bf16[2,4,3,256]{3,2,1,0:T(4,128)(2,1)S(1)} %get-tuple-element.90), channel_id=1, source_target_pairs={{1,2},{3,4},{5,6},{7,0},{2,1},{4,3},{6,5},{0,7},{9,10},{11,12},{13... | collective-permute-start | bytes 36872 | tf_op jit(solution)/shard_map/ppermute | solution.py:33
  8.1 0.9 %copy-start.3 = (bf16[2,16,8,256]{3,2,1,0:T(8,128)(2,1)S(1)}, bf16[2,16,8,256]{3,2,1,0:T(8,128)(2,1)}, u32[]{:S(2)}) copy-start(bf16[2,16,8,256]{3,2,1,0:T(8,128)(2,1)} %param.8) | copy-start | bytes 393220
  8.1 0.7 %copy-start.6 = (f32[256]{0:T(256)S(1)}, f32[256]{0:T(256)}, u32[]{:S(2)}) copy-start(f32[256]{0:T(256)} %param.10) | copy-start | bytes 3076
  8.1 0.7 %copy-start.5 = (f32[256]{0:T(256)S(1)}, f32[256]{0:T(256)}, u32[]{:S(2)}) copy-start(f32[256]{0:T(256)} %param.13) | copy-start | bytes 3076
  8.8 2.2 %copy-start.2 = (bf16[2,4,32,256]{3,2,1,0:T(8,128)(2,1)S(1)}, bf16[2,4,32,256]{3,2,1,0:T(8,128)(2,1)}, u32[]{:S(2)}) copy-start(bf16[2,4,32,256]{3,2,1,0:T(8,128)(2,1)} %param.7) | copy-start | bytes 393220
  9.0 3.8 %copy-start.1 = (bf16[1024,256]{1,0:T(8,128)(2,1)S(1)}, bf16[1024,256]{1,0:T(8,128)(2,1)}, u32[]{:S(2)}) copy-start(bf16[1024,256]{1,0:T(8,128)(2,1)} %w_out_ref.3) | copy-start | bytes 1572868
  9.0 3.8 %copy-start = (bf16[256,1024]{1,0:T(8,128)(2,1)S(1)}, bf16[256,1024]{1,0:T(8,128)(2,1)}, u32[]{:S(2)}) copy-start(bf16[256,1024]{1,0:T(8,128)(2,1)} %w_in_ref.3) | copy-start | bytes 1572868
  9.0 4.3 %collective-permute-start.4 = (bf16[2,2,4,1,8,256]{5,4,2,1,0,3:T(8,128)(2,1)S(1)}, bf16[2,2,4,1,8,256]{5,4,2,1,0,3:T(8,128)(2,1)S(1)}, u32[]{:S(2)}, u32[]{:S(2)}) collective-permute-start(bf16[2,2,4,1,8,256]{5,4,2,1,0,3:T(8,128)(2,1)S(1)} %get-tuple-element.87), channel_id=1, source_target_pairs={{0,16},{8,24},{16,0},{24,8},{1,17},{9,25},{17,1},{25,9},{2,18},{10... | collective-permute-start | bytes 196616 | tf_op jit(solution)/shard_map/ppermute | solution.py:20
  11.1 2.4 %collective-permute-start.2 = (bf16[2,3,38,256]{3,2,1,0:T(8,128)(2,1)S(1)}, bf16[2,3,38,256]{3,2,1,0:T(8,128)(2,1)S(1)}, u32[]{:S(2)}, u32[]{:S(2)}) collective-permute-start(bf16[2,3,38,256]{3,2,1,0:T(8,128)(2,1)S(1)} %get-tuple-element.82), channel_id=1, source_target_pairs={{0,8},{8,0},{16,24},{24,16},{1,9},{9,1},{17,25},{25,17},{2,10},{10... | collective-permute-start | bytes 350216 | tf_op jit(solution)/shard_map/ppermute | solution.py:20
  11.2 5.1 %collective-permute-start.3 = (bf16[2,3,38,256]{3,2,1,0:T(8,128)(2,1)S(1)}, bf16[2,3,38,256]{3,2,1,0:T(8,128)(2,1)S(1)}, u32[]{:S(2)}, u32[]{:S(2)}) collective-permute-start(bf16[2,3,38,256]{3,2,1,0:T(8,128)(2,1)S(1)} %get-tuple-element.81), channel_id=1, source_target_pairs={{8,16},{24,0},{16,8},{0,24},{9,17},{25,1},{17,9},{1,25},{10,18},{2... | collective-permute-start | bytes 350216 | tf_op jit(solution)/shard_map/ppermute | solution.py:33
  13.4 3.6 %collective-permute-start.5 = (bf16[2,1,4,2,8,256]{5,4,3,2,0,1:T(8,128)(2,1)S(1)}, bf16[2,1,4,2,8,256]{5,4,3,2,0,1:T(8,128)(2,1)S(1)}, u32[]{:S(2)}, u32[]{:S(2)}) collective-permute-start(bf16[2,1,4,2,8,256]{5,4,3,2,0,1:T(8,128)(2,1)S(1)} %bitcast.40), channel_id=1, source_target_pairs={{0,8},{8,0},{16,24},{24,16},{1,9},{9,1},{17,25},{25,17},{2,10},{10... | collective-permute-start | bytes 196616 | tf_op jit(solution)/shard_map/ppermute | solution.py:20
  18.3 3.0 %collective-permute-start.15 = (bf16[512,256]{1,0:T(8,128)(2,1)S(1)}, bf16[512,256]{1,0:T(8,128)(2,1)S(1)}, u32[]{:S(2)}, u32[]{:S(2)}) collective-permute-start(bf16[512,256]{1,0:T(8,128)(2,1)S(1)} %get-tuple-element.46), channel_id=1, source_target_pairs={{0,8},{8,0},{16,24},{24,16},{1,9},{9,1},{17,25},{25,17},{2,10},{10... | collective-permute-start | bytes 786440 | tf_op jit(solution)/shard_map/ppermute | solution.py:20
  19.6 1.8 %collective-permute-start.6 = (bf16[512,256]{1,0:T(8,128)(2,1)S(1)}, bf16[512,256]{1,0:T(8,128)(2,1)S(1)}, u32[]{:S(2)}, u32[]{:S(2)}) collective-permute-start(bf16[512,256]{1,0:T(8,128)(2,1)S(1)} %get-tuple-element.41), channel_id=1, source_target_pairs={{0,8},{8,0},{16,24},{24,16},{1,9},{9,1},{17,25},{25,17},{2,10},{10... | collective-permute-start | bytes 786440 | tf_op jit(solution)/shard_map/ppermute | solution.py:20
  19.8 1.7 %collective-permute-start.7 = (bf16[2,3,32,256]{3,2,1,0:T(8,128)(2,1)S(1)}, bf16[2,3,32,256]{3,2,1,0:T(8,128)(2,1)S(1)}, u32[]{:S(2)}, u32[]{:S(2)}) collective-permute-start(bf16[2,3,32,256]{3,2,1,0:T(8,128)(2,1)S(1)} %get-tuple-element.83), channel_id=1, source_target_pairs={{0,8},{8,0},{16,24},{24,16},{1,9},{9,1},{17,25},{25,17},{2,10},{10... | collective-permute-start | bytes 294920 | tf_op jit(solution)/shard_map/ppermute | solution.py:20
  21.4 5.6 %collective-permute-start.16 = (bf16[256,256]{1,0:T(8,128)(2,1)S(1)}, bf16[256,256]{1,0:T(8,128)(2,1)S(1)}, u32[]{:S(2)}, u32[]{:S(2)}) collective-permute-start(bf16[256,256]{1,0:T(8,128)(2,1)S(1)} %get-tuple-element.69), channel_id=1, source_target_pairs={{0,2},{1,3},{2,0},{3,1},{4,6},{5,7},{6,4},{7,5},{8,10},{9,11},{10,... | collective-permute-start | bytes 393224 | tf_op jit(solution)/shard_map/ppermute | solution.py:20
  21.6 8.0 %collective-permute-start.8 = (bf16[480,256]{1,0:T(8,128)(2,1)S(1)}, bf16[480,256]{1,0:T(8,128)(2,1)S(1)}, u32[]{:S(2)}, u32[]{:S(2)}) collective-permute-start(bf16[480,256]{1,0:T(8,128)(2,1)S(1)} %pad_maximum_fusion.2), channel_id=1, source_target_pairs={{0,16},{8,24},{16,0},{24,8},{1,17},{9,25},{17,1},{25,9},{2,18},{10... | collective-permute-start | bytes 737288 | tf_op jit(solution)/shard_map/ppermute | solution.py:20
  23.1 6.5 %collective-permute-start.9 = (bf16[2,3,32,256]{3,2,1,0:T(8,128)(2,1)S(1)}, bf16[2,3,32,256]{3,2,1,0:T(8,128)(2,1)S(1)}, u32[]{:S(2)}, u32[]{:S(2)}) collective-permute-start(bf16[2,3,32,256]{3,2,1,0:T(8,128)(2,1)S(1)} %get-tuple-element.84), channel_id=1, source_target_pairs={{0,8},{8,0},{16,24},{24,16},{1,9},{9,1},{17,25},{25,17},{2,10},{10... | collective-permute-start | bytes 294920 | tf_op jit(solution)/shard_map/ppermute | solution.py:20
  27.0 5.7 %collective-permute-start.17 = (bf16[128,256]{1,0:T(8,128)(2,1)S(1)}, bf16[128,256]{1,0:T(8,128)(2,1)S(1)}, u32[]{:S(2)}, u32[]{:S(2)}) collective-permute-start(bf16[128,256]{1,0:T(8,128)(2,1)S(1)} %get-tuple-element.73), channel_id=1, source_target_pairs={{0,4},{1,5},{2,6},{3,7},{4,0},{5,1},{6,2},{7,3},{8,12},{9,13},{10,... | collective-permute-start | bytes 196616 | tf_op jit(solution)/shard_map/ppermute | solution.py:20
  30.0 5.1 %collective-permute-start.10 = (bf16[264,256]{1,0:T(8,128)(2,1)S(1)}, bf16[264,256]{1,0:T(8,128)(2,1)S(1)}, u32[]{:S(2)}, u32[]{:S(2)}) collective-permute-start(bf16[264,256]{1,0:T(8,128)(2,1)S(1)} %pad_maximum_fusion.5), channel_id=1, source_target_pairs={{0,1},{1,0},{2,3},{3,2},{4,5},{5,4},{6,7},{7,6},{8,9},{9,8},{10,11... | collective-permute-start | bytes 405512 | tf_op jit(solution)/shard_map/ppermute | solution.py:20
  32.7 5.0 %collective-permute-start.18 = (f32[128,256]{1,0:T(8,128)S(1)}, f32[128,256]{1,0:T(8,128)S(1)}, u32[]{:S(2)}, u32[]{:S(2)}) collective-permute-start(f32[128,256]{1,0:T(8,128)S(1)} %convert_add_fusion.2), channel_id=1, source_target_pairs={{0,16},{8,24},{16,0},{24,8},{1,17},{9,25},{17,1},{25,9},{2,18},{10... | collective-permute-start | bytes 393224 | tf_op jit(solution)/shard_map/ppermute | solution.py:20
  35.2 5.9 %collective-permute-start.11 = (f32[204,256]{1,0:T(8,128)S(1)}, f32[204,256]{1,0:T(8,128)S(1)}, u32[]{:S(2)}, u32[]{:S(2)}) collective-permute-start(f32[204,256]{1,0:T(8,128)S(1)} %pad_maximum_fusion.3), channel_id=1, source_target_pairs={{0,2},{1,3},{2,0},{3,1},{4,6},{5,7},{6,4},{7,5},{8,10},{9,11},{10,... | collective-permute-start | bytes 626696 | tf_op jit(solution)/shard_map/ppermute | solution.py:20
  37.7 6.1 %collective-permute-start.19 = (bf16[128,256]{1,0:T(8,128)(2,1)S(1)}, bf16[128,256]{1,0:T(8,128)(2,1)S(1)}, u32[]{:S(2)}, u32[]{:S(2)}) collective-permute-start(bf16[128,256]{1,0:T(8,128)(2,1)S(1)} %get-tuple-element.61), channel_id=1, source_target_pairs={{0,1},{1,0},{2,3},{3,2},{4,5},{5,4},{6,7},{7,6},{8,9},{9,8},{10,11... | collective-permute-start | bytes 196616 | tf_op jit(solution)/shard_map/ppermute | solution.py:20
  41.2 5.7 %collective-permute-start.12 = (bf16[204,256]{1,0:T(8,128)(2,1)S(1)}, bf16[204,256]{1,0:T(8,128)(2,1)S(1)}, u32[]{:S(2)}, u32[]{:S(2)}) collective-permute-start(bf16[204,256]{1,0:T(8,128)(2,1)S(1)} %pad_maximum_fusion.6), channel_id=1, source_target_pairs={{0,4},{1,5},{2,6},{3,7},{4,0},{5,1},{6,2},{7,3},{8,12},{9,13},{10,... | collective-permute-start | bytes 313352 | tf_op jit(solution)/shard_map/ppermute | solution.py:20
  43.9 6.2 %collective-permute-start.20 = (bf16[1,128,256]{2,1,0:T(8,128)(2,1)S(1)}, bf16[1,128,256]{2,1,0:T(8,128)(2,1)S(1)}, u32[]{:S(2)}, u32[]{:S(2)}) collective-permute-start(bf16[1,128,256]{2,1,0:T(8,128)(2,1)S(1)} %fusion.1), channel_id=1, source_target_pairs={{0,4},{1,5},{2,6},{3,7},{4,0},{5,1},{6,2},{7,3},{8,12},{9,13},{10,... | collective-permute-start | bytes 196616 | tf_op jit(solution)/shard_map/ppermute | solution.py:20
  46.9 5.5 %collective-permute-start.13 = (bf16[1,288,128]{2,1,0:T(8,128)(2,1)S(1)}, bf16[1,288,128]{2,1,0:T(8,128)(2,1)S(1)}, u32[]{:S(2)}, u32[]{:S(2)}) collective-permute-start(bf16[1,288,128]{2,1,0:T(8,128)(2,1)S(1)} %finish_columns.1._), channel_id=1, source_target_pairs={{0,1},{1,0},{2,3},{3,2},{4,5},{5,4},{6,7},{7,6},{8,9},{9,8},{10,11... | collective-permute-start | bytes 221192 | tf_op jit(solution)/shard_map/ppermute | solution.py:20
  50.1 5.0 %collective-permute-start.21 = (bf16[2,128,256]{2,1,0:T(8,128)(2,1)S(1)}, bf16[2,128,256]{2,1,0:T(8,128)(2,1)S(1)}, u32[]{:S(2)}, u32[]{:S(2)}) collective-permute-start(bf16[2,128,256]{2,1,0:T(8,128)(2,1)S(1)} %maximum_select_fusion.4), channel_id=1, source_target_pairs={{0,2},{1,3},{2,0},{3,1},{4,6},{5,7},{6,4},{7,5},{8,10},{9,11},{10,... | collective-permute-start | bytes 393224 | tf_op jit(solution)/shard_map/ppermute | solution.py:20
  52.4 5.7 %collective-permute-start.14 = (bf16[2,288,128]{2,1,0:T(8,128)(2,1)S(1)}, bf16[2,288,128]{2,1,0:T(8,128)(2,1)S(1)}, u32[]{:S(2)}, u32[]{:S(2)}) collective-permute-start(bf16[2,288,128]{2,1,0:T(8,128)(2,1)S(1)} %maximum_select_fusion.1.mine), channel_id=1, source_target_pairs={{0,16},{8,24},{16,0},{24,8},{1,17},{9,25},{17,1},{25,9},{2,18},{10... | collective-permute-start | bytes 442376 | tf_op jit(solution)/shard_map/ppermute | solution.py:20
  55.2 1.9 %collective-permute-start.22 = (bf16[4,128,256]{2,1,0:T(8,128)(2,1)S(1)}, bf16[4,128,256]{2,1,0:T(8,128)(2,1)S(1)}, u32[]{:S(2)}, u32[]{:S(2)}) collective-permute-start(bf16[4,128,256]{2,1,0:T(8,128)(2,1)S(1)} %maximum_select_fusion.mine), channel_id=1, source_target_pairs={{0,8},{8,0},{16,24},{24,16},{1,9},{9,1},{17,25},{25,17},{2,10},{10... | collective-permute-start | bytes 786440 | tf_op jit(solution)/shard_map/ppermute | solution.py:20
  58.1 1.8 %collective-permute-start.23 = (bf16[4,288,128]{2,1,0:T(8,128)(2,1)S(1)}, bf16[4,288,128]{2,1,0:T(8,128)(2,1)S(1)}, u32[]{:S(2)}, u32[]{:S(2)}) collective-permute-start(bf16[4,288,128]{2,1,0:T(8,128)(2,1)S(1)} %join.1.mine), channel_id=1, source_target_pairs={{0,8},{8,0},{16,24},{24,16},{1,9},{9,1},{17,25},{25,17},{2,10},{10... | collective-permute-start | bytes 884744 | tf_op jit(solution)/shard_map/ppermute | solution.py:20

commit v9 on v8

--- a/solution.py
+++ b/solution.py
@@ -567,32 +567,6 @@
     return [pl.BlockSpec(memory_space=pltpu.VMEM)] * count
 
 
-def forward(side, normed, student, target, w_in, w_out, params):
-    cells, channel_count = normed.shape
-    hidden_size = w_in.shape[1]
-    shape = jax.ShapeDtypeStruct
-    return pl.pallas_call(
-        forward_kernel,
-        in_specs=[pl.BlockSpec(memory_space=pltpu.SMEM)] + vmem_specs(6),
-        out_specs=vmem_specs(5),
-        out_shape=(
-            shape((cells, hidden_size), jnp.float32),
-            shape((cells, channel_count), jnp.float32),
-            shape((cells, channel_count), jnp.bfloat16),
-            shape((hidden_size // 2, channel_count), jnp.bfloat16),
-            shape((hidden_size // 2, channel_count), jnp.float32),
-        ),
-        scratch_shapes=[pltpu.VMEM((cells, hidden_size), jnp.bfloat16)],
-        compiler_params=pltpu.CompilerParams(vmem_limit_bytes=6 << 20),
-        cost_estimate=pl.CostEstimate(
-            flops=6 * cells * channel_count * hidden_size,
-            bytes_accessed=4 << 20,
-            transcendentals=cells * hidden_size,
-        ),
-        name="forward",
-    )(side, normed, student, target, w_in, w_out, params)
-
-
 def backward_kernel(
     side_ref, slope_ref, out_grad_ref, normed_ref, unit_ref, inv_ref, w_in_ref, w_out_ref, params_ref,
     conv_grad_ref, sent_ref, kept_ref, preact_grad,
@@ -619,26 +593,53 @@
     kept_ref[...] = product(half_columns(preact_grad, side), normed_ref[...], 0, 0)
 
 
-def backward(side, slope, out_grad, normed, unit_norm, inv_std, w_in, w_out, params):
+def mlp_kernel(
+    side_ref, normed_ref, unit_ref, inv_ref, student_ref, target_ref, w_in_ref, w_out_ref, params_ref,
+    misfit_ref, conv_grad_ref, out_sent, out_kept, in_sent, in_kept,
+    slope, out_grad, hidden, preact_grad,
+):
+    forward_kernel(
+        side_ref, normed_ref, student_ref, target_ref, w_in_ref, w_out_ref, params_ref,
+        slope, misfit_ref, out_grad, out_sent, out_kept, hidden,
+    )
+    backward_kernel(
+        side_ref, slope, out_grad, normed_ref, unit_ref, inv_ref, w_in_ref, w_out_ref, params_ref,
+        conv_grad_ref, in_sent, in_kept, preact_grad,
+    )
+
+
+def mlp(side, normed, unit_norm, inv_std, student, target, w_in, w_out, params):
     cells, channel_count = normed.shape
     hidden_size = w_in.shape[1]
     shape = jax.ShapeDtypeStruct
-    return pl.pallas_call(
-        backward_kernel,
+    halves = [
+        shape((hidden_size // 2, channel_count), jnp.bfloat16),
+        shape((hidden_size // 2, channel_count), jnp.float32),
+    ]
+    return pl.pallas_call(
+        mlp_kernel,
         in_specs=[pl.BlockSpec(memory_space=pltpu.SMEM)] + vmem_specs(8),
-        out_specs=vmem_specs(3),
-        out_shape=(
+        out_specs=vmem_specs(6),
+        out_shape=[
+            shape((cells, channel_count), jnp.float32),
             shape((cells, channel_count), jnp.bfloat16),
-            shape((hidden_size // 2, channel_count), jnp.bfloat16),
-            shape((hidden_size // 2, channel_count), jnp.float32),
+        ]
+        + halves
+        + halves,
+        scratch_shapes=[
+            pltpu.VMEM((cells, hidden_size), jnp.float32),
+            pltpu.VMEM((cells, channel_count), jnp.bfloat16),
+            pltpu.VMEM((cells, hidden_size), jnp.bfloat16),
+            pltpu.VMEM((cells, hidden_size), jnp.bfloat16),
+        ],
+        compiler_params=pltpu.CompilerParams(vmem_limit_bytes=10 << 20),
+        cost_estimate=pl.CostEstimate(
+            flops=12 * cells * channel_count * hidden_size,
+            bytes_accessed=4 << 20,
+            transcendentals=cells * hidden_size,
         ),
-        scratch_shapes=[pltpu.VMEM((cells, hidden_size), jnp.bfloat16)],
-        compiler_params=pltpu.CompilerParams(vmem_limit_bytes=6 << 20),
-        cost_estimate=pl.CostEstimate(
-            flops=6 * cells * channel_count * hidden_size, bytes_accessed=4 << 20, transcendentals=0
-        ),
-        name="backward",
-    )(side, slope, out_grad, normed, unit_norm, inv_std, w_in, w_out, params)
+        name="mlp",
+    )(side, normed, unit_norm, inv_std, student, target, w_in, w_out, params)
 
 
 def local(student, teacher, dw_weight, norm_gain, w_in, w_out, layer_scale):
@@ -661,14 +662,10 @@
     upper = lax.axis_index("lat") % 2
     side = upper.astype(jnp.int32).reshape(1)
     rows = lambda block: block.reshape(-1, channel_count)
-    slope, misfit, out_grad, sent, kept_out = forward(
-        side, normed, rows(student), rows(target), w_in, w_out, params
-    )
-    got_out = swap(sent, "lat", 1)
-    conv_grad, sent, kept_in = backward(
-        side, slope, out_grad, normed, unit_norm, inv_std, w_in, w_out, params
-    )
-    got_in = swap(sent, "lat", 1)
+    misfit, conv_grad, out_sent, kept_out, in_sent, kept_in = mlp(
+        side, normed, unit_norm, inv_std, rows(student), rows(target), w_in, w_out, params
+    )
+    got_out, got_in = swap(out_sent, "lat", 1), swap(in_sent, "lat", 1)
     conv_grid = conv_grad.reshape(student.shape)
     inner, outer = [swap(edge, "lat", 1) for edge in edges(conv_grid, "lat", 1, half_kernel)]
     part_dw = tap_sums(padded_bf, conv_grid, round_up(tap_count, 64))

time: 61.2 us -> 60.7 us (level)
    pallas_call x2 -> x1, Pallas kernels: 2.13 us -> 1.72 us  [mlp(): pl.pallas_call(mlp_kernel, in_specs=[pl.BlockSpec(memory_space=pltpu.SMEM...]
  transfers between devices with their start and end apart: 24 -> 24, of which waited for: 13 -> 13; matrix products, arithmetic and copies ran while one was open for 2% -> 2% of each run, Pallas kernels for 9% -> 8%
where the time goes in v9:
time: 60.7 us; the launch traced here: 60.5 us
  starting transfers between devices  25.5 us (42%)
  waiting for transfers between devices  23.2 us (38%)
  Pallas kernels  7.58 us (12%)
  other arithmetic  1.94 us (3%)
  between operations  1.16 us (2%)
  local copies, waits for them, and re-layouts  1.09 us (2%)
    ppermute x22, starting transfers between devices, swap(): lax.ppermute(value, axis, [(i, i ^ bit) for i in range(lax.axis_size(axis...  20.4 us
    ppermute x22, waiting for transfers between devices, swap(): lax.ppermute(value, axis, [(i, i ^ bit) for i in range(lax.axis_size(axis...  20 us
    ppermute x2, starting transfers between devices, swap_outer(): got = lax.ppermute(edge, axis, pairs + [(j, i) for i, j in pairs])  5.15 us
    ppermute x2, waiting for transfers between devices, swap_outer(): got = lax.ppermute(edge, axis, pairs + [(j, i) for i, j in pairs])  3.13 us
    pallas_call x1, Pallas kernels, mlp(): pl.pallas_call(mlp_kernel, in_specs=[pl.BlockSpec(memory_space=pltpu.SMEM...  1.72 us
    pallas_call x1, Pallas kernels, conv_back(): pl.pallas_call(conv_back_kernel, out_shape=(jax.ShapeDtypeStruct(misfit.s...  1.55 us
  transfers between devices with their start and end apart: 24, of which 13 were waited for; matrix products, arithmetic and copies ran while one was open for 2% of the time, Pallas kernels for 8%

profile of v9, /device:TPU:0, one launch (start us, length us, event | category | flops | bytes accessed | tf_op | source)
XLA Modules:
  0.0 60.5 jit_solution(17383992419566983206)
XLA Ops:
  0.7 0.8 %broadcast_select_fusion.14 = (bf16[2,4,3,256]{3,2,1,0:T(4,128)(2,1)S(1)}, bf16[2,4,3,256]{3,2,1,0:T(4,128)(2,1)S(1)}) fusion(pred[]{:T(512)S(6)} %eq.71, bf16[2,4,32,256]{3,2,1,0:T(8,128)(2,1)} %param.7), kind=kLoop, calls=%fused_computation.61 | loop fusion | flops 12288 | bytes 49153 | tf_op jit(solution)/shard_map/jit(_where)/select_n | solution.py:27
  1.5 3.0 %collective-permute-start = (bf16[2,4,3,256]{3,2,1,0:T(4,128)(2,1)S(1)}, bf16[2,4,3,256]{3,2,1,0:T(4,128)(2,1)S(1)}, u32[]{:S(2)}, u32[]{:S(2)}) collective-permute-start(bf16[2,4,3,256]{3,2,1,0:T(4,128)(2,1)S(1)} %get-tuple-element.85), channel_id=1, source_target_pairs={{0,1},{1,0},{2,3},{3,2},{4,5},{5,4},{6,7},{7,6},{8,9},{9,8},{10,11... | collective-permute-start | bytes 36872 | tf_op jit(solution)/shard_map/ppermute | solution.py:20
  4.5 3.5 %collective-permute-start.1 = (bf16[2,4,3,256]{3,2,1,0:T(4,128)(2,1)S(1)}, bf16[2,4,3,256]{3,2,1,0:T(4,128)(2,1)S(1)}, u32[]{:S(2)}, u32[]{:S(2)}) collective-permute-start(bf16[2,4,3,256]{3,2,1,0:T(4,128)(2,1)S(1)} %get-tuple-element.86), channel_id=1, source_target_pairs={{1,2},{3,4},{5,6},{7,0},{2,1},{4,3},{6,5},{0,7},{9,10},{11,12},{13... | collective-permute-start | bytes 36872 | tf_op jit(solution)/shard_map/ppermute | solution.py:33
  8.1 0.7 %copy-done.6 = f32[256]{0:T(256)S(1)} copy-done((f32[256]{0:T(256)S(1)}, f32[256]{0:T(256)}, u32[]{:S(2)}) %copy-start.6) | copy-done | bytes 1048
  9.0 1.6 %collective-permute-start.4 = (bf16[2,2,4,1,8,256]{5,4,2,1,0,3:T(8,128)(2,1)S(1)}, bf16[2,2,4,1,8,256]{5,4,2,1,0,3:T(8,128)(2,1)S(1)}, u32[]{:S(2)}, u32[]{:S(2)}) collective-permute-start(bf16[2,2,4,1,8,256]{5,4,2,1,0,3:T(8,128)(2,1)S(1)} %get-tuple-element.83), channel_id=1, source_target_pairs={{0,16},{8,24},{16,0},{24,8},{1,17},{9,25},{17,1},{25,9},{2,18},{10... | collective-permute-start | bytes 196616 | tf_op jit(solution)/shard_map/ppermute | solution.py:20
  11.2 1.6 %collective-permute-start.3 = (bf16[2,3,38,256]{3,2,1,0:T(8,128)(2,1)S(1)}, bf16[2,3,38,256]{3,2,1,0:T(8,128)(2,1)S(1)}, u32[]{:S(2)}, u32[]{:S(2)}) collective-permute-start(bf16[2,3,38,256]{3,2,1,0:T(8,128)(2,1)S(1)} %get-tuple-element.77), channel_id=1, source_target_pairs={{8,16},{24,0},{16,8},{0,24},{9,17},{25,1},{17,9},{1,25},{10,18},{2... | collective-permute-start | bytes 350216 | tf_op jit(solution)/shard_map/ppermute | solution.py:33
  12.8 0.5 conv_own.1.own_ref
  13.5 2.8 %collective-permute-done.3 = bf16[2,3,38,256]{3,2,1,0:T(8,128)(2,1)S(1)} collective-permute-done((bf16[2,3,38,256]{3,2,1,0:T(8,128)(2,1)S(1)}, bf16[2,3,38,256]{3,2,1,0:T(8,128)(2,1)S(1)}, u32[]{:S(2)}, u32[]{:S(2)}) %collective-permute-start.3) | collective-permute-done | bytes 116768 | tf_op jit(solution)/shard_map/ppermute | solution.py:33
  16.4 0.7 %conv_norm.1 = (bf16[256,256]{1,0:T(8,128)(2,1)S(1)}, f32[256,256]{1,0:T(8,128)S(1)}, f32[256,1]{1,0:T(8,128)S(1)}) custom-call(f32[2,256,128]{2,1,0:T(8,128)S(1)} %conv_own.1.own_ref, bf16[2,10,38,256]{3,2,1,0:T(8,128)(2,1)S(1)} %pad_maximum_fusion.padded_ref, f32[51,256]{1,0:T(8,128)S(1)} %pad_maximum_fusion.8.params_ref), custom_call_target="tpu_custom_call" | custom-call | flops 6422528 | bytes 1048576 | tf_op jit(solution)/shard_map/conv_norm/pallas_call | solution.py:333
  17.1 1.7 %mlp.1 = (f32[256,256]{1,0:T(8,128)S(1)}, bf16[256,256]{1,0:T(8,128)(2,1)S(1)}, bf16[512,256]{1,0:T(8,128)(2,1)S(1)}, f32[512,256]{1,0:T(8,128)S(1)}, bf16[512,2...) custom-call(s32[1]{0:T(128)} %bitcast.side_ref, bf16[256,256]{1,0:T(8,128)(2,1)S(1)} %get-tuple-element.32.normed_ref, ...), custom_call_target="tpu_custom_call" | custom-call | flops 805306368 | bytes 4194304 | tf_op jit(solution)/shard_map/mlp/pallas_call | solution.py:619
  19.8 1.0 %tap_sums.1 = f32[64,256]{1,0:T(8,128)S(1)} custom-call(bf16[2,10,38,256]{3,2,1,0:T(8,128)(2,1)S(1)} %pad_maximum_fusion.padded_ref, bf16[2,4,32,256]{3,2,1,0:T(8,128)(2,1)S(1)} %bitcast.30), custom_call_target="tpu_custom_call" | custom-call | flops 6422528 | bytes 1048576 | tf_op jit(solution)/shard_map/tap_sums/pallas_call | solution.py:424
  21.1 1.6 %collective-permute-start.8 = (bf16[480,256]{1,0:T(8,128)(2,1)S(1)}, bf16[480,256]{1,0:T(8,128)(2,1)S(1)}, u32[]{:S(2)}, u32[]{:S(2)}) collective-permute-start(bf16[480,256]{1,0:T(8,128)(2,1)S(1)} %pad_maximum_fusion.2), channel_id=1, source_target_pairs={{0,16},{8,24},{16,0},{24,8},{1,17},{9,25},{17,1},{25,9},{2,18},{10... | collective-permute-start | bytes 737288 | tf_op jit(solution)/shard_map/ppermute | solution.py:20
  22.7 3.8 %collective-permute-done.16 = bf16[256,256]{1,0:T(8,128)(2,1)S(1)} collective-permute-done((bf16[256,256]{1,0:T(8,128)(2,1)S(1)}, bf16[256,256]{1,0:T(8,128)(2,1)S(1)}, u32[]{:S(2)}, u32[]{:S(2)}) %collective-permute-start.16) | collective-permute-done | bytes 131104 | tf_op jit(solution)/shard_map/ppermute | solution.py:20
  26.5 0.9 %collective-permute-start.17 = (bf16[128,256]{1,0:T(8,128)(2,1)S(1)}, bf16[128,256]{1,0:T(8,128)(2,1)S(1)}, u32[]{:S(2)}, u32[]{:S(2)}) collective-permute-start(bf16[128,256]{1,0:T(8,128)(2,1)S(1)} %get-tuple-element.69), channel_id=1, source_target_pairs={{0,4},{1,5},{2,6},{3,7},{4,0},{5,1},{6,2},{7,3},{8,12},{9,13},{10,... | collective-permute-start | bytes 196616 | tf_op jit(solution)/shard_map/ppermute | solution.py:20
  27.4 1.8 %collective-permute-done.8 = bf16[480,256]{1,0:T(8,128)(2,1)S(1)} collective-permute-done((bf16[480,256]{1,0:T(8,128)(2,1)S(1)}, bf16[480,256]{1,0:T(8,128)(2,1)S(1)}, u32[]{:S(2)}, u32[]{:S(2)}) %collective-permute-start.8) | collective-permute-done | bytes 245792 | tf_op jit(solution)/shard_map/ppermute | solution.py:20
  30.0 2.2 %collective-permute-done.17 = bf16[128,256]{1,0:T(8,128)(2,1)S(1)} collective-permute-done((bf16[128,256]{1,0:T(8,128)(2,1)S(1)}, bf16[128,256]{1,0:T(8,128)(2,1)S(1)}, u32[]{:S(2)}, u32[]{:S(2)}) %collective-permute-start.17) | collective-permute-done | bytes 65568 | tf_op jit(solution)/shard_map/ppermute | solution.py:20
  32.2 1.6 %collective-permute-start.18 = (f32[128,256]{1,0:T(8,128)S(1)}, f32[128,256]{1,0:T(8,128)S(1)}, u32[]{:S(2)}, u32[]{:S(2)}) collective-permute-start(f32[128,256]{1,0:T(8,128)S(1)} %convert_add_fusion.2), channel_id=1, source_target_pairs={{0,16},{8,24},{16,0},{24,8},{1,17},{9,25},{17,1},{25,9},{2,18},{10... | collective-permute-start | bytes 393224 | tf_op jit(solution)/shard_map/ppermute | solution.py:20
  33.8 0.9 %collective-permute-done.10 = bf16[264,256]{1,0:T(8,128)(2,1)S(1)} collective-permute-done((bf16[264,256]{1,0:T(8,128)(2,1)S(1)}, bf16[264,256]{1,0:T(8,128)(2,1)S(1)}, u32[]{:S(2)}, u32[]{:S(2)}) %collective-permute-start.10) | collective-permute-done | bytes 135200 | tf_op jit(solution)/shard_map/ppermute | solution.py:20
  34.8 1.7 %collective-permute-start.11 = (f32[204,256]{1,0:T(8,128)S(1)}, f32[204,256]{1,0:T(8,128)S(1)}, u32[]{:S(2)}, u32[]{:S(2)}) collective-permute-start(f32[204,256]{1,0:T(8,128)S(1)} %pad_maximum_fusion.3), channel_id=1, source_target_pairs={{0,2},{1,3},{2,0},{3,1},{4,6},{5,7},{6,4},{7,5},{8,10},{9,11},{10,... | collective-permute-start | bytes 626696 | tf_op jit(solution)/shard_map/ppermute | solution.py:20
  36.5 0.7 %collective-permute-done.18 = f32[128,256]{1,0:T(8,128)S(1)} collective-permute-done((f32[128,256]{1,0:T(8,128)S(1)}, f32[128,256]{1,0:T(8,128)S(1)}, u32[]{:S(2)}, u32[]{:S(2)}) %collective-permute-start.18) | collective-permute-done | bytes 131104 | tf_op jit(solution)/shard_map/ppermute | solution.py:20
  37.4 3.3 %collective-permute-done.11 = f32[204,256]{1,0:T(8,128)S(1)} collective-permute-done((f32[204,256]{1,0:T(8,128)S(1)}, f32[204,256]{1,0:T(8,128)S(1)}, u32[]{:S(2)}, u32[]{:S(2)}) %collective-permute-start.11) | collective-permute-done | bytes 208928 | tf_op jit(solution)/shard_map/ppermute | solution.py:20
  40.8 2.6 %collective-permute-start.12 = (bf16[204,256]{1,0:T(8,128)(2,1)S(1)}, bf16[204,256]{1,0:T(8,128)(2,1)S(1)}, u32[]{:S(2)}, u32[]{:S(2)}) collective-permute-start(bf16[204,256]{1,0:T(8,128)(2,1)S(1)} %pad_maximum_fusion.6), channel_id=1, source_target_pairs={{0,4},{1,5},{2,6},{3,7},{4,0},{5,1},{6,2},{7,3},{8,12},{9,13},{10,... | collective-permute-start | bytes 313352 | tf_op jit(solution)/shard_map/ppermute | solution.py:20
  43.9 2.6 %collective-permute-done.12.got_ref = bf16[204,256]{1,0:T(8,128)(2,1)S(1)} collective-permute-done((bf16[204,256]{1,0:T(8,128)(2,1)S(1)}, bf16[204,256]{1,0:T(8,128)(2,1)S(1)}, u32[]{:S(2)}, u32[]{:S(2)}) %collective-permute-start.12) | collective-permute-done | bytes 104480 | tf_op jit(solution)/shard_map/ppermute | solution.py:20
  46.6 3.0 %collective-permute-start.13 = (bf16[1,288,128]{2,1,0:T(8,128)(2,1)S(1)}, bf16[1,288,128]{2,1,0:T(8,128)(2,1)S(1)}, u32[]{:S(2)}, u32[]{:S(2)}) collective-permute-start(bf16[1,288,128]{2,1,0:T(8,128)(2,1)S(1)} %finish_columns.1._), channel_id=1, source_target_pairs={{0,1},{1,0},{2,3},{3,2},{4,5},{5,4},{6,7},{7,6},{8,9},{9,8},{10,11... | collective-permute-start | bytes 221192 | tf_op jit(solution)/shard_map/ppermute | solution.py:20
  49.7 2.2 %collective-permute-done.13 = bf16[1,288,128]{2,1,0:T(8,128)(2,1)S(1)} collective-permute-done((bf16[1,288,128]{2,1,0:T(8,128)(2,1)S(1)}, bf16[1,288,128]{2,1,0:T(8,128)(2,1)S(1)}, u32[]{:S(2)}, u32[]{:S(2)}) %collective-permute-start.13) | collective-permute-done | bytes 73760 | tf_op jit(solution)/shard_map/ppermute | solution.py:20
  51.9 1.6 %collective-permute-start.14 = (bf16[2,288,128]{2,1,0:T(8,128)(2,1)S(1)}, bf16[2,288,128]{2,1,0:T(8,128)(2,1)S(1)}, u32[]{:S(2)}, u32[]{:S(2)}) collective-permute-start(bf16[2,288,128]{2,1,0:T(8,128)(2,1)S(1)} %maximum_select_fusion.1.mine), channel_id=1, source_target_pairs={{0,16},{8,24},{16,0},{24,8},{1,17},{9,25},{17,1},{25,9},{2,18},{10... | collective-permute-start | bytes 442376 | tf_op jit(solution)/shard_map/ppermute | solution.py:20
  53.5 1.1 %collective-permute-done.21 = bf16[2,128,256]{2,1,0:T(8,128)(2,1)S(1)} collective-permute-done((bf16[2,128,256]{2,1,0:T(8,128)(2,1)S(1)}, bf16[2,128,256]{2,1,0:T(8,128)(2,1)S(1)}, u32[]{:S(2)}, u32[]{:S(2)}) %collective-permute-start.21) | collective-permute-done | bytes 131104 | tf_op jit(solution)/shard_map/ppermute | solution.py:20
  55.1 1.6 %conv_back.1 = (bf16[2,4,32,256]{3,2,1,0:T(8,128)(2,1)}, f32[8,128]{1,0:T(8,128)S(1)}) custom-call(bf16[2,10,38,256]{3,2,1,0:T(8,128)(2,1)S(1)} %pad_maximum_fusion.1.padded_ref, f32[51,256]{1,0:T(8,128)S(1)} %pad_maximum_fusion.8.params_ref, f32[2,4,32,256]{3,2,1,0:T(8,128)S(1)} %bitcast.33, bf16[1,288,128]{2,1,0:T(8,128)(2,1)S(1)} %finish_columns.1._), custom_call_target="tpu_custom_call" | custom-call | flops 6422528 | bytes 1048576 | tf_op jit(solution)/shard_map/conv_back/pallas_call | solution.py:373
  56.6 1.0 %assemble_rows.1 = (f32[1024,256]{1,0:T(8,128)}, f32[8,128]{1,0:T(8,128)S(1)}) custom-call(s32[1]{0:T(128)} %bitcast.side_ref, bf16[4,128,256]{2,1,0:T(8,128)(2,1)S(1)} %maximum_select_fusion.mine, bf16[4,128,256]{2,1,0:T(8,128)(2,1)S(1)} %collective-permute-done.22.got, f32[8,128]{1,0:T(8,128)S(1)} %get-tuple-element.51._), custom_call_target="tpu_custom_call" | custom-call | bytes 1572864 | tf_op jit(solution)/shard_map/assemble_rows/pallas_call | solution.py:484
  57.7 0.6 collective-permute-start.23
  58.2 1.2 %collective-permute-done.23.got = bf16[4,288,128]{2,1,0:T(8,128)(2,1)S(1)} collective-permute-done((bf16[4,288,128]{2,1,0:T(8,128)(2,1)S(1)}, bf16[4,288,128]{2,1,0:T(8,128)(2,1)S(1)}, u32[]{:S(2)}, u32[]{:S(2)}) %collective-permute-start.23) | collective-permute-done | bytes 294944 | tf_op jit(solution)/shard_map/ppermute | solution.py:20
  59.4 1.1 %assemble_columns.1 = (f32[256,1024]{1,0:T(8,128)}, f32[7,7,256]{2,1,0:T(8,128)}) custom-call(s32[1]{0:T(128)} %bitcast.side_ref, bf16[4,288,128]{2,1,0:T(8,128)(2,1)S(1)} %join.1.mine, bf16[4,288,128]{2,1,0:T(8,128)(2,1)S(1)} %collective-permute-done.23.got), custom_call_target="tpu_custom_call" | custom-call | bytes 1572864 | tf_op jit(solution)/shard_map/assemble_columns/pallas_call | solution.py:499
  (89 shorter events, 4.5 us)
Async XLA Ops:
  0.6 7.4 %copy-start.4 = (f32[7,7,256]{2,1,0:T(8,128)S(1)}, f32[7,7,256]{2,1,0:T(8,128)}, u32[]{:S(2)}) copy-start(f32[7,7,256]{2,1,0:T(8,128)} %param.9) | copy-start | bytes 150532
  1.5 9.1 %collective-permute-start = (bf16[2,4,3,256]{3,2,1,0:T(4,128)(2,1)S(1)}, bf16[2,4,3,256]{3,2,1,0:T(4,128)(2,1)S(1)}, u32[]{:S(2)}, u32[]{:S(2)}) collective-permute-start(bf16[2,4,3,256]{3,2,1,0:T(4,128)(2,1)S(1)} %get-tuple-element.85), channel_id=1, source_target_pairs={{0,1},{1,0},{2,3},{3,2},{4,5},{5,4},{6,7},{7,6},{8,9},{9,8},{10,11... | collective-permute-start | bytes 36872 | tf_op jit(solution)/shard_map/ppermute | solution.py:20
  4.5 6.4 %collective-permute-start.1 = (bf16[2,4,3,256]{3,2,1,0:T(4,128)(2,1)S(1)}, bf16[2,4,3,256]{3,2,1,0:T(4,128)(2,1)S(1)}, u32[]{:S(2)}, u32[]{:S(2)}) collective-permute-start(bf16[2,4,3,256]{3,2,1,0:T(4,128)(2,1)S(1)} %get-tuple-element.86), channel_id=1, source_target_pairs={{1,2},{3,4},{5,6},{7,0},{2,1},{4,3},{6,5},{0,7},{9,10},{11,12},{13... | collective-permute-start | bytes 36872 | tf_op jit(solution)/shard_map/ppermute | solution.py:33
  8.1 0.9 %copy-start.3 = (bf16[2,16,8,256]{3,2,1,0:T(8,128)(2,1)S(1)}, bf16[2,16,8,256]{3,2,1,0:T(8,128)(2,1)}, u32[]{:S(2)}) copy-start(bf16[2,16,8,256]{3,2,1,0:T(8,128)(2,1)} %param.8) | copy-start | bytes 393220
  8.1 0.7 %copy-start.6 = (f32[256]{0:T(256)S(1)}, f32[256]{0:T(256)}, u32[]{:S(2)}) copy-start(f32[256]{0:T(256)} %param.10) | copy-start | bytes 3076
  8.1 0.7 %copy-start.5 = (f32[256]{0:T(256)S(1)}, f32[256]{0:T(256)}, u32[]{:S(2)}) copy-start(f32[256]{0:T(256)} %param.13) | copy-start | bytes 3076
  8.8 2.2 %copy-start.2 = (bf16[2,4,32,256]{3,2,1,0:T(8,128)(2,1)S(1)}, bf16[2,4,32,256]{3,2,1,0:T(8,128)(2,1)}, u32[]{:S(2)}) copy-start(bf16[2,4,32,256]{3,2,1,0:T(8,128)(2,1)} %param.7) | copy-start | bytes 393220
  9.0 3.8 %copy-start.1 = (bf16[1024,256]{1,0:T(8,128)(2,1)S(1)}, bf16[1024,256]{1,0:T(8,128)(2,1)}, u32[]{:S(2)}) copy-start(bf16[1024,256]{1,0:T(8,128)(2,1)} %w_out_ref.1) | copy-start | bytes 1572868
  9.0 3.8 %copy-start = (bf16[256,1024]{1,0:T(8,128)(2,1)S(1)}, bf16[256,1024]{1,0:T(8,128)(2,1)}, u32[]{:S(2)}) copy-start(bf16[256,1024]{1,0:T(8,128)(2,1)} %w_in_ref.1) | copy-start | bytes 1572868
  9.0 4.3 %collective-permute-start.4 = (bf16[2,2,4,1,8,256]{5,4,2,1,0,3:T(8,128)(2,1)S(1)}, bf16[2,2,4,1,8,256]{5,4,2,1,0,3:T(8,128)(2,1)S(1)}, u32[]{:S(2)}, u32[]{:S(2)}) collective-permute-start(bf16[2,2,4,1,8,256]{5,4,2,1,0,3:T(8,128)(2,1)S(1)} %get-tuple-element.83), channel_id=1, source_target_pairs={{0,16},{8,24},{16,0},{24,8},{1,17},{9,25},{17,1},{25,9},{2,18},{10... | collective-permute-start | bytes 196616 | tf_op jit(solution)/shard_map/ppermute | solution.py:20
  11.1 2.4 %collective-permute-start.2 = (bf16[2,3,38,256]{3,2,1,0:T(8,128)(2,1)S(1)}, bf16[2,3,38,256]{3,2,1,0:T(8,128)(2,1)S(1)}, u32[]{:S(2)}, u32[]{:S(2)}) collective-permute-start(bf16[2,3,38,256]{3,2,1,0:T(8,128)(2,1)S(1)} %get-tuple-element.78), channel_id=1, source_target_pairs={{0,8},{8,0},{16,24},{24,16},{1,9},{9,1},{17,25},{25,17},{2,10},{10... | collective-permute-start | bytes 350216 | tf_op jit(solution)/shard_map/ppermute | solution.py:20
  11.2 5.1 %collective-permute-start.3 = (bf16[2,3,38,256]{3,2,1,0:T(8,128)(2,1)S(1)}, bf16[2,3,38,256]{3,2,1,0:T(8,128)(2,1)S(1)}, u32[]{:S(2)}, u32[]{:S(2)}) collective-permute-start(bf16[2,3,38,256]{3,2,1,0:T(8,128)(2,1)S(1)} %get-tuple-element.77), channel_id=1, source_target_pairs={{8,16},{24,0},{16,8},{0,24},{9,17},{25,1},{17,9},{1,25},{10,18},{2... | collective-permute-start | bytes 350216 | tf_op jit(solution)/shard_map/ppermute | solution.py:33
  13.4 3.6 %collective-permute-start.5 = (bf16[2,1,4,2,8,256]{5,4,3,2,0,1:T(8,128)(2,1)S(1)}, bf16[2,1,4,2,8,256]{5,4,3,2,0,1:T(8,128)(2,1)S(1)}, u32[]{:S(2)}, u32[]{:S(2)}) collective-permute-start(bf16[2,1,4,2,8,256]{5,4,3,2,0,1:T(8,128)(2,1)S(1)} %bitcast.40), channel_id=1, source_target_pairs={{0,8},{8,0},{16,24},{24,16},{1,9},{9,1},{17,25},{25,17},{2,10},{10... | collective-permute-start | bytes 196616 | tf_op jit(solution)/shard_map/ppermute | solution.py:20
  18.8 2.0 %collective-permute-start.15 = (bf16[512,256]{1,0:T(8,128)(2,1)S(1)}, bf16[512,256]{1,0:T(8,128)(2,1)S(1)}, u32[]{:S(2)}, u32[]{:S(2)}) collective-permute-start(bf16[512,256]{1,0:T(8,128)(2,1)S(1)} %get-tuple-element.42), channel_id=1, source_target_pairs={{0,8},{8,0},{16,24},{24,16},{1,9},{9,1},{17,25},{25,17},{2,10},{10... | collective-permute-start | bytes 786440 | tf_op jit(solution)/shard_map/ppermute | solution.py:20
  19.2 1.8 %collective-permute-start.6 = (bf16[512,256]{1,0:T(8,128)(2,1)S(1)}, bf16[512,256]{1,0:T(8,128)(2,1)S(1)}, u32[]{:S(2)}, u32[]{:S(2)}) collective-permute-start(bf16[512,256]{1,0:T(8,128)(2,1)S(1)} %get-tuple-element.37), channel_id=1, source_target_pairs={{0,8},{8,0},{16,24},{24,16},{1,9},{9,1},{17,25},{25,17},{2,10},{10... | collective-permute-start | bytes 786440 | tf_op jit(solution)/shard_map/ppermute | solution.py:20
  19.4 1.7 %collective-permute-start.7 = (bf16[2,3,32,256]{3,2,1,0:T(8,128)(2,1)S(1)}, bf16[2,3,32,256]{3,2,1,0:T(8,128)(2,1)S(1)}, u32[]{:S(2)}, u32[]{:S(2)}) collective-permute-start(bf16[2,3,32,256]{3,2,1,0:T(8,128)(2,1)S(1)} %get-tuple-element.79), channel_id=1, source_target_pairs={{0,8},{8,0},{16,24},{24,16},{1,9},{9,1},{17,25},{25,17},{2,10},{10... | collective-permute-start | bytes 294920 | tf_op jit(solution)/shard_map/ppermute | solution.py:20
  20.9 5.6 %collective-permute-start.16 = (bf16[256,256]{1,0:T(8,128)(2,1)S(1)}, bf16[256,256]{1,0:T(8,128)(2,1)S(1)}, u32[]{:S(2)}, u32[]{:S(2)}) collective-permute-start(bf16[256,256]{1,0:T(8,128)(2,1)S(1)} %get-tuple-element.65), channel_id=1, source_target_pairs={{0,2},{1,3},{2,0},{3,1},{4,6},{5,7},{6,4},{7,5},{8,10},{9,11},{10,... | collective-permute-start | bytes 393224 | tf_op jit(solution)/shard_map/ppermute | solution.py:20
  21.1 8.1 %collective-permute-start.8 = (bf16[480,256]{1,0:T(8,128)(2,1)S(1)}, bf16[480,256]{1,0:T(8,128)(2,1)S(1)}, u32[]{:S(2)}, u32[]{:S(2)}) collective-permute-start(bf16[480,256]{1,0:T(8,128)(2,1)S(1)} %pad_maximum_fusion.2), channel_id=1, source_target_pairs={{0,16},{8,24},{16,0},{24,8},{1,17},{9,25},{17,1},{25,9},{2,18},{10... | collective-permute-start | bytes 737288 | tf_op jit(solution)/shard_map/ppermute | solution.py:20
  22.7 6.6 %collective-permute-start.9 = (bf16[2,3,32,256]{3,2,1,0:T(8,128)(2,1)S(1)}, bf16[2,3,32,256]{3,2,1,0:T(8,128)(2,1)S(1)}, u32[]{:S(2)}, u32[]{:S(2)}) collective-permute-start(bf16[2,3,32,256]{3,2,1,0:T(8,128)(2,1)S(1)} %get-tuple-element.80), channel_id=1, source_target_pairs={{0,8},{8,0},{16,24},{24,16},{1,9},{9,1},{17,25},{25,17},{2,10},{10... | collective-permute-start | bytes 294920 | tf_op jit(solution)/shard_map/ppermute | solution.py:20
  26.5 5.7 %collective-permute-start.17 = (bf16[128,256]{1,0:T(8,128)(2,1)S(1)}, bf16[128,256]{1,0:T(8,128)(2,1)S(1)}, u32[]{:S(2)}, u32[]{:S(2)}) collective-permute-start(bf16[128,256]{1,0:T(8,128)(2,1)S(1)} %get-tuple-element.69), channel_id=1, source_target_pairs={{0,4},{1,5},{2,6},{3,7},{4,0},{5,1},{6,2},{7,3},{8,12},{9,13},{10,... | collective-permute-start | bytes 196616 | tf_op jit(solution)/shard_map/ppermute | solution.py:20
  29.6 5.1 %collective-permute-start.10 = (bf16[264,256]{1,0:T(8,128)(2,1)S(1)}, bf16[264,256]{1,0:T(8,128)(2,1)S(1)}, u32[]{:S(2)}, u32[]{:S(2)}) collective-permute-start(bf16[264,256]{1,0:T(8,128)(2,1)S(1)} %pad_maximum_fusion.5), channel_id=1, source_target_pairs={{0,1},{1,0},{2,3},{3,2},{4,5},{5,4},{6,7},{7,6},{8,9},{9,8},{10,11... | collective-permute-start | bytes 405512 | tf_op jit(solution)/shard_map/ppermute | solution.py:20
  32.2 5.0 %collective-permute-start.18 = (f32[128,256]{1,0:T(8,128)S(1)}, f32[128,256]{1,0:T(8,128)S(1)}, u32[]{:S(2)}, u32[]{:S(2)}) collective-permute-start(f32[128,256]{1,0:T(8,128)S(1)} %convert_add_fusion.2), channel_id=1, source_target_pairs={{0,16},{8,24},{16,0},{24,8},{1,17},{9,25},{17,1},{25,9},{2,18},{10... | collective-permute-start | bytes 393224 | tf_op jit(solution)/shard_map/ppermute | solution.py:20
  34.8 5.9 %collective-permute-start.11 = (f32[204,256]{1,0:T(8,128)S(1)}, f32[204,256]{1,0:T(8,128)S(1)}, u32[]{:S(2)}, u32[]{:S(2)}) collective-permute-start(f32[204,256]{1,0:T(8,128)S(1)} %pad_maximum_fusion.3), channel_id=1, source_target_pairs={{0,2},{1,3},{2,0},{3,1},{4,6},{5,7},{6,4},{7,5},{8,10},{9,11},{10,... | collective-permute-start | bytes 626696 | tf_op jit(solution)/shard_map/ppermute | solution.py:20
  37.3 6.1 %collective-permute-start.19 = (bf16[128,256]{1,0:T(8,128)(2,1)S(1)}, bf16[128,256]{1,0:T(8,128)(2,1)S(1)}, u32[]{:S(2)}, u32[]{:S(2)}) collective-permute-start(bf16[128,256]{1,0:T(8,128)(2,1)S(1)} %get-tuple-element.57), channel_id=1, source_target_pairs={{0,1},{1,0},{2,3},{3,2},{4,5},{5,4},{6,7},{7,6},{8,9},{9,8},{10,11... | collective-permute-start | bytes 196616 | tf_op jit(solution)/shard_map/ppermute | solution.py:20
  40.8 5.7 %collective-permute-start.12 = (bf16[204,256]{1,0:T(8,128)(2,1)S(1)}, bf16[204,256]{1,0:T(8,128)(2,1)S(1)}, u32[]{:S(2)}, u32[]{:S(2)}) collective-permute-start(bf16[204,256]{1,0:T(8,128)(2,1)S(1)} %pad_maximum_fusion.6), channel_id=1, source_target_pairs={{0,4},{1,5},{2,6},{3,7},{4,0},{5,1},{6,2},{7,3},{8,12},{9,13},{10,... | collective-permute-start | bytes 313352 | tf_op jit(solution)/shard_map/ppermute | solution.py:20
  43.4 6.2 %collective-permute-start.20 = (bf16[1,128,256]{2,1,0:T(8,128)(2,1)S(1)}, bf16[1,128,256]{2,1,0:T(8,128)(2,1)S(1)}, u32[]{:S(2)}, u32[]{:S(2)}) collective-permute-start(bf16[1,128,256]{2,1,0:T(8,128)(2,1)S(1)} %fusion.1), channel_id=1, source_target_pairs={{0,4},{1,5},{2,6},{3,7},{4,0},{5,1},{6,2},{7,3},{8,12},{9,13},{10,... | collective-permute-start | bytes 196616 | tf_op jit(solution)/shard_map/ppermute | solution.py:20
  46.6 5.3 %collective-permute-start.13 = (bf16[1,288,128]{2,1,0:T(8,128)(2,1)S(1)}, bf16[1,288,128]{2,1,0:T(8,128)(2,1)S(1)}, u32[]{:S(2)}, u32[]{:S(2)}) collective-permute-start(bf16[1,288,128]{2,1,0:T(8,128)(2,1)S(1)} %finish_columns.1._), channel_id=1, source_target_pairs={{0,1},{1,0},{2,3},{3,2},{4,5},{5,4},{6,7},{7,6},{8,9},{9,8},{10,11... | collective-permute-start | bytes 221192 | tf_op jit(solution)/shard_map/ppermute | solution.py:20
  49.6 5.0 %collective-permute-start.21 = (bf16[2,128,256]{2,1,0:T(8,128)(2,1)S(1)}, bf16[2,128,256]{2,1,0:T(8,128)(2,1)S(1)}, u32[]{:S(2)}, u32[]{:S(2)}) collective-permute-start(bf16[2,128,256]{2,1,0:T(8,128)(2,1)S(1)} %maximum_select_fusion.4), channel_id=1, source_target_pairs={{0,2},{1,3},{2,0},{3,1},{4,6},{5,7},{6,4},{7,5},{8,10},{9,11},{10,... | collective-permute-start | bytes 393224 | tf_op jit(solution)/shard_map/ppermute | solution.py:20
  51.9 5.7 %collective-permute-start.14 = (bf16[2,288,128]{2,1,0:T(8,128)(2,1)S(1)}, bf16[2,288,128]{2,1,0:T(8,128)(2,1)S(1)}, u32[]{:S(2)}, u32[]{:S(2)}) collective-permute-start(bf16[2,288,128]{2,1,0:T(8,128)(2,1)S(1)} %maximum_select_fusion.1.mine), channel_id=1, source_target_pairs={{0,16},{8,24},{16,0},{24,8},{1,17},{9,25},{17,1},{25,9},{2,18},{10... | collective-permute-start | bytes 442376 | tf_op jit(solution)/shard_map/ppermute | solution.py:20
  54.7 1.9 %collective-permute-start.22 = (bf16[4,128,256]{2,1,0:T(8,128)(2,1)S(1)}, bf16[4,128,256]{2,1,0:T(8,128)(2,1)S(1)}, u32[]{:S(2)}, u32[]{:S(2)}) collective-permute-start(bf16[4,128,256]{2,1,0:T(8,128)(2,1)S(1)} %maximum_select_fusion.mine), channel_id=1, source_target_pairs={{0,8},{8,0},{16,24},{24,16},{1,9},{9,1},{17,25},{25,17},{2,10},{10... | collective-permute-start | bytes 786440 | tf_op jit(solution)/shard_map/ppermute | solution.py:20
  57.7 1.8 %collective-permute-start.23 = (bf16[4,288,128]{2,1,0:T(8,128)(2,1)S(1)}, bf16[4,288,128]{2,1,0:T(8,128)(2,1)S(1)}, u32[]{:S(2)}, u32[]{:S(2)}) collective-permute-start(bf16[4,288,128]{2,1,0:T(8,128)(2,1)S(1)} %join.1.mine), channel_id=1, source_target_pairs={{0,8},{8,0},{16,24},{24,16},{1,9},{9,1},{17,25},{25,17},{2,10},{10... | collective-permute-start | bytes 884744 | tf_op jit(solution)/shard_map/ppermute | solution.py:20

commit v10 on v9

--- a/solution.py
+++ b/solution.py
@@ -229,12 +229,13 @@
 scale_row = gain_row + 1
 
 
-def spread(padded_ref, wide):
+def spread(padded_ref, wide, used=None):
     batch_size, rows, cols, channel_count = padded_ref.shape
     for group in range(channel_count // lane_count):
         lanes = slice(group * lane_count, (group + 1) * lane_count)
         for b in range(batch_size):
-            wide[group, b, :, :cols, :] = padded_ref[b, :, :, lanes].astype(jnp.float32)
+            for r in range(rows) if used is None else used:
+                wide[group, b, r, :cols, :] = padded_ref[b, r, :, lanes].astype(jnp.float32)
 
 
 def stencil(wide, params, group, b, rows, tile_cols, used, first, flipped):
@@ -290,9 +291,9 @@
     cells = smooth.shape[1]
     tile_rows = pad_rows - kernel_side + 1
     tile_cols = pad_cols - kernel_side + 1
-    spread(padded_ref, wide)
     first = kernel_side // 2
     used = [r for r in range(pad_rows) if r < first or r >= first + tile_rows]
+    spread(padded_ref, wide, used)
     for group in range(wide.shape[0]):
         for b in range(batch_size):
             places = [

time: 60.7 us -> 60.7 us (level)
  no operation moved by 1% of the time
where the time goes in v10:
time: 60.7 us; the launch traced here: 60.5 us
  starting transfers between devices  25.5 us (42%)
  waiting for transfers between devices  23.2 us (38%)
  Pallas kernels  7.58 us (12%)
  other arithmetic  1.94 us (3%)
  between operations  1.16 us (2%)
  local copies, waits for them, and re-layouts  1.09 us (2%)
    ppermute x22, starting transfers between devices, swap(): lax.ppermute(value, axis, [(i, i ^ bit) for i in range(lax.axis_size(axis...  20.3 us
    ppermute x22, waiting for transfers between devices, swap(): lax.ppermute(value, axis, [(i, i ^ bit) for i in range(lax.axis_size(axis...  20.1 us
    ppermute x2, starting transfers between devices, swap_outer(): got = lax.ppermute(edge, axis, pairs + [(j, i) for i, j in pairs])  5.15 us
    ppermute x2, waiting for transfers between devices, swap_outer(): got = lax.ppermute(edge, axis, pairs + [(j, i) for i, j in pairs])  3.13 us
    pallas_call x1, Pallas kernels, mlp(): pl.pallas_call(mlp_kernel, in_specs=[pl.BlockSpec(memory_space=pltpu.SMEM...  1.72 us
    pallas_call x1, Pallas kernels, conv_back(): pl.pallas_call(conv_back_kernel, out_shape=(jax.ShapeDtypeStruct(misfit.s...  1.55 us
  transfers between devices with their start and end apart: 24, of which 13 were waited for; matrix products, arithmetic and copies ran while one was open for 2% of the time, Pallas kernels for 8%

profile of v10, /device:TPU:0, one launch (start us, length us, event | category | flops | bytes accessed | tf_op | source)
XLA Modules:
  0.0 60.5 jit_solution(12844294253794814714)
XLA Ops:
  0.7 0.8 %broadcast_select_fusion.14 = (bf16[2,4,3,256]{3,2,1,0:T(4,128)(2,1)S(1)}, bf16[2,4,3,256]{3,2,1,0:T(4,128)(2,1)S(1)}) fusion(pred[]{:T(512)S(6)} %eq.71, bf16[2,4,32,256]{3,2,1,0:T(8,128)(2,1)} %param.7), kind=kLoop, calls=%fused_computation.61 | loop fusion | flops 12288 | bytes 49153 | tf_op jit(solution)/shard_map/jit(_where)/select_n | solution.py:27
  1.5 3.0 %collective-permute-start = (bf16[2,4,3,256]{3,2,1,0:T(4,128)(2,1)S(1)}, bf16[2,4,3,256]{3,2,1,0:T(4,128)(2,1)S(1)}, u32[]{:S(2)}, u32[]{:S(2)}) collective-permute-start(bf16[2,4,3,256]{3,2,1,0:T(4,128)(2,1)S(1)} %get-tuple-element.85), channel_id=1, source_target_pairs={{0,1},{1,0},{2,3},{3,2},{4,5},{5,4},{6,7},{7,6},{8,9},{9,8},{10,11... | collective-permute-start | bytes 36872 | tf_op jit(solution)/shard_map/ppermute | solution.py:20
  4.5 3.5 %collective-permute-start.1 = (bf16[2,4,3,256]{3,2,1,0:T(4,128)(2,1)S(1)}, bf16[2,4,3,256]{3,2,1,0:T(4,128)(2,1)S(1)}, u32[]{:S(2)}, u32[]{:S(2)}) collective-permute-start(bf16[2,4,3,256]{3,2,1,0:T(4,128)(2,1)S(1)} %get-tuple-element.86), channel_id=1, source_target_pairs={{1,2},{3,4},{5,6},{7,0},{2,1},{4,3},{6,5},{0,7},{9,10},{11,12},{13... | collective-permute-start | bytes 36872 | tf_op jit(solution)/shard_map/ppermute | solution.py:33
  8.1 0.7 %copy-done.6 = f32[256]{0:T(256)S(1)} copy-done((f32[256]{0:T(256)S(1)}, f32[256]{0:T(256)}, u32[]{:S(2)}) %copy-start.6) | copy-done | bytes 1048
  9.0 1.6 %collective-permute-start.4 = (bf16[2,2,4,1,8,256]{5,4,2,1,0,3:T(8,128)(2,1)S(1)}, bf16[2,2,4,1,8,256]{5,4,2,1,0,3:T(8,128)(2,1)S(1)}, u32[]{:S(2)}, u32[]{:S(2)}) collective-permute-start(bf16[2,2,4,1,8,256]{5,4,2,1,0,3:T(8,128)(2,1)S(1)} %get-tuple-element.83), channel_id=1, source_target_pairs={{0,16},{8,24},{16,0},{24,8},{1,17},{9,25},{17,1},{25,9},{2,18},{10... | collective-permute-start | bytes 196616 | tf_op jit(solution)/shard_map/ppermute | solution.py:20
  11.2 1.6 %collective-permute-start.3 = (bf16[2,3,38,256]{3,2,1,0:T(8,128)(2,1)S(1)}, bf16[2,3,38,256]{3,2,1,0:T(8,128)(2,1)S(1)}, u32[]{:S(2)}, u32[]{:S(2)}) collective-permute-start(bf16[2,3,38,256]{3,2,1,0:T(8,128)(2,1)S(1)} %get-tuple-element.77), channel_id=1, source_target_pairs={{8,16},{24,0},{16,8},{0,24},{9,17},{25,1},{17,9},{1,25},{10,18},{2... | collective-permute-start | bytes 350216 | tf_op jit(solution)/shard_map/ppermute | solution.py:33
  12.8 0.5 conv_own.1.own_ref
  13.5 2.8 %collective-permute-done.3 = bf16[2,3,38,256]{3,2,1,0:T(8,128)(2,1)S(1)} collective-permute-done((bf16[2,3,38,256]{3,2,1,0:T(8,128)(2,1)S(1)}, bf16[2,3,38,256]{3,2,1,0:T(8,128)(2,1)S(1)}, u32[]{:S(2)}, u32[]{:S(2)}) %collective-permute-start.3) | collective-permute-done | bytes 116768 | tf_op jit(solution)/shard_map/ppermute | solution.py:33
  16.4 0.7 %conv_norm.1 = (bf16[256,256]{1,0:T(8,128)(2,1)S(1)}, f32[256,256]{1,0:T(8,128)S(1)}, f32[256,1]{1,0:T(8,128)S(1)}) custom-call(f32[2,256,128]{2,1,0:T(8,128)S(1)} %conv_own.1.own_ref, bf16[2,10,38,256]{3,2,1,0:T(8,128)(2,1)S(1)} %pad_maximum_fusion.padded_ref, f32[51,256]{1,0:T(8,128)S(1)} %pad_maximum_fusion.8.params_ref), custom_call_target="tpu_custom_call" | custom-call | flops 6422528 | bytes 1048576 | tf_op jit(solution)/shard_map/conv_norm/pallas_call | solution.py:334
  17.1 1.7 %mlp.1 = (f32[256,256]{1,0:T(8,128)S(1)}, bf16[256,256]{1,0:T(8,128)(2,1)S(1)}, bf16[512,256]{1,0:T(8,128)(2,1)S(1)}, f32[512,256]{1,0:T(8,128)S(1)}, bf16[512,2...) custom-call(s32[1]{0:T(128)} %bitcast.side_ref, bf16[256,256]{1,0:T(8,128)(2,1)S(1)} %get-tuple-element.32.normed_ref, ...), custom_call_target="tpu_custom_call" | custom-call | flops 805306368 | bytes 4194304 | tf_op jit(solution)/shard_map/mlp/pallas_call | solution.py:620
  19.9 1.0 %tap_sums.1 = f32[64,256]{1,0:T(8,128)S(1)} custom-call(bf16[2,10,38,256]{3,2,1,0:T(8,128)(2,1)S(1)} %pad_maximum_fusion.padded_ref, bf16[2,4,32,256]{3,2,1,0:T(8,128)(2,1)S(1)} %bitcast.30), custom_call_target="tpu_custom_call" | custom-call | flops 6422528 | bytes 1048576 | tf_op jit(solution)/shard_map/tap_sums/pallas_call | solution.py:425
  21.1 1.6 %collective-permute-start.8 = (bf16[480,256]{1,0:T(8,128)(2,1)S(1)}, bf16[480,256]{1,0:T(8,128)(2,1)S(1)}, u32[]{:S(2)}, u32[]{:S(2)}) collective-permute-start(bf16[480,256]{1,0:T(8,128)(2,1)S(1)} %pad_maximum_fusion.2), channel_id=1, source_target_pairs={{0,16},{8,24},{16,0},{24,8},{1,17},{9,25},{17,1},{25,9},{2,18},{10... | collective-permute-start | bytes 737288 | tf_op jit(solution)/shard_map/ppermute | solution.py:20
  22.7 3.8 %collective-permute-done.16 = bf16[256,256]{1,0:T(8,128)(2,1)S(1)} collective-permute-done((bf16[256,256]{1,0:T(8,128)(2,1)S(1)}, bf16[256,256]{1,0:T(8,128)(2,1)S(1)}, u32[]{:S(2)}, u32[]{:S(2)}) %collective-permute-start.16) | collective-permute-done | bytes 131104 | tf_op jit(solution)/shard_map/ppermute | solution.py:20
  26.6 0.9 %collective-permute-start.17 = (bf16[128,256]{1,0:T(8,128)(2,1)S(1)}, bf16[128,256]{1,0:T(8,128)(2,1)S(1)}, u32[]{:S(2)}, u32[]{:S(2)}) collective-permute-start(bf16[128,256]{1,0:T(8,128)(2,1)S(1)} %get-tuple-element.69), channel_id=1, source_target_pairs={{0,4},{1,5},{2,6},{3,7},{4,0},{5,1},{6,2},{7,3},{8,12},{9,13},{10,... | collective-permute-start | bytes 196616 | tf_op jit(solution)/shard_map/ppermute | solution.py:20
  27.4 1.8 %collective-permute-done.8 = bf16[480,256]{1,0:T(8,128)(2,1)S(1)} collective-permute-done((bf16[480,256]{1,0:T(8,128)(2,1)S(1)}, bf16[480,256]{1,0:T(8,128)(2,1)S(1)}, u32[]{:S(2)}, u32[]{:S(2)}) %collective-permute-start.8) | collective-permute-done | bytes 245792 | tf_op jit(solution)/shard_map/ppermute | solution.py:20
  30.0 2.2 %collective-permute-done.17 = bf16[128,256]{1,0:T(8,128)(2,1)S(1)} collective-permute-done((bf16[128,256]{1,0:T(8,128)(2,1)S(1)}, bf16[128,256]{1,0:T(8,128)(2,1)S(1)}, u32[]{:S(2)}, u32[]{:S(2)}) %collective-permute-start.17) | collective-permute-done | bytes 65568 | tf_op jit(solution)/shard_map/ppermute | solution.py:20
  32.2 1.6 %collective-permute-start.18 = (f32[128,256]{1,0:T(8,128)S(1)}, f32[128,256]{1,0:T(8,128)S(1)}, u32[]{:S(2)}, u32[]{:S(2)}) collective-permute-start(f32[128,256]{1,0:T(8,128)S(1)} %convert_add_fusion.2), channel_id=1, source_target_pairs={{0,16},{8,24},{16,0},{24,8},{1,17},{9,25},{17,1},{25,9},{2,18},{10... | collective-permute-start | bytes 393224 | tf_op jit(solution)/shard_map/ppermute | solution.py:20
  33.8 0.9 %collective-permute-done.10 = bf16[264,256]{1,0:T(8,128)(2,1)S(1)} collective-permute-done((bf16[264,256]{1,0:T(8,128)(2,1)S(1)}, bf16[264,256]{1,0:T(8,128)(2,1)S(1)}, u32[]{:S(2)}, u32[]{:S(2)}) %collective-permute-start.10) | collective-permute-done | bytes 135200 | tf_op jit(solution)/shard_map/ppermute | solution.py:20
  34.8 1.7 %collective-permute-start.11 = (f32[204,256]{1,0:T(8,128)S(1)}, f32[204,256]{1,0:T(8,128)S(1)}, u32[]{:S(2)}, u32[]{:S(2)}) collective-permute-start(f32[204,256]{1,0:T(8,128)S(1)} %pad_maximum_fusion.3), channel_id=1, source_target_pairs={{0,2},{1,3},{2,0},{3,1},{4,6},{5,7},{6,4},{7,5},{8,10},{9,11},{10,... | collective-permute-start | bytes 626696 | tf_op jit(solution)/shard_map/ppermute | solution.py:20
  36.5 0.7 %collective-permute-done.18 = f32[128,256]{1,0:T(8,128)S(1)} collective-permute-done((f32[128,256]{1,0:T(8,128)S(1)}, f32[128,256]{1,0:T(8,128)S(1)}, u32[]{:S(2)}, u32[]{:S(2)}) %collective-permute-start.18) | collective-permute-done | bytes 131104 | tf_op jit(solution)/shard_map/ppermute | solution.py:20
  37.4 3.3 %collective-permute-done.11 = f32[204,256]{1,0:T(8,128)S(1)} collective-permute-done((f32[204,256]{1,0:T(8,128)S(1)}, f32[204,256]{1,0:T(8,128)S(1)}, u32[]{:S(2)}, u32[]{:S(2)}) %collective-permute-start.11) | collective-permute-done | bytes 208928 | tf_op jit(solution)/shard_map/ppermute | solution.py:20
  40.8 2.6 %collective-permute-start.12 = (bf16[204,256]{1,0:T(8,128)(2,1)S(1)}, bf16[204,256]{1,0:T(8,128)(2,1)S(1)}, u32[]{:S(2)}, u32[]{:S(2)}) collective-permute-start(bf16[204,256]{1,0:T(8,128)(2,1)S(1)} %pad_maximum_fusion.6), channel_id=1, source_target_pairs={{0,4},{1,5},{2,6},{3,7},{4,0},{5,1},{6,2},{7,3},{8,12},{9,13},{10,... | collective-permute-start | bytes 313352 | tf_op jit(solution)/shard_map/ppermute | solution.py:20
  43.9 2.6 %collective-permute-done.12.got_ref = bf16[204,256]{1,0:T(8,128)(2,1)S(1)} collective-permute-done((bf16[204,256]{1,0:T(8,128)(2,1)S(1)}, bf16[204,256]{1,0:T(8,128)(2,1)S(1)}, u32[]{:S(2)}, u32[]{:S(2)}) %collective-permute-start.12) | collective-permute-done | bytes 104480 | tf_op jit(solution)/shard_map/ppermute | solution.py:20
  46.6 3.0 %collective-permute-start.13 = (bf16[1,288,128]{2,1,0:T(8,128)(2,1)S(1)}, bf16[1,288,128]{2,1,0:T(8,128)(2,1)S(1)}, u32[]{:S(2)}, u32[]{:S(2)}) collective-permute-start(bf16[1,288,128]{2,1,0:T(8,128)(2,1)S(1)} %finish_columns.1._), channel_id=1, source_target_pairs={{0,1},{1,0},{2,3},{3,2},{4,5},{5,4},{6,7},{7,6},{8,9},{9,8},{10,11... | collective-permute-start | bytes 221192 | tf_op jit(solution)/shard_map/ppermute | solution.py:20
  49.7 2.2 %collective-permute-done.13 = bf16[1,288,128]{2,1,0:T(8,128)(2,1)S(1)} collective-permute-done((bf16[1,288,128]{2,1,0:T(8,128)(2,1)S(1)}, bf16[1,288,128]{2,1,0:T(8,128)(2,1)S(1)}, u32[]{:S(2)}, u32[]{:S(2)}) %collective-permute-start.13) | collective-permute-done | bytes 73760 | tf_op jit(solution)/shard_map/ppermute | solution.py:20
  51.9 1.6 %collective-permute-start.14 = (bf16[2,288,128]{2,1,0:T(8,128)(2,1)S(1)}, bf16[2,288,128]{2,1,0:T(8,128)(2,1)S(1)}, u32[]{:S(2)}, u32[]{:S(2)}) collective-permute-start(bf16[2,288,128]{2,1,0:T(8,128)(2,1)S(1)} %maximum_select_fusion.1.mine), channel_id=1, source_target_pairs={{0,16},{8,24},{16,0},{24,8},{1,17},{9,25},{17,1},{25,9},{2,18},{10... | collective-permute-start | bytes 442376 | tf_op jit(solution)/shard_map/ppermute | solution.py:20
  53.5 1.1 %collective-permute-done.21 = bf16[2,128,256]{2,1,0:T(8,128)(2,1)S(1)} collective-permute-done((bf16[2,128,256]{2,1,0:T(8,128)(2,1)S(1)}, bf16[2,128,256]{2,1,0:T(8,128)(2,1)S(1)}, u32[]{:S(2)}, u32[]{:S(2)}) %collective-permute-start.21) | collective-permute-done | bytes 131104 | tf_op jit(solution)/shard_map/ppermute | solution.py:20
  55.1 1.5 %conv_back.1 = (bf16[2,4,32,256]{3,2,1,0:T(8,128)(2,1)}, f32[8,128]{1,0:T(8,128)S(1)}) custom-call(bf16[2,10,38,256]{3,2,1,0:T(8,128)(2,1)S(1)} %pad_maximum_fusion.1.padded_ref, f32[51,256]{1,0:T(8,128)S(1)} %pad_maximum_fusion.8.params_ref, f32[2,4,32,256]{3,2,1,0:T(8,128)S(1)} %bitcast.33, bf16[1,288,128]{2,1,0:T(8,128)(2,1)S(1)} %finish_columns.1._), custom_call_target="tpu_custom_call" | custom-call | flops 6422528 | bytes 1048576 | tf_op jit(solution)/shard_map/conv_back/pallas_call | solution.py:374
  56.6 1.0 %assemble_rows.1 = (f32[1024,256]{1,0:T(8,128)}, f32[8,128]{1,0:T(8,128)S(1)}) custom-call(s32[1]{0:T(128)} %bitcast.side_ref, bf16[4,128,256]{2,1,0:T(8,128)(2,1)S(1)} %maximum_select_fusion.mine, bf16[4,128,256]{2,1,0:T(8,128)(2,1)S(1)} %collective-permute-done.22.got, f32[8,128]{1,0:T(8,128)S(1)} %get-tuple-element.51._), custom_call_target="tpu_custom_call" | custom-call | bytes 1572864 | tf_op jit(solution)/shard_map/assemble_rows/pallas_call | solution.py:485
  57.7 0.6 collective-permute-start.23
  58.2 1.2 %collective-permute-done.23.got = bf16[4,288,128]{2,1,0:T(8,128)(2,1)S(1)} collective-permute-done((bf16[4,288,128]{2,1,0:T(8,128)(2,1)S(1)}, bf16[4,288,128]{2,1,0:T(8,128)(2,1)S(1)}, u32[]{:S(2)}, u32[]{:S(2)}) %collective-permute-start.23) | collective-permute-done | bytes 294944 | tf_op jit(solution)/shard_map/ppermute | solution.py:20
  59.4 1.1 %assemble_columns.1 = (f32[256,1024]{1,0:T(8,128)}, f32[7,7,256]{2,1,0:T(8,128)}) custom-call(s32[1]{0:T(128)} %bitcast.side_ref, bf16[4,288,128]{2,1,0:T(8,128)(2,1)S(1)} %join.1.mine, bf16[4,288,128]{2,1,0:T(8,128)(2,1)S(1)} %collective-permute-done.23.got), custom_call_target="tpu_custom_call" | custom-call | bytes 1572864 | tf_op jit(solution)/shard_map/assemble_columns/pallas_call | solution.py:500
  (89 shorter events, 4.5 us)
Async XLA Ops:
  0.6 7.4 %copy-start.4 = (f32[7,7,256]{2,1,0:T(8,128)S(1)}, f32[7,7,256]{2,1,0:T(8,128)}, u32[]{:S(2)}) copy-start(f32[7,7,256]{2,1,0:T(8,128)} %param.9) | copy-start | bytes 150532
  1.5 9.1 %collective-permute-start = (bf16[2,4,3,256]{3,2,1,0:T(4,128)(2,1)S(1)}, bf16[2,4,3,256]{3,2,1,0:T(4,128)(2,1)S(1)}, u32[]{:S(2)}, u32[]{:S(2)}) collective-permute-start(bf16[2,4,3,256]{3,2,1,0:T(4,128)(2,1)S(1)} %get-tuple-element.85), channel_id=1, source_target_pairs={{0,1},{1,0},{2,3},{3,2},{4,5},{5,4},{6,7},{7,6},{8,9},{9,8},{10,11... | collective-permute-start | bytes 36872 | tf_op jit(solution)/shard_map/ppermute | solution.py:20
  4.5 6.4 %collective-permute-start.1 = (bf16[2,4,3,256]{3,2,1,0:T(4,128)(2,1)S(1)}, bf16[2,4,3,256]{3,2,1,0:T(4,128)(2,1)S(1)}, u32[]{:S(2)}, u32[]{:S(2)}) collective-permute-start(bf16[2,4,3,256]{3,2,1,0:T(4,128)(2,1)S(1)} %get-tuple-element.86), channel_id=1, source_target_pairs={{1,2},{3,4},{5,6},{7,0},{2,1},{4,3},{6,5},{0,7},{9,10},{11,12},{13... | collective-permute-start | bytes 36872 | tf_op jit(solution)/shard_map/ppermute | solution.py:33
  8.1 0.9 %copy-start.3 = (bf16[2,16,8,256]{3,2,1,0:T(8,128)(2,1)S(1)}, bf16[2,16,8,256]{3,2,1,0:T(8,128)(2,1)}, u32[]{:S(2)}) copy-start(bf16[2,16,8,256]{3,2,1,0:T(8,128)(2,1)} %param.8) | copy-start | bytes 393220
  8.1 0.7 %copy-start.6 = (f32[256]{0:T(256)S(1)}, f32[256]{0:T(256)}, u32[]{:S(2)}) copy-start(f32[256]{0:T(256)} %param.10) | copy-start | bytes 3076
  8.1 0.7 %copy-start.5 = (f32[256]{0:T(256)S(1)}, f32[256]{0:T(256)}, u32[]{:S(2)}) copy-start(f32[256]{0:T(256)} %param.13) | copy-start | bytes 3076
  8.8 2.2 %copy-start.2 = (bf16[2,4,32,256]{3,2,1,0:T(8,128)(2,1)S(1)}, bf16[2,4,32,256]{3,2,1,0:T(8,128)(2,1)}, u32[]{:S(2)}) copy-start(bf16[2,4,32,256]{3,2,1,0:T(8,128)(2,1)} %param.7) | copy-start | bytes 393220
  9.0 3.8 %copy-start.1 = (bf16[1024,256]{1,0:T(8,128)(2,1)S(1)}, bf16[1024,256]{1,0:T(8,128)(2,1)}, u32[]{:S(2)}) copy-start(bf16[1024,256]{1,0:T(8,128)(2,1)} %w_out_ref.1) | copy-start | bytes 1572868
  9.0 3.8 %copy-start = (bf16[256,1024]{1,0:T(8,128)(2,1)S(1)}, bf16[256,1024]{1,0:T(8,128)(2,1)}, u32[]{:S(2)}) copy-start(bf16[256,1024]{1,0:T(8,128)(2,1)} %w_in_ref.1) | copy-start | bytes 1572868
  9.0 4.3 %collective-permute-start.4 = (bf16[2,2,4,1,8,256]{5,4,2,1,0,3:T(8,128)(2,1)S(1)}, bf16[2,2,4,1,8,256]{5,4,2,1,0,3:T(8,128)(2,1)S(1)}, u32[]{:S(2)}, u32[]{:S(2)}) collective-permute-start(bf16[2,2,4,1,8,256]{5,4,2,1,0,3:T(8,128)(2,1)S(1)} %get-tuple-element.83), channel_id=1, source_target_pairs={{0,16},{8,24},{16,0},{24,8},{1,17},{9,25},{17,1},{25,9},{2,18},{10... | collective-permute-start | bytes 196616 | tf_op jit(solution)/shard_map/ppermute | solution.py:20
  11.1 2.4 %collective-permute-start.2 = (bf16[2,3,38,256]{3,2,1,0:T(8,128)(2,1)S(1)}, bf16[2,3,38,256]{3,2,1,0:T(8,128)(2,1)S(1)}, u32[]{:S(2)}, u32[]{:S(2)}) collective-permute-start(bf16[2,3,38,256]{3,2,1,0:T(8,128)(2,1)S(1)} %get-tuple-element.78), channel_id=1, source_target_pairs={{0,8},{8,0},{16,24},{24,16},{1,9},{9,1},{17,25},{25,17},{2,10},{10... | collective-permute-start | bytes 350216 | tf_op jit(solution)/shard_map/ppermute | solution.py:20
  11.2 5.1 %collective-permute-start.3 = (bf16[2,3,38,256]{3,2,1,0:T(8,128)(2,1)S(1)}, bf16[2,3,38,256]{3,2,1,0:T(8,128)(2,1)S(1)}, u32[]{:S(2)}, u32[]{:S(2)}) collective-permute-start(bf16[2,3,38,256]{3,2,1,0:T(8,128)(2,1)S(1)} %get-tuple-element.77), channel_id=1, source_target_pairs={{8,16},{24,0},{16,8},{0,24},{9,17},{25,1},{17,9},{1,25},{10,18},{2... | collective-permute-start | bytes 350216 | tf_op jit(solution)/shard_map/ppermute | solution.py:33
  13.4 3.6 %collective-permute-start.5 = (bf16[2,1,4,2,8,256]{5,4,3,2,0,1:T(8,128)(2,1)S(1)}, bf16[2,1,4,2,8,256]{5,4,3,2,0,1:T(8,128)(2,1)S(1)}, u32[]{:S(2)}, u32[]{:S(2)}) collective-permute-start(bf16[2,1,4,2,8,256]{5,4,3,2,0,1:T(8,128)(2,1)S(1)} %bitcast.40), channel_id=1, source_target_pairs={{0,8},{8,0},{16,24},{24,16},{1,9},{9,1},{17,25},{25,17},{2,10},{10... | collective-permute-start | bytes 196616 | tf_op jit(solution)/shard_map/ppermute | solution.py:20
  18.8 2.0 %collective-permute-start.15 = (bf16[512,256]{1,0:T(8,128)(2,1)S(1)}, bf16[512,256]{1,0:T(8,128)(2,1)S(1)}, u32[]{:S(2)}, u32[]{:S(2)}) collective-permute-start(bf16[512,256]{1,0:T(8,128)(2,1)S(1)} %get-tuple-element.42), channel_id=1, source_target_pairs={{0,8},{8,0},{16,24},{24,16},{1,9},{9,1},{17,25},{25,17},{2,10},{10... | collective-permute-start | bytes 786440 | tf_op jit(solution)/shard_map/ppermute | solution.py:20
  19.3 1.8 %collective-permute-start.6 = (bf16[512,256]{1,0:T(8,128)(2,1)S(1)}, bf16[512,256]{1,0:T(8,128)(2,1)S(1)}, u32[]{:S(2)}, u32[]{:S(2)}) collective-permute-start(bf16[512,256]{1,0:T(8,128)(2,1)S(1)} %get-tuple-element.37), channel_id=1, source_target_pairs={{0,8},{8,0},{16,24},{24,16},{1,9},{9,1},{17,25},{25,17},{2,10},{10... | collective-permute-start | bytes 786440 | tf_op jit(solution)/shard_map/ppermute | solution.py:20
  19.4 1.7 %collective-permute-start.7 = (bf16[2,3,32,256]{3,2,1,0:T(8,128)(2,1)S(1)}, bf16[2,3,32,256]{3,2,1,0:T(8,128)(2,1)S(1)}, u32[]{:S(2)}, u32[]{:S(2)}) collective-permute-start(bf16[2,3,32,256]{3,2,1,0:T(8,128)(2,1)S(1)} %get-tuple-element.79), channel_id=1, source_target_pairs={{0,8},{8,0},{16,24},{24,16},{1,9},{9,1},{17,25},{25,17},{2,10},{10... | collective-permute-start | bytes 294920 | tf_op jit(solution)/shard_map/ppermute | solution.py:20
  20.9 5.6 %collective-permute-start.16 = (bf16[256,256]{1,0:T(8,128)(2,1)S(1)}, bf16[256,256]{1,0:T(8,128)(2,1)S(1)}, u32[]{:S(2)}, u32[]{:S(2)}) collective-permute-start(bf16[256,256]{1,0:T(8,128)(2,1)S(1)} %get-tuple-element.65), channel_id=1, source_target_pairs={{0,2},{1,3},{2,0},{3,1},{4,6},{5,7},{6,4},{7,5},{8,10},{9,11},{10,... | collective-permute-start | bytes 393224 | tf_op jit(solution)/shard_map/ppermute | solution.py:20
  21.1 8.1 %collective-permute-start.8 = (bf16[480,256]{1,0:T(8,128)(2,1)S(1)}, bf16[480,256]{1,0:T(8,128)(2,1)S(1)}, u32[]{:S(2)}, u32[]{:S(2)}) collective-permute-start(bf16[480,256]{1,0:T(8,128)(2,1)S(1)} %pad_maximum_fusion.2), channel_id=1, source_target_pairs={{0,16},{8,24},{16,0},{24,8},{1,17},{9,25},{17,1},{25,9},{2,18},{10... | collective-permute-start | bytes 737288 | tf_op jit(solution)/shard_map/ppermute | solution.py:20
  22.7 6.6 %collective-permute-start.9 = (bf16[2,3,32,256]{3,2,1,0:T(8,128)(2,1)S(1)}, bf16[2,3,32,256]{3,2,1,0:T(8,128)(2,1)S(1)}, u32[]{:S(2)}, u32[]{:S(2)}) collective-permute-start(bf16[2,3,32,256]{3,2,1,0:T(8,128)(2,1)S(1)} %get-tuple-element.80), channel_id=1, source_target_pairs={{0,8},{8,0},{16,24},{24,16},{1,9},{9,1},{17,25},{25,17},{2,10},{10... | collective-permute-start | bytes 294920 | tf_op jit(solution)/shard_map/ppermute | solution.py:20
  26.6 5.7 %collective-permute-start.17 = (bf16[128,256]{1,0:T(8,128)(2,1)S(1)}, bf16[128,256]{1,0:T(8,128)(2,1)S(1)}, u32[]{:S(2)}, u32[]{:S(2)}) collective-permute-start(bf16[128,256]{1,0:T(8,128)(2,1)S(1)} %get-tuple-element.69), channel_id=1, source_target_pairs={{0,4},{1,5},{2,6},{3,7},{4,0},{5,1},{6,2},{7,3},{8,12},{9,13},{10,... | collective-permute-start | bytes 196616 | tf_op jit(solution)/shard_map/ppermute | solution.py:20
  29.6 5.1 %collective-permute-start.10 = (bf16[264,256]{1,0:T(8,128)(2,1)S(1)}, bf16[264,256]{1,0:T(8,128)(2,1)S(1)}, u32[]{:S(2)}, u32[]{:S(2)}) collective-permute-start(bf16[264,256]{1,0:T(8,128)(2,1)S(1)} %pad_maximum_fusion.5), channel_id=1, source_target_pairs={{0,1},{1,0},{2,3},{3,2},{4,5},{5,4},{6,7},{7,6},{8,9},{9,8},{10,11... | collective-permute-start | bytes 405512 | tf_op jit(solution)/shard_map/ppermute | solution.py:20
  32.2 5.0 %collective-permute-start.18 = (f32[128,256]{1,0:T(8,128)S(1)}, f32[128,256]{1,0:T(8,128)S(1)}, u32[]{:S(2)}, u32[]{:S(2)}) collective-permute-start(f32[128,256]{1,0:T(8,128)S(1)} %convert_add_fusion.2), channel_id=1, source_target_pairs={{0,16},{8,24},{16,0},{24,8},{1,17},{9,25},{17,1},{25,9},{2,18},{10... | collective-permute-start | bytes 393224 | tf_op jit(solution)/shard_map/ppermute | solution.py:20
  34.8 5.9 %collective-permute-start.11 = (f32[204,256]{1,0:T(8,128)S(1)}, f32[204,256]{1,0:T(8,128)S(1)}, u32[]{:S(2)}, u32[]{:S(2)}) collective-permute-start(f32[204,256]{1,0:T(8,128)S(1)} %pad_maximum_fusion.3), channel_id=1, source_target_pairs={{0,2},{1,3},{2,0},{3,1},{4,6},{5,7},{6,4},{7,5},{8,10},{9,11},{10,... | collective-permute-start | bytes 626696 | tf_op jit(solution)/shard_map/ppermute | solution.py:20
  37.3 6.1 %collective-permute-start.19 = (bf16[128,256]{1,0:T(8,128)(2,1)S(1)}, bf16[128,256]{1,0:T(8,128)(2,1)S(1)}, u32[]{:S(2)}, u32[]{:S(2)}) collective-permute-start(bf16[128,256]{1,0:T(8,128)(2,1)S(1)} %get-tuple-element.57), channel_id=1, source_target_pairs={{0,1},{1,0},{2,3},{3,2},{4,5},{5,4},{6,7},{7,6},{8,9},{9,8},{10,11... | collective-permute-start | bytes 196616 | tf_op jit(solution)/shard_map/ppermute | solution.py:20
  40.8 5.7 %collective-permute-start.12 = (bf16[204,256]{1,0:T(8,128)(2,1)S(1)}, bf16[204,256]{1,0:T(8,128)(2,1)S(1)}, u32[]{:S(2)}, u32[]{:S(2)}) collective-permute-start(bf16[204,256]{1,0:T(8,128)(2,1)S(1)} %pad_maximum_fusion.6), channel_id=1, source_target_pairs={{0,4},{1,5},{2,6},{3,7},{4,0},{5,1},{6,2},{7,3},{8,12},{9,13},{10,... | collective-permute-start | bytes 313352 | tf_op jit(solution)/shard_map/ppermute | solution.py:20
  43.4 6.2 %collective-permute-start.20 = (bf16[1,128,256]{2,1,0:T(8,128)(2,1)S(1)}, bf16[1,128,256]{2,1,0:T(8,128)(2,1)S(1)}, u32[]{:S(2)}, u32[]{:S(2)}) collective-permute-start(bf16[1,128,256]{2,1,0:T(8,128)(2,1)S(1)} %fusion.1), channel_id=1, source_target_pairs={{0,4},{1,5},{2,6},{3,7},{4,0},{5,1},{6,2},{7,3},{8,12},{9,13},{10,... | collective-permute-start | bytes 196616 | tf_op jit(solution)/shard_map/ppermute | solution.py:20
  46.6 5.3 %collective-permute-start.13 = (bf16[1,288,128]{2,1,0:T(8,128)(2,1)S(1)}, bf16[1,288,128]{2,1,0:T(8,128)(2,1)S(1)}, u32[]{:S(2)}, u32[]{:S(2)}) collective-permute-start(bf16[1,288,128]{2,1,0:T(8,128)(2,1)S(1)} %finish_columns.1._), channel_id=1, source_target_pairs={{0,1},{1,0},{2,3},{3,2},{4,5},{5,4},{6,7},{7,6},{8,9},{9,8},{10,11... | collective-permute-start | bytes 221192 | tf_op jit(solution)/shard_map/ppermute | solution.py:20
  49.6 5.0 %collective-permute-start.21 = (bf16[2,128,256]{2,1,0:T(8,128)(2,1)S(1)}, bf16[2,128,256]{2,1,0:T(8,128)(2,1)S(1)}, u32[]{:S(2)}, u32[]{:S(2)}) collective-permute-start(bf16[2,128,256]{2,1,0:T(8,128)(2,1)S(1)} %maximum_select_fusion.4), channel_id=1, source_target_pairs={{0,2},{1,3},{2,0},{3,1},{4,6},{5,7},{6,4},{7,5},{8,10},{9,11},{10,... | collective-permute-start | bytes 393224 | tf_op jit(solution)/shard_map/ppermute | solution.py:20
  51.9 5.7 %collective-permute-start.14 = (bf16[2,288,128]{2,1,0:T(8,128)(2,1)S(1)}, bf16[2,288,128]{2,1,0:T(8,128)(2,1)S(1)}, u32[]{:S(2)}, u32[]{:S(2)}) collective-permute-start(bf16[2,288,128]{2,1,0:T(8,128)(2,1)S(1)} %maximum_select_fusion.1.mine), channel_id=1, source_target_pairs={{0,16},{8,24},{16,0},{24,8},{1,17},{9,25},{17,1},{25,9},{2,18},{10... | collective-permute-start | bytes 442376 | tf_op jit(solution)/shard_map/ppermute | solution.py:20
  54.7 1.9 %collective-permute-start.22 = (bf16[4,128,256]{2,1,0:T(8,128)(2,1)S(1)}, bf16[4,128,256]{2,1,0:T(8,128)(2,1)S(1)}, u32[]{:S(2)}, u32[]{:S(2)}) collective-permute-start(bf16[4,128,256]{2,1,0:T(8,128)(2,1)S(1)} %maximum_select_fusion.mine), channel_id=1, source_target_pairs={{0,8},{8,0},{16,24},{24,16},{1,9},{9,1},{17,25},{25,17},{2,10},{10... | collective-permute-start | bytes 786440 | tf_op jit(solution)/shard_map/ppermute | solution.py:20
  57.7 1.8 %collective-permute-start.23 = (bf16[4,288,128]{2,1,0:T(8,128)(2,1)S(1)}, bf16[4,288,128]{2,1,0:T(8,128)(2,1)S(1)}, u32[]{:S(2)}, u32[]{:S(2)}) collective-permute-start(bf16[4,288,128]{2,1,0:T(8,128)(2,1)S(1)} %join.1.mine), channel_id=1, source_target_pairs={{0,8},{8,0},{16,24},{24,16},{1,9},{9,1},{17,25},{25,17},{2,10},{10... | collective-permute-start | bytes 884744 | tf_op jit(solution)/shard_map/ppermute | solution.py:20
